TPU v7x, 32 devices: a whole 2x2x4 slice. The times are simulated.
32 devices in a mesh: band: 16 (over z, y, x), grp: 2 (over core).
Axes of the slice: x: 2, y: 2, z: 4, core: 2. Of those that a mesh axis runs over, the one named last changes fastest.
Arguments:
- tokens: bfloat16 [2, 2048, 1024], P('grp', 'band'), may hold values from -6 to 6
- segment_ids: int32 [2, 2048], P('grp', 'band'), may hold values from 0 to 3, as said below
- lead_index: int32 [2, 4], P('grp'), may hold values from 0 to 15
- lead_table: bfloat16 [16, 1024], P(None, ('band', 'grp')), may hold values from -3 to 3
- ln1_gain: bfloat16 [1024], P(('band', 'grp')), may hold values from 0.25 to 1.75
- ln1_bias: bfloat16 [1024], P(('band', 'grp')), may hold values from -1.5 to 1.5
- qkv_weight: bfloat16 [1024, 3072], P(('band', 'grp')), may hold values from -0.25 to 0.25
- q_bias: bfloat16 [1024], P(('band', 'grp')), may hold values from -1.5 to 1.5
- v_bias: bfloat16 [1024], P(('band', 'grp')), may hold values from -1.5 to 1.5
- out_weight: bfloat16 [1024, 1024], P(('band', 'grp')), may hold values from -0.75 to 0.75
- out_bias: bfloat16 [1024], P(('band', 'grp')), may hold values from -1 to 1
- ln2_gain: bfloat16 [1024], P(('band', 'grp')), may hold values from 0.25 to 1.75
- ln2_bias: bfloat16 [1024], P(('band', 'grp')), may hold values from -1.5 to 1.5
- up_weight: bfloat16 [1024, 4096], P(('band', 'grp')), may hold values from -0.1875 to 0.1875
- up_bias: bfloat16 [4096], P(('band', 'grp')), may hold values from -2.5 to 2.5
- down_weight: bfloat16 [4096, 1024], P(('band', 'grp')), may hold values from -0.125 to 0.125
- down_bias: bfloat16 [1024], P(('band', 'grp')), may hold values from -1 to 1
- d_out: bfloat16 [2, 2048, 1024], P('grp', 'band'), may hold values from -6 to 6
Outputs:
- layer_out: bfloat16 [2, 2048, 1024], P('grp', 'band')
- d_tokens: float32 [2, 2048, 1024], P('grp', 'band')
- d_lead_table: float32 [16, 1024], P(None, ('band', 'grp'))
- d_ln1_gain: float32 [1024], P(('band', 'grp'))
- d_ln1_bias: float32 [1024], P(('band', 'grp'))
- d_qkv_weight: float32 [1024, 3072], P(('band', 'grp'))
- d_q_bias: float32 [1024], P(('band', 'grp'))
- d_v_bias: float32 [1024], P(('band', 'grp'))
- d_out_weight: float32 [1024, 1024], P(('band', 'grp'))
- d_out_bias: float32 [1024], P(('band', 'grp'))
- d_ln2_gain: float32 [1024], P(('band', 'grp'))
- d_ln2_bias: float32 [1024], P(('band', 'grp'))
- d_up_weight: float32 [1024, 4096], P(('band', 'grp'))
- d_up_bias: float32 [4096], P(('band', 'grp'))
- d_down_weight: float32 [4096, 1024], P(('band', 'grp'))
- d_down_bias: float32 [1024], P(('band', 'grp'))
Inputs may be any that keep to these rules, and one draw needn't show every extreme that they name: `segment_ids`: A group holds either one sample (every id 0) or 4 samples; each of the 4 samples fills one equal run of 32 rows of every device's 128 rows, the runs holding the ids in an order drawn from the seed for each group; every latitude band of a group holds the same ids in the same order; max(1, 0) groups, which ones drawn from the seed, hold one sample.
All inputs are finite; a program needn't handle non-finite values.
Results may differ from a plain program's by a relative error of at most 0.017.
Values may be sent and summed in bfloat16 or wider, within the bound.
No kernel may reach another device: no remote copies, remote signals or barrier semaphores. Data moves between devices by JAX's collectives and lax.ppermute only.
A program may use at most 192 MiB of HBM per device.

v0:
```python
import math

import jax
import jax.numpy as jnp
from jax import lax
from jax.sharding import PartitionSpec as P

HEADS = 16


epsilon = 1e-05
score_scale = 0.125
masked_score = -1e30


def norm_rows(values, norm_gain, norm_bias):
    row_mean = jnp.mean(values, -1, keepdims=True)
    centred = values - row_mean
    row_var = jnp.mean(centred * centred, -1, keepdims=True)
    return centred * lax.rsqrt(row_var + epsilon) * norm_gain + norm_bias


def gelu_exact(values):
    return jax.nn.gelu(values, approximate=False)


def split_blocks(values, block_rows):
    return values.reshape((values.shape[0] // block_rows, block_rows) + values.shape[1:])


def block_scores(query_heads, key_heads, allowed):
    raw_scores = (
        jnp.einsum("qhd,khd->hqk", query_heads, key_heads, preferred_element_type=jnp.float32)
        * score_scale
    )
    return jnp.where(allowed[None], raw_scores, masked_score)


def softmax_rows(query_heads, key_heads, allowed, log_total):
    scores = block_scores(query_heads, key_heads, allowed)
    return jnp.where(allowed[None], jnp.exp(scores - log_total[:, :, None]), 0.0)


def score_grads(query_heads, key_heads, value_heads, d_heads, allowed, log_total, row_delta):
    soft_rows = softmax_rows(query_heads, key_heads, allowed, log_total)
    d_soft = jnp.einsum("qhd,khd->hqk", d_heads, value_heads, preferred_element_type=jnp.float32)
    d_scores = (soft_rows * (d_soft - row_delta[:, :, None])).astype(jnp.bfloat16)
    return (soft_rows.astype(jnp.bfloat16), d_scores)


def local(
    tokens,
    segment_ids,
    lead_index,
    lead_table,
    ln1_gain,
    ln1_bias,
    qkv_weight,
    q_bias,
    v_bias,
    out_weight,
    out_bias,
    ln2_gain,
    ln2_bias,
    up_weight,
    up_bias,
    down_weight,
    down_bias,
    d_out,
):
    (
        table_full,
        first_gain,
        first_shift,
        project_full,
        query_shift,
        value_shift,
        out_full,
        out_shift,
        second_gain,
        second_shift,
        up_full,
        up_shift,
        down_full,
        down_shift,
    ) = (
        lax.all_gather(lead_table, ("band", "grp"), axis=1, tiled=True),
        lax.all_gather(ln1_gain, ("band", "grp"), axis=0, tiled=True),
        lax.all_gather(ln1_bias, ("band", "grp"), axis=0, tiled=True),
        lax.all_gather(qkv_weight, ("band", "grp"), axis=0, tiled=True),
        lax.all_gather(q_bias, ("band", "grp"), axis=0, tiled=True),
        lax.all_gather(v_bias, ("band", "grp"), axis=0, tiled=True),
        lax.all_gather(out_weight, ("band", "grp"), axis=0, tiled=True),
        lax.all_gather(out_bias, ("band", "grp"), axis=0, tiled=True),
        lax.all_gather(ln2_gain, ("band", "grp"), axis=0, tiled=True),
        lax.all_gather(ln2_bias, ("band", "grp"), axis=0, tiled=True),
        lax.all_gather(up_weight, ("band", "grp"), axis=0, tiled=True),
        lax.all_gather(up_bias, ("band", "grp"), axis=0, tiled=True),
        lax.all_gather(down_weight, ("band", "grp"), axis=0, tiled=True),
        lax.all_gather(down_bias, ("band", "grp"), axis=0, tiled=True),
    )
    tok_rows = tokens.shape[1]
    features = tokens.shape[2]
    head_dim = features // HEADS
    band_count = lax.axis_size("band")
    group_rows = tok_rows * band_count
    block_rows = math.gcd(group_rows, 1024)
    own_segments = segment_ids[0]
    group_segments = jnp.tile(own_segments, band_count)
    sample_count = lead_index.shape[1]
    lead_count = lead_table.shape[0]
    sample_hot = (
        own_segments[:, None] == jnp.arange(sample_count, dtype=jnp.int32)[None, :]
    ).astype(jnp.float32)
    lead_hot = (lead_index[0][:, None] == jnp.arange(lead_count, dtype=jnp.int32)[None, :]).astype(
        jnp.float32
    )
    lead_pick = jnp.dot(sample_hot, lead_hot, precision=lax.Precision.HIGHEST)
    embedded = tokens[0].astype(jnp.float32) + jnp.dot(
        lead_pick.astype(jnp.bfloat16), table_full, preferred_element_type=jnp.float32
    )
    normed_first = norm_rows(
        embedded, first_gain.astype(jnp.float32), first_shift.astype(jnp.float32)
    ).astype(jnp.bfloat16)
    projected = jnp.dot(normed_first, project_full, preferred_element_type=jnp.float32)
    query_rows = (projected[:, :features] + query_shift.astype(jnp.float32)).astype(jnp.bfloat16)
    key_rows = projected[:, features : 2 * features].astype(jnp.bfloat16)
    value_rows = (projected[:, 2 * features :] + value_shift.astype(jnp.float32)).astype(
        jnp.bfloat16
    )
    key_all, value_all = (
        lax.all_gather(key_rows, "band", axis=0, tiled=True),
        lax.all_gather(value_rows, "band", axis=0, tiled=True),
    )
    query_heads = query_rows.reshape(tok_rows, HEADS, head_dim)
    key_blocks = split_blocks(key_all.reshape(group_rows, HEADS, head_dim), block_rows)
    value_blocks = split_blocks(value_all.reshape(group_rows, HEADS, head_dim), block_rows)
    segment_blocks = split_blocks(group_segments, block_rows)

    def stats_step(running, block_data):
        running_max, running_sum = running
        key_block, key_segments = block_data
        allowed = own_segments[:, None] == key_segments[None, :]
        scores = block_scores(query_heads, key_block, allowed)
        new_max = jnp.maximum(running_max, jnp.max(scores, -1))
        block_sum = jnp.sum(
            jnp.where(allowed[None], jnp.exp(scores - new_max[:, :, None]), 0.0), -1
        )
        return ((new_max, running_sum * jnp.exp(running_max - new_max) + block_sum), None)

    start_max = jnp.full((HEADS, tok_rows), masked_score, jnp.float32)
    start_sum = jnp.zeros((HEADS, tok_rows), jnp.float32)
    (final_max, final_sum), unused_out = lax.scan(
        stats_step, (start_max, start_sum), (key_blocks, segment_blocks)
    )
    log_total = final_max + jnp.log(final_sum)

    def output_step(running, block_data):
        high_part, low_part = running
        key_block, value_block, key_segments = block_data
        allowed = own_segments[:, None] == key_segments[None, :]
        soft_rows = softmax_rows(query_heads, key_block, allowed, log_total)
        soft_low = soft_rows.astype(jnp.bfloat16)
        soft_rest = (soft_rows - soft_low.astype(jnp.float32)).astype(jnp.bfloat16)
        high_part = high_part + jnp.einsum(
            "hqk,khd->qhd", soft_low, value_block, preferred_element_type=jnp.float32
        )
        low_part = low_part + jnp.einsum(
            "hqk,khd->qhd", soft_rest, value_block, preferred_element_type=jnp.float32
        )
        return ((high_part, low_part), None)

    empty_heads = jnp.zeros((tok_rows, HEADS, head_dim), jnp.float32)
    (attn_high, attn_low), unused_out = lax.scan(
        output_step, (empty_heads, empty_heads), (key_blocks, value_blocks, segment_blocks)
    )
    attended = attn_high.reshape(tok_rows, features).astype(jnp.bfloat16)
    middle = (
        embedded
        + jnp.dot(attended, out_full, preferred_element_type=jnp.float32)
        + out_shift.astype(jnp.float32)
    )
    normed_second = norm_rows(
        middle, second_gain.astype(jnp.float32), second_shift.astype(jnp.float32)
    ).astype(jnp.bfloat16)
    hidden = jnp.dot(normed_second, up_full, preferred_element_type=jnp.float32) + up_shift.astype(
        jnp.float32
    )
    activated = gelu_exact(hidden).astype(jnp.bfloat16)
    result = (
        middle
        + jnp.dot(activated, down_full, preferred_element_type=jnp.float32)
        + down_shift.astype(jnp.float32)
    )
    layer_out = result.astype(jnp.bfloat16)[None]
    first_gain_back, project_back, out_back, second_gain_back, up_back, down_back = (
        lax.all_gather(ln1_gain, ("band", "grp"), axis=0, tiled=True),
        lax.all_gather(qkv_weight, ("band", "grp"), axis=0, tiled=True),
        lax.all_gather(out_weight, ("band", "grp"), axis=0, tiled=True),
        lax.all_gather(ln2_gain, ("band", "grp"), axis=0, tiled=True),
        lax.all_gather(up_weight, ("band", "grp"), axis=0, tiled=True),
        lax.all_gather(down_weight, ("band", "grp"), axis=0, tiled=True),
    )
    d_rows = d_out[0]
    d_down_shift = jnp.sum(d_rows.astype(jnp.float32), 0)
    d_down = jnp.einsum("tf,td->fd", activated, d_rows, preferred_element_type=jnp.float32)
    d_act = jnp.einsum("td,fd->tf", d_rows, down_back, preferred_element_type=jnp.float32)
    unused_gelu, gelu_back = jax.vjp(gelu_exact, hidden)
    d_hidden = gelu_back(d_act)[0].astype(jnp.bfloat16)
    d_up_shift = jnp.sum(d_hidden.astype(jnp.float32), 0)
    d_up = jnp.einsum("td,tf->df", normed_second, d_hidden, preferred_element_type=jnp.float32)
    d_normed_second = jnp.einsum("tf,df->td", d_hidden, up_back, preferred_element_type=jnp.float32)
    unused_second, second_back = jax.vjp(
        norm_rows, middle, second_gain_back.astype(jnp.float32), second_shift.astype(jnp.float32)
    )
    d_middle_part, d_gain_second, d_shift_second = second_back(d_normed_second)
    d_middle = d_rows.astype(jnp.float32) + d_middle_part
    d_branch = d_middle.astype(jnp.bfloat16)
    d_out_shift = jnp.sum(d_branch.astype(jnp.float32), 0)
    d_out_full = jnp.einsum("ti,to->io", attended, d_branch, preferred_element_type=jnp.float32)
    d_attended = jnp.einsum(
        "to,io->ti", d_branch, out_back, preferred_element_type=jnp.float32
    ).astype(jnp.bfloat16)
    d_heads = d_attended.reshape(tok_rows, HEADS, head_dim)
    row_delta = jnp.sum(d_heads.astype(jnp.float32) * (attn_high + attn_low), -1).T

    def query_grad(d_query_acc, key_block, value_block, key_segments):
        allowed = own_segments[:, None] == key_segments[None, :]
        soft_low, d_scores = score_grads(
            query_heads, key_block, value_block, d_heads, allowed, log_total, row_delta
        )
        d_query_acc = d_query_acc + jnp.einsum(
            "hqk,khd->qhd", d_scores, key_block, preferred_element_type=jnp.float32
        )
        return (d_query_acc, soft_low, d_scores)

    def owner_step(d_query_acc, block_data):
        key_block, value_block, key_segments = block_data
        d_query_acc, soft_low, d_scores = query_grad(
            d_query_acc, key_block, value_block, key_segments
        )
        d_key_block = (
            jnp.einsum("hqk,qhd->khd", d_scores, query_heads, preferred_element_type=jnp.float32)
            * score_scale
        )
        d_value_block = jnp.einsum(
            "hqk,qhd->khd", soft_low, d_heads, preferred_element_type=jnp.float32
        )
        return (d_query_acc, (d_key_block, d_value_block))

    d_query_sum, (d_key_parts, d_value_parts) = lax.scan(
        owner_step, empty_heads, (key_blocks, value_blocks, segment_blocks)
    )
    d_key_sum, d_value_sum = (
        lax.psum_scatter(
            d_key_parts.reshape(group_rows, features).astype(jnp.bfloat16),
            "band",
            scatter_dimension=0,
            tiled=True,
        ).astype(jnp.float32),
        lax.psum_scatter(
            d_value_parts.reshape(group_rows, features).astype(jnp.bfloat16),
            "band",
            scatter_dimension=0,
            tiled=True,
        ).astype(jnp.float32),
    )
    d_query = (d_query_sum.reshape(tok_rows, features) * score_scale).astype(jnp.bfloat16)
    d_key = d_key_sum.astype(jnp.bfloat16)
    d_value = d_value_sum.astype(jnp.bfloat16)
    d_query_shift = jnp.sum(d_query.astype(jnp.float32), 0)
    d_value_shift = jnp.sum(d_value.astype(jnp.float32), 0)
    d_project_rows = jnp.concatenate([d_query, d_key, d_value], 1)
    d_project = jnp.einsum(
        "ti,to->io", normed_first, d_project_rows, preferred_element_type=jnp.float32
    )
    d_normed_first = jnp.einsum(
        "to,io->ti", d_project_rows, project_back, preferred_element_type=jnp.float32
    )
    unused_first, first_back = jax.vjp(
        norm_rows, embedded, first_gain_back.astype(jnp.float32), first_shift.astype(jnp.float32)
    )
    d_embed_part, d_gain_first, d_shift_first = first_back(d_normed_first)
    d_embedded = d_middle + d_embed_part
    d_table = jnp.einsum("tl,td->ld", lead_pick, d_embedded, precision=lax.Precision.HIGHEST)
    shards = (
        lax.psum_scatter(d_table, ("band", "grp"), scatter_dimension=1, tiled=True),
        lax.psum_scatter(d_gain_first, ("band", "grp"), scatter_dimension=0, tiled=True),
        lax.psum_scatter(d_shift_first, ("band", "grp"), scatter_dimension=0, tiled=True),
        lax.psum_scatter(d_project, ("band", "grp"), scatter_dimension=0, tiled=True),
        lax.psum_scatter(d_query_shift, ("band", "grp"), scatter_dimension=0, tiled=True),
        lax.psum_scatter(d_value_shift, ("band", "grp"), scatter_dimension=0, tiled=True),
        lax.psum_scatter(d_out_full, ("band", "grp"), scatter_dimension=0, tiled=True),
        lax.psum_scatter(d_out_shift, ("band", "grp"), scatter_dimension=0, tiled=True),
        lax.psum_scatter(d_gain_second, ("band", "grp"), scatter_dimension=0, tiled=True),
        lax.psum_scatter(d_shift_second, ("band", "grp"), scatter_dimension=0, tiled=True),
        lax.psum_scatter(d_up, ("band", "grp"), scatter_dimension=0, tiled=True),
        lax.psum_scatter(d_up_shift, ("band", "grp"), scatter_dimension=0, tiled=True),
        lax.psum_scatter(d_down, ("band", "grp"), scatter_dimension=0, tiled=True),
        lax.psum_scatter(d_down_shift, ("band", "grp"), scatter_dimension=0, tiled=True),
    )
    return (layer_out, d_embedded[None]) + tuple(shards)


def solution(mesh):
    return jax.shard_map(
        local,
        mesh=mesh,
        in_specs=(
            P("grp", "band", None),
            P("grp", "band"),
            P("grp", None),
            P(None, ("band", "grp")),
            P(("band", "grp")),
            P(("band", "grp")),
            P(("band", "grp"), None),
            P(("band", "grp")),
            P(("band", "grp")),
            P(("band", "grp"), None),
            P(("band", "grp")),
            P(("band", "grp")),
            P(("band", "grp")),
            P(("band", "grp"), None),
            P(("band", "grp")),
            P(("band", "grp"), None),
            P(("band", "grp")),
            P("grp", "band", None),
        ),
        out_specs=(
            P("grp", "band", None),
            P("grp", "band", None),
            P(None, ("band", "grp")),
            P(("band", "grp")),
            P(("band", "grp")),
            P(("band", "grp"), None),
            P(("band", "grp")),
            P(("band", "grp")),
            P(("band", "grp"), None),
            P(("band", "grp")),
            P(("band", "grp")),
            P(("band", "grp")),
            P(("band", "grp"), None),
            P(("band", "grp")),
            P(("band", "grp"), None),
            P(("band", "grp")),
        ),
        check_vma=False,
    )
```

profile of v0, /device:TPU:0, one launch (start us, length us, event | category | flops | bytes accessed | tf_op | source)
XLA Modules:
  0.0 1560.5 jit_solution(7334183457851714069)
XLA Ops:
  14.7 42.6 %all-reduce.18 = (bf16[1024]{0:T(1024)(128)(2,1)S(1)}, bf16[1024]{0:T(1024)(128)(2,1)S(1)}, bf16[1024]{0:T(1024)(128)(2,1)S(1)}, bf16[1024]{0:T(1024)(128)(2,1)S...) all-reduce(bf16[1024]{0:T(1024)(128)(2,1)S(1)} %dynamic-update-slic, ...), channel_id=1, replica_groups=mesh['band'=16,'grp'=2] {'band','grp'}, use_global_device_ids=true, to_apply=%add.1 | all-reduce | flops 8192 | bytes 32768
  57.3 41.4 %all-gather = bf16[32,32,16]{1,2,0:T(8,128)(2,1)S(1)} all-gather(bf16[1,32,16]{1,2,0:T(8,128)(2,1)} %bitcast.269), channel_id=1, replica_groups=mesh['band'=16,'grp'=2] {'band','grp'}, dimensions={0}, use_global_device_ids=true | all-gather | bytes 33792 | tf_op jit(solution)/shard_map/all_gather | solution.py:87
  99.8 1.3 fusion.116
  101.4 3.8 fusion.111
  108.9 36.5 %all-gather.1 = bf16[32,1,128]{2,1,0:T(2,128)(2,1)S(1)} all-gather(bf16[1,1,128]{2,1,0:T(2,128)(2,1)S(1)} %bitcast.270), channel_id=1, replica_groups=mesh['band'=16,'grp'=2] {'band','grp'}, dimensions={0}, use_global_device_ids=true | all-gather | bytes 8448 | tf_op jit(solution)/shard_map/all_gather | solution.py:98
  145.6 32.9 %all-gather.13.cloned.1.call-done = bf16[2048,1024]{1,0:T(8,128)(2,1)} async-done(((bf16[128,1024]{1,0:T(8,128)(2,1)}), bf16[2048,1024]{1,0:T(8,128)(2,1)}) %all-gather.13.cloned.1.call-update) | async-done | bytes 4194320 | tf_op jit(solution)/shard_map/all_gather | solution.py:132
  178.5 11.7 reshape.248
  190.2 9.8 copy.77
  199.9 56.3 %all-gather.11.cloned.1.call-done = bf16[2048,1024]{1,0:T(8,128)(2,1)} async-done(((bf16[128,1024]{1,0:T(8,128)(2,1)}), bf16[2048,1024]{1,0:T(8,128)(2,1)}) %all-gather.11.cloned.1.call-update) | async-done | bytes 4194320 | tf_op jit(solution)/shard_map/all_gather | solution.py:133
  256.3 11.6 reshape.247
  267.9 9.8 copy.76
  277.7 11.4 while.41
  277.9 3.4 fusion.168
  281.4 2.0 select_reduce_fusion.2
  283.6 3.4 fusion.168
  287.1 2.0 select_reduce_fusion.2
  289.1 19.0 %while.42 = (s32[]{:T(128)}, f32[128,16,64]{0,2,1:T(8,128)S(1)}, f32[128,16,64]{0,2,1:T(8,128)S(1)}, bf16[2,1024,16,64]{1,3,2,0:T(8,128)(2,1)}, s32[1,128]{1,0:T...) while((s32[]{:T(128)}, f32[128,16,64]{0,2,1:T(8,128)S(1)}, ...), condition=%wide.region_7.8_spmd.clone, body=%wide.region_6.7_spmd.clone.sunk | while | flops 833224704 | bytes 51016360 | solution.py:174
  289.9 3.1 fusion.175
  293.0 3.0 fusion.177
  296.0 2.8 fusion.176
  299.1 3.1 fusion.175
  302.2 3.0 fusion.177
  305.3 2.8 fusion.176
  308.2 5.8 all-gather.15.cloned.1.call-done
  314.0 2.1 fusion.117
  316.4 76.7 %all-gather.17.cloned.1.call-done = bf16[1024,4096]{1,0:T(8,128)(2,1)} async-done(((bf16[32,4096]{1,0:T(8,128)(2,1)}), bf16[1024,4096]{1,0:T(8,128)(2,1)}) %all-gather.17.cloned.1.call-update) | async-done | bytes 8388624 | tf_op jit(solution)/shard_map/all_gather | solution.py:97
  393.1 6.1 convolution_add_fusion
  399.2 72.7 %all-gather.19.cloned.1.call-done = bf16[4096,1024]{1,0:T(8,128)(2,1)} async-done(((bf16[128,1024]{1,0:T(8,128)(2,1)}), bf16[4096,1024]{1,0:T(8,128)(2,1)}) %all-gather.19.cloned.1.call-update) | async-done | bytes 8388624 | tf_op jit(solution)/shard_map/all_gather | solution.py:99
  471.9 10.7 convert_reduce_fusion
  482.6 3.6 multiply_reduce_fusion
  487.9 1.5 convolution_convert_fusion
  489.4 1.8 copy.78
  491.2 1.4 multiply_reduce_fusion.3
  492.6 33.7 %while.43 = (s32[]{:T(128)}, f32[128,16,64]{0,2,1:T(8,128)S(1)}, bf16[2,1024,16,64]{1,3,2,0:T(8,128)(2,1)}, bf16[2,1024,16,64]{1,3,2,0:T(8,128)(2,1)}, bf16[2,10...) while((s32[]{:T(128)}, f32[128,16,64]{0,2,1:T(8,128)S(1)}, ...), condition=%wide.region_14.15_spmd.clone, body=%wide.region_13.14_spmd.clone.sunk | while | flops 1368784896 | bytes 123114296 | solution.py:251
  492.9 3.1 fusion.188
  496.0 3.7 fusion.189
  499.8 4.0 bitcast_dynamic-update-slice_fusion.5
  506.0 1.6 bitcast_dynamic-update-slice_fusion.4
  507.6 2.0 copy-done.6
  509.8 3.1 fusion.188
  512.9 3.7 fusion.189
  516.6 4.0 bitcast_dynamic-update-slice_fusion.5
  522.8 1.6 bitcast_dynamic-update-slice_fusion.4
  524.4 2.0 copy-done.6
  526.3 10.9 copy.99
  537.3 12.1 reshape.243
  549.4 10.9 copy.98
  560.4 11.9 reshape.241
  573.2 70.1 %reduce-scatter.24.cloned.1.call-done = bf16[128,1024]{1,0:T(8,128)(2,1)} async-done(((bf16[2048,1024]{1,0:T(8,128)(2,1)}), bf16[128,1024]{1,0:T(8,128)(2,1)}) %reduce-scatter.24.cloned.1.call-update) | async-done | bytes 262160
  644.4 95.9 %reduce-scatter.22.cloned.1.call-done = bf16[128,1024]{1,0:T(8,128)(2,1)} async-done(((bf16[2048,1024]{1,0:T(8,128)(2,1)}), bf16[128,1024]{1,0:T(8,128)(2,1)}) %reduce-scatter.22.cloned.1.call-update) | async-done | bytes 262160
  741.5 5.3 multiply_reduce_fusion.1
  747.1 1.9 convolution_bitcast_fusion
  749.1 3.6 fusion.118
  753.7 7.4 fusion.94
  762.1 11.0 fusion.96
  773.7 8.2 fusion.112
  782.6 10.2 fusion.90
  794.0 39.5 %all-reduce.17 = (f32[1024]{0:T(1024)S(1)}, f32[1024]{0:T(1024)S(1)}, f32[1024]{0:T(1024)S(1)}, f32[1024]{0:T(1024)S(1)}, f32[1024]{0:T(1024)S(1)}, /*index=5*/f...) all-reduce(f32[1024]{0:T(1024)S(1)} %get-tuple-element.352, ...), channel_id=5, replica_groups=mesh['band'=16,'grp'=2] {'band','grp'}, use_global_device_ids=true, to_apply=%region_21.22.clone | all-reduce | flops 12288 | bytes 98304
  838.8 43.9 %reduce-scatter.26.cloned.1.call-done = f32[32,16]{1,0:T(8,128)} async-done(((f32[1024,16]{1,0:T(8,128)}), f32[32,16]{1,0:T(8,128)}) %reduce-scatter.26.cloned.1.call-update) | async-done | bytes 2064
  882.7 1.4 copy.93
  884.1 138.4 %reduce-scatter.16.cloned.1.call-done = f32[32,1024]{1,0:T(8,128)} async-done(((f32[1024,1024]{1,0:T(8,128)}), f32[32,1024]{1,0:T(8,128)}) %reduce-scatter.16.cloned.1.call-update) | async-done | bytes 131088 | tf_op jit(solution)/shard_map/reduce_scatter | solution.py:293
  1022.5 158.9 %reduce-scatter.14.cloned.1.call-done = f32[32,3072]{1,0:T(8,128)} async-done(((f32[1024,3072]{1,0:T(8,128)}), f32[32,3072]{1,0:T(8,128)}) %reduce-scatter.14.cloned.1.call-update) | async-done | bytes 393232 | tf_op jit(solution)/shard_map/reduce_scatter | solution.py:290
  1181.4 184.8 %reduce-scatter.20.cloned.1.call-done = f32[128,1024]{1,0:T(8,128)} async-done(((f32[4096,1024]{1,0:T(8,128)}), f32[128,1024]{1,0:T(8,128)}) %reduce-scatter.20.cloned.1.call-update) | async-done | bytes 524304 | tf_op jit(solution)/shard_map/reduce_scatter | solution.py:299
  1366.2 187.3 %reduce-scatter.18.cloned.1.call-done = f32[32,4096]{1,0:T(8,128)} async-done(((f32[1024,4096]{1,0:T(8,128)}), f32[32,4096]{1,0:T(8,128)}) %reduce-scatter.18.cloned.1.call-update) | async-done | bytes 524304 | tf_op jit(solution)/shard_map/reduce_scatter | solution.py:297
  (211 shorter events, 33.4 us)
Async XLA Ops:
  7.2 94.2 %all-gather.9.cloned.1.call-start = ((), (), s32[]{:S(2)}) async-start(), calls=%async_computation.7 | async-start | bytes 6488064 | tf_op jit(solution)/shard_map/all_gather | solution.py:90
  7.9 170.6 %all-gather.13.cloned.1.call-start = ((), (), s32[]{:S(2)}) async-start(), calls=%async_computation.9 | async-start | bytes 4456448 | tf_op jit(solution)/shard_map/all_gather | solution.py:132
  57.2 48.0 %copy-start.23 = (f32[1024]{0:T(1024)}, f32[1024]{0:T(1024)S(1)}, u32[]{:S(2)}) copy-start(f32[1024]{0:T(1024)S(1)} %convert_element_type.136) | copy-start | bytes 12292
  57.2 48.0 %copy-start.21 = (f32[1024]{0:T(1024)}, f32[1024]{0:T(1024)S(1)}, u32[]{:S(2)}) copy-start(f32[1024]{0:T(1024)S(1)} %convert_element_type.135) | copy-start | bytes 12292
  99.8 5.5 copy-start.28
  101.1 4.2 copy-start.30
  101.3 4.0 copy-start.40
  101.4 3.9 copy-start.36
  105.3 3.6 copy-start.39
  105.3 40.1 %copy-start.27 = (s32[1,128]{1,0:T(1,128)S(1)}, s32[1,128]{1,0:T(1,128)}, u32[]{:S(2)}) copy-start(s32[1,128]{1,0:T(1,128)} %param.25) | copy-start | bytes 1540
  106.1 150.2 %all-gather.11.cloned.1.call-start = ((), (), s32[]{:S(2)}) async-start(), calls=%async_computation.8 | async-start | bytes 4456448 | tf_op jit(solution)/shard_map/all_gather | solution.py:133
  107.0 207.0 %all-gather.15.cloned.1.call-start = ((), (), s32[]{:S(2)}) async-start(), calls=%async_computation.10 | async-start | bytes 2162688 | tf_op jit(solution)/shard_map/all_gather | solution.py:93
  107.6 285.5 %all-gather.17.cloned.1.call-start = ((), (), s32[]{:S(2)}) async-start(), calls=%async_computation.11 | async-start | bytes 8650752 | tf_op jit(solution)/shard_map/all_gather | solution.py:97
  108.2 363.7 %all-gather.19.cloned.1.call-start = ((), (), s32[]{:S(2)}) async-start(), calls=%async_computation.12 | async-start | bytes 8650752 | tf_op jit(solution)/shard_map/all_gather | solution.py:99
  108.8 534.5 %reduce-scatter.24.cloned.1.call-start = ((), (), s32[]{:S(2)}) async-start(), calls=%async_computation.18 | async-start | bytes 4456448
  108.9 284.2 %copy-start.25 = (f32[1024]{0:T(1024)}, f32[1024]{0:T(1024)S(1)}, u32[]{:S(2)}) copy-start(f32[1024]{0:T(1024)S(1)} %convert_element_type.146) | copy-start | bytes 12292
  289.8 3.1 copy-start.3
  299.1 3.1 copy-start.3
  308.1 8.0 copy-start.17
  308.2 8.0 copy-start.20
  308.2 91.0 %copy-start.7 = (bf16[128,16,64]{0,2,1:T(8,128)(2,1)}, bf16[128,16,64]{0,2,1:T(8,128)(2,1)S(1)}, u32[]{:S(2)}) copy-start(bf16[128,16,64]{0,2,1:T(8,128)(2,1)S(1)} %convert_element_type.142) | copy-start | bytes 786436
  393.1 78.8 %copy-start.9 = (bf16[1,128,1024]{2,1,0:T(8,128)(2,1)S(1)}, bf16[1,128,1024]{2,1,0:T(8,128)(2,1)}, u32[]{:S(2)}) copy-start(bf16[1,128,1024]{2,1,0:T(8,128)(2,1)} %param.41) | copy-start | bytes 786436
  471.9 10.7 copy-start.1
  482.6 3.9 copy-start.10
  486.2 1.8 copy-start.2
  487.2 0.7 copy-start.13
  492.9 3.1 copy-start.4
  492.9 3.1 copy-start.18
  499.7 4.0 copy-start
  503.8 2.2 copy-start.5
  507.6 2.0 copy-start.6
  509.7 3.1 copy-start.4
  509.8 3.1 copy-start.18
  516.6 4.0 copy-start
  520.6 2.2 copy-start.5
  524.4 2.0 copy-start.6
  549.4 190.9 %reduce-scatter.22.cloned.1.call-start = ((), (), s32[]{:S(2)}) async-start(), calls=%async_computation.17 | async-start | bytes 4456448
  572.3 169.2 %copy-start.22 = (f32[1024]{0:T(1024)S(1)}, f32[1024]{0:T(1024)}, u32[]{:S(2)}) copy-start(f32[1024]{0:T(1024)} %copy-done.21) | copy-start | bytes 12292
  572.3 169.2 %copy-start.31 = (f32[128]{0:T(128)S(1)}, f32[128]{0:T(128)}, u32[]{:S(2)}) copy-start(f32[128]{0:T(128)} %copy-done.30) | copy-start | bytes 1540
  572.3 169.2 %copy-start.37 = (f32[128]{0:T(128)S(1)}, f32[128]{0:T(128)}, u32[]{:S(2)}) copy-start(f32[128]{0:T(128)} %copy-done.36) | copy-start | bytes 1540
  572.3 310.4 %reduce-scatter.26.cloned.1.call-start = ((), (), s32[]{:S(2)}) async-start(), calls=%async_computation.19 | async-start | bytes 540672
  644.4 97.1 %copy-start.14 = (bf16[128,1024]{0,1:T(8,128)(2,1)}, bf16[128,1024]{0,1:T(8,128)(2,1)S(1)}, u32[]{:S(2)}) copy-start(bf16[128,1024]{0,1:T(8,128)(2,1)S(1)} %copy.91) | copy-start | bytes 786436
  741.4 5.4 copy-start.19
  741.5 5.3 copy-start.41
  741.5 5.6 copy-start.11
  741.5 5.6 copy-start.29
  746.8 2.3 copy-start.8
  749.0 273.5 %reduce-scatter.16.cloned.1.call-start = ((), (), s32[]{:S(2)}) async-start(), calls=%async_computation.14 | async-start | bytes 4325376 | tf_op jit(solution)/shard_map/reduce_scatter | solution.py:293
  752.7 0.9 copy-start.15
  752.7 1.0 copy-start.24
  752.7 428.7 %reduce-scatter.14.cloned.1.call-start = ((), (), s32[]{:S(2)}) async-start(), calls=%async_computation.13 | async-start | bytes 12976128 | tf_op jit(solution)/shard_map/reduce_scatter | solution.py:290
  761.1 1.0 copy-start.12
  761.1 605.1 %reduce-scatter.20.cloned.1.call-start = ((), (), s32[]{:S(2)}) async-start(), calls=%async_computation.16 | async-start | bytes 17301504 | tf_op jit(solution)/shard_map/reduce_scatter | solution.py:299
  773.0 0.7 copy-start.26
  773.1 780.5 %reduce-scatter.18.cloned.1.call-start = ((), (), s32[]{:S(2)}) async-start(), calls=%async_computation.15 | async-start | bytes 17301504 | tf_op jit(solution)/shard_map/reduce_scatter | solution.py:297
  781.9 0.7 copy-start.38
  782.6 10.2 copy-start.16
  792.8 1.2 copy-start.32
  792.8 1.2 copy-start.33
  792.8 1.2 copy-start.34
  792.8 1.2 copy-start.35
Sparse Core Ops, SparseCore 0:
  10.9 73.0 all-gather.8
  106.2 72.2 all-gather.12
  181.8 74.4 all-gather.10
  259.0 54.9 all-gather.14
  316.7 76.3 all-gather.16
  395.8 76.0 all-gather.18
  549.5 93.7 reduce-scatter.23
  645.5 94.7 reduce-scatter.21
  749.1 133.4 reduce-scatter.25
  885.5 136.9 reduce-scatter.15
  1030.1 151.2 reduce-scatter.13
  1184.1 182.0 reduce-scatter.19
  1369.1 184.3 reduce-scatter.17
where the time goes:
time: 1570 us; the launch traced here: 1560 us
  waiting for transfers between devices  1130 us (72%)
  blocking collectives  160 us (10%)
  matrix products  129 us (8%)
  local copies, waits for them, and re-layouts  117 us (7%)
    unnamed x16, waiting for transfers between devices  212 us
    reduce_scatter x1, waiting for transfers between devices, local(): lax.psum_scatter(d_up, ('band', 'grp'), scatter_dimension=0, tiled=True)  187 us
    reduce_scatter x1, waiting for transfers between devices, local(): lax.psum_scatter(d_down, ('band', 'grp'), scatter_dimension=0, tiled=True)  185 us
    reduce_scatter x1, waiting for transfers between devices, local(): lax.psum_scatter(d_project, ('band', 'grp'), scatter_dimension=0, tiled=T...  159 us
    reduce_scatter x1, waiting for transfers between devices, local(): lax.psum_scatter(d_out_full, ('band', 'grp'), scatter_dimension=0, tiled=...  138 us
    unnamed x107, local copies, waits for them, and re-layouts  84.8 us
    unnamed x2, blocking collectives  82.1 us
    all_gather x1, waiting for transfers between devices, local(): lax.all_gather(up_weight, ('band', 'grp'), axis=0, tiled=True)  76.7 us
  transfers between devices with their start and end apart: 13, of which 12 were waited for; matrix products, arithmetic and copies ran while one was open for 11% of the time, Pallas kernels for 0%

commit v1 on v0

--- a/solution.py
+++ b/solution.py
@@ -1,9 +1,15 @@
+import functools
 import math
 
 import jax
 import jax.numpy as jnp
 from jax import lax
+from jax.experimental import pallas as pl
+from jax.experimental.pallas import tpu as pltpu
+from jax.sharding import Mesh
 from jax.sharding import PartitionSpec as P
+
+bf16, f32 = jnp.bfloat16, jnp.float32
 
 HEADS = 16
 
@@ -302,47 +308,621 @@
     return (layer_out, d_embedded[None]) + tuple(shards)
 
 
+DEPTH = 4
+PLANE = 4
+BIG = 1e30
+VMEM = pltpu.MemorySpace.VMEM
+SMEM = pltpu.MemorySpace.SMEM
+LEADS, TAB_END = 16, 16
+ROW_G1, ROW_B1, ROW_QB, ROW_VB, ROW_OB, ROW_G2, ROW_B2, ROW_DB = range(16, 24)
+VEC_ROWS = 24
+
+
+def mul(left, right, over_left, over_right):
+    return lax.dot_general(
+        left, right, (((over_left,), (over_right,)), ((), ())), preferred_element_type=jnp.float32
+    )
+
+
+def run(kernel, outs, ins, scratch=(), vmem_mb=48, flops=0, moved=0):
+    specs = [pl.BlockSpec(memory_space=SMEM if a.ndim == 1 else VMEM) for a in ins]
+    return pl.pallas_call(
+        kernel,
+        out_shape=[jax.ShapeDtypeStruct(s, d) for s, d in outs],
+        in_specs=specs,
+        out_specs=[pl.BlockSpec(memory_space=VMEM)] * len(outs),
+        scratch_shapes=[pltpu.VMEM(s, d) for s, d in scratch],
+        compiler_params=pltpu.CompilerParams(vmem_limit_bytes=vmem_mb << 20),
+        cost_estimate=pl.CostEstimate(flops=flops, bytes_accessed=moved, transcendentals=0),
+    )(*ins)
+
+
+def row_stats(values):
+    mean = jnp.mean(values, -1, keepdims=True)
+    centred = values - mean
+    inv = lax.rsqrt(jnp.mean(centred * centred, -1, keepdims=True) + epsilon)
+    return centred * inv, inv
+
+
+def norm_back(d_normal, normal, inv):
+    first = jnp.mean(d_normal, -1, keepdims=True)
+    second = jnp.mean(d_normal * normal, -1, keepdims=True)
+    return inv * (d_normal - first - normal * second)
+
+
+def lead_hot(lead_ref, seg_col_ref):
+    seg = seg_col_ref[...]
+    lead = jnp.zeros_like(seg)
+    for slot in range(lead_ref.shape[0]):
+        lead = jnp.where(seg == slot, lead_ref[slot], lead)
+    slots = lax.broadcasted_iota(jnp.int32, (seg.shape[0], LEADS), 1)
+    return jnp.where(slots == lead, 1.0, 0.0).astype(bf16)
+
+
+def prep_kernel(pos, tok, dout, qkv, up, down, *outs):
+    z, yx = pos[0], pos[1]
+    q_outs, msgs, down_msg = outs[:4], outs[4:8], outs[8]
+    rows = tok.shape[0]
+    d = tok.shape[1]
+    width = d // DEPTH
+    for u in range(DEPTH):
+        zu = (z + u) & (DEPTH - 1)
+        for part in range(3):
+            q_outs[u][:, part * width : (part + 1) * width] = qkv[
+                :, pl.ds(pl.multiple_of(part * d + zu * width, width), width)
+            ]
+    up_rows, up_cols = up.shape
+    fr = up_cols // (DEPTH * PLANE * 2)
+    for k in range(PLANE):
+        msgs[k][0:rows, :] = tok[...]
+        msgs[k][rows : 2 * rows, :] = dout[...]
+        for c in range(2):
+            for zz in range(DEPTH):
+                src = ((zz * PLANE + (yx ^ k)) * 2 + c) * fr
+                dst = (c * DEPTH + zz) * fr
+                msgs[k][2 * rows :, dst : dst + fr] = up[:, pl.ds(pl.multiple_of(src, fr), fr)]
+    down_msg[...] = down[...]
+
+
+def qkv_kernel(pos, lead, seg_col, vec, t0, t1, t2, t3, wa, wb, n1, w, o0, o1, o2, o3, proj):
+    z, yx, c = pos[0], pos[1], pos[2]
+    rows, d = t0.shape
+    rw = wa.shape[2]
+    for k in range(PLANE):
+        for s in range(DEPTH):
+            block = (((z - s) & (DEPTH - 1)) * PLANE + (yx ^ k)) * 2
+            w[pl.ds(pl.multiple_of((block + c) * rw, rw), rw), :] = wa[k, s]
+            w[pl.ds(pl.multiple_of((block + 1 - c) * rw, rw), rw), :] = wb[k, s]
+    shift = mul(lead_hot(lead, seg_col), vec[0:LEADS, :], 1, 0)
+    gain = vec[ROW_G1 : ROW_G1 + 1, :].astype(f32)
+    bias = vec[ROW_B1 : ROW_B1 + 1, :].astype(f32)
+    for s, t in enumerate((t0, t1, t2, t3)):
+        normal, _ = row_stats(t[...].astype(f32) + shift)
+        n1[s * rows : (s + 1) * rows, :] = (normal * gain + bias).astype(bf16)
+    width = d // DEPTH
+    head = width // PLANE
+    at = pl.ds(pl.multiple_of(z * width, width), width)
+    biases = jnp.concatenate(
+        [
+            vec[ROW_QB : ROW_QB + 1, at].astype(f32),
+            jnp.zeros((1, width), f32),
+            vec[ROW_VB : ROW_VB + 1, at].astype(f32),
+        ],
+        1,
+    )
+    first = lax.broadcasted_iota(jnp.int32, (8, 3 * width), 0) == 0
+    biases = jnp.where(first, biases, 0.0).astype(bf16)
+    ones = jnp.ones((8, DEPTH * rows), bf16)
+    found = mul(w[...], n1[...], 0, 1) + mul(biases, ones, 0, 0)
+    proj[...] = found.astype(bf16).reshape(proj.shape)
+    for k, out in enumerate((o0, o1, o2, o3)):
+        for part in range(3):
+            out[part * head : (part + 1) * head, :] = proj[part * PLANE + (yx ^ k)]
+
+
+def hot_rows(seg_row, count, tiles):
+    seg = jnp.concatenate([seg_row[...]] * tiles, 1)
+    slots = lax.broadcasted_iota(jnp.int32, (16, seg.shape[1]), 0)
+    return jnp.where(slots == seg, 1.0, 0.0), slots < count
+
+
+def fill_heads(seg_row, count, blocks, qa, ka, vt):
+    head = blocks[0].shape[0] // 3
+    span = blocks[0].shape[1]
+    hot, real = hot_rows(seg_row, count, span // seg_row.shape[1])
+    q_mark = jnp.where(real, (hot - 1.0) * BIG, 0.0).astype(bf16)
+    k_mark = jnp.where(real, hot, 0.0).astype(bf16)
+    rest = qa.shape[0] - head - 16
+    for k, block in enumerate(blocks):
+        cols = slice(k * span, (k + 1) * span)
+        qa[0:head, cols] = block[0:head, :] * jnp.asarray(score_scale, bf16)
+        qa[head : head + 16, cols] = q_mark
+        qa[head + 16 :, cols] = jnp.zeros((rest, span), bf16)
+        keys = jnp.concatenate([block[head : 2 * head, :], k_mark, jnp.zeros((rest, span), bf16)], 0)
+        ka[cols, :] = keys.T
+        vt[:, cols] = block[2 * head :, :]
+
+
+def attend_kernel(count, seg_row, b0, b1, b2, b3, o0, o1, o2, o3, lse, qa, ka, vt):
+    fill_heads(seg_row, count, (b0, b1, b2, b3), qa, ka, vt)
+    span = b0.shape[1]
+    rows = seg_row.shape[1]
+    outs = (o0, o1, o2, o3)
+
+    def step(k, carry):
+        for half in range(DEPTH // 2):
+            at = pl.ds(pl.multiple_of(k * span + half * 2 * rows, 2 * rows), 2 * rows)
+            scores = mul(ka[...], qa[:, at], 1, 0)
+            top = jnp.max(scores, 0, keepdims=True)
+            soft = jnp.exp(scores - top)
+            total = jnp.sum(soft, 0, keepdims=True)
+            found = mul(vt[...], soft.astype(bf16), 1, 0) / total
+            lse[:, at] = jnp.broadcast_to(top + jnp.log(total), (8, 2 * rows))
+            for i in range(2):
+                outs[half * 2 + i][:, pl.ds(pl.multiple_of(k * rows, rows), rows)] = found[
+                    :, i * rows : (i + 1) * rows
+                ].astype(bf16)
+        return carry
+
+    lax.fori_loop(0, PLANE, step, 0)
+
+
+def mid_kernel(pos, lead, seg_col, vec, up_b, a0, a1, a2, a3, m0, m1, m2, m3, w_out, wa, wb,
+               act, d_hid, n2, w_up, w_down, middle, att_own, p0, p1, p2, p3, d_vec, d_up_b,
+               att, normal, inv, hid, w_scr):
+    z, yx, c = pos[0], pos[1], pos[2]
+    parts = (a0, a1, a2, a3)
+    msgs = (m0, m1, m2, m3)
+    head = a0.shape[1]
+    rows = seg_col.shape[0]
+    d = w_out.shape[1]
+    rw = m0.shape[0] - 2 * rows
+    fr = wa.shape[1] - PLANE * rw
+    for zz in range(DEPTH):
+        for k in range(PLANE):
+            block = (zz * PLANE + (yx ^ k)) * 2
+            src = slice(k * rw, (k + 1) * rw)
+            w_up[pl.ds(pl.multiple_of((block + c) * rw, rw), rw), :] = wa[zz, src, :]
+            w_up[pl.ds(pl.multiple_of((block + 1 - c) * rw, rw), rw), :] = wb[zz, src, :]
+        src = slice(PLANE * rw, PLANE * rw + fr)
+        w_down[pl.ds(pl.multiple_of((c * DEPTH + zz) * fr, fr), fr), :] = wa[zz, src, :]
+        w_down[pl.ds(pl.multiple_of(((1 - c) * DEPTH + zz) * fr, fr), fr), :] = wb[zz, src, :]
+    for u in range(DEPTH):
+        for m in range(PLANE):
+            h = ((z + u) & (DEPTH - 1)) * PLANE + (yx ^ m)
+            for j in range(PLANE):
+                k = m ^ j
+                att[pl.ds(pl.multiple_of(h * head, head), head), j * rows : (j + 1) * rows] = parts[m][
+                    u, :, k * rows : (k + 1) * rows
+                ]
+    att_own[...] = att[:, 0:rows]
+    shift = mul(lead_hot(lead, seg_col), vec[0:LEADS, :], 1, 0)
+    out_b = vec[ROW_OB : ROW_OB + 1, :].astype(f32)
+    gain = vec[ROW_G2 : ROW_G2 + 1, :].astype(f32)
+    bias = vec[ROW_B2 : ROW_B2 + 1, :].astype(f32)
+    branch = mul(att[...], w_out[...], 0, 0)
+    for j in range(PLANE):
+        here = slice(j * rows, (j + 1) * rows)
+        total = msgs[j][0:rows, :].astype(f32) + shift + branch[here, :] + out_b
+        if j == 0:
+            middle[...] = total
+        norm, scale = row_stats(total)
+        normal[here, :] = norm
+        n2[here, :] = (norm * gain + bias).astype(bf16)
+    hid[...] = mul(n2[...], w_up[...], 1, 0) + up_b[...].astype(f32)
+    for j in range(PLANE):
+        here = slice(j * rows, (j + 1) * rows)
+        hidden = hid[here, :]
+        phi = 0.5 * (1.0 + lax.erf(hidden * 0.7071067811865476))
+        act[here, :] = (hidden * phi).astype(bf16)
+        hid[here, :] = phi + hidden * (jnp.exp(-0.5 * hidden * hidden) * 0.3989422804014327)
+    sums = jnp.zeros((1, d), f32)
+    for j in range(PLANE):
+        here = slice(j * rows, (j + 1) * rows)
+        d_act = mul(msgs[j][rows : 2 * rows, :], w_down[...], 1, 1)
+        low = (d_act * hid[here, :]).astype(bf16)
+        d_hid[here, :] = low
+        sums = sums + jnp.sum(low.astype(f32), 0, keepdims=True)
+    d_up_b[...] = sums
+    back = mul(d_hid[...], w_up[...], 1, 1)
+    d_gain = jnp.zeros((1, d), f32)
+    d_bias = jnp.zeros((1, d), f32)
+    for j, out in enumerate((p0, p1, p2, p3)):
+        here = slice(j * rows, (j + 1) * rows)
+        piece = back[here, :]
+        out[...] = piece.astype(out.dtype)
+        d_gain = d_gain + jnp.sum(piece * normal[here, :], 0, keepdims=True)
+        d_bias = d_bias + jnp.sum(piece, 0, keepdims=True)
+    d_down_b = jnp.sum(m0[rows : 2 * rows, :].astype(f32), 0, keepdims=True)
+    d_vec[...] = jnp.concatenate([d_gain, d_bias, d_down_b, jnp.zeros((5, d), f32)], 0)
+
+
+def ffn_grad_kernel(pos, vec, act, d_hid, n2, w_down, middle, m0, m1, m2, m3,
+                    o0, o1, o2, o3, mine, other, grad):
+    c = pos[2]
+    msgs = (m0, m1, m2, m3)
+    rows, d = middle.shape
+    rw = m0.shape[0] - 2 * rows
+    fr = act.shape[1] // (2 * DEPTH)
+    found = mul(act[...], w_down[...], 1, 0)
+    o0[...] = found[0:rows, :] + middle[...] + vec[ROW_DB : ROW_DB + 1, :].astype(f32)
+    for j, out in ((1, o1), (2, o2), (3, o3)):
+        out[...] = found[j * rows : (j + 1) * rows, :].astype(bf16)
+    grad[...] = mul(n2[...], d_hid[...], 0, 0).astype(bf16)
+    for zz in range(DEPTH):
+        for k in range(PLANE):
+            block = (zz * PLANE + k) * 2
+            dst = slice(k * rw, (k + 1) * rw)
+            mine[zz, dst, :] = grad[pl.ds(pl.multiple_of((block + c) * rw, rw), rw), :]
+            other[zz, dst, :] = grad[pl.ds(pl.multiple_of((block + 1 - c) * rw, rw), rw), :]
+    d_down = jnp.zeros(grad.shape, f32)
+    for j in range(PLANE):
+        d_down = d_down + mul(act[j * rows : (j + 1) * rows, :], msgs[j][rows : 2 * rows, :], 0, 0)
+    grad[...] = d_down.astype(bf16)
+    dst = slice(PLANE * rw, PLANE * rw + fr)
+    for zz in range(DEPTH):
+        mine[zz, dst, :] = grad[pl.ds(pl.multiple_of((c * DEPTH + zz) * fr, fr), fr), :]
+        other[zz, dst, :] = grad[pl.ds(pl.multiple_of(((1 - c) * DEPTH + zz) * fr, fr), fr), :]
+
+
+def branch_kernel(pos, vec, middle, dout, w_out, p0, p1, p2, p3, d_mid, d_branch, d_out_b,
+                  o0, o1, o2, o3, d_att):
+    z, yx = pos[0], pos[1]
+    dy = p0[...].astype(f32) + p1[...].astype(f32) + p2[...].astype(f32) + p3[...].astype(f32)
+    normal, inv = row_stats(middle[...])
+    gain = vec[ROW_G2 : ROW_G2 + 1, :].astype(f32)
+    total = dout[...].astype(f32) + norm_back(dy * gain, normal, inv)
+    d_mid[...] = total
+    low = total.astype(bf16)
+    d_branch[...] = low
+    d_out_b[...] = jnp.broadcast_to(jnp.sum(low.astype(f32), 0, keepdims=True), d_out_b.shape)
+    d_att[...] = mul(w_out[...], low, 1, 1).astype(bf16).reshape(d_att.shape)
+    for k, out in enumerate((o0, o1, o2, o3)):
+        for u in range(DEPTH):
+            out[u] = d_att[((z + u) & (DEPTH - 1)) * PLANE + (yx ^ k)]
+
+
+def turn_kernel(b0, b1, b2, b3, *outs):
+    for u, out in enumerate(outs):
+        for m, block in enumerate((b0, b1, b2, b3)):
+            out[m] = block[u]
+
+
+def out_grad_kernel(att_own, d_branch, grad):
+    grad[...] = mul(att_own[...], d_branch[...], 1, 0).astype(bf16)
+
+
+def attend_back_kernel(count, seg_row, b0, b1, b2, b3, c0, c1, c2, c3, lse,
+                       o0, o1, o2, o3, qa, ka, vt, vn, dot, dq, dk, dv):
+    fill_heads(seg_row, count, (b0, b1, b2, b3), qa, ka, vt)
+    span = b0.shape[1]
+    rows = seg_row.shape[1]
+    head = vt.shape[0]
+    total = vt.shape[1]
+    for k in range(PLANE):
+        cols = slice(k * span, (k + 1) * span)
+        vn[cols, :] = vt[:, cols].T
+        for s, block in enumerate((c0, c1, c2, c3)):
+            dot[:, k * span + s * rows : k * span + (s + 1) * rows] = block[k]
+    dk[...] = jnp.zeros_like(dk)
+    dv[...] = jnp.zeros_like(dv)
+
+    def step(i, carry):
+        at = pl.ds(pl.multiple_of(i * 2 * rows, 2 * rows), 2 * rows)
+        scores = mul(ka[...], qa[:, at], 1, 0)
+        soft = jnp.exp(scores - lse[0:1, at])
+        d_out = dot[:, at]
+        d_soft = mul(vn[...], d_out, 1, 0)
+        delta = jnp.sum(soft * d_soft, 0, keepdims=True)
+        d_scores = (soft * (d_soft - delta)).astype(bf16)
+        dv[...] += mul(d_out, soft.astype(bf16), 1, 1)
+        dk[...] += mul(qa[0:head, at], d_scores, 1, 1)
+        keys = ka[:, 0:head]
+        dq[:, at] = (mul(keys, d_scores, 0, 0) * score_scale).astype(bf16)
+        return carry
+
+    lax.fori_loop(0, total // (2 * rows), step, 0)
+    for k, out in enumerate((o0, o1, o2, o3)):
+        cols = slice(k * span, (k + 1) * span)
+        out[0:head, :] = dq[:, cols]
+        out[head : 2 * head, :] = dk[:, cols].astype(bf16)
+        out[2 * head :, :] = dv[:, cols].astype(bf16)
+
+
+def qkv_back_kernel(pos, lead, seg_col, vec, t0, t1, t2, t3, n1, w, g0, g1, g2, g3, d_mid, d_mid_vec, d_out_b,
+                    mine, other, r0, r1, r2, r3, d_vec, joined, grad):
+    z, yx, c = pos[0], pos[1], pos[2]
+    rows, d = t0.shape
+    width = d // DEPTH
+    head = width // PLANE
+    rw = mine.shape[0] // (DEPTH * PLANE)
+    for k, g in enumerate((g0, g1, g2, g3)):
+        for part in range(3):
+            joined[part * PLANE + (yx ^ k)] = g[part * head : (part + 1) * head, :]
+    grads = joined[...].reshape(3 * width, DEPTH * rows)
+    grad[...] = mul(n1[...], grads, 0, 1).astype(bf16)
+    for i in range(DEPTH * PLANE):
+        dst = slice(i * rw, (i + 1) * rw)
+        mine[dst, :] = grad[pl.ds(pl.multiple_of((2 * i + c) * rw, rw), rw), :]
+        other[dst, :] = grad[pl.ds(pl.multiple_of((2 * i + 1 - c) * rw, rw), rw), :]
+    back = mul(grads, w[...], 0, 1)
+    hot = lead_hot(lead, seg_col)
+    shift = mul(hot, vec[0:LEADS, :], 1, 0)
+    gain = vec[ROW_G1 : ROW_G1 + 1, :].astype(f32)
+    d_gain = jnp.zeros((1, d), f32)
+    d_bias = jnp.zeros((1, d), f32)
+    d_emb = d_mid[...]
+    for s, (t, out) in enumerate(zip((t0, t1, t2, t3), (r0, r1, r2, r3))):
+        piece = back[s * rows : (s + 1) * rows, :]
+        out[...] = piece.astype(out.dtype)
+        normal, inv = row_stats(t[...].astype(f32) + shift)
+        d_gain = d_gain + jnp.sum(piece * normal, 0, keepdims=True)
+        d_bias = d_bias + jnp.sum(piece, 0, keepdims=True)
+        d_emb = d_emb + norm_back(piece * gain, normal, inv)
+    high = d_emb.astype(bf16)
+    low = (d_emb - high.astype(f32)).astype(bf16)
+    d_vec[0:LEADS, :] = mul(hot, high, 0, 0) + mul(hot, low, 0, 0)
+    ones = jnp.ones((8, DEPTH * rows), bf16)
+    sums = mul(ones, grads, 1, 1)
+    d_vec[LEADS:, :] = jnp.zeros((VEC_ROWS - LEADS, d), f32)
+    d_vec[ROW_G1 : ROW_G1 + 1, :] = d_gain
+    d_vec[ROW_B1 : ROW_B1 + 1, :] = d_bias
+    at = pl.ds(pl.multiple_of(z * width, width), width)
+    d_vec[ROW_QB : ROW_QB + 1, at] = sums[0:1, 0:width]
+    d_vec[ROW_VB : ROW_VB + 1, at] = sums[0:1, 2 * width :]
+    d_vec[ROW_OB : ROW_OB + 1, :] = d_out_b[0:1, :]
+    d_vec[ROW_G2 : ROW_G2 + 1, :] = d_mid_vec[0:1, :]
+    d_vec[ROW_B2 : ROW_B2 + 1, :] = d_mid_vec[1:2, :]
+    d_vec[ROW_DB : ROW_DB + 1, :] = d_mid_vec[2:3, :]
+
+
+def first_back_kernel(lead, seg_col, vec, tok, d_mid, r0, r1, r2, r3, out):
+    dy = r0[...].astype(f32) + r1[...].astype(f32) + r2[...].astype(f32) + r3[...].astype(f32)
+    shift = mul(lead_hot(lead, seg_col), vec[0:LEADS, :], 1, 0)
+    normal, inv = row_stats(tok[...].astype(f32) + shift)
+    gain = vec[ROW_G1 : ROW_G1 + 1, :].astype(f32)
+    out[...] = d_mid[...] + norm_back(dy * gain, normal, inv)
+
+
+def pair_sum_kernel(mine, other, out):
+    out[...] = (mine[...].astype(f32) + other[...].astype(f32)).astype(bf16)
+
+
+def qkv_pair_kernel(pos, mine, other, o0, o1, o2, o3, total):
+    yx = pos[1]
+    total[...] = (mine[...].astype(f32) + other[...].astype(f32)).astype(bf16)
+    rw = o0.shape[1]
+    for k, out in enumerate((o0, o1, o2, o3)):
+        for zz in range(DEPTH):
+            out[zz] = total[pl.ds(pl.multiple_of((zz * PLANE + (yx ^ k)) * rw, rw), rw), :]
+
+
+def qkv_quad_kernel(pos, b0, b1, b2, b3, o0, o1, o2, o3, total):
+    z = pos[0]
+    total[...] = (
+        b0[...].astype(f32) + b1[...].astype(f32) + b2[...].astype(f32) + b3[...].astype(f32)
+    ).astype(bf16)
+    for u, out in enumerate((o0, o1, o2, o3)):
+        out[...] = total[(z + u) & (DEPTH - 1)]
+
+
+def qkv_join_kernel(pos, b0, b1, b2, b3, out):
+    z = pos[0]
+    width = b0.shape[1] // 3
+    for s, block in enumerate((b0, b1, b2, b3)):
+        at = ((z - s) & (DEPTH - 1)) * width
+        for part in range(3):
+            start = pl.multiple_of(part * DEPTH * width + at, width)
+            out[:, pl.ds(start, width)] = block[:, part * width : (part + 1) * width].astype(f32)
+
+
+def up_pick_kernel(pos, shard, o0, o1, o2, o3, d_down):
+    yx = pos[1]
+    rw = o0.shape[0]
+    for k, out in enumerate((o0, o1, o2, o3)):
+        out[...] = shard[pl.ds(pl.multiple_of((yx ^ k) * rw, rw), rw), :]
+    d_down[...] = shard[PLANE * rw :, :].astype(f32)
+
+
+def up_join_kernel(pos, b0, b1, b2, b3, out):
+    yx = pos[1]
+    fr = b0.shape[1] // (2 * DEPTH)
+    for k, block in enumerate((b0, b1, b2, b3)):
+        for c in range(2):
+            for zz in range(DEPTH):
+                src = (c * DEPTH + zz) * fr
+                dst = pl.multiple_of(((zz * PLANE + (yx ^ k)) * 2 + c) * fr, fr)
+                out[:, pl.ds(dst, fr)] = block[:, src : src + fr].astype(f32)
+
+
+ALL = ("z", "y", "x", "g")
+
+
+def across(blocks):
+    swap = [(0, 1), (1, 0)]
+    return (
+        blocks[0],
+        lax.ppermute(blocks[1], "x", swap),
+        lax.ppermute(blocks[2], "y", swap),
+        lax.ppermute(blocks[3], ("y", "x"), [(i, i ^ 3) for i in range(PLANE)]),
+    )
+
+
+def along(blocks):
+    return (blocks[0],) + tuple(
+        lax.ppermute(blocks[u], "z", [(i, (i + u) % DEPTH) for i in range(DEPTH)])
+        for u in range(1, DEPTH)
+    )
+
+
+def turned(blocks):
+    return (blocks[0], blocks[3], blocks[2], blocks[1])
+
+
+def core_swap(block):
+    return lax.ppermute(block, "g", [(0, 1), (1, 0)])
+
+
+def fast_local(
+    tokens, segment_ids, lead_index, lead_table, ln1_gain, ln1_bias, qkv_weight, q_bias, v_bias,
+    out_weight, out_bias, ln2_gain, ln2_bias, up_weight, up_bias, down_weight, down_bias, d_out,
+):
+    z = lax.axis_index("z")
+    yx = lax.axis_index("y") * 2 + lax.axis_index("x")
+    c = lax.axis_index("g")
+    pos = jnp.stack([z, yx, c]).astype(jnp.int32)
+    tok = tokens[0]
+    rows, d = tok.shape
+    head = d // HEADS
+    span = DEPTH * rows
+    group = PLANE * span
+    rw = qkv_weight.shape[0]
+    fr = down_weight.shape[0]
+    ff = 2 * DEPTH * fr
+    devices = DEPTH * PLANE * 2
+    seg_row = segment_ids
+    seg_col = segment_ids.reshape(rows, 1)
+    lead = lead_index[0]
+    count = lead.shape[0]
+    width = 3 * d // DEPTH
+
+    flat = jnp.concatenate(
+        [lead_table.reshape(-1), ln1_gain, ln1_bias, q_bias, v_bias, out_bias, ln2_gain, ln2_bias, down_bias, up_bias]
+    )
+    padded = -(-flat.shape[0] // 1024) * 1024
+    flat = jnp.pad(flat, (0, padded - flat.shape[0])).reshape(8, padded // 8)
+    smalls = lax.all_to_all(
+        jnp.broadcast_to(flat[None], (devices,) + flat.shape), ALL, split_axis=0, concat_axis=0, tiled=True
+    ).reshape(devices, padded)
+    vec = smalls[:, : VEC_ROWS * rw].reshape(devices, VEC_ROWS, rw).transpose(1, 0, 2).reshape(VEC_ROWS, d)
+    up_b = smalls[:, VEC_ROWS * rw : VEC_ROWS * rw + fr].reshape(DEPTH, PLANE, 2, fr)
+    up_b = lax.dynamic_index_in_dim(up_b, yx, 1, keepdims=False).transpose(1, 0, 2).reshape(1, ff)
+
+    w_out = lax.all_gather(out_weight, ALL, axis=0, tiled=True)
+
+    prep = run(
+        prep_kernel,
+        [((rw, width), bf16)] * 4 + [((2 * rows + rw, d), bf16)] * 4 + [((fr, d), bf16)],
+        [pos, tok, d_out[0], qkv_weight, up_weight, down_weight],
+    )
+    q_rows = along(prep[:4])
+    toks = along((tok,) * DEPTH)
+    q_stack = jnp.stack(q_rows)
+    q_plane = across((q_stack,) * PLANE)
+    wa = jnp.stack(q_plane)
+    wb = core_swap(wa)
+    msgs = across(prep[4:8])
+    shard = jnp.concatenate([m[2 * rows :] for m in msgs] + [down_weight], 0)
+    fa = lax.all_gather(shard[None], "z", axis=0, tiled=True)
+    fb = core_swap(fa)
+
+    n1, w_qkv, *blocks = run(
+        qkv_kernel,
+        [((span, d), bf16), ((d, width), bf16)] + [((3 * head, span), bf16)] * 4,
+        [pos, lead, seg_col, vec, *toks, wa, wb],
+        [((3 * PLANE, head, span), bf16)],
+    )
+    blocks = across(blocks)
+    *att_parts, lse = run(
+        functools.partial(attend_kernel, count),
+        [((head, PLANE * rows), bf16)] * 4 + [((8, group), f32)],
+        [seg_row, *blocks],
+        [((128, group), bf16), ((group, 128), bf16), ((head, group), bf16)],
+    )
+    a0, a1, a2, a3 = along(turned(att_parts))
+    att_parts = across((jnp.stack(turned((a0, a1, a2, a3))),) * PLANE)
+    act, d_hid, n2, w_up, w_down, middle, att_own, p0, p1, p2, p3, d_mid_vec, d_up_b = run(
+        mid_kernel,
+        [((span, ff), bf16), ((span, ff), bf16), ((span, d), bf16), ((d, ff), bf16), ((ff, d), bf16),
+         ((rows, d), f32), ((d, rows), bf16), ((rows, d), f32)] + [((rows, d), bf16)] * 3
+        + [((8, d), f32), ((1, ff), f32)],
+        [pos, lead, seg_col, vec, up_b, *att_parts, *msgs, w_out, fa, fb],
+        [((d, span), bf16), ((span, d), f32), ((span, 128), f32), ((span, ff), f32), ((8, 128), f32)],
+        vmem_mb=56,
+    )
+    parts = across((p0, p1, p2, p3))
+    o0, o1, o2, o3, mine, other = run(
+        ffn_grad_kernel,
+        [((rows, d), f32)] + [((rows, d), bf16)] * 3 + [((DEPTH, PLANE * rw + fr, d), bf16)] * 2,
+        [pos, vec, act, d_hid, n2, w_down, middle, *msgs],
+        [((d, ff), bf16)],
+    )
+    o0, o1, o2, o3 = across((o0, o1, o2, o3))
+    layer_out = (o0 + o1.astype(f32) + o2.astype(f32) + o3.astype(f32)).astype(bf16)
+    (ffn_sum,) = run(pair_sum_kernel, [(mine.shape, bf16)], [mine, core_swap(other)])
+    ffn_shard = lax.psum_scatter(ffn_sum, "z", scatter_dimension=0, tiled=True)[0]
+
+    d_mid, d_branch, d_out_b, *d_att = run(
+        branch_kernel,
+        [((rows, d), f32), ((rows, d), bf16), ((8, d), f32)] + [((DEPTH, head, rows), bf16)] * 4,
+        [pos, vec, middle, d_out[0], w_out, *parts],
+        [((HEADS, head, rows), bf16)],
+    )
+    d_att = along(run(turn_kernel, [((PLANE, head, rows), bf16)] * 4, list(across(d_att))))
+    (out_grad,) = run(out_grad_kernel, [((d, d), bf16)], [att_own, d_branch])
+    d_out_weight = lax.psum_scatter(out_grad, ALL, scatter_dimension=0, tiled=True).astype(f32)
+    d_blocks = run(
+        functools.partial(attend_back_kernel, count),
+        [((3 * head, span), bf16)] * 4,
+        [seg_row, *blocks, *d_att, lse],
+        [((128, group), bf16), ((group, 128), bf16), ((head, group), bf16), ((group, head), bf16),
+         ((head, group), bf16), ((head, group), bf16), ((head, group), f32), ((head, group), f32)],
+    )
+    d_blocks = across(d_blocks)
+    mine, other, r0, r1, r2, r3, d_vec = run(
+        qkv_back_kernel,
+        [((DEPTH * PLANE * rw, width), bf16)] * 2 + [((rows, d), f32)] + [((rows, d), bf16)] * 3
+        + [((VEC_ROWS, d), f32)],
+        [pos, lead, seg_col, vec, *toks, n1, w_qkv, *d_blocks, d_mid, d_mid_vec, d_out_b],
+        [((3 * PLANE, head, span), bf16), ((d, width), bf16)],
+    )
+    back = along(turned((r0, r1, r2, r3)))
+    other = core_swap(other)
+    quads = run(qkv_pair_kernel, [((DEPTH, rw, width), bf16)] * 4, [pos, mine, other],
+                [(mine.shape, bf16)])
+    quads = across(quads)
+    cols = along(run(qkv_quad_kernel, [((rw, width), bf16)] * 4, [pos, *quads], [((DEPTH, rw, width), bf16)]))
+    (d_qkv,) = run(qkv_join_kernel, [((rw, 3 * d), f32)], [pos, *cols])
+    (d_tokens,) = run(first_back_kernel, [((rows, d), f32)], [lead, seg_col, vec, tok, d_mid, *back])
+
+    *ups, d_down = run(up_pick_kernel, [((rw, ff), bf16)] * 4 + [((fr, d), f32)], [pos, ffn_shard])
+    (d_up,) = run(up_join_kernel, [((rw, PLANE * ff), f32)], [pos, *across(ups)])
+
+    sums = d_vec.reshape(VEC_ROWS, devices, rw).transpose(1, 0, 2).reshape(devices, VEC_ROWS * rw)
+    up_sums = d_up_b.reshape(2, DEPTH, fr).transpose(1, 0, 2)[:, None]
+    up_sums = jnp.where(jnp.arange(PLANE)[None, :, None, None] == yx, up_sums, 0.0).reshape(devices, fr)
+    flat = jnp.concatenate([sums, up_sums], 1)
+    flat = jnp.pad(flat, ((0, 0), (0, padded - flat.shape[1]))).reshape(devices, 8, padded // 8)
+    flat = jnp.sum(lax.all_to_all(flat, ALL, split_axis=0, concat_axis=0, tiled=True), 0).reshape(padded)
+    table = flat[: LEADS * rw].reshape(LEADS, rw)
+    vecs = flat[LEADS * rw : VEC_ROWS * rw].reshape(VEC_ROWS - LEADS, rw)
+    d_g1, d_b1, d_qb, d_vb, d_ob, d_g2, d_b2, d_db = (vecs[i] for i in range(8))
+    d_ub = flat[VEC_ROWS * rw : VEC_ROWS * rw + fr]
+    return (
+        layer_out[None], d_tokens[None], table, d_g1, d_b1, d_qkv, d_qb, d_vb, d_out_weight, d_ob,
+        d_g2, d_b2, d_up, d_ub, d_down, d_db,
+    )
+
+
+def specs(band, grp):
+    every = band + grp
+    rows = P(grp, band, None)
+    in_specs = (
+        rows, P(grp, band), P(grp, None), P(None, every), P(every), P(every), P(every, None), P(every), P(every),
+        P(every, None), P(every), P(every), P(every), P(every, None), P(every), P(every, None), P(every), rows,
+    )
+    out_specs = (
+        rows, rows, P(None, every), P(every), P(every), P(every, None), P(every), P(every), P(every, None), P(every),
+        P(every), P(every), P(every, None), P(every), P(every, None), P(every),
+    )
+    return in_specs, out_specs
+
+
 def solution(mesh):
-    return jax.shard_map(
-        local,
-        mesh=mesh,
-        in_specs=(
-            P("grp", "band", None),
-            P("grp", "band"),
-            P("grp", None),
-            P(None, ("band", "grp")),
-            P(("band", "grp")),
-            P(("band", "grp")),
-            P(("band", "grp"), None),
-            P(("band", "grp")),
-            P(("band", "grp")),
-            P(("band", "grp"), None),
-            P(("band", "grp")),
-            P(("band", "grp")),
-            P(("band", "grp")),
-            P(("band", "grp"), None),
-            P(("band", "grp")),
-            P(("band", "grp"), None),
-            P(("band", "grp")),
-            P("grp", "band", None),
-        ),
-        out_specs=(
-            P("grp", "band", None),
-            P("grp", "band", None),
-            P(None, ("band", "grp")),
-            P(("band", "grp")),
-            P(("band", "grp")),
-            P(("band", "grp"), None),
-            P(("band", "grp")),
-            P(("band", "grp")),
-            P(("band", "grp"), None),
-            P(("band", "grp")),
-            P(("band", "grp")),
-            P(("band", "grp")),
-            P(("band", "grp"), None),
-            P(("band", "grp")),
-            P(("band", "grp"), None),
-            P(("band", "grp")),
-        ),
-        check_vma=False,
-    )
+    band, grp = mesh.shape["band"], mesh.shape["grp"]
+    if band == HEADS and grp == 2:
+        mesh = Mesh(mesh.devices.reshape(DEPTH, 2, 2, grp), ("z", "y", "x", "g"))
+        in_specs, out_specs = specs(("z", "y", "x"), ("g",))
+        return jax.shard_map(fast_local, mesh=mesh, in_specs=in_specs, out_specs=out_specs, check_vma=False)
+    in_specs, out_specs = specs(("band",), ("grp",))
+    return jax.shard_map(local, mesh=mesh, in_specs=in_specs, out_specs=out_specs, check_vma=False)

time: 1570 us -> 428 us (0.27)
  waiting for transfers between devices: 1130 us -> 222 us
  blocking collectives: 160 us -> 0 us
  matrix products: 129 us -> 0 us
  local copies, waits for them, and re-layouts: 117 us -> 30.9 us
  starting transfers between devices: 0.78 us -> 78 us
  Pallas kernels: 0 us -> 76.3 us
    reduce_scatter x4 -> x2, waiting for transfers between devices: 669 us -> 53.3 us  [the longest x1 53.3 us: fast_local(): lax.psum_scatter(out_grad, ALL, scatter_dimension=0, tiled=True).astype(f32)]
    unnamed x16 -> x4, waiting for transfers between devices: 212 us -> 0.75 us
    all_gather x6 -> x2, waiting for transfers between devices: 244 us -> 45.6 us  [the longest x1 45.6 us: fast_local(): fa = lax.all_gather(shard[None], 'z', axis=0, tiled=True)]
    dot_general x32 -> x0, matrix products: 127 us -> none  [the longest x6 19.3 us: block_scores(): jnp.einsum('qhd,khd->hqk', query_heads, key_heads, preferred_element_type...]
    ppermute x0 -> x52, waiting for transfers between devices: none -> 99.2 us  [the longest x10 32.5 us: across(): lax.ppermute(blocks[1], 'x', swap)]
    unnamed x2 -> x0, blocking collectives: 82.1 us -> none
    all_gather x2 -> x0, blocking collectives: 77.9 us -> none  [the longest x1 41.4 us: local(): lax.all_gather(lead_table, ('band', 'grp'), axis=1, tiled=True)]
    pallas_call x0 -> x17, Pallas kernels: none -> 76.3 us  [run(): pl.pallas_call(kernel, out_shape=[jax.ShapeDtypeStruct(s, d) for s, d in...]
  transfers between devices with their start and end apart: 13 -> 58, of which waited for: 12 -> 34; matrix products, arithmetic and copies ran while one was open for 11% -> 3% of each run, Pallas kernels for 0% -> 11%
where the time goes in v1:
time: 428 us; the launch traced here: 427 us
  waiting for transfers between devices  222 us (52%)
  starting transfers between devices  78 us (18%)
  Pallas kernels  76.3 us (18%)
  local copies, waits for them, and re-layouts  30.9 us (7%)
  between operations  14.6 us (3%)
  other arithmetic  5.39 us (1%)
    pallas_call x17, Pallas kernels, run(): pl.pallas_call(kernel, out_shape=[jax.ShapeDtypeStruct(s, d) for s, d in...  76.3 us
    reduce_scatter x1, waiting for transfers between devices, fast_local(): lax.psum_scatter(out_grad, ALL, scatter_dimension=0, tiled=True).astype(f32)  53.3 us
    all_gather x1, waiting for transfers between devices, fast_local(): fa = lax.all_gather(shard[None], 'z', axis=0, tiled=True)  45.6 us
    ppermute x10, waiting for transfers between devices, across(): lax.ppermute(blocks[1], 'x', swap)  32.5 us
    ppermute x18, starting transfers between devices, along(): lax.ppermute(blocks[u], 'z', [(i, (i + u) % DEPTH) for i in range(DEPTH)])  31.3 us
    ppermute x10, waiting for transfers between devices, across(): lax.ppermute(blocks[2], 'y', swap)  29.7 us
    unnamed x172, local copies, waits for them, and re-layouts  24.5 us
    all_to_all x1, waiting for transfers between devices, fast_local(): lax.all_to_all(jnp.broadcast_to(flat[None], (devices,) + flat.shape), ALL...  21.6 us
  transfers between devices with their start and end apart: 58, of which 34 were waited for; matrix products, arithmetic and copies ran while one was open for 3% of the time, Pallas kernels for 11%

profile of v1, /device:TPU:0, one launch (start us, length us, event | category | flops | bytes accessed | tf_op | source)
XLA Modules:
  0.0 427.5 jit_solution(3634417668297186017)
XLA Ops:
  12.0 1.4 shard_map.297
  13.6 3.0 collective-permute-start.19
  16.6 1.5 collective-permute-start.20
  18.2 12.6 %collective-permute-done.19.m1 = bf16[288,1024]{1,0:T(8,128)(2,1)S(1)} collective-permute-done((bf16[288,1024]{1,0:T(8,128)(2,1)S(1)}, bf16[288,1024]{1,0:T(8,128)(2,1)S(1)}, u32[]{:S(2)}, u32[]{:S(2)}) %collective-permute-start.19) | collective-permute-done | bytes 589856 | tf_op jit(solution)/shard_map/ppermute | solution.py:745
  30.8 13.3 %collective-permute-done.20.m2 = bf16[288,1024]{1,0:T(8,128)(2,1)S(1)} collective-permute-done((bf16[288,1024]{1,0:T(8,128)(2,1)S(1)}, bf16[288,1024]{1,0:T(8,128)(2,1)S(1)}, u32[]{:S(2)}, u32[]{:S(2)}) %collective-permute-start.20) | collective-permute-done | bytes 589856 | tf_op jit(solution)/shard_map/ppermute | solution.py:746
  45.8 45.6 %all-gather.6.cloned.1.call-done = bf16[1024,1024]{1,0:T(8,128)(2,1)} async-done(((bf16[256,1024]{1,0:T(8,128)(2,1)}), bf16[1024,1024]{1,0:T(8,128)(2,1)}) %all-gather.6.cloned.1.call-update) | async-done | bytes 2097168 | tf_op jit(solution)/shard_map/all_gather | solution.py:816
  91.4 1.8 collective-permute-start.4
  93.2 2.2 collective-permute-start.5
  95.4 2.4 collective-permute-done.3
  98.6 1.6 collective-permute-start.7
  100.2 1.5 collective-permute-start.6
  102.2 3.9 collective-permute-done.7
  106.1 2.4 collective-permute-done.6
  108.5 2.9 collective-permute-done.8
  111.5 1.8 collective-permute-start.2
  116.4 5.7 %all-to-all-start = ((bf16[32,8,128]{2,1,0:T(8,128)(2,1)}), bf16[32,8,128]{2,1,0:T(8,128)(2,1)S(1)}, u32[]{:S(2)}, u32[]{:S(2)}) async-start(bf16[32,8,128]{2,1,0:T(8,128)(2,1)} %broadcast_in_dim.45), calls=%async_computation | async-start | bytes 131072 | tf_op jit(solution)/shard_map/all_to_all | solution.py:794
  122.3 21.6 %all-to-all-done = bf16[32,8,128]{2,1,0:T(8,128)(2,1)S(1)} async-done(((bf16[32,8,128]{2,1,0:T(8,128)(2,1)}), bf16[32,8,128]{2,1,0:T(8,128)(2,1)S(1)}, u32[]{:S(2)}, u32[]{:S(2)}) %all-to-all-start) | async-done | bytes 65568 | tf_op jit(solution)/shard_map/all_to_all | solution.py:794
  145.1 3.3 shard_map.298
  151.8 2.3 collective-permute-start.12
  154.0 4.3 %collective-permute-done.10.b1 = bf16[192,512]{1,0:T(8,128)(2,1)S(1)} collective-permute-done((bf16[192,512]{1,0:T(8,128)(2,1)S(1)}, bf16[192,512]{1,0:T(8,128)(2,1)S(1)}, u32[]{:S(2)}, u32[]{:S(2)}) %collective-permute-start.10) | collective-permute-done | bytes 196640 | tf_op jit(solution)/shard_map/ppermute | solution.py:745
  158.4 3.8 collective-permute-done.11.b2
  162.2 10.4 %shard_map.299 = (bf16[64,512]{1,0:T(8,128)(2,1)S(1)}, bf16[64,512]{1,0:T(8,128)(2,1)S(1)}, bf16[64,512]{1,0:T(8,128)(2,1)S(1)}, bf16[64,512]{1,0:T(8,128)(2,1)S(1)}, f32[8,2048]{1,0:T(8,128)S(1)}) custom-call(s32[1,128]{1,0:T(1,128)S(1)} %copy-done.55, bf16[192,512]{1,0:T(8,128)(2,1)S(1)} %get-tuple-element.92.b0, ...), custom_call_target="tpu_custom_call" | custom-call | tf_op jit(solution)/shard_map/pallas_call | solution.py:329
  172.6 2.3 collective-permute-start.13
  176.9 3.5 collective-permute-done.14
  181.2 1.6 collective-permute-start.18
  186.2 5.2 %collective-permute-done.18.a3 = bf16[4,64,512]{2,1,0:T(8,128)(2,1)S(1)} collective-permute-done((bf16[4,64,512]{2,1,0:T(8,128)(2,1)S(1)}, bf16[4,64,512]{2,1,0:T(8,128)(2,1)S(1)}, u32[]{:S(2)}, u32[]{:S(2)}) %collective-permute-start.18) | collective-permute-done | bytes 262176 | tf_op jit(solution)/shard_map/ppermute | solution.py:747
  191.4 2.9 collective-permute-done.17.a2
  194.3 13.0 %shard_map.300 = (bf16[512,1024]{1,0:T(8,128)(2,1)}, bf16[512,1024]{1,0:T(8,128)(2,1)}, bf16[512,1024]{1,0:T(8,128)(2,1)}, bf16[1024,1024]{1,0:T(8,128)(2,1)}, b...) custom-call(s32[3]{0:T(128)} %copy-done.42, ...), custom_call_target="tpu_custom_call" | custom-call | tf_op jit(solution)/shard_map/pallas_call | solution.py:329
  210.4 9.0 %shard_map.301 = (f32[128,1024]{1,0:T(8,128)S(1)}, bf16[128,1024]{1,0:T(8,128)(2,1)}, bf16[128,1024]{1,0:T(8,128)(2,1)}, bf16[128,1024]{1,0:T(8,128)(2,1)}, bf16...) custom-call(s32[3]{0:T(128)S(1)} %copy-done.43, bf16[24,1024]{1,0:T(8,128)(2,1)S(1)} %copy-done.12, ...), custom_call_target="tpu_custom_call" | custom-call | tf_op jit(solution)/shard_map/pallas_call | solution.py:329
  220.2 4.4 %collective-permute-done.48.other = bf16[4,256,1024]{2,1,0:T(8,128)(2,1)S(1)} collective-permute-done((bf16[4,256,1024]{2,1,0:T(8,128)(2,1)}, bf16[4,256,1024]{2,1,0:T(8,128)(2,1)S(1)}, u32[]{:S(2)}, u32[]{:S(2)}) %collective-permute-start.48) | collective-permute-done | bytes 2097184 | tf_op jit(solution)/shard_map/ppermute | solution.py:763
  226.0 1.6 copy-done.14
  227.6 3.5 shard_map.311
  233.3 1.6 collective-permute-start.28
  235.0 5.9 %collective-permute-done.26.p1 = bf16[128,1024]{1,0:T(8,128)(2,1)S(1)} collective-permute-done((bf16[128,1024]{1,0:T(8,128)(2,1)}, bf16[128,1024]{1,0:T(8,128)(2,1)S(1)}, u32[]{:S(2)}, u32[]{:S(2)}) %collective-permute-start.26) | collective-permute-done | bytes 262176 | tf_op jit(solution)/shard_map/ppermute | solution.py:745
  241.2 4.8 %collective-permute-done.28.p3 = bf16[128,1024]{1,0:T(8,128)(2,1)S(1)} collective-permute-done((bf16[128,1024]{1,0:T(8,128)(2,1)S(1)}, bf16[128,1024]{1,0:T(8,128)(2,1)S(1)}, u32[]{:S(2)}, u32[]{:S(2)}) %collective-permute-start.28) | collective-permute-done | bytes 262176 | tf_op jit(solution)/shard_map/ppermute | solution.py:747
  248.0 1.7 shard_map.302
  252.9 2.0 shard_map.310
  257.1 1.5 collective-permute-start.31
  262.7 1.8 collective-permute-start.33
  264.6 2.8 collective-permute-start.34
  267.4 3.2 collective-permute-done.32.c1
  270.7 3.2 collective-permute-done.33.c2
  273.9 17.1 %shard_map.304 = (bf16[192,512]{1,0:T(8,128)(2,1)S(1)}, bf16[192,512]{1,0:T(8,128)(2,1)S(1)}, bf16[192,512]{1,0:T(8,128)(2,1)S(1)}, bf16[192,512]{1,0:T(8,128)(2,1)S(1)}) custom-call(s32[1,128]{1,0:T(1,128)S(1)} %copy-done.55, bf16[192,512]{1,0:T(8,128)(2,1)S(1)} %copy-done.26, bf16[192,512]{1,0:T(8,128)(2,1)S(1)} %copy-done.28, ...), custom_call_target="tpu_custom_call" | custom-call | tf_op jit(solution)/shard_map/pallas_call | solution.py:329
  291.1 1.7 collective-permute-start.35
  292.8 1.4 collective-permute-start.36
  294.6 5.4 %collective-permute-done.35.g1 = bf16[192,512]{1,0:T(8,128)(2,1)S(1)} collective-permute-done((bf16[192,512]{1,0:T(8,128)(2,1)S(1)}, bf16[192,512]{1,0:T(8,128)(2,1)S(1)}, u32[]{:S(2)}, u32[]{:S(2)}) %collective-permute-start.35) | collective-permute-done | bytes 196640 | tf_op jit(solution)/shard_map/ppermute | solution.py:745
  300.2 3.6 collective-permute-done.37.g3
  303.9 5.8 %shard_map.305 = (bf16[512,768]{1,0:T(8,128)(2,1)S(1)}, bf16[512,768]{1,0:T(8,128)(2,1)}, f32[128,1024]{1,0:T(8,128)S(1)}, bf16[128,1024]{1,0:T(8,128)(2,1)S(1)}...) custom-call(s32[3]{0:T(128)S(1)} %copy-done.44, s32[4]{0:T(128)S(1)} %bitcast.79, ...), custom_call_target="tpu_custom_call" | custom-call | tf_op jit(solution)/shard_map/pallas_call | solution.py:329
  313.9 1.5 collective-permute-start.25
  315.5 1.7 shard_map.307
  319.9 4.1 collective-permute-start.38
  325.2 3.8 all-to-all-start.1
  329.1 2.7 collective-permute-start.39
  331.7 1.5 collective-permute-start.40
  333.2 1.6 collective-permute-start.43
  336.5 2.0 fusion
  338.4 1.8 all-to-all-done.1
  341.3 4.1 collective-permute-done.43.b2
  346.5 3.1 collective-permute-start.45
  350.2 2.9 collective-permute-start.46
  358.2 2.0 collective-permute-start.51
  361.4 2.0 shard_map.306
  364.7 53.3 %reduce-scatter.3.cloned.1.call-done = bf16[32,1024]{1,0:T(8,128)(2,1)} async-done(((bf16[1024,1024]{1,0:T(8,128)(2,1)}), bf16[32,1024]{1,0:T(8,128)(2,1)}) %reduce-scatter.3.cloned.1.call-update) | async-done | bytes 65552 | tf_op jit(solution)/shard_map/reduce_scatter | solution.py:863
  418.0 1.5 convert_element_type.23
  (282 shorter events, 63.4 us)
Async XLA Ops:
  7.2 84.2 %all-gather.6.cloned.1.call-start = ((), (), s32[]{:S(2)}) async-start(), calls=%async_computation.7 | async-start | bytes 2621440 | tf_op jit(solution)/shard_map/all_gather | solution.py:816
  7.3 137.8 %copy-start.42 = (s32[3]{0:T(128)}, s32[3]{0:T(128)S(1)}, u32[]{:S(2)}) copy-start(s32[3]{0:T(128)S(1)} %pad_add_fusion.pos) | copy-start | bytes 40
  13.5 130.4 %copy-start.3 = (bf16[288,1024]{1,0:T(8,128)(2,1)}, bf16[288,1024]{1,0:T(8,128)(2,1)S(1)}, u32[]{:S(2)}) copy-start(bf16[288,1024]{1,0:T(8,128)(2,1)S(1)} %get-tuple-element.100.m0) | copy-start | bytes 1769476
  13.5 101.5 %copy-start.73 = (bf16[32]{0:T(256)(128)(2,1)S(1)}, bf16[32]{0:T(256)(128)(2,1)}, u32[]{:S(2)}) copy-start(bf16[32]{0:T(256)(128)(2,1)} %param.22) | copy-start | bytes 196
  13.5 101.5 %copy-start.74 = (bf16[32]{0:T(256)(128)(2,1)S(1)}, bf16[32]{0:T(256)(128)(2,1)}, u32[]{:S(2)}) copy-start(bf16[32]{0:T(256)(128)(2,1)} %param.23) | copy-start | bytes 196
  13.6 108.6 %copy-start.55 = (s32[1,128]{1,0:T(1,128)S(1)}, s32[1,128]{1,0:T(1,128)}, u32[]{:S(2)}) copy-start(s32[1,128]{1,0:T(1,128)} %seg_row.3) | copy-start | bytes 1540
  13.6 17.2 %collective-permute-start.19 = (bf16[288,1024]{1,0:T(8,128)(2,1)S(1)}, bf16[288,1024]{1,0:T(8,128)(2,1)S(1)}, u32[]{:S(2)}, u32[]{:S(2)}) collective-permute-start(bf16[288,1024]{1,0:T(8,128)(2,1)S(1)} %get-tuple-element.101), channel_id=1, source_target_pairs={{0,2},{2,0},{1,3},{3,1},{4,6},{6,4},{5,7},{7,5},{8,10},{10,8},{9,1... | collective-permute-start | bytes 1769480 | tf_op jit(solution)/shard_map/ppermute | solution.py:745
  16.6 27.4 %collective-permute-start.20 = (bf16[288,1024]{1,0:T(8,128)(2,1)S(1)}, bf16[288,1024]{1,0:T(8,128)(2,1)S(1)}, u32[]{:S(2)}, u32[]{:S(2)}) collective-permute-start(bf16[288,1024]{1,0:T(8,128)(2,1)S(1)} %get-tuple-element.102), channel_id=1, source_target_pairs={{0,4},{4,0},{1,5},{5,1},{2,6},{6,2},{3,7},{7,3},{8,12},{12,8},{9,1... | collective-permute-start | bytes 1769480 | tf_op jit(solution)/shard_map/ppermute | solution.py:746
  18.1 25.9 %collective-permute-start.21 = (bf16[288,1024]{1,0:T(8,128)(2,1)S(1)}, bf16[288,1024]{1,0:T(8,128)(2,1)S(1)}, u32[]{:S(2)}, u32[]{:S(2)}) collective-permute-start(bf16[288,1024]{1,0:T(8,128)(2,1)S(1)} %get-tuple-element.103), channel_id=1, source_target_pairs={{0,6},{2,4},{4,2},{6,0},{1,7},{3,5},{5,3},{7,1},{8,14},{10,12},{12... | collective-permute-start | bytes 1769480 | tf_op jit(solution)/shard_map/ppermute | solution.py:747
  30.8 113.8 %copy-start.5 = (bf16[288,1024]{1,0:T(8,128)(2,1)}, bf16[288,1024]{1,0:T(8,128)(2,1)S(1)}, u32[]{:S(2)}) copy-start(bf16[288,1024]{1,0:T(8,128)(2,1)S(1)} %collective-permute-done.19.m1) | copy-start | bytes 1769476
  45.0 149.3 %all-gather.4.cloned.1.call-start = ((), (), s32[]{:S(2)}) async-start(), calls=%async_computation.4 | async-start | bytes 2162688 | tf_op jit(solution)/shard_map/all_gather | solution.py:801
  91.4 102.9 %collective-permute-start.22 = (bf16[4,256,1024]{2,1,0:T(8,128)(2,1)}, bf16[4,256,1024]{2,1,0:T(8,128)(2,1)}, u32[]{:S(2)}, u32[]{:S(2)}) collective-permute-start(bf16[4,256,1024]{2,1,0:T(8,128)(2,1)} %bitcast.82), channel_id=1, source_target_pairs={{0,1},{1,0},{2,3},{3,2},{4,5},{5,4},{6,7},{7,6},{8,9},{9,8},{10,11... | collective-permute-start | bytes 6291464 | tf_op jit(solution)/shard_map/ppermute | solution.py:763
  91.4 6.4 %collective-permute-start.3 = (bf16[32,768]{1,0:T(8,128)(2,1)S(1)}, bf16[32,768]{1,0:T(8,128)(2,1)S(1)}, u32[]{:S(2)}, u32[]{:S(2)}) collective-permute-start(bf16[32,768]{1,0:T(8,128)(2,1)S(1)} %get-tuple-element.89), channel_id=1, source_target_pairs={{0,8},{8,16},{16,24},{24,0},{1,9},{9,17},{17,25},{25,1},{2,10},{10... | collective-permute-start | bytes 147464 | tf_op jit(solution)/shard_map/ppermute | solution.py:753
  91.4 6.9 %collective-permute-start.4 = (bf16[32,768]{1,0:T(8,128)(2,1)S(1)}, bf16[32,768]{1,0:T(8,128)(2,1)S(1)}, u32[]{:S(2)}, u32[]{:S(2)}) collective-permute-start(bf16[32,768]{1,0:T(8,128)(2,1)S(1)} %get-tuple-element.90), channel_id=1, source_target_pairs={{0,16},{8,24},{16,0},{24,8},{1,17},{9,25},{17,1},{25,9},{2,18},{10... | collective-permute-start | bytes 147464 | tf_op jit(solution)/shard_map/ppermute | solution.py:753
  93.2 5.4 %collective-permute-start.5 = (bf16[32,768]{1,0:T(8,128)(2,1)S(1)}, bf16[32,768]{1,0:T(8,128)(2,1)S(1)}, u32[]{:S(2)}, u32[]{:S(2)}) collective-permute-start(bf16[32,768]{1,0:T(8,128)(2,1)S(1)} %get-tuple-element.91), channel_id=1, source_target_pairs={{0,24},{8,0},{16,8},{24,16},{1,25},{9,1},{17,9},{25,17},{2,26},{10... | collective-permute-start | bytes 147464 | tf_op jit(solution)/shard_map/ppermute | solution.py:753
  98.6 7.5 %collective-permute-start.7 = (bf16[4,32,768]{2,1,0:T(8,128)(2,1)S(1)}, bf16[4,32,768]{2,1,0:T(8,128)(2,1)S(1)}, u32[]{:S(2)}, u32[]{:S(2)}) collective-permute-start(bf16[4,32,768]{2,1,0:T(8,128)(2,1)S(1)} %get-tuple-element.161), channel_id=1, source_target_pairs={{0,4},{4,0},{1,5},{5,1},{2,6},{6,2},{3,7},{7,3},{8,12},{12,8},{9,1... | collective-permute-start | bytes 589832 | tf_op jit(solution)/shard_map/ppermute | solution.py:746
  100.2 8.3 %collective-permute-start.6 = (bf16[4,32,768]{2,1,0:T(8,128)(2,1)S(1)}, bf16[4,32,768]{2,1,0:T(8,128)(2,1)S(1)}, u32[]{:S(2)}, u32[]{:S(2)}) collective-permute-start(bf16[4,32,768]{2,1,0:T(8,128)(2,1)S(1)} %get-tuple-element.161), channel_id=1, source_target_pairs={{0,2},{2,0},{1,3},{3,1},{4,6},{6,4},{5,7},{7,5},{8,10},{10,8},{9,1... | collective-permute-start | bytes 589832 | tf_op jit(solution)/shard_map/ppermute | solution.py:745
  101.6 9.7 %collective-permute-start.8 = (bf16[4,32,768]{2,1,0:T(8,128)(2,1)S(1)}, bf16[4,32,768]{2,1,0:T(8,128)(2,1)S(1)}, u32[]{:S(2)}, u32[]{:S(2)}) collective-permute-start(bf16[4,32,768]{2,1,0:T(8,128)(2,1)S(1)} %get-tuple-element.161), channel_id=1, source_target_pairs={{0,6},{2,4},{4,2},{6,0},{1,7},{3,5},{5,3},{7,1},{8,14},{10,12},{12... | collective-permute-start | bytes 589832 | tf_op jit(solution)/shard_map/ppermute | solution.py:747
  111.4 33.6 %collective-permute-start.9 = (bf16[4,4,32,768]{3,2,1,0:T(8,128)(2,1)S(1)}, bf16[4,4,32,768]{3,2,1,0:T(8,128)(2,1)}, u32[]{:S(2)}, u32[]{:S(2)}) collective-permute-start(bf16[4,4,32,768]{3,2,1,0:T(8,128)(2,1)S(1)} %pad_maximum_fusion.wa), channel_id=1, source_target_pairs={{0,1},{1,0},{2,3},{3,2},{4,5},{5,4},{6,7},{7,6},{8,9},{9,8},{10,11... | collective-permute-start | bytes 2359304 | tf_op jit(solution)/shard_map/ppermute | solution.py:763
  111.5 33.5 %collective-permute-start.2 = (bf16[128,1024]{1,0:T(8,128)(2,1)S(1)}, bf16[128,1024]{1,0:T(8,128)(2,1)}, u32[]{:S(2)}, u32[]{:S(2)}) collective-permute-start(bf16[128,1024]{1,0:T(8,128)(2,1)S(1)} %bitcast.66), channel_id=1, source_target_pairs={{0,24},{8,0},{16,8},{24,16},{1,25},{9,1},{17,9},{25,17},{2,26},{10... | collective-permute-start | bytes 786440 | tf_op jit(solution)/shard_map/ppermute | solution.py:753
  113.3 31.7 %collective-permute-start.1 = (bf16[128,1024]{1,0:T(8,128)(2,1)S(1)}, bf16[128,1024]{1,0:T(8,128)(2,1)}, u32[]{:S(2)}, u32[]{:S(2)}) collective-permute-start(bf16[128,1024]{1,0:T(8,128)(2,1)S(1)} %bitcast.67), channel_id=1, source_target_pairs={{0,16},{8,24},{16,0},{24,8},{1,17},{9,25},{17,1},{25,9},{2,18},{10... | collective-permute-start | bytes 786440 | tf_op jit(solution)/shard_map/ppermute | solution.py:753
  114.5 30.5 %collective-permute-start = (bf16[128,1024]{1,0:T(8,128)(2,1)S(1)}, bf16[128,1024]{1,0:T(8,128)(2,1)}, u32[]{:S(2)}, u32[]{:S(2)}) collective-permute-start(bf16[128,1024]{1,0:T(8,128)(2,1)S(1)} %bitcast.68), channel_id=1, source_target_pairs={{0,8},{8,16},{16,24},{24,0},{1,9},{9,17},{17,25},{25,1},{2,10},{10... | collective-permute-start | bytes 786440 | tf_op jit(solution)/shard_map/ppermute | solution.py:753
  116.4 27.5 %all-to-all-start = ((bf16[32,8,128]{2,1,0:T(8,128)(2,1)}), bf16[32,8,128]{2,1,0:T(8,128)(2,1)S(1)}, u32[]{:S(2)}, u32[]{:S(2)}) async-start(bf16[32,8,128]{2,1,0:T(8,128)(2,1)} %broadcast_in_dim.45), calls=%async_computation | async-start | bytes 131072 | tf_op jit(solution)/shard_map/all_to_all | solution.py:794
  122.1 230.9 %reduce-scatter.5.cloned.1.call-start = ((), (), s32[]{:S(2)}) async-start(), calls=%async_computation.6 | async-start | bytes 2621440 | tf_op jit(solution)/shard_map/reduce_scatter | solution.py:853
  150.6 7.8 %collective-permute-start.10 = (bf16[192,512]{1,0:T(8,128)(2,1)S(1)}, bf16[192,512]{1,0:T(8,128)(2,1)S(1)}, u32[]{:S(2)}, u32[]{:S(2)}) collective-permute-start(bf16[192,512]{1,0:T(8,128)(2,1)S(1)} %get-tuple-element.93), channel_id=1, source_target_pairs={{0,2},{2,0},{1,3},{3,1},{4,6},{6,4},{5,7},{7,5},{8,10},{10,8},{9,1... | collective-permute-start | bytes 589832 | tf_op jit(solution)/shard_map/ppermute | solution.py:745
  151.3 10.9 %collective-permute-start.11 = (bf16[192,512]{1,0:T(8,128)(2,1)S(1)}, bf16[192,512]{1,0:T(8,128)(2,1)S(1)}, u32[]{:S(2)}, u32[]{:S(2)}) collective-permute-start(bf16[192,512]{1,0:T(8,128)(2,1)S(1)} %get-tuple-element.94), channel_id=1, source_target_pairs={{0,4},{4,0},{1,5},{5,1},{2,6},{6,2},{3,7},{7,3},{8,12},{12,8},{9,1... | collective-permute-start | bytes 589832 | tf_op jit(solution)/shard_map/ppermute | solution.py:746
  151.8 10.4 %collective-permute-start.12 = (bf16[192,512]{1,0:T(8,128)(2,1)S(1)}, bf16[192,512]{1,0:T(8,128)(2,1)S(1)}, u32[]{:S(2)}, u32[]{:S(2)}) collective-permute-start(bf16[192,512]{1,0:T(8,128)(2,1)S(1)} %get-tuple-element.95), channel_id=1, source_target_pairs={{0,6},{2,4},{4,2},{6,0},{1,7},{3,5},{5,3},{7,1},{8,14},{10,12},{12... | collective-permute-start | bytes 589832 | tf_op jit(solution)/shard_map/ppermute | solution.py:747
  172.6 4.3 %collective-permute-start.13 = (bf16[64,512]{1,0:T(8,128)(2,1)S(1)}, bf16[64,512]{1,0:T(8,128)(2,1)S(1)}, u32[]{:S(2)}, u32[]{:S(2)}) collective-permute-start(bf16[64,512]{1,0:T(8,128)(2,1)S(1)} %get-tuple-element.97), channel_id=1, source_target_pairs={{0,24},{8,0},{16,8},{24,16},{1,25},{9,1},{17,9},{25,17},{2,26},{10... | collective-permute-start | bytes 196616 | tf_op jit(solution)/shard_map/ppermute | solution.py:753
  174.9 5.6 %collective-permute-start.14 = (bf16[64,512]{1,0:T(8,128)(2,1)S(1)}, bf16[64,512]{1,0:T(8,128)(2,1)S(1)}, u32[]{:S(2)}, u32[]{:S(2)}) collective-permute-start(bf16[64,512]{1,0:T(8,128)(2,1)S(1)} %get-tuple-element.98), channel_id=1, source_target_pairs={{0,16},{8,24},{16,0},{24,8},{1,17},{9,25},{17,1},{25,9},{2,18},{10... | collective-permute-start | bytes 196616 | tf_op jit(solution)/shard_map/ppermute | solution.py:753
  174.9 6.3 %collective-permute-start.15 = (bf16[64,512]{1,0:T(8,128)(2,1)S(1)}, bf16[64,512]{1,0:T(8,128)(2,1)S(1)}, u32[]{:S(2)}, u32[]{:S(2)}) collective-permute-start(bf16[64,512]{1,0:T(8,128)(2,1)S(1)} %get-tuple-element.99), channel_id=1, source_target_pairs={{0,8},{8,16},{16,24},{24,0},{1,9},{9,17},{17,25},{25,1},{2,10},{10... | collective-permute-start | bytes 196616 | tf_op jit(solution)/shard_map/ppermute | solution.py:753
  181.2 10.2 %collective-permute-start.18 = (bf16[4,64,512]{2,1,0:T(8,128)(2,1)S(1)}, bf16[4,64,512]{2,1,0:T(8,128)(2,1)S(1)}, u32[]{:S(2)}, u32[]{:S(2)}) collective-permute-start(bf16[4,64,512]{2,1,0:T(8,128)(2,1)S(1)} %pad_maximum_fusion.1.a0), channel_id=1, source_target_pairs={{0,6},{2,4},{4,2},{6,0},{1,7},{3,5},{5,3},{7,1},{8,14},{10,12},{12... | collective-permute-start | bytes 786440 | tf_op jit(solution)/shard_map/ppermute | solution.py:747
  182.8 11.4 %collective-permute-start.17 = (bf16[4,64,512]{2,1,0:T(8,128)(2,1)S(1)}, bf16[4,64,512]{2,1,0:T(8,128)(2,1)}, u32[]{:S(2)}, u32[]{:S(2)}) collective-permute-start(bf16[4,64,512]{2,1,0:T(8,128)(2,1)S(1)} %pad_maximum_fusion.1.a0), channel_id=1, source_target_pairs={{0,4},{4,0},{1,5},{5,1},{2,6},{6,2},{3,7},{7,3},{8,12},{12,8},{9,1... | collective-permute-start | bytes 786440 | tf_op jit(solution)/shard_map/ppermute | solution.py:746
  183.9 10.4 %collective-permute-start.16 = (bf16[4,64,512]{2,1,0:T(8,128)(2,1)S(1)}, bf16[4,64,512]{2,1,0:T(8,128)(2,1)}, u32[]{:S(2)}, u32[]{:S(2)}) collective-permute-start(bf16[4,64,512]{2,1,0:T(8,128)(2,1)S(1)} %pad_maximum_fusion.1.a0), channel_id=1, source_target_pairs={{0,2},{2,0},{1,3},{3,1},{4,6},{6,4},{5,7},{7,5},{8,10},{10,8},{9,1... | collective-permute-start | bytes 786440 | tf_op jit(solution)/shard_map/ppermute | solution.py:745
  220.2 4.4 %collective-permute-start.48 = (bf16[4,256,1024]{2,1,0:T(8,128)(2,1)}, bf16[4,256,1024]{2,1,0:T(8,128)(2,1)S(1)}, u32[]{:S(2)}, u32[]{:S(2)}) collective-permute-start(bf16[4,256,1024]{2,1,0:T(8,128)(2,1)} %get-tuple-element.154), channel_id=1, source_target_pairs={{0,1},{1,0},{2,3},{3,2},{4,5},{5,4},{6,7},{7,6},{8,9},{9,8},{10,11... | collective-permute-start | bytes 6291464 | tf_op jit(solution)/shard_map/ppermute | solution.py:763
  231.1 186.9 %reduce-scatter.3.cloned.1.call-start = ((), (), s32[]{:S(2)}) async-start(), calls=%async_computation.5 | async-start | bytes 2162688 | tf_op jit(solution)/shard_map/reduce_scatter | solution.py:863
  231.4 9.4 %collective-permute-start.26 = (bf16[128,1024]{1,0:T(8,128)(2,1)}, bf16[128,1024]{1,0:T(8,128)(2,1)S(1)}, u32[]{:S(2)}, u32[]{:S(2)}) collective-permute-start(bf16[128,1024]{1,0:T(8,128)(2,1)} %get-tuple-element.114), channel_id=1, source_target_pairs={{0,2},{2,0},{1,3},{3,1},{4,6},{6,4},{5,7},{7,5},{8,10},{10,8},{9,1... | collective-permute-start | bytes 786440 | tf_op jit(solution)/shard_map/ppermute | solution.py:745
  232.3 8.9 %collective-permute-start.27 = (bf16[128,1024]{1,0:T(8,128)(2,1)S(1)}, bf16[128,1024]{1,0:T(8,128)(2,1)S(1)}, u32[]{:S(2)}, u32[]{:S(2)}) collective-permute-start(bf16[128,1024]{1,0:T(8,128)(2,1)S(1)} %copy-done.82), channel_id=1, source_target_pairs={{0,4},{4,0},{1,5},{5,1},{2,6},{6,2},{3,7},{7,3},{8,12},{12,8},{9,1... | collective-permute-start | bytes 786440 | tf_op jit(solution)/shard_map/ppermute | solution.py:746
  233.3 12.6 %collective-permute-start.28 = (bf16[128,1024]{1,0:T(8,128)(2,1)S(1)}, bf16[128,1024]{1,0:T(8,128)(2,1)S(1)}, u32[]{:S(2)}, u32[]{:S(2)}) collective-permute-start(bf16[128,1024]{1,0:T(8,128)(2,1)S(1)} %copy-done.81), channel_id=1, source_target_pairs={{0,6},{2,4},{4,2},{6,0},{1,7},{3,5},{5,3},{7,1},{8,14},{10,12},{12... | collective-permute-start | bytes 786440 | tf_op jit(solution)/shard_map/ppermute | solution.py:747
  255.0 4.8 %collective-permute-start.29 = (bf16[4,64,128]{2,1,0:T(8,128)(2,1)S(1)}, bf16[4,64,128]{2,1,0:T(8,128)(2,1)S(1)}, u32[]{:S(2)}, u32[]{:S(2)}) collective-permute-start(bf16[4,64,128]{2,1,0:T(8,128)(2,1)S(1)} %copy-done.65), channel_id=1, source_target_pairs={{0,2},{2,0},{1,3},{3,1},{4,6},{6,4},{5,7},{7,5},{8,10},{10,8},{9,1... | collective-permute-start | bytes 196616 | tf_op jit(solution)/shard_map/ppermute | solution.py:745
  256.3 4.7 %collective-permute-start.30 = (bf16[4,64,128]{2,1,0:T(8,128)(2,1)S(1)}, bf16[4,64,128]{2,1,0:T(8,128)(2,1)S(1)}, u32[]{:S(2)}, u32[]{:S(2)}) collective-permute-start(bf16[4,64,128]{2,1,0:T(8,128)(2,1)S(1)} %copy-done.63), channel_id=1, source_target_pairs={{0,4},{4,0},{1,5},{5,1},{2,6},{6,2},{3,7},{7,3},{8,12},{12,8},{9,1... | collective-permute-start | bytes 196616 | tf_op jit(solution)/shard_map/ppermute | solution.py:746
  257.1 5.2 %collective-permute-start.31 = (bf16[4,64,128]{2,1,0:T(8,128)(2,1)S(1)}, bf16[4,64,128]{2,1,0:T(8,128)(2,1)S(1)}, u32[]{:S(2)}, u32[]{:S(2)}) collective-permute-start(bf16[4,64,128]{2,1,0:T(8,128)(2,1)S(1)} %copy-done.61), channel_id=1, source_target_pairs={{0,6},{2,4},{4,2},{6,0},{1,7},{3,5},{5,3},{7,1},{8,14},{10,12},{12... | collective-permute-start | bytes 196616 | tf_op jit(solution)/shard_map/ppermute | solution.py:747
  262.3 8.4 %collective-permute-start.32 = (bf16[4,64,128]{2,1,0:T(8,128)(2,1)S(1)}, bf16[4,64,128]{2,1,0:T(8,128)(2,1)S(1)}, u32[]{:S(2)}, u32[]{:S(2)}) collective-permute-start(bf16[4,64,128]{2,1,0:T(8,128)(2,1)S(1)} %get-tuple-element.125), channel_id=1, source_target_pairs={{0,8},{8,16},{16,24},{24,0},{1,9},{9,17},{17,25},{25,1},{2,10},{10... | collective-permute-start | bytes 196616 | tf_op jit(solution)/shard_map/ppermute | solution.py:753
  262.7 11.1 %collective-permute-start.33 = (bf16[4,64,128]{2,1,0:T(8,128)(2,1)S(1)}, bf16[4,64,128]{2,1,0:T(8,128)(2,1)S(1)}, u32[]{:S(2)}, u32[]{:S(2)}) collective-permute-start(bf16[4,64,128]{2,1,0:T(8,128)(2,1)S(1)} %get-tuple-element.126), channel_id=1, source_target_pairs={{0,16},{8,24},{16,0},{24,8},{1,17},{9,25},{17,1},{25,9},{2,18},{10... | collective-permute-start | bytes 196616 | tf_op jit(solution)/shard_map/ppermute | solution.py:753
  264.6 9.3 %collective-permute-start.34 = (bf16[4,64,128]{2,1,0:T(8,128)(2,1)S(1)}, bf16[4,64,128]{2,1,0:T(8,128)(2,1)S(1)}, u32[]{:S(2)}, u32[]{:S(2)}) collective-permute-start(bf16[4,64,128]{2,1,0:T(8,128)(2,1)S(1)} %get-tuple-element.127), channel_id=1, source_target_pairs={{0,24},{8,0},{16,8},{24,16},{1,25},{9,1},{17,9},{25,17},{2,26},{10... | collective-permute-start | bytes 196616 | tf_op jit(solution)/shard_map/ppermute | solution.py:753
  291.1 8.9 %collective-permute-start.35 = (bf16[192,512]{1,0:T(8,128)(2,1)S(1)}, bf16[192,512]{1,0:T(8,128)(2,1)S(1)}, u32[]{:S(2)}, u32[]{:S(2)}) collective-permute-start(bf16[192,512]{1,0:T(8,128)(2,1)S(1)} %get-tuple-element.130), channel_id=1, source_target_pairs={{0,2},{2,0},{1,3},{3,1},{4,6},{6,4},{5,7},{7,5},{8,10},{10,8},{9,1... | collective-permute-start | bytes 589832 | tf_op jit(solution)/shard_map/ppermute | solution.py:745
  292.8 7.4 %collective-permute-start.36 = (bf16[192,512]{1,0:T(8,128)(2,1)S(1)}, bf16[192,512]{1,0:T(8,128)(2,1)S(1)}, u32[]{:S(2)}, u32[]{:S(2)}) collective-permute-start(bf16[192,512]{1,0:T(8,128)(2,1)S(1)} %get-tuple-element.131), channel_id=1, source_target_pairs={{0,4},{4,0},{1,5},{5,1},{2,6},{6,2},{3,7},{7,3},{8,12},{12,8},{9,1... | collective-permute-start | bytes 589832 | tf_op jit(solution)/shard_map/ppermute | solution.py:746
  294.2 9.6 %collective-permute-start.37 = (bf16[192,512]{1,0:T(8,128)(2,1)S(1)}, bf16[192,512]{1,0:T(8,128)(2,1)S(1)}, u32[]{:S(2)}, u32[]{:S(2)}) collective-permute-start(bf16[192,512]{1,0:T(8,128)(2,1)S(1)} %get-tuple-element.132), channel_id=1, source_target_pairs={{0,6},{2,4},{4,2},{6,0},{1,7},{3,5},{5,3},{7,1},{8,14},{10,12},{12... | collective-permute-start | bytes 589832 | tf_op jit(solution)/shard_map/ppermute | solution.py:747
  311.2 4.3 collective-permute-start.41
  311.9 17.1 %collective-permute-start.23 = (bf16[128,1024]{1,0:T(8,128)(2,1)}, bf16[128,1024]{1,0:T(8,128)(2,1)}, u32[]{:S(2)}, u32[]{:S(2)}) collective-permute-start(bf16[128,1024]{1,0:T(8,128)(2,1)} %get-tuple-element.110), channel_id=1, source_target_pairs={{0,2},{2,0},{1,3},{3,1},{4,6},{6,4},{5,7},{7,5},{8,10},{10,8},{9,1... | collective-permute-start | bytes 786440 | tf_op jit(solution)/shard_map/ppermute | solution.py:745
  313.3 18.4 %collective-permute-start.24 = (bf16[128,1024]{1,0:T(8,128)(2,1)}, bf16[128,1024]{1,0:T(8,128)(2,1)}, u32[]{:S(2)}, u32[]{:S(2)}) collective-permute-start(bf16[128,1024]{1,0:T(8,128)(2,1)} %get-tuple-element.111), channel_id=1, source_target_pairs={{0,4},{4,0},{1,5},{5,1},{2,6},{6,2},{3,7},{7,3},{8,12},{12,8},{9,1... | collective-permute-start | bytes 786440 | tf_op jit(solution)/shard_map/ppermute | solution.py:746
  313.9 19.2 %collective-permute-start.25 = (bf16[128,1024]{1,0:T(8,128)(2,1)}, bf16[128,1024]{1,0:T(8,128)(2,1)}, u32[]{:S(2)}, u32[]{:S(2)}) collective-permute-start(bf16[128,1024]{1,0:T(8,128)(2,1)} %get-tuple-element.112), channel_id=1, source_target_pairs={{0,6},{2,4},{4,2},{6,0},{1,7},{3,5},{5,3},{7,1},{8,14},{10,12},{12... | collective-permute-start | bytes 786440 | tf_op jit(solution)/shard_map/ppermute | solution.py:747
  317.8 17.6 %collective-permute-start.42 = (bf16[4,32,768]{2,1,0:T(8,128)(2,1)}, bf16[4,32,768]{2,1,0:T(8,128)(2,1)S(1)}, u32[]{:S(2)}, u32[]{:S(2)}) collective-permute-start(bf16[4,32,768]{2,1,0:T(8,128)(2,1)} %get-tuple-element.144), channel_id=1, source_target_pairs={{0,2},{2,0},{1,3},{3,1},{4,6},{6,4},{5,7},{7,5},{8,10},{10,8},{9,1... | collective-permute-start | bytes 589832 | tf_op jit(solution)/shard_map/ppermute | solution.py:745
  319.9 35.6 %collective-permute-start.38 = (bf16[128,1024]{1,0:T(8,128)(2,1)}, bf16[128,1024]{1,0:T(8,128)(2,1)S(1)}, u32[]{:S(2)}, u32[]{:S(2)}) collective-permute-start(bf16[128,1024]{1,0:T(8,128)(2,1)} %copy-done.57), channel_id=1, source_target_pairs={{0,8},{8,16},{16,24},{24,0},{1,9},{9,17},{17,25},{25,1},{2,10},{10... | collective-permute-start | bytes 786440 | tf_op jit(solution)/shard_map/ppermute | solution.py:753
  325.2 15.1 %all-to-all-start.1 = ((f32[32,8,128]{2,1,0:T(8,128)}), f32[32,8,128]{2,1,0:T(8,128)}, u32[]{:S(2)}, u32[]{:S(2)}) async-start(f32[32,8,128]{2,1,0:T(8,128)} %bitcast.46), calls=%async_computation.1 | async-start | bytes 262144 | tf_op jit(solution)/shard_map/all_to_all | solution.py:896
  329.1 27.6 %collective-permute-start.39 = (bf16[128,1024]{1,0:T(8,128)(2,1)}, bf16[128,1024]{1,0:T(8,128)(2,1)S(1)}, u32[]{:S(2)}, u32[]{:S(2)}) collective-permute-start(bf16[128,1024]{1,0:T(8,128)(2,1)} %get-tuple-element.137), channel_id=1, source_target_pairs={{0,16},{8,24},{16,0},{24,8},{1,17},{9,25},{17,1},{25,9},{2,18},{10... | collective-permute-start | bytes 786440 | tf_op jit(solution)/shard_map/ppermute | solution.py:753
  331.7 26.1 %collective-permute-start.40 = (bf16[128,1024]{1,0:T(8,128)(2,1)}, bf16[128,1024]{1,0:T(8,128)(2,1)S(1)}, u32[]{:S(2)}, u32[]{:S(2)}) collective-permute-start(bf16[128,1024]{1,0:T(8,128)(2,1)} %copy-done.56), channel_id=1, source_target_pairs={{0,24},{8,0},{16,8},{24,16},{1,25},{9,1},{17,9},{25,17},{2,26},{10... | collective-permute-start | bytes 786440 | tf_op jit(solution)/shard_map/ppermute | solution.py:753
  333.2 12.2 %collective-permute-start.43 = (bf16[4,32,768]{2,1,0:T(8,128)(2,1)}, bf16[4,32,768]{2,1,0:T(8,128)(2,1)S(1)}, u32[]{:S(2)}, u32[]{:S(2)}) collective-permute-start(bf16[4,32,768]{2,1,0:T(8,128)(2,1)} %copy-done.59), channel_id=1, source_target_pairs={{0,4},{4,0},{1,5},{5,1},{2,6},{6,2},{3,7},{7,3},{8,12},{12,8},{9,1... | collective-permute-start | bytes 589832 | tf_op jit(solution)/shard_map/ppermute | solution.py:746
  335.5 9.9 %collective-permute-start.44 = (bf16[4,32,768]{2,1,0:T(8,128)(2,1)}, bf16[4,32,768]{2,1,0:T(8,128)(2,1)}, u32[]{:S(2)}, u32[]{:S(2)}) collective-permute-start(bf16[4,32,768]{2,1,0:T(8,128)(2,1)} %copy-done.58), channel_id=1, source_target_pairs={{0,6},{2,4},{4,2},{6,0},{1,7},{3,5},{5,3},{7,1},{8,14},{10,12},{12... | collective-permute-start | bytes 589832 | tf_op jit(solution)/shard_map/ppermute | solution.py:747
  346.5 11.7 %collective-permute-start.45 = (bf16[32,768]{1,0:T(8,128)(2,1)S(1)}, bf16[32,768]{1,0:T(8,128)(2,1)S(1)}, u32[]{:S(2)}, u32[]{:S(2)}) collective-permute-start(bf16[32,768]{1,0:T(8,128)(2,1)S(1)} %get-tuple-element.148), channel_id=1, source_target_pairs={{0,8},{8,16},{16,24},{24,0},{1,9},{9,17},{17,25},{25,1},{2,10},{10... | collective-permute-start | bytes 147464 | tf_op jit(solution)/shard_map/ppermute | solution.py:753
  350.2 13.2 %collective-permute-start.46 = (bf16[32,768]{1,0:T(8,128)(2,1)S(1)}, bf16[32,768]{1,0:T(8,128)(2,1)S(1)}, u32[]{:S(2)}, u32[]{:S(2)}) collective-permute-start(bf16[32,768]{1,0:T(8,128)(2,1)S(1)} %get-tuple-element.149), channel_id=1, source_target_pairs={{0,16},{8,24},{16,0},{24,8},{1,17},{9,25},{17,1},{25,9},{2,18},{10... | collective-permute-start | bytes 147464 | tf_op jit(solution)/shard_map/ppermute | solution.py:753
  355.5 7.9 %collective-permute-start.47 = (bf16[32,768]{1,0:T(8,128)(2,1)S(1)}, bf16[32,768]{1,0:T(8,128)(2,1)S(1)}, u32[]{:S(2)}, u32[]{:S(2)}) collective-permute-start(bf16[32,768]{1,0:T(8,128)(2,1)S(1)} %get-tuple-element.150), channel_id=1, source_target_pairs={{0,24},{8,0},{16,8},{24,16},{1,25},{9,1},{17,9},{25,17},{2,26},{10... | collective-permute-start | bytes 147464 | tf_op jit(solution)/shard_map/ppermute | solution.py:753
  356.7 62.9 %collective-permute-start.49 = (bf16[32,1024]{1,0:T(8,128)(2,1)S(1)}, bf16[32,1024]{1,0:T(8,128)(2,1)S(1)}, u32[]{:S(2)}, u32[]{:S(2)}) collective-permute-start(bf16[32,1024]{1,0:T(8,128)(2,1)S(1)} %get-tuple-element.156), channel_id=1, source_target_pairs={{0,2},{2,0},{1,3},{3,1},{4,6},{6,4},{5,7},{7,5},{8,10},{10,8},{9,1... | collective-permute-start | bytes 196616 | tf_op jit(solution)/shard_map/ppermute | solution.py:745
  357.8 61.7 %collective-permute-start.50 = (bf16[32,1024]{1,0:T(8,128)(2,1)S(1)}, bf16[32,1024]{1,0:T(8,128)(2,1)S(1)}, u32[]{:S(2)}, u32[]{:S(2)}) collective-permute-start(bf16[32,1024]{1,0:T(8,128)(2,1)S(1)} %get-tuple-element.157), channel_id=1, source_target_pairs={{0,4},{4,0},{1,5},{5,1},{2,6},{6,2},{3,7},{7,3},{8,12},{12,8},{9,1... | collective-permute-start | bytes 196616 | tf_op jit(solution)/shard_map/ppermute | solution.py:746
  358.2 61.4 %collective-permute-start.51 = (bf16[32,1024]{1,0:T(8,128)(2,1)S(1)}, bf16[32,1024]{1,0:T(8,128)(2,1)S(1)}, u32[]{:S(2)}, u32[]{:S(2)}) collective-permute-start(bf16[32,1024]{1,0:T(8,128)(2,1)S(1)} %get-tuple-element.158), channel_id=1, source_target_pairs={{0,6},{2,4},{4,2},{6,0},{1,7},{3,5},{5,3},{7,1},{8,14},{10,12},{12... | collective-permute-start | bytes 196616 | tf_op jit(solution)/shard_map/ppermute | solution.py:747
  (77 other events, 1980.3 us)
Sparse Core Ops, SparseCore 0:
  45.1 46.2 all-gather.5
  94.2 65.2 all-gather.3
  231.3 46.7 reduce-scatter.4
  280.2 137.7 reduce-scatter.2

commit v2 on v0

--- a/solution.py
+++ b/solution.py
@@ -1,9 +1,15 @@
+import functools
 import math
 
 import jax
 import jax.numpy as jnp
 from jax import lax
+from jax.experimental import pallas as pl
+from jax.experimental.pallas import tpu as pltpu
+from jax.sharding import Mesh
 from jax.sharding import PartitionSpec as P
+
+bf16, f32 = jnp.bfloat16, jnp.float32
 
 HEADS = 16
 
@@ -302,47 +308,714 @@
     return (layer_out, d_embedded[None]) + tuple(shards)
 
 
+DEPTH = 4
+PLANE = 4
+BIG = 1e30
+HBM = pltpu.MemorySpace.HBM
+VMEM = pltpu.MemorySpace.VMEM
+SMEM = pltpu.MemorySpace.SMEM
+LEADS = 16
+ROW_G1, ROW_B1, ROW_QB, ROW_VB, ROW_OB, ROW_G2, ROW_B2, ROW_DB = range(16, 24)
+VEC_ROWS = 24
+
+
+def mul(left, right, over_left, over_right):
+    return lax.dot_general(
+        left, right, (((over_left,), (over_right,)), ((), ())), preferred_element_type=jnp.float32
+    )
+
+
+class Mover:
+    def __init__(self, sems):
+        self.sems, self.used, self.open = sems, 0, []
+
+    def start(self, source, target):
+        copy = pltpu.make_async_copy(source, target, self.sems.at[self.used])
+        self.used += 1
+        copy.start()
+        self.open.append(copy)
+        return copy
+
+    def wait(self, copies=None):
+        for copy in list(self.open if copies is None else copies):
+            copy.wait()
+            self.open = [other for other in self.open if other is not copy]
+
+
+class Far:
+    def __init__(self, value):
+        self.value = value
+
+
+class Raw(Far):
+    pass
+
+
+class Given:
+    def __init__(self, ref, held, mover):
+        self.ref, self.mover, self.copy = held, mover, mover.start(ref, held)
+        self.shape, self.dtype = ref.shape, ref.dtype
+
+    def ready(self):
+        if self.copy is not None:
+            self.mover.wait([self.copy])
+            self.copy = None
+        return self.ref
+
+    def __getitem__(self, at):
+        return self.ready()[at]
+
+
+def run(order, kernel, outs, ins, scratch=(), after=()):
+    after = list(after) + order
+    kinds = [type(a) if isinstance(a, Far) else None for a in ins]
+    ins = [a.value if kind else a for a, kind in zip(ins, kinds)]
+    staged = [pltpu.VMEM(a.shape, a.dtype) for a, kind in zip(ins, kinds) if kind is Far]
+    outs = [o if len(o) == 3 else o + ("",) for o in outs]
+    staged += [pltpu.VMEM(o[0], o[1]) for o in outs if o[2] == "far"]
+    n_in, n_after, n_out, n_staged = len(ins), len(after), len(outs), len(staged)
+    name = getattr(kernel, "func", kernel).__name__
+    micros, room = COSTS[name]
+    cost = pl.CostEstimate(flops=micros * 1_100_000_000, bytes_accessed=micros * 3_600_000, transcendentals=0)
+
+    def body(*refs):
+        mover = Mover(refs[-1])
+        held = list(refs[len(refs) - 1 - n_staged : -1])
+        given = [
+            Given(ref, held.pop(0), mover) if kind is Far else ref for ref, kind in zip(refs[:n_in], kinds)
+        ]
+        refs = refs[n_in + n_after : len(refs) - 1 - n_staged]
+        made = [held.pop(0) if o[2] == "far" else ref for ref, o in zip(refs, outs)]
+        kernel(mover, *given, *made, *refs[n_out + 1 :])
+        for ref, written, o in zip(refs, made, outs):
+            if o[2] == "far":
+                mover.start(written, ref)
+        for operand in given:
+            if isinstance(operand, Given):
+                operand.ready()
+        refs[n_out][...] = jnp.zeros_like(refs[n_out])
+        mover.wait()
+
+    spaces = [pl.ANY if kind else SMEM if a.ndim == 1 else VMEM for a, kind in zip(ins, kinds)]
+    results = pl.pallas_call(
+        body,
+        name=name,
+        out_shape=[HBM(o[0], o[1]) if o[2] else jax.ShapeDtypeStruct(o[0], o[1]) for o in outs]
+        + [jax.ShapeDtypeStruct((8, 128), f32)],
+        in_specs=[pl.BlockSpec(memory_space=space) for space in spaces + [pl.ANY] * n_after],
+        out_specs=[pl.BlockSpec(memory_space=pl.ANY if o[2] else VMEM) for o in outs] + [pl.BlockSpec(memory_space=VMEM)],
+        scratch_shapes=[pltpu.VMEM(s, d) for s, d in scratch] + staged + [pltpu.SemaphoreType.DMA((64,))],
+        compiler_params=pltpu.CompilerParams(vmem_limit_bytes=room << 20),
+        cost_estimate=cost,
+    )(*[pltpu.with_memory_space_constraint(a, HBM) if kind else a for a, kind in zip(ins, kinds)], *after)
+    order[:] = results[n_out:]
+    return results[:n_out]
+
+
+def row_stats(values):
+    mean = jnp.mean(values, -1, keepdims=True)
+    centred = values - mean
+    inv = lax.rsqrt(jnp.mean(centred * centred, -1, keepdims=True) + epsilon)
+    return centred * inv, inv
+
+
+def norm_back(d_normal, normal, inv):
+    first = jnp.mean(d_normal, -1, keepdims=True)
+    second = jnp.mean(d_normal * normal, -1, keepdims=True)
+    return inv * (d_normal - first - normal * second)
+
+
+def lead_hot(lead, seg_row):
+    seg = seg_row[...]
+    found = jnp.zeros_like(seg)
+    for slot in range(lead.shape[0]):
+        found = jnp.where(seg == slot, lead[slot], found)
+    slots = lax.broadcasted_iota(jnp.int32, (LEADS, seg.shape[1]), 0)
+    return jnp.where(slots == found, 1.0, 0.0).astype(bf16)
+
+
+def vec_row(vec, row):
+    return vec[row : row + 1, :].astype(f32)
+
+
+def q_prep_kernel(mover, pos, qkv, o0, o1, o2, o3):
+    z = pos[0]
+    width = o0.shape[1] // 3
+    d = qkv.shape[1] // 3
+    for u, out in enumerate((o0, o1, o2, o3)):
+        for part in range(3):
+            start = pl.multiple_of(part * d + (z ^ u) * width, width)
+            mover.start(qkv.at[:, pl.ds(start, width)], out.at[:, part * width : (part + 1) * width])
+
+
+def q_stack_kernel(mover, pos, b0, b1, b2, b3, out):
+    for u, block in enumerate((b0, b1, b2, b3)):
+        mover.start(block, out.at[pos[0] ^ u])
+
+
+def up_prep_kernel(mover, up, out):
+    fr = up.shape[1] // (DEPTH * PLANE * 2)
+    for k in range(PLANE):
+        for c in range(2):
+            for zz in range(DEPTH):
+                src = ((zz * PLANE + k) * 2 + c) * fr
+                dst = (c * DEPTH + zz) * fr
+                out[k, :, dst : dst + fr] = up[:, src : src + fr]
+
+
+def shard_kernel(mover, ups, down, out_rows, out):
+    out[0:PLANE] = ups[...]
+    out[PLANE : 2 * PLANE] = down[...].reshape(PLANE, -1, down.shape[1])
+    out[2 * PLANE] = out_rows[...]
+
+
+def qkv_kernel(mover, pos, lead, seg_row, vec, t0, t1, t2, t3, *refs):
+    z, yx, c = pos[0], pos[1], pos[2]
+    qa, qc, (n1, w_out, o0, o1, o2, o3, w, proj) = refs[:4], refs[4:8], refs[8:]
+    rows, d = t0.shape
+    pending = [mover.start(qa[k], w.at[:, yx ^ k, c]) for k in range(PLANE)]
+    pending += [mover.start(qc[k], w.at[:, yx ^ k, 1 - c]) for k in range(PLANE)]
+    shift = mul(lead_hot(lead, seg_row), vec[0:LEADS, :], 0, 0)
+    gain, bias = vec_row(vec, ROW_G1), vec_row(vec, ROW_B1)
+    for s, t in enumerate((t0, t1, t2, t3)):
+        normal, _ = row_stats(t[...].astype(f32) + shift)
+        n1[s * rows : (s + 1) * rows, :] = (normal * gain + bias).astype(bf16)
+    width = d // DEPTH
+    head = width // PLANE
+    at = pl.ds(pl.multiple_of(z * width, width), width)
+    held = vec
+    biases = jnp.concatenate(
+        [held[ROW_QB : ROW_QB + 1, at].astype(f32), jnp.zeros((1, width), f32), held[ROW_VB : ROW_VB + 1, at].astype(f32)],
+        1,
+    )
+    first = lax.broadcasted_iota(jnp.int32, (8, 3 * width), 0) == 0
+    biases = jnp.where(first, biases, 0.0).astype(bf16)
+    ones = jnp.ones((8, DEPTH * rows), bf16)
+    mover.wait(pending)
+    mover.start(w, w_out)
+    found = mul(w[...].reshape(d, 3 * width), n1[...], 0, 1) + mul(biases, ones, 0, 0)
+    proj[...] = found.astype(bf16).reshape(proj.shape)
+    for k, out in enumerate((o0, o1, o2, o3)):
+        for part in range(3):
+            mover.start(proj.at[part * PLANE + (yx ^ k)], out.at[part * head : (part + 1) * head])
+
+
+def fill_heads(seg_row, count, blocks, qa, ka, vt):
+    head = blocks[0].shape[0] // 3
+    span = blocks[0].shape[1]
+    seg = jnp.concatenate([seg_row[...]] * (span // seg_row.shape[1]), 1)
+    slots = lax.broadcasted_iota(jnp.int32, (16, span), 0)
+    hot, real = jnp.where(slots == seg, 1.0, 0.0), slots < count
+    q_mark = jnp.where(real, (hot - 1.0) * BIG, 0.0).astype(bf16)
+    k_mark = jnp.where(real, hot, 0.0).astype(bf16)
+    rest = qa.shape[0] - head - 16
+    for k, block in enumerate(blocks):
+        cols = slice(k * span, (k + 1) * span)
+        qa[0:head, cols] = block[0:head, :] * jnp.asarray(score_scale, bf16)
+        qa[head : head + 16, cols] = q_mark
+        qa[head + 16 :, cols] = jnp.zeros((rest, span), bf16)
+        keys = jnp.concatenate([block[head : 2 * head, :], k_mark, jnp.zeros((rest, span), bf16)], 0)
+        ka[cols, :] = keys.T
+        vt[:, cols] = block[2 * head :, :]
+
+
+def attend_kernel(count, mover, seg_row, b0, b1, b2, b3, o0, o1, o2, o3, lse, qa, ka, vt):
+    fill_heads(seg_row, count, (b0, b1, b2, b3), qa, ka, vt)
+    span = b0.shape[1]
+    rows = seg_row.shape[1]
+    outs = (o0, o1, o2, o3)
+
+    def step(k, carry):
+        for half in range(DEPTH // 2):
+            at = pl.ds(pl.multiple_of(k * span + half * 2 * rows, 2 * rows), 2 * rows)
+            scores = mul(ka[...], qa[:, at], 1, 0)
+            top = jnp.max(scores, 0, keepdims=True)
+            soft = jnp.exp(scores - top)
+            total = jnp.sum(soft, 0, keepdims=True)
+            found = mul(vt[...], soft.astype(bf16), 1, 0) / total
+            lse[:, at] = jnp.broadcast_to(top + jnp.log(total), (8, 2 * rows))
+            for i in range(2):
+                outs[half * 2 + i][:, pl.ds(pl.multiple_of(k * rows, rows), rows)] = found[
+                    :, i * rows : (i + 1) * rows
+                ].astype(bf16)
+        return carry
+
+    lax.fori_loop(0, PLANE, step, 0)
+
+
+def out_kernel(mover, pos, a0, a1, a2, a3, ff, p0, p1, p2, p3, att, w_out):
+    z = pos[0]
+    head = a0.shape[0]
+    rows, d = p0.shape
+    pending = [mover.start(ff.at[:, :, 2 * PLANE], w_out)]
+    for u, block in enumerate((a0, a1, a2, a3)):
+        att[pl.ds(pl.multiple_of((z ^ u) * head, head), head), :] = block[...]
+    mover.wait(pending)
+    found = mul(att[...], w_out[...].reshape(-1, d), 0, 0)
+    for j, out in enumerate((p0, p1, p2, p3)):
+        out[...] = found[j * rows : (j + 1) * rows, :].astype(out.dtype)
+
+
+def norm_kernel(mover, lead, seg_row, vec, tok, p0, p1, p2, p3, middle, n2):
+    shift = mul(lead_hot(lead, seg_row), vec[0:LEADS, :], 0, 0) + vec_row(vec, ROW_OB)
+    total = p0[...].astype(f32) + p1[...].astype(f32) + p2[...].astype(f32) + p3[...].astype(f32)
+    total = tok[...].astype(f32) + shift + total
+    middle[...] = total
+    normal, _ = row_stats(total)
+    n2[...] = (normal * vec_row(vec, ROW_G2) + vec_row(vec, ROW_B2)).astype(bf16)
+
+
+def ffn_kernel(mover, pos, up_b, n0, n1, n2, n3, d_outs, ff, act, d_hid, p0, p1, p2, p3, d_up_b, w_up, w_down, hid):
+    yx = pos[1]
+    rows, d = n0.shape
+    for_up = [mover.start(ff.at[:, c, 0:PLANE], w_up.at[:, :, c]) for c in range(2)]
+    for_down = [mover.start(ff.at[:, c, PLANE : 2 * PLANE], w_down.at[c]) for c in range(2)]
+    mover.wait(for_up)
+    normed = jnp.concatenate([n0[...], n1[...], n2[...], n3[...]], 0)
+    up = w_up[...].reshape(d, -1)
+    hid[...] = mul(normed, up, 1, 0) + up_b[...].astype(f32)
+    mover.wait(for_down)
+    down = w_down[...].reshape(-1, d)
+    sums = jnp.zeros(d_up_b.shape, f32)
+    for j in range(PLANE):
+        here = slice(j * rows, (j + 1) * rows)
+        hidden = hid[here, :]
+        phi = 0.5 * (1.0 + lax.erf(hidden * 0.7071067811865476))
+        act[here, :] = (hidden * phi).astype(bf16)
+        slope = phi + hidden * (jnp.exp(-0.5 * hidden * hidden) * 0.3989422804014327)
+        d_act = mul(d_outs[yx ^ j], down, 1, 1)
+        low = (d_act * slope).astype(bf16)
+        d_hid[here, :] = low
+        sums = sums + jnp.sum(low.astype(f32), 0, keepdims=True)
+    d_up_b[...] = sums
+    back = mul(d_hid[...], up, 1, 1)
+    for j, out in enumerate((p0, p1, p2, p3)):
+        out[...] = back[j * rows : (j + 1) * rows, :].astype(out.dtype)
+
+
+def ffn_grad_kernel(mover, pos, act, d_hid, n0, n1, n2, n3, ff, d_outs, grads, outs, up_grad, down_grad, w_down):
+    yx = pos[1]
+    rows, d = outs.shape[1:]
+    pending = [mover.start(ff.at[:, c, PLANE : 2 * PLANE], w_down.at[c]) for c in range(2)]
+    normed = jnp.concatenate([n0[...], n1[...], n2[...], n3[...]], 0)
+    up_grad[...] = mul(normed, d_hid[...], 0, 0).astype(bf16).reshape(up_grad.shape)
+    for c in range(2):
+        mover.start(up_grad.at[:, :, c], grads.at[:, c, 0:PLANE])
+    d_down = jnp.zeros((act.shape[1], d), f32)
+    for j in range(PLANE):
+        d_down = d_down + mul(act[j * rows : (j + 1) * rows, :], d_outs[yx ^ j], 0, 0)
+    down_grad[...] = d_down.astype(bf16).reshape(down_grad.shape)
+    for c in range(2):
+        mover.start(down_grad.at[c], grads.at[:, c, PLANE:])
+    mover.wait(pending)
+    found = mul(act[...], w_down[...].reshape(-1, d), 1, 0)
+    for j in range(PLANE):
+        outs[yx ^ j] = found[j * rows : (j + 1) * rows, :].astype(bf16)
+
+
+def ffn_last_kernel(mover, shard, ups, down):
+    ups[...] = shard[0:PLANE]
+    down[...] = shard[PLANE:].astype(f32).reshape(down.shape)
+
+
+def branch_kernel(mover, vec, middle, d_out, p0, p1, p2, p3, d_mid, d_branch, d_vec):
+    dy = p0[...].astype(f32) + p1[...].astype(f32) + p2[...].astype(f32) + p3[...].astype(f32)
+    normal, inv = row_stats(middle[...])
+    d_rows = d_out[...].astype(f32)
+    total = d_rows + norm_back(dy * vec_row(vec, ROW_G2), normal, inv)
+    d_mid[...] = total
+    low = total.astype(bf16)
+    d_branch[...] = low
+    sums = [jnp.sum(v, 0, keepdims=True) for v in (dy * normal, dy, d_rows, low.astype(f32))]
+    d_vec[...] = jnp.concatenate(sums + [jnp.zeros((4, dy.shape[1]), f32)], 0)
+
+
+def out_back_kernel(mover, pos, att, w_out, b0, b1, b2, b3, o0, o1, o2, o3, grad, d_att):
+    z = pos[0]
+    head = o0.shape[0]
+    branch = jnp.concatenate([b0[...], b1[...], b2[...], b3[...]], 0)
+    d = branch.shape[1]
+    d_att[...] = mul(w_out[...].reshape(-1, d), branch, 1, 1).astype(bf16).reshape(d_att.shape)
+    for u, out in enumerate((o0, o1, o2, o3)):
+        out[...] = d_att[z ^ u]
+    grad[...] = mul(att[...], branch, 1, 0).astype(bf16).reshape(grad.shape)
+
+
+def attend_back_kernel(count, mover, seg_row, b0, b1, b2, b3, c0, c1, c2, c3, lse,
+                       o0, o1, o2, o3, qa, ka, vt, vn, dot, dq, dk, dv):
+    fill_heads(seg_row, count, (b0, b1, b2, b3), qa, ka, vt)
+    span = b0.shape[1]
+    rows = seg_row.shape[1]
+    head, total = vt.shape
+    for k in range(PLANE):
+        cols = slice(k * span, (k + 1) * span)
+        vn[cols, :] = vt[:, cols].T
+        for s, block in enumerate((c0, c1, c2, c3)):
+            dot[:, k * span + s * rows : k * span + (s + 1) * rows] = block[:, k * rows : (k + 1) * rows]
+    dk[...] = jnp.zeros_like(dk)
+    dv[...] = jnp.zeros_like(dv)
+    logs = lse
+
+    def step(i, carry):
+        at = pl.ds(pl.multiple_of(i * 2 * rows, 2 * rows), 2 * rows)
+        scores = mul(ka[...], qa[:, at], 1, 0)
+        soft = jnp.exp(scores - logs[0:1, at])
+        d_out = dot[:, at]
+        d_soft = mul(vn[...], d_out, 1, 0)
+        delta = jnp.sum(soft * d_soft, 0, keepdims=True)
+        d_scores = (soft * (d_soft - delta)).astype(bf16)
+        dv[...] += mul(d_out, soft.astype(bf16), 1, 1)
+        dk[...] += mul(qa[0:head, at], d_scores, 1, 1)
+        dq[:, at] = (mul(ka[:, 0:head], d_scores, 0, 0) * score_scale).astype(bf16)
+        return carry
+
+    lax.fori_loop(0, total // (2 * rows), step, 0)
+    for k, out in enumerate((o0, o1, o2, o3)):
+        cols = slice(k * span, (k + 1) * span)
+        out[0:head, :] = dq[:, cols]
+        out[head : 2 * head, :] = dk[:, cols].astype(bf16)
+        out[2 * head :, :] = dv[:, cols].astype(bf16)
+
+
+def join_heads(yx, blocks, joined):
+    head = blocks[0].shape[0] // 3
+    for k, block in enumerate(blocks):
+        for part in range(3):
+            joined[part * PLANE + (yx ^ k)] = block[part * head : (part + 1) * head, :]
+    return joined[...].reshape(3 * PLANE * head, -1)
+
+
+def qkv_back_kernel(mover, pos, w, g0, g1, g2, g3, r0, r1, r2, r3, back, joined):
+    grads = join_heads(pos[1], (g0, g1, g2, g3), joined)
+    rows, d = r0.shape
+    found = mul(grads, w[...].reshape(d, -1), 0, 1)
+    back[...] = found
+    for s, out in enumerate((r0, r1, r2, r3)):
+        out[...] = found[s * rows : (s + 1) * rows, :].astype(out.dtype)
+
+
+def qkv_grad_kernel(mover, pos, lead, seg_row, vec, t0, t1, t2, t3, n1, g0, g1, g2, g3, back, d_mid, d_mid_vec, d_up_b,
+                    out, joined, d_vec):
+    z, yx = pos[0], pos[1]
+    rows, d = t0.shape
+    width = d // DEPTH
+    grads = join_heads(yx, (g0, g1, g2, g3), joined)
+    rw = out.shape[3]
+    cols = 3 * width
+    grad = mul(n1[...], grads, 0, 1).astype(bf16)
+    hot = lead_hot(lead, seg_row)
+    shift = mul(hot, vec[0:LEADS, :], 0, 0)
+    gain = vec_row(vec, ROW_G1)
+    d_gain = jnp.zeros((1, d), f32)
+    d_bias = jnp.zeros((1, d), f32)
+    d_emb = d_mid[...]
+    for s, t in enumerate((t0, t1, t2, t3)):
+        piece = back[s * rows : (s + 1) * rows, :]
+        normal, inv = row_stats(t[...].astype(f32) + shift)
+        d_gain = d_gain + jnp.sum(piece * normal, 0, keepdims=True)
+        d_bias = d_bias + jnp.sum(piece, 0, keepdims=True)
+        d_emb = d_emb + norm_back(piece * gain, normal, inv)
+    high = d_emb.astype(bf16)
+    low = (d_emb - high.astype(f32)).astype(bf16)
+    d_vec[...] = jnp.zeros_like(d_vec)
+    d_vec[0:LEADS, :] = mul(hot, high, 1, 0) + mul(hot, low, 1, 0)
+    sums = mul(jnp.ones((8, DEPTH * rows), bf16), grads, 1, 1)
+    d_vec[ROW_G1 : ROW_G1 + 1, :] = d_gain
+    d_vec[ROW_B1 : ROW_B1 + 1, :] = d_bias
+    at = pl.ds(pl.multiple_of(z * width, width), width)
+    d_vec[ROW_QB : ROW_QB + 1, at] = sums[0:1, 0:width]
+    d_vec[ROW_VB : ROW_VB + 1, at] = sums[0:1, 2 * width :]
+    for i, row in enumerate((ROW_G2, ROW_B2, ROW_DB, ROW_OB)):
+        d_vec[row : row + 1, :] = d_mid_vec[i : i + 1, :]
+    small = d_vec[...].astype(bf16)
+    fr = out.shape[4] - cols
+    for zz in range(DEPTH):
+        for k in range(PLANE):
+            for c in range(2):
+                i = (zz * PLANE + k) * 2 + c
+                out[k, c, zz, :, 0:cols] = grad[i * rw : (i + 1) * rw, :]
+                side = jnp.concatenate([small[:, i * rw : (i + 1) * rw], jnp.zeros((rw, fr - rw), bf16)], 1)
+                start = (c * DEPTH + zz) * fr
+                last = jnp.where(yx == k, d_up_b[:, start : start + fr], 0.0).astype(bf16)
+                mark = lax.broadcasted_iota(jnp.int32, (rw, fr), 0) == VEC_ROWS
+                out[k, c, zz, :, cols:] = jnp.where(mark, last.astype(f32), side.astype(f32)).astype(bf16)
+
+
+def first_back_kernel(mover, lead, seg_row, vec, tok, d_mid, r0, r1, r2, r3, out):
+    shift = mul(lead_hot(lead, seg_row), vec[0:LEADS, :], 0, 0)
+    normal, inv = row_stats(tok[...].astype(f32) + shift)
+    dy = r0[...].astype(f32) + r1[...].astype(f32) + r2[...].astype(f32) + r3[...].astype(f32)
+    out[...] = d_mid[...] + norm_back(dy * vec_row(vec, ROW_G1), normal, inv)
+
+
+def layer_out_kernel(mover, vec, middle, blocks, out):
+    total = middle[...] + vec_row(vec, ROW_DB)
+    for k in range(PLANE):
+        total = total + blocks[k].astype(f32)
+    out[...] = total.astype(bf16)
+
+
+def octet_kernel(mover, pos, blocks, o0, o1, o2, o3, total):
+    found = jnp.zeros(total.shape, f32)
+    for k in range(PLANE):
+        for c in range(2):
+            found = found + blocks[k, c].astype(f32)
+    total[...] = found.astype(bf16)
+    for u, out in enumerate((o0, o1, o2, o3)):
+        out[...] = total[pos[0] ^ u]
+
+
+def qkv_join_kernel(mover, pos, b0, b1, b2, b3, out, table, *rest):
+    z = pos[0]
+    rw = out.shape[0]
+    width = out.shape[1] // (3 * DEPTH)
+    side = jnp.zeros((rw, b0.shape[1] - 3 * width), f32)
+    for s, block in enumerate((b0, b1, b2, b3)):
+        for part in range(3):
+            start = pl.multiple_of((part * DEPTH + (z ^ s)) * width, width)
+            out[:, pl.ds(start, width)] = block[:, part * width : (part + 1) * width].astype(f32)
+        side = side + block[:, 3 * width :].astype(f32)
+    table[...] = side[0:LEADS, 0:rw]
+    for i, row in enumerate(rest[:-1]):
+        row[...] = side[LEADS + i : LEADS + i + 1, 0:rw]
+    rest[-1][...] = side[VEC_ROWS : VEC_ROWS + 1, :]
+
+
+def up_join_kernel(mover, blocks, out):
+    fr = blocks.shape[2] // (2 * DEPTH)
+    for k in range(PLANE):
+        for c in range(2):
+            for zz in range(DEPTH):
+                src = (c * DEPTH + zz) * fr
+                dst = ((zz * PLANE + k) * 2 + c) * fr
+                out[:, dst : dst + fr] = blocks[k, :, src : src + fr].astype(f32)
+
+
+COSTS = {
+    "q_prep_kernel": (1, 4), "q_stack_kernel": (1, 4), "up_prep_kernel": (1, 4), "shard_kernel": (1, 4), "qkv_kernel": (5, 20),
+    "attend_kernel": (11, 16), "out_kernel": (2, 12), "norm_kernel": (2, 8), "ffn_kernel": (8, 32), "ffn_grad_kernel": (8, 32),
+    "branch_kernel": (2, 12), "out_back_kernel": (3, 12), "attend_back_kernel": (19, 24),
+    "qkv_back_kernel": (3, 16), "qkv_grad_kernel": (6, 24), "first_back_kernel": (2, 8), "layer_out_kernel": (1, 8),
+    "octet_kernel": (2, 8), "qkv_join_kernel": (1, 4), "up_join_kernel": (2, 8), "ffn_last_kernel": (1, 8),
+}
+PLANE_AXES = ("y", "x")
+
+
+def trade(blocks, axes):
+    return lax.all_to_all(blocks, axes, split_axis=0, concat_axis=0, tiled=True)
+
+
+ALL = ("z", "y", "x", "g")
+
+
+def across(blocks):
+    swap = [(0, 1), (1, 0)]
+    return (
+        blocks[0],
+        lax.ppermute(blocks[1], "x", swap),
+        lax.ppermute(blocks[2], "y", swap),
+        lax.ppermute(blocks[3], ("y", "x"), [(i, i ^ 3) for i in range(PLANE)]),
+    )
+
+
+def to_depth(block, step):
+    return lax.ppermute(block, "z", [(i, i ^ step) for i in range(DEPTH)])
+
+
+def along(blocks):
+    return (blocks[0],) + tuple(to_depth(blocks[u], u) for u in range(1, DEPTH))
+
+
+def spread(block):
+    far = to_depth(block, 2)
+    return block, to_depth(block, 1), far, to_depth(far, 1)
+
+
+def core_swap(block):
+    return lax.ppermute(block, "g", [(0, 1), (1, 0)])
+
+
+def far(blocks):
+    return [Far(block) for block in blocks]
+
+
+def raw(blocks):
+    return [Raw(block) for block in blocks]
+
+
+def fast_local(
+    tokens, segment_ids, lead_index, lead_table, ln1_gain, ln1_bias, qkv_weight, q_bias, v_bias,
+    out_weight, out_bias, ln2_gain, ln2_bias, up_weight, up_bias, down_weight, down_bias, d_out,
+):
+    z = lax.axis_index("z")
+    yx = lax.axis_index("y") * 2 + lax.axis_index("x")
+    c = lax.axis_index("g")
+    pos = jnp.stack([z, yx, c]).astype(jnp.int32)
+    tok, d_rows = tokens[0], d_out[0]
+    rows, d = tok.shape
+    head = d // HEADS
+    span = DEPTH * rows
+    group = PLANE * span
+    rw = qkv_weight.shape[0]
+    fr = down_weight.shape[0]
+    ff = 2 * DEPTH * fr
+    devices = DEPTH * PLANE * 2
+    lead = lead_index[0]
+    count = lead.shape[0]
+    width = 3 * d // DEPTH
+    seg_row = segment_ids
+    up_shape, down_shape = (DEPTH, PLANE, 2, rw, ff), (2, DEPTH, PLANE, rw, d)
+
+    order = []
+    call = functools.partial(run, order)
+    flat = jnp.concatenate(
+        [lead_table.reshape(-1), ln1_gain, ln1_bias, q_bias, v_bias, out_bias, ln2_gain, ln2_bias, down_bias, up_bias]
+    )
+    padded = -(-flat.shape[0] // 1024) * 1024
+    flat = jnp.pad(flat, (0, padded - flat.shape[0])).reshape(8, padded // 8)
+    smalls = lax.all_to_all(
+        jnp.broadcast_to(flat[None], (devices,) + flat.shape), ALL, split_axis=0, concat_axis=0, tiled=True
+    ).reshape(devices, padded)
+    vec = smalls[:, : VEC_ROWS * rw].reshape(devices, VEC_ROWS, rw).transpose(1, 0, 2).reshape(VEC_ROWS, d)
+    up_b = smalls[:, VEC_ROWS * rw : VEC_ROWS * rw + fr].reshape(DEPTH, PLANE, 2, fr)
+    up_b = lax.dynamic_index_in_dim(up_b, yx, 1, keepdims=False).transpose(1, 0, 2).reshape(1, ff)
+
+    q_rows = along(call(q_prep_kernel, [((rw, width), bf16)] * 4, [pos, qkv_weight]))
+    toks = spread(tok)
+    (up_cols,) = call(up_prep_kernel, [((PLANE, rw, ff), bf16)], [up_weight])
+    up_cols = trade(up_cols, PLANE_AXES)
+    d_outs = lax.all_gather(d_rows, PLANE_AXES, axis=0)
+    (q_stack,) = call(
+        q_stack_kernel, [((DEPTH, rw, width), bf16)], [pos, *q_rows], after=[flat, toks[2]]
+    )
+    q_plane = across((q_stack,) * PLANE)
+    q_other = [core_swap(block) for block in q_plane]
+    (ff_shard,) = call(
+        shard_kernel, [((2 * PLANE + 1, rw, d), bf16, "far")], [up_cols, down_weight, out_weight], after=[smalls]
+    )
+    ff_all = lax.all_gather(ff_shard, ("z", "g"), axis=0).reshape(DEPTH, 2, 2 * PLANE + 1, rw, d)
+    n1, w_qkv, *blocks = call(
+        qkv_kernel,
+        [((span, d), bf16, "far"), ((DEPTH, PLANE, 2, rw, width), bf16, "raw")] + [((3 * head, span), bf16)] * 4,
+        [pos, lead, seg_row, vec, *toks, *q_plane, *q_other],
+        [((DEPTH, PLANE, 2, rw, width), bf16), ((3 * PLANE, head, span), bf16)],
+    )
+    blocks = across(blocks)
+
+    *att_parts, lse = call(
+        functools.partial(attend_kernel, count),
+        [((head, PLANE * rows), bf16)] * 4 + [((8, group), f32)],
+        [seg_row, *blocks],
+        [((128, group), bf16), ((group, 128), bf16), ((head, group), bf16)],
+    )
+    att_parts = along(att_parts)
+    *parts, att, w_out = call(
+        out_kernel,
+        [((rows, d), f32)] + [((rows, d), bf16)] * 3 + [((DEPTH * head, span), bf16), ((DEPTH, 2, rw, d), bf16)],
+        [pos, *att_parts, Raw(ff_all)],
+    )
+    parts = across(parts)
+    middle, n2 = call(norm_kernel, [((rows, d), f32, "far"), ((rows, d), bf16)], [lead, seg_row, vec, Far(tok), *parts])
+    n2_plane = across((n2,) * PLANE)
+
+    act, d_hid, p0, p1, p2, p3, d_up_b = call(
+        ffn_kernel,
+        [((span, ff), bf16), ((span, ff), bf16), ((rows, d), f32)] + [((rows, d), bf16)] * 3 + [((1, ff), f32)],
+        [pos, up_b, *n2_plane, Far(d_outs), Raw(ff_all)],
+        [(up_shape, bf16), (down_shape, bf16), ((span, ff), f32)],
+    )
+    parts = across((p0, p1, p2, p3))
+    ff_grad, outs = call(
+        ffn_grad_kernel,
+        [((DEPTH, 2, 2 * PLANE, rw, d), bf16, "raw"), ((PLANE, rows, d), bf16, "far")],
+        [pos, act, d_hid, *n2_plane, Raw(ff_all), Far(d_outs)],
+        [(up_shape, bf16), (down_shape, bf16), (down_shape, bf16)],
+        after=[parts[1]],
+    )
+    ff_grad = lax.psum_scatter(
+        ff_grad.reshape(2 * DEPTH, 2 * PLANE, rw, d), ("z", "g"), scatter_dimension=0, tiled=True
+    )[0]
+    d_mid, d_branch, d_mid_vec = call(
+        branch_kernel,
+        [((rows, d), f32, "far"), ((rows, d), bf16), ((8, d), f32)],
+        [vec, Far(middle), Far(d_rows), *parts],
+    )
+    branch_plane = across((d_branch,) * PLANE)
+    *d_att, out_grad = call(
+        out_back_kernel,
+        [((head, span), bf16)] * 4 + [((DEPTH, 2, rw, d), bf16, "far")],
+        [pos, att, w_out, *branch_plane],
+        [((DEPTH, head, span), bf16)],
+    )
+    d_att = along(d_att)
+    outs = trade(outs, PLANE_AXES)
+    d_out_weight = lax.psum_scatter(
+        out_grad.reshape(2 * DEPTH, rw, d), ("z", "g"), scatter_dimension=0, tiled=True
+    )[0].astype(f32)
+
+    d_blocks = call(
+        functools.partial(attend_back_kernel, count),
+        [((3 * head, span), bf16)] * 4,
+        [seg_row, *blocks, *d_att, lse],
+        [((128, group), bf16), ((group, 128), bf16), ((head, group), bf16), ((group, head), bf16),
+         ((head, group), bf16), ((head, group), bf16), ((head, group), f32), ((head, group), f32)],
+    )
+    d_blocks = across(d_blocks)
+    (layer_out,) = call(layer_out_kernel, [((rows, d), bf16)], [vec, Far(middle), outs])
+    ups, d_down = call(ffn_last_kernel, [((PLANE, rw, ff), bf16), ((fr, d), f32)], [ff_grad])
+    ups = trade(ups, PLANE_AXES)
+    *returned, back = call(
+        qkv_back_kernel,
+        [((rows, d), f32)] + [((rows, d), bf16)] * 3 + [((span, d), f32)],
+        [pos, Far(w_qkv), *d_blocks],
+        [((3 * PLANE, head, span), bf16)],
+        after=[ups],
+    )
+    returned = along(returned)
+    side = width + -(-max(rw, fr) // 128) * 128
+    (octets,) = call(
+        qkv_grad_kernel,
+        [((PLANE, 2, DEPTH, rw, side), bf16)],
+        [pos, lead, seg_row, vec, *far(toks), Far(n1), *d_blocks, back, Far(d_mid), d_mid_vec, d_up_b],
+        [((3 * PLANE, head, span), bf16), ((rw, d), f32)],
+    )
+    octets = trade(octets.reshape(2 * PLANE, DEPTH, rw, side), ("y", "x", "g")).reshape(octets.shape)
+    (d_up,) = call(up_join_kernel, [((rw, PLANE * ff), f32)], [ups])
+    (d_tokens,) = call(
+        first_back_kernel, [((rows, d), f32)], [lead, seg_row, vec, Far(tok), Far(d_mid), *returned]
+    )
+    cols = along(call(octet_kernel, [((rw, side), bf16)] * 4, [pos, octets], [((DEPTH, rw, side), bf16)]))
+    d_qkv, table, *smalls, d_ub = call(
+        qkv_join_kernel,
+        [((rw, 3 * d), f32), ((LEADS, rw), f32)] + [((1, rw), f32)] * 8 + [((1, fr), f32)],
+        [pos, *cols],
+    )
+    d_g1, d_b1, d_qb, d_vb, d_ob, d_g2, d_b2, d_db, d_ub = (small[0] for small in (*smalls, d_ub))
+    return (
+        layer_out[None], d_tokens[None], table, d_g1, d_b1, d_qkv, d_qb, d_vb, d_out_weight, d_ob,
+        d_g2, d_b2, d_up, d_ub, d_down, d_db,
+    )
+
+
+def specs(band, grp):
+    every = band + grp
+    rows = P(grp, band, None)
+    in_specs = (
+        rows, P(grp, band), P(grp, None), P(None, every), P(every), P(every), P(every, None), P(every), P(every),
+        P(every, None), P(every), P(every), P(every), P(every, None), P(every), P(every, None), P(every), rows,
+    )
+    out_specs = (
+        rows, rows, P(None, every), P(every), P(every), P(every, None), P(every), P(every), P(every, None), P(every),
+        P(every), P(every), P(every, None), P(every), P(every, None), P(every),
+    )
+    return in_specs, out_specs
+
+
 def solution(mesh):
-    return jax.shard_map(
-        local,
-        mesh=mesh,
-        in_specs=(
-            P("grp", "band", None),
-            P("grp", "band"),
-            P("grp", None),
-            P(None, ("band", "grp")),
-            P(("band", "grp")),
-            P(("band", "grp")),
-            P(("band", "grp"), None),
-            P(("band", "grp")),
-            P(("band", "grp")),
-            P(("band", "grp"), None),
-            P(("band", "grp")),
-            P(("band", "grp")),
-            P(("band", "grp")),
-            P(("band", "grp"), None),
-            P(("band", "grp")),
-            P(("band", "grp"), None),
-            P(("band", "grp")),
-            P("grp", "band", None),
-        ),
-        out_specs=(
-            P("grp", "band", None),
-            P("grp", "band", None),
-            P(None, ("band", "grp")),
-            P(("band", "grp")),
-            P(("band", "grp")),
-            P(("band", "grp"), None),
-            P(("band", "grp")),
-            P(("band", "grp")),
-            P(("band", "grp"), None),
-            P(("band", "grp")),
-            P(("band", "grp")),
-            P(("band", "grp")),
-            P(("band", "grp"), None),
-            P(("band", "grp")),
-            P(("band", "grp"), None),
-            P(("band", "grp")),
-        ),
-        check_vma=False,
-    )
+    band, grp = mesh.shape["band"], mesh.shape["grp"]
+    if band == HEADS and grp == 2:
+        mesh = Mesh(mesh.devices.reshape(DEPTH, 2, 2, grp), ("z", "y", "x", "g"))
+        in_specs, out_specs = specs(("z", "y", "x"), ("g",))
+        return jax.shard_map(fast_local, mesh=mesh, in_specs=in_specs, out_specs=out_specs, check_vma=False)
+    in_specs, out_specs = specs(("band",), ("grp",))
+    return jax.shard_map(local, mesh=mesh, in_specs=in_specs, out_specs=out_specs, check_vma=False)

time: 1570 us -> 311 us (0.20)
  waiting for transfers between devices: 1130 us -> 110 us
  blocking collectives: 160 us -> 0 us
  matrix products: 129 us -> 0 us
  local copies, waits for them, and re-layouts: 117 us -> 12.4 us
  Pallas kernels: 0 us -> 91.9 us
  starting transfers between devices: 0.78 us -> 79.7 us
    reduce_scatter x4 -> x2, waiting for transfers between devices: 669 us -> 0.02 us  [the longest x1 0.02 us: fast_local(): lax.psum_scatter(ff_grad.reshape(2 * DEPTH, 2 * PLANE, rw, d), ('z', 'g')...]
    all_gather x6 -> x2, waiting for transfers between devices: 244 us -> 4.47 us  [the longest x1 4.47 us: fast_local(): d_outs = lax.all_gather(d_rows, PLANE_AXES, axis=0)]
    unnamed x16 -> x4, waiting for transfers between devices: 212 us -> 0.57 us
    dot_general x32 -> x0, matrix products: 127 us -> none  [the longest x6 19.3 us: block_scores(): jnp.einsum('qhd,khd->hqk', query_heads, key_heads, preferred_element_type...]
    ppermute x0 -> x43, waiting for transfers between devices: none -> 98.7 us  [the longest x18 54.5 us: to_depth(): return lax.ppermute(block, 'z', [(i, i ^ step) for i in range(DEPTH)])]
    pallas_call x0 -> x21, Pallas kernels: none -> 91.9 us  [run(): pl.pallas_call(body, name=name, out_shape=[HBM(o[0], o[1]) if o[2] else j...]
    unnamed x2 -> x0, blocking collectives: 82.1 us -> none
    unnamed x107 -> x37, local copies, waits for them, and re-layouts: 84.8 us -> 4.43 us
  transfers between devices with their start and end apart: 13 -> 52, of which waited for: 12 -> 30; matrix products, arithmetic and copies ran while one was open for 11% -> 1% of each run, Pallas kernels for 0% -> 20%
where the time goes in v2:
time: 311 us; the launch traced here: 310 us
  waiting for transfers between devices  110 us (35%)
  Pallas kernels  91.9 us (30%)
  starting transfers between devices  79.7 us (26%)
  between operations  14.3 us (5%)
  local copies, waits for them, and re-layouts  12.4 us (4%)
    pallas_call x21, Pallas kernels, run(): pl.pallas_call(body, name=name, out_shape=[HBM(o[0], o[1]) if o[2] else j...  91.9 us
    ppermute x18, waiting for transfers between devices, to_depth(): return lax.ppermute(block, 'z', [(i, i ^ step) for i in range(DEPTH)])  54.5 us
    ppermute x18, starting transfers between devices, to_depth(): return lax.ppermute(block, 'z', [(i, i ^ step) for i in range(DEPTH)])  32.8 us
    ppermute x7, waiting for transfers between devices, across(): lax.ppermute(blocks[2], 'y', swap)  22 us
    all_to_all x4, starting transfers between devices, trade(): return lax.all_to_all(blocks, axes, split_axis=0, concat_axis=0, tiled=True)  13.9 us
    ppermute x7, waiting for transfers between devices, across(): lax.ppermute(blocks[3], ('y', 'x'), [(i, i ^ 3) for i in range(PLANE)])  11.3 us
    ppermute x7, starting transfers between devices, across(): lax.ppermute(blocks[3], ('y', 'x'), [(i, i ^ 3) for i in range(PLANE)])  11.3 us
    ppermute x7, waiting for transfers between devices, across(): lax.ppermute(blocks[1], 'x', swap)  10.8 us
  transfers between devices with their start and end apart: 52, of which 30 were waited for; matrix products, arithmetic and copies ran while one was open for 1% of the time, Pallas kernels for 20%

profile of v2, /device:TPU:0, one launch (start us, length us, event | category | flops | bytes accessed | tf_op | source)
XLA Modules:
  0.0 310.3 jit_solution(13810417106157862153)
XLA Ops:
  8.0 6.1 %concatenate.3 = bf16[896]{0:T(1024)(128)(2,1)S(1)} concatenate(bf16[512]{0:T(512)(128)(2,1)S(1)} %reshape.69, bf16[32]{0:T(256)(128)(2,1)} %param.22, bf16[32]{0:T(256)(128)(2,1)} %param.23, bf16[32]{0:T(256)(128)(2,1)} %param.25, bf16[32]{0:T(256)(128)(2,1)} %param.26, bf16[32]{0:T(256)(128)(2,1)} %param.28, bf16[32]{0:T(256)(128)(2,1)} %param.29, bf16[32]{0:T(256)(128)(2,1)} %param.30, ...), dimensions={0} | concatenate | bytes 3584 | tf_op jit(solution)/shard_map/concatenate | solution.py:871
  14.7 7.3 %all-to-all-start = ((bf16[32,8,128]{2,1,0:T(8,128)(2,1)}), bf16[32,8,128]{2,1,0:T(8,128)(2,1)S(1)}, u32[]{:S(2)}, u32[]{:S(2)}) async-start(bf16[32,8,128]{2,1,0:T(8,128)(2,1)} %broadcast_in_dim.14), calls=%async_computation | async-start | bytes 131072 | tf_op jit(solution)/shard_map/all_to_all | solution.py:876
  22.0 2.7 collective-permute-start.1
  29.6 3.4 %all-to-all-start.1 = ((bf16[4,32,1024]{2,1,0:T(8,128)(2,1)}), bf16[4,32,1024]{2,1,0:T(8,128)(2,1)S(1)}, u32[]{:S(2)}, u32[]{:S(2)}) async-start(bf16[4,32,1024]{2,1,0:T(8,128)(2,1)} %get-tuple-element.116), calls=%async_computation.1 | async-start | bytes 524288 | tf_op jit(solution)/shard_map/all_to_all | solution.py:805
  34.4 3.2 %collective-permute-start.5 = (bf16[32,768]{1,0:T(8,128)(2,1)S(1)}, bf16[32,768]{1,0:T(8,128)(2,1)S(1)}, u32[]{:S(2)}, u32[]{:S(2)}) collective-permute-start(bf16[32,768]{1,0:T(8,128)(2,1)S(1)} %get-tuple-element.112), channel_id=1, source_target_pairs={{0,24},{8,16},{16,8},{24,0},{1,25},{9,17},{17,9},{25,1},{2,26},{10... | collective-permute-start | bytes 147464 | tf_op jit(solution)/shard_map/ppermute | solution.py:822
  37.6 2.1 collective-permute-done.3.refs_2_
  39.7 2.4 collective-permute-done.4.refs_3_
  42.1 1.4 q_stack_kernel.1
  43.6 1.5 shard_kernel.1
  46.3 2.5 collective-permute-start.8
  50.7 3.4 %collective-permute-done.refs_5_ = bf16[128,1024]{1,0:T(8,128)(2,1)S(1)} collective-permute-done((bf16[128,1024]{1,0:T(8,128)(2,1)S(1)}, bf16[128,1024]{1,0:T(8,128)(2,1)S(1)}, u32[]{:S(2)}, u32[]{:S(2)}) %collective-permute-start) | collective-permute-done | bytes 262176 | tf_op jit(solution)/shard_map/ppermute | solution.py:822
  55.1 2.5 collective-permute-done.7.refs_10_
  58.6 12.7 %collective-permute-done.2.refs_7_ = bf16[128,1024]{1,0:T(8,128)(2,1)S(1)} collective-permute-done((bf16[128,1024]{1,0:T(8,128)(2,1)S(1)}, bf16[128,1024]{1,0:T(8,128)(2,1)S(1)}, u32[]{:S(2)}, u32[]{:S(2)}) %collective-permute-start.2) | collective-permute-done | bytes 262176 | tf_op jit(solution)/shard_map/ppermute | solution.py:822
  71.3 6.4 %qkv_kernel.1 = (bf16[512,1024]{1,0:T(8,128)(2,1)}, bf16[4,4,2,32,768]{4,3,2,1,0:T(8,128)(2,1)}, bf16[192,512]{1,0:T(8,128)(2,1)S(1)}, bf16[192,512]{1,0:T(8,128...) custom-call(s32[3]{0:T(128)S(1)} %pad_add_fusion.refs_0_, ...), custom_call_target="tpu_custom_call" | custom-call | flops 5500000256 | bytes 18000000 | tf_op jit(solution)/shard_map/qkv_kernel/pallas_call | solution.py:400
  78.4 1.7 collective-permute-start.13
  80.1 1.4 collective-permute-start.14
  82.0 2.3 collective-permute-done.13.refs_2_
  84.3 2.6 collective-permute-done.14.refs_3_
  89.1 11.2 %attend_kernel.1 = (bf16[64,512]{1,0:T(8,128)(2,1)S(1)}, bf16[64,512]{1,0:T(8,128)(2,1)S(1)}, bf16[64,512]{1,0:T(8,128)(2,1)S(1)}, bf16[64,512]{1,0:T(8,128)(2,1...) custom-call(s32[1,128]{1,0:T(1,128)S(1)} %copy-done.10, bf16[192,512]{1,0:T(8,128)(2,1)S(1)} %copy-done.16, ...), custom_call_target="tpu_custom_call" | custom-call | flops 12099999744 | bytes 39600000 | tf_op jit(solution)/shard_map/attend_kernel/pallas_call | solution.py:400
  100.3 4.2 %collective-permute-start.17 = (bf16[64,512]{1,0:T(8,128)(2,1)S(1)}, bf16[64,512]{1,0:T(8,128)(2,1)S(1)}, u32[]{:S(2)}, u32[]{:S(2)}) collective-permute-start(bf16[64,512]{1,0:T(8,128)(2,1)S(1)} %get-tuple-element.126), channel_id=1, source_target_pairs={{0,16},{8,24},{16,0},{24,8},{1,17},{9,25},{17,1},{25,9},{2,18},{10... | collective-permute-start | bytes 196616 | tf_op jit(solution)/shard_map/ppermute | solution.py:822
  104.7 2.8 collective-permute-done.17.refs_3_
  107.5 3.1 %collective-permute-done.18.refs_4_ = bf16[64,512]{1,0:T(8,128)(2,1)S(1)} collective-permute-done((bf16[64,512]{1,0:T(8,128)(2,1)S(1)}, bf16[64,512]{1,0:T(8,128)(2,1)S(1)}, u32[]{:S(2)}, u32[]{:S(2)}) %collective-permute-start.18) | collective-permute-done | bytes 65568 | tf_op jit(solution)/shard_map/ppermute | solution.py:822
  110.6 2.6 out_kernel.1
  115.1 1.7 collective-permute-start.21
  116.8 2.9 collective-permute-done.19.refs_5_
  119.7 4.6 %collective-permute-done.20.refs_6_ = bf16[128,1024]{1,0:T(8,128)(2,1)S(1)} collective-permute-done((bf16[128,1024]{1,0:T(8,128)(2,1)S(1)}, bf16[128,1024]{1,0:T(8,128)(2,1)S(1)}, u32[]{:S(2)}, u32[]{:S(2)}) %collective-permute-start.20) | collective-permute-done | bytes 262176 | tf_op jit(solution)/shard_map/ppermute | solution.py:816
  124.2 2.5 collective-permute-done.21.refs_7_
  126.7 2.9 norm_kernel.1
  129.7 2.4 collective-permute-start.24
  133.3 4.5 %all-gather.4.cloned.1.call-done.refs_6_.refs_8_ = bf16[4,128,1024]{2,1,0:T(8,128)(2,1)} async-done(((bf16[1,128,1024]{2,1,0:T(8,128)(2,1)}), bf16[4,128,1024]{2,1,0:T(8,128)(2,1)}) %all-gather.4.cloned.1.call-update) | async-done | bytes 1048592 | tf_op jit(solution)/shard_map/all_gather | solution.py:887
  137.7 2.4 collective-permute-done.23.refs_4_.refs_5_
  140.2 8.5 %ffn_kernel.1 = (bf16[512,1024]{1,0:T(8,128)(2,1)S(1)}, bf16[512,1024]{1,0:T(8,128)(2,1)S(1)}, f32[128,1024]{1,0:T(8,128)S(1)}, bf16[128,1024]{1,0:T(8,128)(2,1)...) custom-call(s32[3]{0:T(128)S(1)} %pad_add_fusion.refs_0_, ...), custom_call_target="tpu_custom_call" | custom-call | flops 8800000000 | bytes 28800000 | tf_op jit(solution)/shard_map/ffn_kernel/pallas_call | solution.py:400
  150.0 5.2 %collective-permute-done.25.refs_9_.refs_4_ = bf16[128,1024]{1,0:T(8,128)(2,1)S(1)} collective-permute-done((bf16[128,1024]{1,0:T(8,128)(2,1)S(1)}, bf16[128,1024]{1,0:T(8,128)(2,1)S(1)}, u32[]{:S(2)}, u32[]{:S(2)}) %collective-permute-start.25) | collective-permute-done | bytes 262176 | tf_op jit(solution)/shard_map/ppermute | solution.py:815
  155.2 7.8 %ffn_grad_kernel.1 = (bf16[4,2,8,32,1024]{4,3,2,1,0:T(8,128)(2,1)}, bf16[4,128,1024]{2,1,0:T(8,128)(2,1)}, f32[8,128]{1,0:T(8,128)S(1)}) custom-call(s32[3]{0:T(128)S(1)} %pad_add_fusion.refs_0_, bf16[512,1024]{1,0:T(8,128)(2,1)S(1)} %get-tuple-element.138.refs_1_, bf16[512,1024]{1,0:T(8,128)(2,1)S(1)} %get-tuple-element.139.refs_2_, ...), custom_call_target="tpu_custom_call" | custom-call | flops 8800000000 | bytes 28800000 | tf_op jit(solution)/shard_map/ffn_grad_kernel/pallas_call | solution.py:400
  164.0 1.7 collective-permute-start.27
  165.7 7.7 %collective-permute-done.26.refs_5_ = bf16[128,1024]{1,0:T(8,128)(2,1)S(1)} collective-permute-done((bf16[128,1024]{1,0:T(8,128)(2,1)S(1)}, bf16[128,1024]{1,0:T(8,128)(2,1)S(1)}, u32[]{:S(2)}, u32[]{:S(2)}) %collective-permute-start.26) | collective-permute-done | bytes 262176 | tf_op jit(solution)/shard_map/ppermute | solution.py:816
  173.4 3.0 branch_kernel.1
  178.2 1.7 collective-permute-start.28
  179.9 6.7 %collective-permute-done.30.refs_6_ = bf16[128,1024]{1,0:T(8,128)(2,1)S(1)} collective-permute-done((bf16[128,1024]{1,0:T(8,128)(2,1)S(1)}, bf16[128,1024]{1,0:T(8,128)(2,1)S(1)}, u32[]{:S(2)}, u32[]{:S(2)}) %collective-permute-start.30) | collective-permute-done | bytes 262176 | tf_op jit(solution)/shard_map/ppermute | solution.py:817
  186.6 2.1 collective-permute-done.29.refs_5_
  189.0 2.7 out_back_kernel.1
  192.0 3.2 %collective-permute-start.32 = (bf16[64,512]{1,0:T(8,128)(2,1)S(1)}, bf16[64,512]{1,0:T(8,128)(2,1)S(1)}, u32[]{:S(2)}, u32[]{:S(2)}) collective-permute-start(bf16[64,512]{1,0:T(8,128)(2,1)S(1)} %get-tuple-element.153), channel_id=1, source_target_pairs={{0,16},{8,24},{16,0},{24,8},{1,17},{9,25},{17,1},{25,9},{2,18},{10... | collective-permute-start | bytes 196616 | tf_op jit(solution)/shard_map/ppermute | solution.py:822
  196.3 3.5 %all-to-all-start.2 = ((bf16[4,128,1024]{2,1,0:T(8,128)(2,1)}), bf16[4,128,1024]{2,1,0:T(8,128)(2,1)S(1)}, u32[]{:S(2)}, u32[]{:S(2)}) async-start(bf16[4,128,1024]{2,1,0:T(8,128)(2,1)} %get-tuple-element.142), calls=%async_computation.2 | async-start | bytes 2097152 | tf_op jit(solution)/shard_map/all_to_all | solution.py:805
  200.7 5.0 %collective-permute-done.33.refs_8_ = bf16[64,512]{1,0:T(8,128)(2,1)S(1)} collective-permute-done((bf16[64,512]{1,0:T(8,128)(2,1)S(1)}, bf16[64,512]{1,0:T(8,128)(2,1)S(1)}, u32[]{:S(2)}, u32[]{:S(2)}) %collective-permute-start.33) | collective-permute-done | bytes 65568 | tf_op jit(solution)/shard_map/ppermute | solution.py:822
  205.7 17.7 %attend_back_kernel.1 = (bf16[192,512]{1,0:T(8,128)(2,1)S(1)}, bf16[192,512]{1,0:T(8,128)(2,1)S(1)}, bf16[192,512]{1,0:T(8,128)(2,1)S(1)}, bf16[192,512]{1,0:T(8,128)(2,1)S(1)}, f32[8,128]{1,0:T(8,128)S(1)}) custom-call(s32[1,128]{1,0:T(1,128)S(1)} %copy-done.10, bf16[192,512]{1,0:T(8,128)(2,1)S(1)} %copy-done.17, ...), custom_call_target="tpu_custom_call" | custom-call | flops 20899999744 | bytes 68400000 | tf_op jit(solution)/shard_map/attend_back_kernel/pallas_call | solution.py:400
  225.1 1.9 collective-permute-start.36
  227.0 2.5 layer_out_kernel.1
  230.5 1.5 ffn_last_kernel.1
  232.0 3.4 %all-to-all-start.3 = ((bf16[4,32,1024]{2,1,0:T(8,128)(2,1)}), bf16[4,32,1024]{2,1,0:T(8,128)(2,1)S(1)}, u32[]{:S(2)}, u32[]{:S(2)}) async-start(bf16[4,32,1024]{2,1,0:T(8,128)(2,1)} %get-tuple-element.167), calls=%async_computation.4 | async-start | bytes 524288 | tf_op jit(solution)/shard_map/all_to_all | solution.py:805
  235.5 5.3 %all-to-all-done.3.refs_6_.refs_0_ = bf16[4,32,1024]{2,1,0:T(8,128)(2,1)S(1)} async-done(((bf16[4,32,1024]{2,1,0:T(8,128)(2,1)}), bf16[4,32,1024]{2,1,0:T(8,128)(2,1)S(1)}, u32[]{:S(2)}, u32[]{:S(2)}) %all-to-all-start.3) | async-done | bytes 262176 | tf_op jit(solution)/shard_map/all_to_all | solution.py:805
  240.8 3.5 %qkv_back_kernel.1 = (f32[128,1024]{1,0:T(8,128)S(1)}, bf16[128,1024]{1,0:T(8,128)(2,1)S(1)}, bf16[128,1024]{1,0:T(8,128)(2,1)S(1)}, bf16[128,1024]{1,0:T(8,128)...) custom-call(s32[3]{0:T(128)S(1)} %pad_add_fusion.refs_0_, ...), custom_call_target="tpu_custom_call" | custom-call | flops 3300000000 | bytes 10800000 | tf_op jit(solution)/shard_map/qkv_back_kernel/pallas_call | solution.py:400
  245.1 7.8 %qkv_grad_kernel.1 = (bf16[4,2,4,32,896]{4,3,2,1,0:T(8,128)(2,1)}, f32[8,128]{1,0:T(8,128)S(1)}) custom-call(s32[3]{0:T(128)S(1)} %pad_add_fusion.refs_0_, s32[4]{0:T(128)S(1)} %bitcast.54, s32[1,128]{1,0:T(1,128)S(1)} %copy-done.10, bf16[24,1024]{1,0:T(8,128)(2,1)S(1)} %reshape.72.refs_3_.refs_2_.refs_0_, bf16[128,1024]{1,0:T(8,128)(2,1)} %bitcast.48, ...), custom_call_target="tpu_custom_call" | custom-call | flops 6600000000 | bytes 21600000 | tf_op jit(solution)/shard_map/qkv_grad_kernel/pallas_call | solution.py:400
  253.0 3.6 %all-to-all-start.4 = ((bf16[8,4,32,896]{3,2,1,0:T(8,128)(2,1)}), bf16[8,4,32,896]{3,2,1,0:T(8,128)(2,1)S(1)}, u32[]{:S(2)}, u32[]{:S(2)}) async-start(bf16[8,4,32,896]{3,2,1,0:T(8,128)(2,1)} %bitcast.16), calls=%async_computation.5 | async-start | bytes 3670016 | tf_op jit(solution)/shard_map/all_to_all | solution.py:805
  258.5 2.5 collective-permute-start.38
  262.4 1.4 up_join_kernel.1
  263.8 8.5 %collective-permute-done.37.refs_6_ = bf16[128,1024]{1,0:T(8,128)(2,1)S(1)} collective-permute-done((bf16[128,1024]{1,0:T(8,128)(2,1)S(1)}, bf16[128,1024]{1,0:T(8,128)(2,1)S(1)}, u32[]{:S(2)}, u32[]{:S(2)}) %collective-permute-start.37) | collective-permute-done | bytes 262176 | tf_op jit(solution)/shard_map/ppermute | solution.py:822
  272.3 10.5 %collective-permute-done.39.refs_8_ = bf16[128,1024]{1,0:T(8,128)(2,1)S(1)} collective-permute-done((bf16[128,1024]{1,0:T(8,128)(2,1)S(1)}, bf16[128,1024]{1,0:T(8,128)(2,1)S(1)}, u32[]{:S(2)}, u32[]{:S(2)}) %collective-permute-start.39) | collective-permute-done | bytes 262176 | tf_op jit(solution)/shard_map/ppermute | solution.py:822
  282.8 3.5 %first_back_kernel.1 = (f32[128,1024]{1,0:T(8,128)}, f32[8,128]{1,0:T(8,128)S(1)}) custom-call(s32[4]{0:T(128)S(1)} %bitcast.55, s32[1,128]{1,0:T(1,128)S(1)} %copy-done.10, bf16[24,1024]{1,0:T(8,128)(2,1)S(1)} %reshape.72.refs_3_.refs_2_.refs_0_, bf16[128,1024]{1,0:T(8,128)(2,1)} %bitcast.49, f32[128,1024]{1,0:T(8,128)} %get-tuple-element.159.refs_14_.refs_4_, ...), custom_call_target="tpu_custom_call" | custom-call | flops 2200000000 | bytes 7200000 | tf_op jit(solution)/shard_map/first_back_kernel/pallas_call | solution.py:400
  286.3 1.5 octet_kernel.1
  287.9 5.8 %collective-permute-start.40 = (bf16[32,896]{1,0:T(8,128)(2,1)S(1)}, bf16[32,896]{1,0:T(8,128)(2,1)S(1)}, u32[]{:S(2)}, u32[]{:S(2)}) collective-permute-start(bf16[32,896]{1,0:T(8,128)(2,1)S(1)} %get-tuple-element.184), channel_id=1, source_target_pairs={{0,8},{8,0},{16,24},{24,16},{1,9},{9,1},{17,25},{25,17},{2,10},{10... | collective-permute-start | bytes 172040 | tf_op jit(solution)/shard_map/ppermute | solution.py:822
  293.7 2.0 collective-permute-start.41
  297.1 1.5 bitcast_convert_fusion
  299.4 2.4 collective-permute-done.42.refs_4_
  301.8 1.9 qkv_join_kernel.1
  (116 shorter events, 34.9 us)
Async XLA Ops:
  14.7 12.3 %copy-start.1 = (bf16[32,4096]{1,0:T(8,128)(2,1)S(1)}, bf16[32,4096]{1,0:T(8,128)(2,1)}, u32[]{:S(2)}) copy-start(bf16[32,4096]{1,0:T(8,128)(2,1)} %refs_0_.3) | copy-start | bytes 786436
  14.7 15.0 %all-to-all-start = ((bf16[32,8,128]{2,1,0:T(8,128)(2,1)}), bf16[32,8,128]{2,1,0:T(8,128)(2,1)S(1)}, u32[]{:S(2)}, u32[]{:S(2)}) async-start(bf16[32,8,128]{2,1,0:T(8,128)(2,1)} %broadcast_in_dim.14), calls=%async_computation | async-start | bytes 131072 | tf_op jit(solution)/shard_map/all_to_all | solution.py:876
  22.0 20.1 %collective-permute-start.1 = (bf16[128,1024]{1,0:T(8,128)(2,1)}, bf16[128,1024]{1,0:T(8,128)(2,1)S(1)}, u32[]{:S(2)}, u32[]{:S(2)}) collective-permute-start(bf16[128,1024]{1,0:T(8,128)(2,1)} %bitcast.46), channel_id=1, source_target_pairs={{0,16},{8,24},{16,0},{24,8},{1,17},{9,25},{17,1},{25,9},{2,18},{10... | collective-permute-start | bytes 786440 | tf_op jit(solution)/shard_map/ppermute | solution.py:822
  29.6 13.8 %all-to-all-start.1 = ((bf16[4,32,1024]{2,1,0:T(8,128)(2,1)}), bf16[4,32,1024]{2,1,0:T(8,128)(2,1)S(1)}, u32[]{:S(2)}, u32[]{:S(2)}) async-start(bf16[4,32,1024]{2,1,0:T(8,128)(2,1)} %get-tuple-element.116), calls=%async_computation.1 | async-start | bytes 524288 | tf_op jit(solution)/shard_map/all_to_all | solution.py:805
  33.1 77.5 %all-gather.6.cloned.1.call-start = ((), (), s32[]{:S(2)}) async-start(), calls=%async_computation.10 | async-start | bytes 5308416 | tf_op jit(solution)/shard_map/all_gather | solution.py:896
  33.1 6.6 %collective-permute-start.3 = (bf16[32,768]{1,0:T(8,128)(2,1)S(1)}, bf16[32,768]{1,0:T(8,128)(2,1)S(1)}, u32[]{:S(2)}, u32[]{:S(2)}) collective-permute-start(bf16[32,768]{1,0:T(8,128)(2,1)S(1)} %get-tuple-element.110), channel_id=1, source_target_pairs={{0,8},{8,0},{16,24},{24,16},{1,9},{9,1},{17,25},{25,17},{2,10},{10... | collective-permute-start | bytes 147464 | tf_op jit(solution)/shard_map/ppermute | solution.py:822
  33.8 8.2 %collective-permute-start.4 = (bf16[32,768]{1,0:T(8,128)(2,1)S(1)}, bf16[32,768]{1,0:T(8,128)(2,1)S(1)}, u32[]{:S(2)}, u32[]{:S(2)}) collective-permute-start(bf16[32,768]{1,0:T(8,128)(2,1)S(1)} %get-tuple-element.111), channel_id=1, source_target_pairs={{0,16},{8,24},{16,0},{24,8},{1,17},{9,25},{17,1},{25,9},{2,18},{10... | collective-permute-start | bytes 147464 | tf_op jit(solution)/shard_map/ppermute | solution.py:822
  34.4 7.7 %collective-permute-start.5 = (bf16[32,768]{1,0:T(8,128)(2,1)S(1)}, bf16[32,768]{1,0:T(8,128)(2,1)S(1)}, u32[]{:S(2)}, u32[]{:S(2)}) collective-permute-start(bf16[32,768]{1,0:T(8,128)(2,1)S(1)} %get-tuple-element.112), channel_id=1, source_target_pairs={{0,24},{8,16},{16,8},{24,0},{1,25},{9,17},{17,9},{25,1},{2,26},{10... | collective-permute-start | bytes 147464 | tf_op jit(solution)/shard_map/ppermute | solution.py:822
  37.6 5.9 %copy-start.2 = (bf16[128,1024]{1,0:T(8,128)(2,1)S(1)}, bf16[128,1024]{1,0:T(8,128)(2,1)}, u32[]{:S(2)}) copy-start(bf16[128,1024]{1,0:T(8,128)(2,1)} %refs_1_.5) | copy-start | bytes 786436
  37.6 5.9 %copy-start.8 = (bf16[32,1024]{1,0:T(8,128)(2,1)S(1)}, bf16[32,1024]{1,0:T(8,128)(2,1)}, u32[]{:S(2)}) copy-start(bf16[32,1024]{1,0:T(8,128)(2,1)} %refs_2_.3) | copy-start | bytes 196612
  42.1 29.2 %copy-start.4 = (bf16[128,1024]{1,0:T(8,128)(2,1)}, bf16[128,1024]{1,0:T(8,128)(2,1)S(1)}, u32[]{:S(2)}) copy-start(bf16[128,1024]{1,0:T(8,128)(2,1)S(1)} %collective-permute-done.1.refs_6_) | copy-start | bytes 786436
  43.5 27.7 %copy-start.9 = (s32[1,4]{1,0:T(1,128)S(1)}, s32[1,4]{1,0:T(1,128)}, u32[]{:S(2)}) copy-start(s32[1,4]{1,0:T(1,128)} %param.20) | copy-start | bytes 52
  43.5 27.7 %copy-start.10 = (s32[1,128]{1,0:T(1,128)S(1)}, s32[1,128]{1,0:T(1,128)}, u32[]{:S(2)}) copy-start(s32[1,128]{1,0:T(1,128)} %refs_1_.7) | copy-start | bytes 1540
  45.1 92.7 %all-gather.4.cloned.1.call-start = ((), (), s32[]{:S(2)}) async-start(), calls=%async_computation.7 | async-start | bytes 1310720 | tf_op jit(solution)/shard_map/all_gather | solution.py:887
  45.1 9.0 %collective-permute-start = (bf16[128,1024]{1,0:T(8,128)(2,1)S(1)}, bf16[128,1024]{1,0:T(8,128)(2,1)S(1)}, u32[]{:S(2)}, u32[]{:S(2)}) collective-permute-start(bf16[128,1024]{1,0:T(8,128)(2,1)S(1)} %bitcast.50), channel_id=1, source_target_pairs={{0,8},{8,0},{16,24},{24,16},{1,9},{9,1},{17,25},{25,17},{2,10},{10... | collective-permute-start | bytes 786440 | tf_op jit(solution)/shard_map/ppermute | solution.py:822
  46.3 8.7 %collective-permute-start.8 = (bf16[4,32,768]{2,1,0:T(8,128)(2,1)S(1)}, bf16[4,32,768]{2,1,0:T(8,128)(2,1)S(1)}, u32[]{:S(2)}, u32[]{:S(2)}) collective-permute-start(bf16[4,32,768]{2,1,0:T(8,128)(2,1)S(1)} %get-tuple-element.115.refs_8_), channel_id=1, source_target_pairs={{0,6},{2,4},{4,2},{6,0},{1,7},{3,5},{5,3},{7,1},{8,14},{10,12},{12... | collective-permute-start | bytes 589832 | tf_op jit(solution)/shard_map/ppermute | solution.py:817
  48.8 8.8 %collective-permute-start.7 = (bf16[4,32,768]{2,1,0:T(8,128)(2,1)S(1)}, bf16[4,32,768]{2,1,0:T(8,128)(2,1)S(1)}, u32[]{:S(2)}, u32[]{:S(2)}) collective-permute-start(bf16[4,32,768]{2,1,0:T(8,128)(2,1)S(1)} %get-tuple-element.115.refs_8_), channel_id=1, source_target_pairs={{0,4},{4,0},{1,5},{5,1},{2,6},{6,2},{3,7},{7,3},{8,12},{12,8},{9,1... | collective-permute-start | bytes 589832 | tf_op jit(solution)/shard_map/ppermute | solution.py:816
  49.4 8.4 %collective-permute-start.6 = (bf16[4,32,768]{2,1,0:T(8,128)(2,1)S(1)}, bf16[4,32,768]{2,1,0:T(8,128)(2,1)S(1)}, u32[]{:S(2)}, u32[]{:S(2)}) collective-permute-start(bf16[4,32,768]{2,1,0:T(8,128)(2,1)S(1)} %get-tuple-element.115.refs_8_), channel_id=1, source_target_pairs={{0,2},{2,0},{1,3},{3,1},{4,6},{6,4},{5,7},{7,5},{8,10},{10,8},{9,1... | collective-permute-start | bytes 589832 | tf_op jit(solution)/shard_map/ppermute | solution.py:815
  49.8 21.4 %collective-permute-start.2 = (bf16[128,1024]{1,0:T(8,128)(2,1)S(1)}, bf16[128,1024]{1,0:T(8,128)(2,1)S(1)}, u32[]{:S(2)}, u32[]{:S(2)}) collective-permute-start(bf16[128,1024]{1,0:T(8,128)(2,1)S(1)} %collective-permute-done.1.refs_6_), channel_id=1, source_target_pairs={{0,8},{8,0},{16,24},{24,16},{1,9},{9,1},{17,25},{25,17},{2,10},{10... | collective-permute-start | bytes 786440 | tf_op jit(solution)/shard_map/ppermute | solution.py:822
  54.1 23.6 %copy-start.5 = (bf16[128,1024]{1,0:T(8,128)(2,1)}, bf16[128,1024]{1,0:T(8,128)(2,1)S(1)}, u32[]{:S(2)}) copy-start(bf16[128,1024]{1,0:T(8,128)(2,1)S(1)} %collective-permute-done.refs_5_) | copy-start | bytes 786436
  54.1 4.4 %collective-permute-start.9 = (bf16[4,32,768]{2,1,0:T(8,128)(2,1)S(1)}, bf16[4,32,768]{2,1,0:T(8,128)(2,1)S(1)}, u32[]{:S(2)}, u32[]{:S(2)}) collective-permute-start(bf16[4,32,768]{2,1,0:T(8,128)(2,1)S(1)} %get-tuple-element.115.refs_8_), channel_id=1, source_target_pairs={{0,1},{1,0},{2,3},{3,2},{4,5},{5,4},{6,7},{7,6},{8,9},{9,8},{10,11... | collective-permute-start | bytes 589832 | tf_op jit(solution)/shard_map/ppermute | solution.py:835
  55.1 16.2 %collective-permute-start.12 = (bf16[4,32,768]{2,1,0:T(8,128)(2,1)S(1)}, bf16[4,32,768]{2,1,0:T(8,128)(2,1)S(1)}, u32[]{:S(2)}, u32[]{:S(2)}) collective-permute-start(bf16[4,32,768]{2,1,0:T(8,128)(2,1)S(1)} %collective-permute-done.8.refs_11_), channel_id=1, source_target_pairs={{0,1},{1,0},{2,3},{3,2},{4,5},{5,4},{6,7},{7,6},{8,9},{9,8},{10,11... | collective-permute-start | bytes 589832 | tf_op jit(solution)/shard_map/ppermute | solution.py:835
  57.6 13.6 %collective-permute-start.11 = (bf16[4,32,768]{2,1,0:T(8,128)(2,1)S(1)}, bf16[4,32,768]{2,1,0:T(8,128)(2,1)S(1)}, u32[]{:S(2)}, u32[]{:S(2)}) collective-permute-start(bf16[4,32,768]{2,1,0:T(8,128)(2,1)S(1)} %collective-permute-done.7.refs_10_), channel_id=1, source_target_pairs={{0,1},{1,0},{2,3},{3,2},{4,5},{5,4},{6,7},{7,6},{8,9},{9,8},{10,11... | collective-permute-start | bytes 589832 | tf_op jit(solution)/shard_map/ppermute | solution.py:835
  57.8 13.5 %collective-permute-start.10 = (bf16[4,32,768]{2,1,0:T(8,128)(2,1)S(1)}, bf16[4,32,768]{2,1,0:T(8,128)(2,1)S(1)}, u32[]{:S(2)}, u32[]{:S(2)}) collective-permute-start(bf16[4,32,768]{2,1,0:T(8,128)(2,1)S(1)} %collective-permute-done.6.refs_9_), channel_id=1, source_target_pairs={{0,1},{1,0},{2,3},{3,2},{4,5},{5,4},{6,7},{7,6},{8,9},{9,8},{10,11... | collective-permute-start | bytes 589832 | tf_op jit(solution)/shard_map/ppermute | solution.py:835
  71.2 6.5 %copy-start.6 = (bf16[128,1024]{1,0:T(8,128)(2,1)}, bf16[128,1024]{1,0:T(8,128)(2,1)S(1)}, u32[]{:S(2)}) copy-start(bf16[128,1024]{1,0:T(8,128)(2,1)S(1)} %collective-permute-done.2.refs_7_) | copy-start | bytes 786436
  78.4 5.9 %collective-permute-start.13 = (bf16[192,512]{1,0:T(8,128)(2,1)}, bf16[192,512]{1,0:T(8,128)(2,1)S(1)}, u32[]{:S(2)}, u32[]{:S(2)}) collective-permute-start(bf16[192,512]{1,0:T(8,128)(2,1)} %get-tuple-element.120), channel_id=1, source_target_pairs={{0,2},{2,0},{1,3},{3,1},{4,6},{6,4},{5,7},{7,5},{8,10},{10,8},{9,1... | collective-permute-start | bytes 589832 | tf_op jit(solution)/shard_map/ppermute | solution.py:815
  80.1 6.8 %collective-permute-start.14 = (bf16[192,512]{1,0:T(8,128)(2,1)S(1)}, bf16[192,512]{1,0:T(8,128)(2,1)S(1)}, u32[]{:S(2)}, u32[]{:S(2)}) collective-permute-start(bf16[192,512]{1,0:T(8,128)(2,1)S(1)} %get-tuple-element.121), channel_id=1, source_target_pairs={{0,4},{4,0},{1,5},{5,1},{2,6},{6,2},{3,7},{7,3},{8,12},{12,8},{9,1... | collective-permute-start | bytes 589832 | tf_op jit(solution)/shard_map/ppermute | solution.py:816
  81.6 6.6 %collective-permute-start.15 = (bf16[192,512]{1,0:T(8,128)(2,1)S(1)}, bf16[192,512]{1,0:T(8,128)(2,1)S(1)}, u32[]{:S(2)}, u32[]{:S(2)}) collective-permute-start(bf16[192,512]{1,0:T(8,128)(2,1)S(1)} %get-tuple-element.122), channel_id=1, source_target_pairs={{0,6},{2,4},{4,2},{6,0},{1,7},{3,5},{5,3},{7,1},{8,14},{10,12},{12... | collective-permute-start | bytes 589832 | tf_op jit(solution)/shard_map/ppermute | solution.py:817
  81.9 147.6 %reduce-scatter.3.cloned.1.call-start = ((), (), s32[]{:S(2)}) async-start(), calls=%async_computation.8 | async-start | bytes 4718592 | tf_op jit(solution)/shard_map/reduce_scatter | solution.py:935
  100.2 4.5 %collective-permute-start.16 = (bf16[64,512]{1,0:T(8,128)(2,1)S(1)}, bf16[64,512]{1,0:T(8,128)(2,1)S(1)}, u32[]{:S(2)}, u32[]{:S(2)}) collective-permute-start(bf16[64,512]{1,0:T(8,128)(2,1)S(1)} %get-tuple-element.125), channel_id=1, source_target_pairs={{0,8},{8,0},{16,24},{24,16},{1,9},{9,1},{17,25},{25,17},{2,10},{10... | collective-permute-start | bytes 196616 | tf_op jit(solution)/shard_map/ppermute | solution.py:822
  100.3 7.1 %collective-permute-start.17 = (bf16[64,512]{1,0:T(8,128)(2,1)S(1)}, bf16[64,512]{1,0:T(8,128)(2,1)S(1)}, u32[]{:S(2)}, u32[]{:S(2)}) collective-permute-start(bf16[64,512]{1,0:T(8,128)(2,1)S(1)} %get-tuple-element.126), channel_id=1, source_target_pairs={{0,16},{8,24},{16,0},{24,8},{1,17},{9,25},{17,1},{25,9},{2,18},{10... | collective-permute-start | bytes 196616 | tf_op jit(solution)/shard_map/ppermute | solution.py:822
  104.5 6.1 %collective-permute-start.18 = (bf16[64,512]{1,0:T(8,128)(2,1)S(1)}, bf16[64,512]{1,0:T(8,128)(2,1)S(1)}, u32[]{:S(2)}, u32[]{:S(2)}) collective-permute-start(bf16[64,512]{1,0:T(8,128)(2,1)S(1)} %get-tuple-element.127), channel_id=1, source_target_pairs={{0,24},{8,16},{16,8},{24,0},{1,25},{9,17},{17,9},{25,1},{2,26},{10... | collective-permute-start | bytes 196616 | tf_op jit(solution)/shard_map/ppermute | solution.py:822
  113.2 6.4 %collective-permute-start.19 = (bf16[128,1024]{1,0:T(8,128)(2,1)S(1)}, bf16[128,1024]{1,0:T(8,128)(2,1)S(1)}, u32[]{:S(2)}, u32[]{:S(2)}) collective-permute-start(bf16[128,1024]{1,0:T(8,128)(2,1)S(1)} %get-tuple-element.131), channel_id=1, source_target_pairs={{0,2},{2,0},{1,3},{3,1},{4,6},{6,4},{5,7},{7,5},{8,10},{10,8},{9,1... | collective-permute-start | bytes 786440 | tf_op jit(solution)/shard_map/ppermute | solution.py:815
  114.1 10.1 %collective-permute-start.20 = (bf16[128,1024]{1,0:T(8,128)(2,1)S(1)}, bf16[128,1024]{1,0:T(8,128)(2,1)S(1)}, u32[]{:S(2)}, u32[]{:S(2)}) collective-permute-start(bf16[128,1024]{1,0:T(8,128)(2,1)S(1)} %get-tuple-element.132), channel_id=1, source_target_pairs={{0,4},{4,0},{1,5},{5,1},{2,6},{6,2},{3,7},{7,3},{8,12},{12,8},{9,1... | collective-permute-start | bytes 786440 | tf_op jit(solution)/shard_map/ppermute | solution.py:816
  115.1 11.7 %collective-permute-start.21 = (bf16[128,1024]{1,0:T(8,128)(2,1)S(1)}, bf16[128,1024]{1,0:T(8,128)(2,1)S(1)}, u32[]{:S(2)}, u32[]{:S(2)}) collective-permute-start(bf16[128,1024]{1,0:T(8,128)(2,1)S(1)} %get-tuple-element.133), channel_id=1, source_target_pairs={{0,6},{2,4},{4,2},{6,0},{1,7},{3,5},{5,3},{7,1},{8,14},{10,12},{12... | collective-permute-start | bytes 786440 | tf_op jit(solution)/shard_map/ppermute | solution.py:817
  129.7 8.1 %collective-permute-start.24 = (bf16[128,1024]{1,0:T(8,128)(2,1)S(1)}, bf16[128,1024]{1,0:T(8,128)(2,1)S(1)}, u32[]{:S(2)}, u32[]{:S(2)}) collective-permute-start(bf16[128,1024]{1,0:T(8,128)(2,1)S(1)} %get-tuple-element.136.refs_2_.refs_3_), channel_id=1, source_target_pairs={{0,6},{2,4},{4,2},{6,0},{1,7},{3,5},{5,3},{7,1},{8,14},{10,12},{12... | collective-permute-start | bytes 786440 | tf_op jit(solution)/shard_map/ppermute | solution.py:817
  132.1 8.1 %collective-permute-start.23 = (bf16[128,1024]{1,0:T(8,128)(2,1)S(1)}, bf16[128,1024]{1,0:T(8,128)(2,1)S(1)}, u32[]{:S(2)}, u32[]{:S(2)}) collective-permute-start(bf16[128,1024]{1,0:T(8,128)(2,1)S(1)} %get-tuple-element.136.refs_2_.refs_3_), channel_id=1, source_target_pairs={{0,4},{4,0},{1,5},{5,1},{2,6},{6,2},{3,7},{7,3},{8,12},{12,8},{9,1... | collective-permute-start | bytes 786440 | tf_op jit(solution)/shard_map/ppermute | solution.py:816
  132.9 7.2 %collective-permute-start.22 = (bf16[128,1024]{1,0:T(8,128)(2,1)S(1)}, bf16[128,1024]{1,0:T(8,128)(2,1)S(1)}, u32[]{:S(2)}, u32[]{:S(2)}) collective-permute-start(bf16[128,1024]{1,0:T(8,128)(2,1)S(1)} %get-tuple-element.136.refs_2_.refs_3_), channel_id=1, source_target_pairs={{0,2},{2,0},{1,3},{3,1},{4,6},{6,4},{5,7},{7,5},{8,10},{10,8},{9,1... | collective-permute-start | bytes 786440 | tf_op jit(solution)/shard_map/ppermute | solution.py:815
  148.7 14.2 %copy-start.13 = (f32[128,1024]{1,0:T(8,128)}, f32[128,1024]{1,0:T(8,128)S(1)}, u32[]{:S(2)}) copy-start(f32[128,1024]{1,0:T(8,128)S(1)} %get-tuple-element.145.refs_3_) | copy-start | bytes 1572868
  148.7 6.4 %collective-permute-start.25 = (bf16[128,1024]{1,0:T(8,128)(2,1)S(1)}, bf16[128,1024]{1,0:T(8,128)(2,1)S(1)}, u32[]{:S(2)}, u32[]{:S(2)}) collective-permute-start(bf16[128,1024]{1,0:T(8,128)(2,1)S(1)} %get-tuple-element.140), channel_id=1, source_target_pairs={{0,2},{2,0},{1,3},{3,1},{4,6},{6,4},{5,7},{7,5},{8,10},{10,8},{9,1... | collective-permute-start | bytes 786440 | tf_op jit(solution)/shard_map/ppermute | solution.py:815
  162.9 10.4 %copy-start.14 = (f32[128,1024]{1,0:T(8,128)S(1)}, f32[128,1024]{1,0:T(8,128)}, u32[]{:S(2)}) copy-start(f32[128,1024]{1,0:T(8,128)} %copy-done.13) | copy-start | bytes 1572868
  163.0 10.4 %collective-permute-start.26 = (bf16[128,1024]{1,0:T(8,128)(2,1)S(1)}, bf16[128,1024]{1,0:T(8,128)(2,1)S(1)}, u32[]{:S(2)}, u32[]{:S(2)}) collective-permute-start(bf16[128,1024]{1,0:T(8,128)(2,1)S(1)} %get-tuple-element.146), channel_id=1, source_target_pairs={{0,4},{4,0},{1,5},{5,1},{2,6},{6,2},{3,7},{7,3},{8,12},{12,8},{9,1... | collective-permute-start | bytes 786440 | tf_op jit(solution)/shard_map/ppermute | solution.py:816
  164.0 9.4 %collective-permute-start.27 = (bf16[128,1024]{1,0:T(8,128)(2,1)S(1)}, bf16[128,1024]{1,0:T(8,128)(2,1)S(1)}, u32[]{:S(2)}, u32[]{:S(2)}) collective-permute-start(bf16[128,1024]{1,0:T(8,128)(2,1)S(1)} %get-tuple-element.147), channel_id=1, source_target_pairs={{0,6},{2,4},{4,2},{6,0},{1,7},{3,5},{5,3},{7,1},{8,14},{10,12},{12... | collective-permute-start | bytes 786440 | tf_op jit(solution)/shard_map/ppermute | solution.py:817
  176.4 10.2 %collective-permute-start.30 = (bf16[128,1024]{1,0:T(8,128)(2,1)S(1)}, bf16[128,1024]{1,0:T(8,128)(2,1)S(1)}, u32[]{:S(2)}, u32[]{:S(2)}) collective-permute-start(bf16[128,1024]{1,0:T(8,128)(2,1)S(1)} %get-tuple-element.149.refs_3_), channel_id=1, source_target_pairs={{0,6},{2,4},{4,2},{6,0},{1,7},{3,5},{5,3},{7,1},{8,14},{10,12},{12... | collective-permute-start | bytes 786440 | tf_op jit(solution)/shard_map/ppermute | solution.py:817
  177.1 11.6 %collective-permute-start.29 = (bf16[128,1024]{1,0:T(8,128)(2,1)S(1)}, bf16[128,1024]{1,0:T(8,128)(2,1)S(1)}, u32[]{:S(2)}, u32[]{:S(2)}) collective-permute-start(bf16[128,1024]{1,0:T(8,128)(2,1)S(1)} %get-tuple-element.149.refs_3_), channel_id=1, source_target_pairs={{0,4},{4,0},{1,5},{5,1},{2,6},{6,2},{3,7},{7,3},{8,12},{12,8},{9,1... | collective-permute-start | bytes 786440 | tf_op jit(solution)/shard_map/ppermute | solution.py:816
  178.2 10.8 %collective-permute-start.28 = (bf16[128,1024]{1,0:T(8,128)(2,1)S(1)}, bf16[128,1024]{1,0:T(8,128)(2,1)S(1)}, u32[]{:S(2)}, u32[]{:S(2)}) collective-permute-start(bf16[128,1024]{1,0:T(8,128)(2,1)S(1)} %get-tuple-element.149.refs_3_), channel_id=1, source_target_pairs={{0,2},{2,0},{1,3},{3,1},{4,6},{6,4},{5,7},{7,5},{8,10},{10,8},{9,1... | collective-permute-start | bytes 786440 | tf_op jit(solution)/shard_map/ppermute | solution.py:815
  191.6 14.1 %copy-start.17 = (bf16[192,512]{1,0:T(8,128)(2,1)S(1)}, bf16[192,512]{1,0:T(8,128)(2,1)}, u32[]{:S(2)}) copy-start(bf16[192,512]{1,0:T(8,128)(2,1)} %copy-done.15) | copy-start | bytes 589828
  191.7 8.2 %collective-permute-start.31 = (bf16[64,512]{1,0:T(8,128)(2,1)S(1)}, bf16[64,512]{1,0:T(8,128)(2,1)S(1)}, u32[]{:S(2)}, u32[]{:S(2)}) collective-permute-start(bf16[64,512]{1,0:T(8,128)(2,1)S(1)} %get-tuple-element.152), channel_id=1, source_target_pairs={{0,8},{8,0},{16,24},{24,16},{1,9},{9,1},{17,25},{25,17},{2,10},{10... | collective-permute-start | bytes 196616 | tf_op jit(solution)/shard_map/ppermute | solution.py:822
  192.0 8.8 %collective-permute-start.32 = (bf16[64,512]{1,0:T(8,128)(2,1)S(1)}, bf16[64,512]{1,0:T(8,128)(2,1)S(1)}, u32[]{:S(2)}, u32[]{:S(2)}) collective-permute-start(bf16[64,512]{1,0:T(8,128)(2,1)S(1)} %get-tuple-element.153), channel_id=1, source_target_pairs={{0,16},{8,24},{16,0},{24,8},{1,17},{9,25},{17,1},{25,9},{2,18},{10... | collective-permute-start | bytes 196616 | tf_op jit(solution)/shard_map/ppermute | solution.py:822
  195.1 10.6 %collective-permute-start.33 = (bf16[64,512]{1,0:T(8,128)(2,1)S(1)}, bf16[64,512]{1,0:T(8,128)(2,1)S(1)}, u32[]{:S(2)}, u32[]{:S(2)}) collective-permute-start(bf16[64,512]{1,0:T(8,128)(2,1)S(1)} %get-tuple-element.154), channel_id=1, source_target_pairs={{0,24},{8,16},{16,8},{24,0},{1,25},{9,17},{17,9},{25,1},{2,26},{10... | collective-permute-start | bytes 196616 | tf_op jit(solution)/shard_map/ppermute | solution.py:822
  196.3 30.6 %all-to-all-start.2 = ((bf16[4,128,1024]{2,1,0:T(8,128)(2,1)}), bf16[4,128,1024]{2,1,0:T(8,128)(2,1)S(1)}, u32[]{:S(2)}, u32[]{:S(2)}) async-start(bf16[4,128,1024]{2,1,0:T(8,128)(2,1)} %get-tuple-element.142), calls=%async_computation.2 | async-start | bytes 2097152 | tf_op jit(solution)/shard_map/all_to_all | solution.py:805
  223.4 12.0 %collective-permute-start.34 = (bf16[192,512]{1,0:T(8,128)(2,1)S(1)}, bf16[192,512]{1,0:T(8,128)(2,1)S(1)}, u32[]{:S(2)}, u32[]{:S(2)}) collective-permute-start(bf16[192,512]{1,0:T(8,128)(2,1)S(1)} %get-tuple-element.162), channel_id=1, source_target_pairs={{0,2},{2,0},{1,3},{3,1},{4,6},{6,4},{5,7},{7,5},{8,10},{10,8},{9,1... | collective-permute-start | bytes 589832 | tf_op jit(solution)/shard_map/ppermute | solution.py:815
  224.8 10.7 %collective-permute-start.35 = (bf16[192,512]{1,0:T(8,128)(2,1)S(1)}, bf16[192,512]{1,0:T(8,128)(2,1)S(1)}, u32[]{:S(2)}, u32[]{:S(2)}) collective-permute-start(bf16[192,512]{1,0:T(8,128)(2,1)S(1)} %get-tuple-element.163), channel_id=1, source_target_pairs={{0,4},{4,0},{1,5},{5,1},{2,6},{6,2},{3,7},{7,3},{8,12},{12,8},{9,1... | collective-permute-start | bytes 589832 | tf_op jit(solution)/shard_map/ppermute | solution.py:816
  225.1 10.4 %collective-permute-start.36 = (bf16[192,512]{1,0:T(8,128)(2,1)S(1)}, bf16[192,512]{1,0:T(8,128)(2,1)S(1)}, u32[]{:S(2)}, u32[]{:S(2)}) collective-permute-start(bf16[192,512]{1,0:T(8,128)(2,1)S(1)} %get-tuple-element.164), channel_id=1, source_target_pairs={{0,6},{2,4},{4,2},{6,0},{1,7},{3,5},{5,3},{7,1},{8,14},{10,12},{12... | collective-permute-start | bytes 589832 | tf_op jit(solution)/shard_map/ppermute | solution.py:817
  232.0 8.8 %all-to-all-start.3 = ((bf16[4,32,1024]{2,1,0:T(8,128)(2,1)}), bf16[4,32,1024]{2,1,0:T(8,128)(2,1)S(1)}, u32[]{:S(2)}, u32[]{:S(2)}) async-start(bf16[4,32,1024]{2,1,0:T(8,128)(2,1)} %get-tuple-element.167), calls=%async_computation.4 | async-start | bytes 524288 | tf_op jit(solution)/shard_map/all_to_all | solution.py:805
  253.0 33.4 %all-to-all-start.4 = ((bf16[8,4,32,896]{3,2,1,0:T(8,128)(2,1)}), bf16[8,4,32,896]{3,2,1,0:T(8,128)(2,1)S(1)}, u32[]{:S(2)}, u32[]{:S(2)}) async-start(bf16[8,4,32,896]{3,2,1,0:T(8,128)(2,1)} %bitcast.16), calls=%async_computation.5 | async-start | bytes 3670016 | tf_op jit(solution)/shard_map/all_to_all | solution.py:805
  256.6 40.5 %reduce-scatter.5.cloned.1.call-start = ((), (), s32[]{:S(2)}) async-start(), calls=%async_computation.9 | async-start | bytes 589824 | tf_op jit(solution)/shard_map/reduce_scatter | solution.py:952
  257.1 15.2 %collective-permute-start.37 = (bf16[128,1024]{1,0:T(8,128)(2,1)S(1)}, bf16[128,1024]{1,0:T(8,128)(2,1)S(1)}, u32[]{:S(2)}, u32[]{:S(2)}) collective-permute-start(bf16[128,1024]{1,0:T(8,128)(2,1)S(1)} %get-tuple-element.170), channel_id=1, source_target_pairs={{0,8},{8,0},{16,24},{24,16},{1,9},{9,1},{17,25},{25,17},{2,10},{10... | collective-permute-start | bytes 786440 | tf_op jit(solution)/shard_map/ppermute | solution.py:822
  258.5 13.8 %collective-permute-start.38 = (bf16[128,1024]{1,0:T(8,128)(2,1)S(1)}, bf16[128,1024]{1,0:T(8,128)(2,1)S(1)}, u32[]{:S(2)}, u32[]{:S(2)}) collective-permute-start(bf16[128,1024]{1,0:T(8,128)(2,1)S(1)} %get-tuple-element.171), channel_id=1, source_target_pairs={{0,16},{8,24},{16,0},{24,8},{1,17},{9,25},{17,1},{25,9},{2,18},{10... | collective-permute-start | bytes 786440 | tf_op jit(solution)/shard_map/ppermute | solution.py:822
  261.0 21.9 %collective-permute-start.39 = (bf16[128,1024]{1,0:T(8,128)(2,1)S(1)}, bf16[128,1024]{1,0:T(8,128)(2,1)S(1)}, u32[]{:S(2)}, u32[]{:S(2)}) collective-permute-start(bf16[128,1024]{1,0:T(8,128)(2,1)S(1)} %get-tuple-element.172), channel_id=1, source_target_pairs={{0,24},{8,16},{16,8},{24,0},{1,25},{9,17},{17,9},{25,1},{2,26},{10... | collective-permute-start | bytes 786440 | tf_op jit(solution)/shard_map/ppermute | solution.py:822
  262.4 20.5 %copy-start.12 = (f32[128,1024]{1,0:T(8,128)S(1)}, f32[128,1024]{1,0:T(8,128)}, u32[]{:S(2)}) copy-start(f32[128,1024]{1,0:T(8,128)} %copy-done.11) | copy-start | bytes 1572868
  287.9 10.7 %collective-permute-start.40 = (bf16[32,896]{1,0:T(8,128)(2,1)S(1)}, bf16[32,896]{1,0:T(8,128)(2,1)S(1)}, u32[]{:S(2)}, u32[]{:S(2)}) collective-permute-start(bf16[32,896]{1,0:T(8,128)(2,1)S(1)} %get-tuple-element.184), channel_id=1, source_target_pairs={{0,8},{8,0},{16,24},{24,16},{1,9},{9,1},{17,25},{25,17},{2,10},{10... | collective-permute-start | bytes 172040 | tf_op jit(solution)/shard_map/ppermute | solution.py:822
  293.7 5.7 %collective-permute-start.41 = (bf16[32,896]{1,0:T(8,128)(2,1)S(1)}, bf16[32,896]{1,0:T(8,128)(2,1)S(1)}, u32[]{:S(2)}, u32[]{:S(2)}) collective-permute-start(bf16[32,896]{1,0:T(8,128)(2,1)S(1)} %get-tuple-element.185), channel_id=1, source_target_pairs={{0,16},{8,24},{16,0},{24,8},{1,17},{9,25},{17,1},{25,9},{2,18},{10... | collective-permute-start | bytes 172040 | tf_op jit(solution)/shard_map/ppermute | solution.py:822
  295.7 6.1 %collective-permute-start.42 = (bf16[32,896]{1,0:T(8,128)(2,1)S(1)}, bf16[32,896]{1,0:T(8,128)(2,1)S(1)}, u32[]{:S(2)}, u32[]{:S(2)}) collective-permute-start(bf16[32,896]{1,0:T(8,128)(2,1)S(1)} %get-tuple-element.186), channel_id=1, source_target_pairs={{0,24},{8,16},{16,8},{24,0},{1,25},{9,17},{17,9},{25,1},{2,26},{10... | collective-permute-start | bytes 172040 | tf_op jit(solution)/shard_map/ppermute | solution.py:822
  (6 other events, 6.0 us)
Sparse Core Ops, SparseCore 0:
  45.2 53.2 all-gather.5
  100.3 37.3 all-gather.3
  163.1 53.2 reduce-scatter.2
  259.4 36.0 reduce-scatter.4

commit v3 on v2

--- a/solution.py
+++ b/solution.py
@@ -366,7 +366,7 @@
         return self.ready()[at]
 
 
-def run(order, kernel, outs, ins, scratch=(), after=()):
+def run(order, kernel, outs, ins, scratch=(), after=(), alias=None):
     after = list(after) + order
     kinds = [type(a) if isinstance(a, Far) else None for a in ins]
     ins = [a.value if kind else a for a, kind in zip(ins, kinds)]
@@ -396,7 +396,7 @@
         refs[n_out][...] = jnp.zeros_like(refs[n_out])
         mover.wait()
 
-    spaces = [pl.ANY if kind else SMEM if a.ndim == 1 else VMEM for a, kind in zip(ins, kinds)]
+    spaces = [pl.ANY if kind else SMEM if a.dtype == jnp.int32 and a.ndim == 1 else VMEM for a, kind in zip(ins, kinds)]
     results = pl.pallas_call(
         body,
         name=name,
@@ -407,7 +407,11 @@
         scratch_shapes=[pltpu.VMEM(s, d) for s, d in scratch] + staged + [pltpu.SemaphoreType.DMA((64,))],
         compiler_params=pltpu.CompilerParams(vmem_limit_bytes=room << 20),
         cost_estimate=cost,
-    )(*[pltpu.with_memory_space_constraint(a, HBM) if kind else a for a, kind in zip(ins, kinds)], *after)
+        input_output_aliases=dict([alias] if alias else []),
+    )(
+        *[pltpu.with_memory_space_constraint(a, HBM) if kind else a for a, kind in zip(ins, kinds)],
+        *[pltpu.with_memory_space_constraint(a, HBM) if a.size > 4096 else a for a in after],
+    )
     order[:] = results[n_out:]
     return results[:n_out]
 
@@ -438,14 +442,25 @@
     return vec[row : row + 1, :].astype(f32)
 
 
-def q_prep_kernel(mover, pos, qkv, o0, o1, o2, o3):
+def q_prep_kernel(mover, pos, qkv, table, g1, b1, qb, vb, ob, g2, b2, db, ub, *outs):
     z = pos[0]
-    width = o0.shape[1] // 3
+    rw = qkv.shape[0]
     d = qkv.shape[1] // 3
-    for u, out in enumerate((o0, o1, o2, o3)):
+    width = d // DEPTH
+    side = outs[0].shape[1] - 3 * width
+
+    def wide(values):
+        values = values.astype(f32)
+        return jnp.concatenate([values, jnp.zeros((values.shape[0], side - values.shape[1]), f32)], 1)
+
+    rows = [wide(table[...])] + [wide(v[...].reshape(1, -1)) for v in (g1, b1, qb, vb, ob, g2, b2, db)]
+    rows += [ub[...].reshape(1, -1).astype(f32), jnp.zeros((rw - VEC_ROWS - 1, side), f32)]
+    small = jnp.concatenate(rows, 0).astype(bf16)
+    for u, out in enumerate(outs):
         for part in range(3):
             start = pl.multiple_of(part * d + (z ^ u) * width, width)
-            mover.start(qkv.at[:, pl.ds(start, width)], out.at[:, part * width : (part + 1) * width])
+            out[:, part * width : (part + 1) * width] = qkv[:, pl.ds(start, width)]
+        out[:, 3 * width :] = small
 
 
 def q_stack_kernel(mover, pos, b0, b1, b2, b3, out):
@@ -463,37 +478,52 @@
                 out[k, :, dst : dst + fr] = up[:, src : src + fr]
 
 
-def shard_kernel(mover, ups, down, out_rows, out):
+def first_shard_kernel(mover, out_rows, down, out):
+    out[0] = out_rows[...]
+    out[1] = down[0 : out.shape[1], :]
+
+
+def shard_kernel(mover, ups, down, out):
     out[0:PLANE] = ups[...]
-    out[PLANE : 2 * PLANE] = down[...].reshape(PLANE, -1, down.shape[1])
-    out[2 * PLANE] = out_rows[...]
-
-
-def qkv_kernel(mover, pos, lead, seg_row, vec, t0, t1, t2, t3, *refs):
+    out[PLANE:] = down[out.shape[1] :, :].reshape(PLANE - 1, -1, down.shape[1])
+
+
+def qkv_kernel(mover, pos, lead, seg_row, toks, *refs):
     z, yx, c = pos[0], pos[1], pos[2]
-    qa, qc, (n1, w_out, o0, o1, o2, o3, w, proj) = refs[:4], refs[4:8], refs[8:]
-    rows, d = t0.shape
+    qa, qc, (n1, w_out, vec, up_b, o0, o1, o2, o3, w, proj) = refs[:4], refs[4:8], refs[8:]
+    rows, d = toks.shape[1:]
+    width = d // DEPTH
+    head = width // PLANE
+    rw = w.shape[3]
+    fr = w.shape[4] - 3 * width
     pending = [mover.start(qa[k], w.at[:, yx ^ k, c]) for k in range(PLANE)]
     pending += [mover.start(qc[k], w.at[:, yx ^ k, 1 - c]) for k in range(PLANE)]
-    shift = mul(lead_hot(lead, seg_row), vec[0:LEADS, :], 0, 0)
+    mover.wait(pending)
+    mover.start(w.at[:, :, :, :, 0 : 3 * width], w_out)
+    for zz in range(DEPTH):
+        for k in range(PLANE):
+            for core in range(2):
+                i = (zz * PLANE + k) * 2 + core
+                side = w[zz, k, core, :, 3 * width :].astype(f32)
+                vec[:, i * rw : (i + 1) * rw] = side[0:VEC_ROWS, 0:rw]
+        for core in range(2):
+            side = w[zz, yx, core, :, 3 * width :].astype(f32)
+            start = (core * DEPTH + zz) * fr
+            up_b[:, start : start + fr] = side[VEC_ROWS : VEC_ROWS + 1, :]
+    shift = mul(lead_hot(lead, seg_row), vec[0:LEADS, :].astype(bf16), 0, 0)
     gain, bias = vec_row(vec, ROW_G1), vec_row(vec, ROW_B1)
-    for s, t in enumerate((t0, t1, t2, t3)):
-        normal, _ = row_stats(t[...].astype(f32) + shift)
+    for s in range(DEPTH):
+        normal, _ = row_stats(toks[z ^ s].astype(f32) + shift)
         n1[s * rows : (s + 1) * rows, :] = (normal * gain + bias).astype(bf16)
-    width = d // DEPTH
-    head = width // PLANE
     at = pl.ds(pl.multiple_of(z * width, width), width)
-    held = vec
     biases = jnp.concatenate(
-        [held[ROW_QB : ROW_QB + 1, at].astype(f32), jnp.zeros((1, width), f32), held[ROW_VB : ROW_VB + 1, at].astype(f32)],
-        1,
+        [vec[ROW_QB : ROW_QB + 1, at], jnp.zeros((1, width), f32), vec[ROW_VB : ROW_VB + 1, at]], 1
     )
     first = lax.broadcasted_iota(jnp.int32, (8, 3 * width), 0) == 0
     biases = jnp.where(first, biases, 0.0).astype(bf16)
     ones = jnp.ones((8, DEPTH * rows), bf16)
-    mover.wait(pending)
-    mover.start(w, w_out)
-    found = mul(w[...].reshape(d, 3 * width), n1[...], 0, 1) + mul(biases, ones, 0, 0)
+    weight = w[:, :, :, :, 0 : 3 * width].reshape(d, 3 * width)
+    found = mul(weight, n1[...], 0, 1) + mul(biases, ones, 0, 0)
     proj[...] = found.astype(bf16).reshape(proj.shape)
     for k, out in enumerate((o0, o1, o2, o3)):
         for part in range(3):
@@ -543,11 +573,11 @@
     lax.fori_loop(0, PLANE, step, 0)
 
 
-def out_kernel(mover, pos, a0, a1, a2, a3, ff, p0, p1, p2, p3, att, w_out):
+def out_kernel(mover, pos, a0, a1, a2, a3, first, p0, p1, p2, p3, att, w_out):
     z = pos[0]
     head = a0.shape[0]
     rows, d = p0.shape
-    pending = [mover.start(ff.at[:, :, 2 * PLANE], w_out)]
+    pending = [mover.start(first.at[:, :, 0], w_out)]
     for u, block in enumerate((a0, a1, a2, a3)):
         att[pl.ds(pl.multiple_of((z ^ u) * head, head), head), :] = block[...]
     mover.wait(pending)
@@ -557,7 +587,7 @@
 
 
 def norm_kernel(mover, lead, seg_row, vec, tok, p0, p1, p2, p3, middle, n2):
-    shift = mul(lead_hot(lead, seg_row), vec[0:LEADS, :], 0, 0) + vec_row(vec, ROW_OB)
+    shift = mul(lead_hot(lead, seg_row), vec[0:LEADS, :].astype(bf16), 0, 0) + vec_row(vec, ROW_OB)
     total = p0[...].astype(f32) + p1[...].astype(f32) + p2[...].astype(f32) + p3[...].astype(f32)
     total = tok[...].astype(f32) + shift + total
     middle[...] = total
@@ -565,11 +595,16 @@
     n2[...] = (normal * vec_row(vec, ROW_G2) + vec_row(vec, ROW_B2)).astype(bf16)
 
 
-def ffn_kernel(mover, pos, up_b, n0, n1, n2, n3, d_outs, ff, act, d_hid, p0, p1, p2, p3, d_up_b, w_up, w_down, hid):
+def down_copies(mover, first, ff, w_down):
+    copies = [mover.start(first.at[:, c, 1], w_down.at[c, :, 0]) for c in range(2)]
+    return copies + [mover.start(ff.at[:, c, PLANE:], w_down.at[c, :, 1:]) for c in range(2)]
+
+
+def ffn_kernel(mover, pos, up_b, n0, n1, n2, n3, d_outs, first, ff, act, d_hid, p0, p1, p2, p3, d_up_b, w_up, w_down, hid):
     yx = pos[1]
     rows, d = n0.shape
     for_up = [mover.start(ff.at[:, c, 0:PLANE], w_up.at[:, :, c]) for c in range(2)]
-    for_down = [mover.start(ff.at[:, c, PLANE : 2 * PLANE], w_down.at[c]) for c in range(2)]
+    for_down = down_copies(mover, first, ff, w_down)
     mover.wait(for_up)
     normed = jnp.concatenate([n0[...], n1[...], n2[...], n3[...]], 0)
     up = w_up[...].reshape(d, -1)
@@ -593,10 +628,10 @@
         out[...] = back[j * rows : (j + 1) * rows, :].astype(out.dtype)
 
 
-def ffn_grad_kernel(mover, pos, act, d_hid, n0, n1, n2, n3, ff, d_outs, grads, outs, up_grad, down_grad, w_down):
+def ffn_grad_kernel(mover, pos, act, d_hid, n0, n1, n2, n3, first, ff, d_outs, grads, outs, up_grad, down_grad, w_down):
     yx = pos[1]
     rows, d = outs.shape[1:]
-    pending = [mover.start(ff.at[:, c, PLANE : 2 * PLANE], w_down.at[c]) for c in range(2)]
+    pending = down_copies(mover, first, ff, w_down)
     normed = jnp.concatenate([n0[...], n1[...], n2[...], n3[...]], 0)
     up_grad[...] = mul(normed, d_hid[...], 0, 0).astype(bf16).reshape(up_grad.shape)
     for c in range(2):
@@ -606,16 +641,17 @@
         d_down = d_down + mul(act[j * rows : (j + 1) * rows, :], d_outs[yx ^ j], 0, 0)
     down_grad[...] = d_down.astype(bf16).reshape(down_grad.shape)
     for c in range(2):
-        mover.start(down_grad.at[c], grads.at[:, c, PLANE:])
+        mover.start(down_grad.at[c], grads.at[:, c, PLANE : 2 * PLANE])
     mover.wait(pending)
     found = mul(act[...], w_down[...].reshape(-1, d), 1, 0)
     for j in range(PLANE):
         outs[yx ^ j] = found[j * rows : (j + 1) * rows, :].astype(bf16)
 
 
-def ffn_last_kernel(mover, shard, ups, down):
+def ffn_last_kernel(mover, shard, ups, down, out_rows):
     ups[...] = shard[0:PLANE]
-    down[...] = shard[PLANE:].astype(f32).reshape(down.shape)
+    down[...] = shard[PLANE : 2 * PLANE].astype(f32).reshape(down.shape)
+    out_rows[...] = shard[2 * PLANE].astype(f32)
 
 
 def branch_kernel(mover, vec, middle, d_out, p0, p1, p2, p3, d_mid, d_branch, d_vec):
@@ -630,7 +666,7 @@
     d_vec[...] = jnp.concatenate(sums + [jnp.zeros((4, dy.shape[1]), f32)], 0)
 
 
-def out_back_kernel(mover, pos, att, w_out, b0, b1, b2, b3, o0, o1, o2, o3, grad, d_att):
+def out_back_kernel(mover, pos, att, w_out, b0, b1, b2, b3, others, o0, o1, o2, o3, grads, d_att, grad):
     z = pos[0]
     head = o0.shape[0]
     branch = jnp.concatenate([b0[...], b1[...], b2[...], b3[...]], 0)
@@ -639,6 +675,7 @@
     for u, out in enumerate((o0, o1, o2, o3)):
         out[...] = d_att[z ^ u]
     grad[...] = mul(att[...], branch, 1, 0).astype(bf16).reshape(grad.shape)
+    mover.start(grad, grads.at[:, :, 2 * PLANE])
 
 
 def attend_back_kernel(count, mover, seg_row, b0, b1, b2, b3, c0, c1, c2, c3, lse,
@@ -685,33 +722,33 @@
     return joined[...].reshape(3 * PLANE * head, -1)
 
 
-def qkv_back_kernel(mover, pos, w, g0, g1, g2, g3, r0, r1, r2, r3, back, joined):
+def qkv_back_kernel(mover, pos, w, g0, g1, g2, g3, out, back, joined):
     grads = join_heads(pos[1], (g0, g1, g2, g3), joined)
-    rows, d = r0.shape
+    rows, d = out.shape[1:]
     found = mul(grads, w[...].reshape(d, -1), 0, 1)
     back[...] = found
-    for s, out in enumerate((r0, r1, r2, r3)):
-        out[...] = found[s * rows : (s + 1) * rows, :].astype(out.dtype)
-
-
-def qkv_grad_kernel(mover, pos, lead, seg_row, vec, t0, t1, t2, t3, n1, g0, g1, g2, g3, back, d_mid, d_mid_vec, d_up_b,
-                    out, joined, d_vec):
-    z, yx = pos[0], pos[1]
-    rows, d = t0.shape
+    for s in range(DEPTH):
+        out[pos[0] ^ s] = found[s * rows : (s + 1) * rows, :].astype(bf16)
+
+
+def qkv_grad_kernel(mover, pos, lead, seg_row, vec, toks, n1, g0, g1, g2, g3, back, d_mid, d_mid_vec, d_up_b,
+                    mine, o0, o1, joined, d_vec, both):
+    z, yx, core = pos[0], pos[1], pos[2]
+    rows, d = toks.shape[1:]
     width = d // DEPTH
     grads = join_heads(yx, (g0, g1, g2, g3), joined)
-    rw = out.shape[3]
+    rw = mine.shape[2]
     cols = 3 * width
     grad = mul(n1[...], grads, 0, 1).astype(bf16)
     hot = lead_hot(lead, seg_row)
-    shift = mul(hot, vec[0:LEADS, :], 0, 0)
+    shift = mul(hot, vec[0:LEADS, :].astype(bf16), 0, 0)
     gain = vec_row(vec, ROW_G1)
     d_gain = jnp.zeros((1, d), f32)
     d_bias = jnp.zeros((1, d), f32)
     d_emb = d_mid[...]
-    for s, t in enumerate((t0, t1, t2, t3)):
+    for s in range(DEPTH):
         piece = back[s * rows : (s + 1) * rows, :]
-        normal, inv = row_stats(t[...].astype(f32) + shift)
+        normal, inv = row_stats(toks[z ^ s].astype(f32) + shift)
         d_gain = d_gain + jnp.sum(piece * normal, 0, keepdims=True)
         d_bias = d_bias + jnp.sum(piece, 0, keepdims=True)
         d_emb = d_emb + norm_back(piece * gain, normal, inv)
@@ -728,23 +765,30 @@
     for i, row in enumerate((ROW_G2, ROW_B2, ROW_DB, ROW_OB)):
         d_vec[row : row + 1, :] = d_mid_vec[i : i + 1, :]
     small = d_vec[...].astype(bf16)
-    fr = out.shape[4] - cols
+    fr = mine.shape[3] - cols
     for zz in range(DEPTH):
         for k in range(PLANE):
             for c in range(2):
                 i = (zz * PLANE + k) * 2 + c
-                out[k, c, zz, :, 0:cols] = grad[i * rw : (i + 1) * rw, :]
                 side = jnp.concatenate([small[:, i * rw : (i + 1) * rw], jnp.zeros((rw, fr - rw), bf16)], 1)
                 start = (c * DEPTH + zz) * fr
                 last = jnp.where(yx == k, d_up_b[:, start : start + fr], 0.0).astype(bf16)
                 mark = lax.broadcasted_iota(jnp.int32, (rw, fr), 0) == VEC_ROWS
-                out[k, c, zz, :, cols:] = jnp.where(mark, last.astype(f32), side.astype(f32)).astype(bf16)
-
-
-def first_back_kernel(mover, lead, seg_row, vec, tok, d_mid, r0, r1, r2, r3, out):
-    shift = mul(lead_hot(lead, seg_row), vec[0:LEADS, :], 0, 0)
+                whole = jnp.concatenate(
+                    [grad[i * rw : (i + 1) * rw, :], jnp.where(mark, last.astype(f32), side.astype(f32)).astype(bf16)], 1
+                )
+                both[zz, k, c] = whole
+    mover.start(both.at[0:2, :, 1 - core], o0)
+    mover.start(both.at[2:4, :, 1 - core], o1)
+    mover.start(both.at[:, :, core], mine)
+
+
+def first_back_kernel(mover, lead, seg_row, vec, tok, d_mid, blocks, out):
+    shift = mul(lead_hot(lead, seg_row), vec[0:LEADS, :].astype(bf16), 0, 0)
     normal, inv = row_stats(tok[...].astype(f32) + shift)
-    dy = r0[...].astype(f32) + r1[...].astype(f32) + r2[...].astype(f32) + r3[...].astype(f32)
+    dy = blocks[0].astype(f32)
+    for s in range(1, DEPTH):
+        dy = dy + blocks[s].astype(f32)
     out[...] = d_mid[...] + norm_back(dy * vec_row(vec, ROW_G1), normal, inv)
 
 
@@ -755,11 +799,16 @@
     out[...] = total.astype(bf16)
 
 
-def octet_kernel(mover, pos, blocks, o0, o1, o2, o3, total):
-    found = jnp.zeros(total.shape, f32)
-    for k in range(PLANE):
-        for c in range(2):
-            found = found + blocks[k, c].astype(f32)
+def pair_kernel(mover, pos, mine, o0, o1, p0, p1, p2, p3, total):
+    yx = pos[1]
+    total[0:2] = (mine[0:2].astype(f32) + o0[...].astype(f32)).astype(bf16)
+    total[2:4] = (mine[2:4].astype(f32) + o1[...].astype(f32)).astype(bf16)
+    for k, out in enumerate((p0, p1, p2, p3)):
+        mover.start(total.at[:, yx ^ k], out)
+
+
+def quad_kernel(mover, pos, b0, b1, b2, b3, o0, o1, o2, o3, total):
+    found = b0[...].astype(f32) + b1[...].astype(f32) + b2[...].astype(f32) + b3[...].astype(f32)
     total[...] = found.astype(bf16)
     for u, out in enumerate((o0, o1, o2, o3)):
         out[...] = total[pos[0] ^ u]
@@ -777,8 +826,8 @@
         side = side + block[:, 3 * width :].astype(f32)
     table[...] = side[0:LEADS, 0:rw]
     for i, row in enumerate(rest[:-1]):
-        row[...] = side[LEADS + i : LEADS + i + 1, 0:rw]
-    rest[-1][...] = side[VEC_ROWS : VEC_ROWS + 1, :]
+        row[...] = side[LEADS + i : LEADS + i + 1, 0:rw].reshape(rw)
+    rest[-1][...] = side[VEC_ROWS : VEC_ROWS + 1, :].reshape(-1)
 
 
 def up_join_kernel(mover, blocks, out):
@@ -792,11 +841,11 @@
 
 
 COSTS = {
-    "q_prep_kernel": (1, 4), "q_stack_kernel": (1, 4), "up_prep_kernel": (1, 4), "shard_kernel": (1, 4), "qkv_kernel": (5, 20),
+    "q_prep_kernel": (1, 4), "q_stack_kernel": (1, 4), "up_prep_kernel": (1, 4), "shard_kernel": (1, 4), "first_shard_kernel": (1, 4), "qkv_kernel": (5, 20),
     "attend_kernel": (11, 16), "out_kernel": (2, 12), "norm_kernel": (2, 8), "ffn_kernel": (8, 32), "ffn_grad_kernel": (8, 32),
     "branch_kernel": (2, 12), "out_back_kernel": (3, 12), "attend_back_kernel": (19, 24),
     "qkv_back_kernel": (3, 16), "qkv_grad_kernel": (6, 24), "first_back_kernel": (2, 8), "layer_out_kernel": (1, 8),
-    "octet_kernel": (2, 8), "qkv_join_kernel": (1, 4), "up_join_kernel": (2, 8), "ffn_last_kernel": (1, 8),
+    "pair_kernel": (2, 8), "quad_kernel": (1, 8), "qkv_join_kernel": (1, 4), "up_join_kernel": (2, 8), "ffn_last_kernel": (1, 8),
 }
 PLANE_AXES = ("y", "x")
 
@@ -824,11 +873,6 @@
 
 def along(blocks):
     return (blocks[0],) + tuple(to_depth(blocks[u], u) for u in range(1, DEPTH))
-
-
-def spread(block):
-    far = to_depth(block, 2)
-    return block, to_depth(block, 1), far, to_depth(far, 1)
 
 
 def core_swap(block):
@@ -859,7 +903,6 @@
     rw = qkv_weight.shape[0]
     fr = down_weight.shape[0]
     ff = 2 * DEPTH * fr
-    devices = DEPTH * PLANE * 2
     lead = lead_index[0]
     count = lead.shape[0]
     width = 3 * d // DEPTH
@@ -868,38 +911,34 @@
 
     order = []
     call = functools.partial(run, order)
-    flat = jnp.concatenate(
-        [lead_table.reshape(-1), ln1_gain, ln1_bias, q_bias, v_bias, out_bias, ln2_gain, ln2_bias, down_bias, up_bias]
-    )
-    padded = -(-flat.shape[0] // 1024) * 1024
-    flat = jnp.pad(flat, (0, padded - flat.shape[0])).reshape(8, padded // 8)
-    smalls = lax.all_to_all(
-        jnp.broadcast_to(flat[None], (devices,) + flat.shape), ALL, split_axis=0, concat_axis=0, tiled=True
-    ).reshape(devices, padded)
-    vec = smalls[:, : VEC_ROWS * rw].reshape(devices, VEC_ROWS, rw).transpose(1, 0, 2).reshape(VEC_ROWS, d)
-    up_b = smalls[:, VEC_ROWS * rw : VEC_ROWS * rw + fr].reshape(DEPTH, PLANE, 2, fr)
-    up_b = lax.dynamic_index_in_dim(up_b, yx, 1, keepdims=False).transpose(1, 0, 2).reshape(1, ff)
-
-    q_rows = along(call(q_prep_kernel, [((rw, width), bf16)] * 4, [pos, qkv_weight]))
-    toks = spread(tok)
+    side = width + -(-max(rw, fr) // 128) * 128
+
+    q_rows = along(
+        call(
+            q_prep_kernel,
+            [((rw, side), bf16)] * 4,
+            [pos]
+            + far((qkv_weight, lead_table, ln1_gain, ln1_bias, q_bias, v_bias, out_bias, ln2_gain, ln2_bias, down_bias, up_bias)),
+        )
+    )
+    toks = lax.all_gather(tok, "z", axis=0)
+    d_outs = trade(jnp.broadcast_to(d_rows[None], (PLANE, rows, d)), PLANE_AXES)
+    (q_stack,) = call(q_stack_kernel, [((DEPTH, rw, side), bf16)], [pos, *q_rows], after=[d_outs])
+    q_plane = across((q_stack,) * PLANE)
+    q_other = [core_swap(block) for block in q_plane]
+    (first_shard,) = call(first_shard_kernel, [((2, rw, d), bf16, "far")], [out_weight, down_weight])
+    first = lax.all_gather(first_shard, ("z", "g"), axis=0).reshape(DEPTH, 2, 2, rw, d)
     (up_cols,) = call(up_prep_kernel, [((PLANE, rw, ff), bf16)], [up_weight])
     up_cols = trade(up_cols, PLANE_AXES)
-    d_outs = lax.all_gather(d_rows, PLANE_AXES, axis=0)
-    (q_stack,) = call(
-        q_stack_kernel, [((DEPTH, rw, width), bf16)], [pos, *q_rows], after=[flat, toks[2]]
-    )
-    q_plane = across((q_stack,) * PLANE)
-    q_other = [core_swap(block) for block in q_plane]
-    (ff_shard,) = call(
-        shard_kernel, [((2 * PLANE + 1, rw, d), bf16, "far")], [up_cols, down_weight, out_weight], after=[smalls]
-    )
-    ff_all = lax.all_gather(ff_shard, ("z", "g"), axis=0).reshape(DEPTH, 2, 2 * PLANE + 1, rw, d)
-    n1, w_qkv, *blocks = call(
+    n1, w_qkv, vec, up_b, *blocks = call(
         qkv_kernel,
-        [((span, d), bf16, "far"), ((DEPTH, PLANE, 2, rw, width), bf16, "raw")] + [((3 * head, span), bf16)] * 4,
-        [pos, lead, seg_row, vec, *toks, *q_plane, *q_other],
-        [((DEPTH, PLANE, 2, rw, width), bf16), ((3 * PLANE, head, span), bf16)],
-    )
+        [((span, d), bf16, "far"), ((DEPTH, PLANE, 2, rw, width), bf16, "raw"), ((VEC_ROWS, d), f32), ((1, ff), f32)]
+        + [((3 * head, span), bf16)] * 4,
+        [pos, lead, seg_row, Far(toks), *q_plane, *q_other],
+        [((DEPTH, PLANE, 2, rw, side), bf16), ((3 * PLANE, head, span), bf16)],
+    )
+    (ff_shard,) = call(shard_kernel, [((2 * PLANE - 1, rw, d), bf16, "far")], [up_cols, down_weight])
+    ff_all = lax.all_gather(ff_shard, ("z", "g"), axis=0).reshape(DEPTH, 2, 2 * PLANE - 1, rw, d)
     blocks = across(blocks)
 
     *att_parts, lse = call(
@@ -912,7 +951,7 @@
     *parts, att, w_out = call(
         out_kernel,
         [((rows, d), f32)] + [((rows, d), bf16)] * 3 + [((DEPTH * head, span), bf16), ((DEPTH, 2, rw, d), bf16)],
-        [pos, *att_parts, Raw(ff_all)],
+        [pos, *att_parts, Raw(first)],
     )
     parts = across(parts)
     middle, n2 = call(norm_kernel, [((rows, d), f32, "far"), ((rows, d), bf16)], [lead, seg_row, vec, Far(tok), *parts])
@@ -921,37 +960,34 @@
     act, d_hid, p0, p1, p2, p3, d_up_b = call(
         ffn_kernel,
         [((span, ff), bf16), ((span, ff), bf16), ((rows, d), f32)] + [((rows, d), bf16)] * 3 + [((1, ff), f32)],
-        [pos, up_b, *n2_plane, Far(d_outs), Raw(ff_all)],
+        [pos, up_b, *n2_plane, Far(d_outs), Raw(first), Raw(ff_all)],
         [(up_shape, bf16), (down_shape, bf16), ((span, ff), f32)],
     )
     parts = across((p0, p1, p2, p3))
     ff_grad, outs = call(
         ffn_grad_kernel,
-        [((DEPTH, 2, 2 * PLANE, rw, d), bf16, "raw"), ((PLANE, rows, d), bf16, "far")],
-        [pos, act, d_hid, *n2_plane, Raw(ff_all), Far(d_outs)],
+        [((DEPTH, 2, 2 * PLANE + 1, rw, d), bf16, "raw"), ((PLANE, rows, d), bf16, "far")],
+        [pos, act, d_hid, *n2_plane, Raw(first), Raw(ff_all), Far(d_outs)],
         [(up_shape, bf16), (down_shape, bf16), (down_shape, bf16)],
-        after=[parts[1]],
-    )
-    ff_grad = lax.psum_scatter(
-        ff_grad.reshape(2 * DEPTH, 2 * PLANE, rw, d), ("z", "g"), scatter_dimension=0, tiled=True
-    )[0]
+    )
     d_mid, d_branch, d_mid_vec = call(
         branch_kernel,
         [((rows, d), f32, "far"), ((rows, d), bf16), ((8, d), f32)],
         [vec, Far(middle), Far(d_rows), *parts],
     )
     branch_plane = across((d_branch,) * PLANE)
-    *d_att, out_grad = call(
+    *d_att, ff_grad = call(
         out_back_kernel,
-        [((head, span), bf16)] * 4 + [((DEPTH, 2, rw, d), bf16, "far")],
-        [pos, att, w_out, *branch_plane],
-        [((DEPTH, head, span), bf16)],
+        [((head, span), bf16)] * 4 + [(ff_grad.shape, bf16, "raw")],
+        [pos, att, w_out, *branch_plane, Raw(ff_grad)],
+        [((DEPTH, head, span), bf16), ((DEPTH, 2, rw, d), bf16)],
+        alias=(7, 4),
     )
     d_att = along(d_att)
+    ff_grad = lax.psum_scatter(
+        ff_grad.reshape(2 * DEPTH, 2 * PLANE + 1, rw, d), ("z", "g"), scatter_dimension=0, tiled=True
+    )[0]
     outs = trade(outs, PLANE_AXES)
-    d_out_weight = lax.psum_scatter(
-        out_grad.reshape(2 * DEPTH, rw, d), ("z", "g"), scatter_dimension=0, tiled=True
-    )[0].astype(f32)
 
     d_blocks = call(
         functools.partial(attend_back_kernel, count),
@@ -962,35 +998,40 @@
     )
     d_blocks = across(d_blocks)
     (layer_out,) = call(layer_out_kernel, [((rows, d), bf16)], [vec, Far(middle), outs])
-    ups, d_down = call(ffn_last_kernel, [((PLANE, rw, ff), bf16), ((fr, d), f32)], [ff_grad])
-    ups = trade(ups, PLANE_AXES)
-    *returned, back = call(
+    returned, back = call(
         qkv_back_kernel,
-        [((rows, d), f32)] + [((rows, d), bf16)] * 3 + [((span, d), f32)],
+        [((DEPTH, rows, d), bf16), ((span, d), f32, "far")],
         [pos, Far(w_qkv), *d_blocks],
         [((3 * PLANE, head, span), bf16)],
-        after=[ups],
-    )
-    returned = along(returned)
-    side = width + -(-max(rw, fr) // 128) * 128
-    (octets,) = call(
+    )
+    returned = trade(returned, ("z",))
+    mine, o0, o1 = call(
         qkv_grad_kernel,
-        [((PLANE, 2, DEPTH, rw, side), bf16)],
-        [pos, lead, seg_row, vec, *far(toks), Far(n1), *d_blocks, back, Far(d_mid), d_mid_vec, d_up_b],
-        [((3 * PLANE, head, span), bf16), ((rw, d), f32)],
-    )
-    octets = trade(octets.reshape(2 * PLANE, DEPTH, rw, side), ("y", "x", "g")).reshape(octets.shape)
+        [((DEPTH, PLANE, rw, side), bf16, "raw")] + [((DEPTH // 2, PLANE, rw, side), bf16)] * 2,
+        [pos, lead, seg_row, vec, Far(toks), Far(n1), *d_blocks, Far(back), Far(d_mid), d_mid_vec, d_up_b],
+        [((3 * PLANE, head, span), bf16), ((rw, d), f32), ((DEPTH, PLANE, 2, rw, side), bf16)],
+    )
+    quads = call(
+        pair_kernel,
+        [((DEPTH, rw, side), bf16, "raw")] + [((DEPTH, rw, side), bf16)] * 3,
+        [pos, Far(mine), core_swap(o0), core_swap(o1)],
+        [((DEPTH, PLANE, rw, side), bf16)],
+    )
+    quads = across(quads)
+    ups, d_down, d_out_weight = call(
+        ffn_last_kernel, [((PLANE, rw, ff), bf16), ((fr, d), f32), ((rw, d), f32)], [ff_grad]
+    )
+    ups = trade(ups, PLANE_AXES)
+    cols = along(call(quad_kernel, [((rw, side), bf16)] * 4, [pos, Far(quads[0]), *quads[1:]], [((DEPTH, rw, side), bf16)]))
+    (d_tokens,) = call(
+        first_back_kernel, [((rows, d), f32)], [lead, seg_row, vec, Far(tok), Far(d_mid), returned]
+    )
+    d_qkv, table, d_g1, d_b1, d_qb, d_vb, d_ob, d_g2, d_b2, d_db, d_ub = call(
+        qkv_join_kernel,
+        [((rw, 3 * d), f32), ((LEADS, rw), f32)] + [((rw,), f32)] * 8 + [((fr,), f32)],
+        [pos, *cols],
+    )
     (d_up,) = call(up_join_kernel, [((rw, PLANE * ff), f32)], [ups])
-    (d_tokens,) = call(
-        first_back_kernel, [((rows, d), f32)], [lead, seg_row, vec, Far(tok), Far(d_mid), *returned]
-    )
-    cols = along(call(octet_kernel, [((rw, side), bf16)] * 4, [pos, octets], [((DEPTH, rw, side), bf16)]))
-    d_qkv, table, *smalls, d_ub = call(
-        qkv_join_kernel,
-        [((rw, 3 * d), f32), ((LEADS, rw), f32)] + [((1, rw), f32)] * 8 + [((1, fr), f32)],
-        [pos, *cols],
-    )
-    d_g1, d_b1, d_qb, d_vb, d_ob, d_g2, d_b2, d_db, d_ub = (small[0] for small in (*smalls, d_ub))
     return (
         layer_out[None], d_tokens[None], table, d_g1, d_b1, d_qkv, d_qb, d_vb, d_out_weight, d_ob,
         d_g2, d_b2, d_up, d_ub, d_down, d_db,

time: 311 us -> 268 us (0.86)
  waiting for transfers between devices: 110 us -> 78.8 us
  starting transfers between devices: 79.7 us -> 69.8 us
  local copies, waits for them, and re-layouts: 12.4 us -> 4.11 us
  Pallas kernels: 91.9 us -> 99.7 us
    ppermute x18 -> x12, waiting for transfers between devices: 54.5 us -> 17.9 us  [to_depth(): return lax.ppermute(block, 'z', [(i, i ^ step) for i in range(DEPTH)])]
    ppermute x18 -> x12, starting transfers between devices: 32.8 us -> 20.5 us  [to_depth(): return lax.ppermute(block, 'z', [(i, i ^ step) for i in range(DEPTH)])]
    pallas_call x21 -> x23, Pallas kernels: 91.9 us -> 99.7 us  [run(): pl.pallas_call(body, name=name, out_shape=[HBM(o[0], o[1]) if o[2] else j...]
    all_to_all x1 -> x0, starting transfers between devices: 7.3 us -> none  [fast_local(): lax.all_to_all(jnp.broadcast_to(flat[None], (devices,) + flat.shape), ALL...]
    ppermute x7 -> x8, waiting for transfers between devices: 11.3 us -> 17.8 us  [across(): lax.ppermute(blocks[3], ('y', 'x'), [(i, i ^ 3) for i in range(PLANE)])]
    concatenate x1 -> x0, local copies, waits for them, and re-layouts: 6.09 us -> none  [fast_local(): jnp.concatenate([lead_table.reshape(-1), ln1_gain, ln1_bias, q_bias, v_bi...]
    all_to_all x4 -> x5, starting transfers between devices: 13.9 us -> 19.6 us  [trade(): return lax.all_to_all(blocks, axes, split_axis=0, concat_axis=0, tiled=True)]
    all_to_all x4 -> x5, waiting for transfers between devices: 5.31 us -> 0.01 us  [trade(): return lax.all_to_all(blocks, axes, split_axis=0, concat_axis=0, tiled=True)]
  transfers between devices with their start and end apart: 52 -> 51, of which waited for: 30 -> 23; matrix products, arithmetic and copies ran while one was open for 1% -> 1% of each run, Pallas kernels for 20% -> 32%
where the time goes in v3:
time: 268 us; the launch traced here: 267 us
  Pallas kernels  99.7 us (37%)
  waiting for transfers between devices  78.8 us (29%)
  starting transfers between devices  69.8 us (26%)
  between operations  14.2 us (5%)
  local copies, waits for them, and re-layouts  4.11 us (2%)
    pallas_call x23, Pallas kernels, run(): pl.pallas_call(body, name=name, out_shape=[HBM(o[0], o[1]) if o[2] else j...  99.7 us
    ppermute x8, waiting for transfers between devices, across(): lax.ppermute(blocks[2], 'y', swap)  27 us
    ppermute x12, starting transfers between devices, to_depth(): return lax.ppermute(block, 'z', [(i, i ^ step) for i in range(DEPTH)])  20.5 us
    all_to_all x5, starting transfers between devices, trade(): return lax.all_to_all(blocks, axes, split_axis=0, concat_axis=0, tiled=True)  19.6 us
    ppermute x12, waiting for transfers between devices, to_depth(): return lax.ppermute(block, 'z', [(i, i ^ step) for i in range(DEPTH)])  17.9 us
    ppermute x8, waiting for transfers between devices, across(): lax.ppermute(blocks[3], ('y', 'x'), [(i, i ^ 3) for i in range(PLANE)])  17.8 us
    ppermute x8, waiting for transfers between devices, across(): lax.ppermute(blocks[1], 'x', swap)  13.3 us
    ppermute x8, starting transfers between devices, across(): lax.ppermute(blocks[3], ('y', 'x'), [(i, i ^ 3) for i in range(PLANE)])  11.7 us
  transfers between devices with their start and end apart: 51, of which 23 were waited for; matrix products, arithmetic and copies ran while one was open for 1% of the time, Pallas kernels for 32%

profile of v3, /device:TPU:0, one launch (start us, length us, event | category | flops | bytes accessed | tf_op | source)
XLA Modules:
  0.0 266.7 jit_solution(17236435593899304654)
XLA Ops:
  7.9 2.0 broadcast_in_dim.14
  9.9 5.2 %all-to-all-start = ((bf16[4,128,1024]{2,1,0:T(8,128)(2,1)}), bf16[4,128,1024]{2,1,0:T(8,128)(2,1)S(1)}, u32[]{:S(2)}, u32[]{:S(2)}) async-start(bf16[4,128,1024]{2,1,0:T(8,128)(2,1)} %broadcast_in_dim.14), calls=%async_computation | async-start | bytes 2097152 | tf_op jit(solution)/shard_map/all_to_all | solution.py:854
  15.2 2.1 q_prep_kernel.1
  17.3 1.6 collective-permute-start
  18.9 2.6 collective-permute-start.1
  21.7 7.8 %collective-permute-done.1.refs_3_ = bf16[32,896]{1,0:T(8,128)(2,1)S(1)} collective-permute-done((bf16[32,896]{1,0:T(8,128)(2,1)S(1)}, bf16[32,896]{1,0:T(8,128)(2,1)S(1)}, u32[]{:S(2)}, u32[]{:S(2)}) %collective-permute-start.1) | collective-permute-done | bytes 57376 | tf_op jit(solution)/shard_map/ppermute | solution.py:871
  30.5 1.4 q_stack_kernel.1
  33.2 2.7 %collective-permute-start.5 = (bf16[4,32,896]{2,1,0:T(8,128)(2,1)S(1)}, bf16[4,32,896]{2,1,0:T(8,128)(2,1)S(1)}, u32[]{:S(2)}, u32[]{:S(2)}) collective-permute-start(bf16[4,32,896]{2,1,0:T(8,128)(2,1)S(1)} %get-tuple-element.123.refs_4_), channel_id=1, source_target_pairs={{0,6},{2,4},{4,2},{6,0},{1,7},{3,5},{5,3},{7,1},{8,14},{10,12},{12... | collective-permute-start | bytes 688136 | tf_op jit(solution)/shard_map/ppermute | solution.py:866
  36.8 5.8 %collective-permute-done.5.refs_7_ = bf16[4,32,896]{2,1,0:T(8,128)(2,1)S(1)} collective-permute-done((bf16[4,32,896]{2,1,0:T(8,128)(2,1)S(1)}, bf16[4,32,896]{2,1,0:T(8,128)(2,1)S(1)}, u32[]{:S(2)}, u32[]{:S(2)}) %collective-permute-start.5) | collective-permute-done | bytes 229408 | tf_op jit(solution)/shard_map/ppermute | solution.py:866
  42.6 2.3 collective-permute-done.4.refs_6_
  46.8 3.4 %all-to-all-start.1 = ((bf16[4,32,1024]{2,1,0:T(8,128)(2,1)}), bf16[4,32,1024]{2,1,0:T(8,128)(2,1)S(1)}, u32[]{:S(2)}, u32[]{:S(2)}) async-start(bf16[4,32,1024]{2,1,0:T(8,128)(2,1)} %get-tuple-element.132), calls=%async_computation.1 | async-start | bytes 524288 | tf_op jit(solution)/shard_map/all_to_all | solution.py:854
  50.4 6.1 %qkv_kernel.1 = (bf16[512,1024]{1,0:T(8,128)(2,1)}, bf16[4,4,2,32,768]{4,3,2,1,0:T(8,128)(2,1)}, f32[24,1024]{1,0:T(8,128)S(1)}, f32[1,1024]{1,0:T(1,128)S(1)}, ...) custom-call(s32[3]{0:T(128)S(1)} %pad_add_fusion.refs_0_, ...), custom_call_target="tpu_custom_call" | custom-call | flops 5500000256 | bytes 18000000 | tf_op jit(solution)/shard_map/qkv_kernel/pallas_call | solution.py:400
  56.5 1.4 shard_kernel.1
  57.9 2.0 collective-permute-start.10
  59.9 1.5 collective-permute-start.11
  61.5 4.3 %collective-permute-done.10.refs_2_ = bf16[192,512]{1,0:T(8,128)(2,1)S(1)} collective-permute-done((bf16[192,512]{1,0:T(8,128)(2,1)S(1)}, bf16[192,512]{1,0:T(8,128)(2,1)S(1)}, u32[]{:S(2)}, u32[]{:S(2)}) %collective-permute-start.10) | collective-permute-done | bytes 196640 | tf_op jit(solution)/shard_map/ppermute | solution.py:864
  65.8 4.6 %collective-permute-done.11.refs_3_ = bf16[192,512]{1,0:T(8,128)(2,1)S(1)} collective-permute-done((bf16[192,512]{1,0:T(8,128)(2,1)S(1)}, bf16[192,512]{1,0:T(8,128)(2,1)S(1)}, u32[]{:S(2)}, u32[]{:S(2)}) %collective-permute-start.11) | collective-permute-done | bytes 196640 | tf_op jit(solution)/shard_map/ppermute | solution.py:865
  70.4 11.2 %attend_kernel.1 = (bf16[64,512]{1,0:T(8,128)(2,1)S(1)}, bf16[64,512]{1,0:T(8,128)(2,1)S(1)}, bf16[64,512]{1,0:T(8,128)(2,1)S(1)}, bf16[64,512]{1,0:T(8,128)(2,1...) custom-call(s32[1,128]{1,0:T(1,128)S(1)} %copy-done.5, bf16[192,512]{1,0:T(8,128)(2,1)S(1)} %get-tuple-element.128.refs_1_, ...), custom_call_target="tpu_custom_call" | custom-call | flops 12099999744 | bytes 39600000 | tf_op jit(solution)/shard_map/attend_kernel/pallas_call | solution.py:400
  81.6 2.4 collective-permute-start.13
  84.0 3.3 %collective-permute-start.14 = (bf16[64,512]{1,0:T(8,128)(2,1)S(1)}, bf16[64,512]{1,0:T(8,128)(2,1)S(1)}, u32[]{:S(2)}, u32[]{:S(2)}) collective-permute-start(bf16[64,512]{1,0:T(8,128)(2,1)S(1)} %get-tuple-element.137), channel_id=1, source_target_pairs={{0,16},{8,24},{16,0},{24,8},{1,17},{9,25},{17,1},{25,9},{2,18},{10... | collective-permute-start | bytes 196616 | tf_op jit(solution)/shard_map/ppermute | solution.py:871
  87.3 1.4 collective-permute-start.15
  88.7 2.3 collective-permute-done.13.refs_2_
  91.0 3.8 %collective-permute-done.14.refs_3_ = bf16[64,512]{1,0:T(8,128)(2,1)S(1)} collective-permute-done((bf16[64,512]{1,0:T(8,128)(2,1)S(1)}, bf16[64,512]{1,0:T(8,128)(2,1)S(1)}, u32[]{:S(2)}, u32[]{:S(2)}) %collective-permute-start.14) | collective-permute-done | bytes 65568 | tf_op jit(solution)/shard_map/ppermute | solution.py:871
  94.8 3.1 %collective-permute-done.15.refs_4_ = bf16[64,512]{1,0:T(8,128)(2,1)S(1)} collective-permute-done((bf16[64,512]{1,0:T(8,128)(2,1)S(1)}, bf16[64,512]{1,0:T(8,128)(2,1)S(1)}, u32[]{:S(2)}, u32[]{:S(2)}) %collective-permute-start.15) | collective-permute-done | bytes 65568 | tf_op jit(solution)/shard_map/ppermute | solution.py:871
  97.9 2.6 out_kernel.1
  102.6 1.5 collective-permute-start.18
  104.1 5.2 %collective-permute-done.16.refs_5_ = bf16[128,1024]{1,0:T(8,128)(2,1)S(1)} collective-permute-done((bf16[128,1024]{1,0:T(8,128)(2,1)S(1)}, bf16[128,1024]{1,0:T(8,128)(2,1)S(1)}, u32[]{:S(2)}, u32[]{:S(2)}) %collective-permute-start.16) | collective-permute-done | bytes 262176 | tf_op jit(solution)/shard_map/ppermute | solution.py:864
  109.2 4.2 %collective-permute-done.17.refs_6_ = bf16[128,1024]{1,0:T(8,128)(2,1)S(1)} collective-permute-done((bf16[128,1024]{1,0:T(8,128)(2,1)S(1)}, bf16[128,1024]{1,0:T(8,128)(2,1)S(1)}, u32[]{:S(2)}, u32[]{:S(2)}) %collective-permute-start.17) | collective-permute-done | bytes 262176 | tf_op jit(solution)/shard_map/ppermute | solution.py:865
  113.5 3.0 %norm_kernel.1 = (f32[128,1024]{1,0:T(8,128)}, bf16[128,1024]{1,0:T(8,128)(2,1)S(1)}, f32[8,128]{1,0:T(8,128)S(1)}) custom-call(s32[4]{0:T(128)S(1)} %bitcast.14, s32[1,128]{1,0:T(1,128)S(1)} %copy-done.5, f32[24,1024]{1,0:T(8,128)S(1)} %get-tuple-element.127.refs_2_.refs_0_.refs_3_, bf16[128,1024]{1,0:T(8,128)(2,1)} %bitcast.20, ...), custom_call_target="tpu_custom_call" | custom-call | flops 2200000000 | bytes 7200000 | tf_op jit(solution)/shard_map/norm_kernel/pallas_call | solution.py:400
  116.5 1.4 collective-permute-start.21
  118.3 1.7 collective-permute-start.19
  120.0 6.7 %collective-permute-done.21.refs_5_.refs_6_ = bf16[128,1024]{1,0:T(8,128)(2,1)S(1)} collective-permute-done((bf16[128,1024]{1,0:T(8,128)(2,1)S(1)}, bf16[128,1024]{1,0:T(8,128)(2,1)S(1)}, u32[]{:S(2)}, u32[]{:S(2)}) %collective-permute-start.21) | collective-permute-done | bytes 262176 | tf_op jit(solution)/shard_map/ppermute | solution.py:866
  126.7 2.5 collective-permute-done.20.refs_4_.refs_5_
  129.1 8.5 %ffn_kernel.1 = (bf16[512,1024]{1,0:T(8,128)(2,1)S(1)}, bf16[512,1024]{1,0:T(8,128)(2,1)S(1)}, f32[128,1024]{1,0:T(8,128)S(1)}, bf16[128,1024]{1,0:T(8,128)(2,1)...) custom-call(s32[3]{0:T(128)S(1)} %pad_add_fusion.refs_0_, ...), custom_call_target="tpu_custom_call" | custom-call | flops 8800000000 | bytes 28800000 | tf_op jit(solution)/shard_map/ffn_kernel/pallas_call | solution.py:400
  137.9 1.5 collective-permute-start.23
  139.4 1.8 collective-permute-start.24
  141.2 7.8 %ffn_grad_kernel.1 = (bf16[4,2,9,32,1024]{4,3,2,1,0:T(8,128)(2,1)}, bf16[4,128,1024]{2,1,0:T(8,128)(2,1)}, f32[8,128]{1,0:T(8,128)S(1)}) custom-call(s32[3]{0:T(128)S(1)} %pad_add_fusion.refs_0_, bf16[512,1024]{1,0:T(8,128)(2,1)S(1)} %get-tuple-element.151.refs_1_, bf16[512,1024]{1,0:T(8,128)(2,1)S(1)} %get-tuple-element.152.refs_2_, ...), custom_call_target="tpu_custom_call" | custom-call | flops 8800000000 | bytes 28800000 | tf_op jit(solution)/shard_map/ffn_grad_kernel/pallas_call | solution.py:400
  149.0 1.8 collective-permute-done.23.refs_5_
  150.8 3.0 %branch_kernel.1 = (f32[128,1024]{1,0:T(8,128)}, bf16[128,1024]{1,0:T(8,128)(2,1)S(1)}, f32[8,1024]{1,0:T(8,128)S(1)}, f32[8,128]{1,0:T(8,128)S(1)}) custom-call(f32[24,1024]{1,0:T(8,128)S(1)} %get-tuple-element.127.refs_2_.refs_0_.refs_3_, f32[128,1024]{1,0:T(8,128)} %get-tuple-element.146.refs_1_, bf16[128,1024]{1,0:T(8,128)(2,1)} %bitcast.19, ...), custom_call_target="tpu_custom_call" | custom-call | flops 2200000000 | bytes 7200000 | tf_op jit(solution)/shard_map/branch_kernel/pallas_call | solution.py:400
  153.8 1.9 collective-permute-start.27
  157.4 5.3 %collective-permute-done.27.refs_6_ = bf16[128,1024]{1,0:T(8,128)(2,1)S(1)} collective-permute-done((bf16[128,1024]{1,0:T(8,128)(2,1)S(1)}, bf16[128,1024]{1,0:T(8,128)(2,1)S(1)}, u32[]{:S(2)}, u32[]{:S(2)}) %collective-permute-start.27) | collective-permute-done | bytes 262176 | tf_op jit(solution)/shard_map/ppermute | solution.py:866
  162.7 3.0 %collective-permute-done.26.refs_5_ = bf16[128,1024]{1,0:T(8,128)(2,1)S(1)} collective-permute-done((bf16[128,1024]{1,0:T(8,128)(2,1)S(1)}, bf16[128,1024]{1,0:T(8,128)(2,1)S(1)}, u32[]{:S(2)}, u32[]{:S(2)}) %collective-permute-start.26) | collective-permute-done | bytes 262176 | tf_op jit(solution)/shard_map/ppermute | solution.py:865
  166.8 2.7 %out_back_kernel.1 = (bf16[64,512]{1,0:T(8,128)(2,1)S(1)}, bf16[64,512]{1,0:T(8,128)(2,1)S(1)}, bf16[64,512]{1,0:T(8,128)(2,1)S(1)}, bf16[64,512]{1,0:T(8,128)(2...) custom-call(s32[3]{0:T(128)S(1)} %pad_add_fusion.refs_0_, ...), custom_call_target="tpu_custom_call", output_to_operand_aliasing={{4}: (7, {})} | custom-call | flops 3300000000 | bytes 10800000 | tf_op jit(solution)/shard_map/out_back_kernel/pallas_call | solution.py:400
  169.5 2.7 %collective-permute-start.29 = (bf16[64,512]{1,0:T(8,128)(2,1)S(1)}, bf16[64,512]{1,0:T(8,128)(2,1)S(1)}, u32[]{:S(2)}, u32[]{:S(2)}) collective-permute-start(bf16[64,512]{1,0:T(8,128)(2,1)S(1)} %get-tuple-element.167), channel_id=1, source_target_pairs={{0,16},{8,24},{16,0},{24,8},{1,17},{9,25},{17,1},{25,9},{2,18},{10... | collective-permute-start | bytes 196616 | tf_op jit(solution)/shard_map/ppermute | solution.py:871
  172.3 1.7 collective-permute-start.30
  173.9 3.5 %all-to-all-start.2 = ((bf16[4,128,1024]{2,1,0:T(8,128)(2,1)}), bf16[4,128,1024]{2,1,0:T(8,128)(2,1)S(1)}, u32[]{:S(2)}, u32[]{:S(2)}) async-start(bf16[4,128,1024]{2,1,0:T(8,128)(2,1)} %get-tuple-element.154), calls=%async_computation.2 | async-start | bytes 2097152 | tf_op jit(solution)/shard_map/all_to_all | solution.py:854
  178.5 17.7 %attend_back_kernel.1 = (bf16[192,512]{1,0:T(8,128)(2,1)S(1)}, bf16[192,512]{1,0:T(8,128)(2,1)S(1)}, bf16[192,512]{1,0:T(8,128)(2,1)S(1)}, bf16[192,512]{1,0:T(8,128)(2,1)S(1)}, f32[8,128]{1,0:T(8,128)S(1)}) custom-call(s32[1,128]{1,0:T(1,128)S(1)} %copy-done.5, bf16[192,512]{1,0:T(8,128)(2,1)S(1)} %get-tuple-element.128.refs_1_, ...), custom_call_target="tpu_custom_call" | custom-call | flops 20899999744 | bytes 68400000 | tf_op jit(solution)/shard_map/attend_back_kernel/pallas_call | solution.py:400
  196.2 1.6 collective-permute-start.31
  199.7 2.5 layer_out_kernel.1
  202.7 3.7 %collective-permute-done.32.refs_4_.refs_8_ = bf16[192,512]{1,0:T(8,128)(2,1)S(1)} collective-permute-done((bf16[192,512]{1,0:T(8,128)(2,1)S(1)}, bf16[192,512]{1,0:T(8,128)(2,1)S(1)}, u32[]{:S(2)}, u32[]{:S(2)}) %collective-permute-start.32) | collective-permute-done | bytes 196640 | tf_op jit(solution)/shard_map/ppermute | solution.py:865
  206.4 5.9 %qkv_back_kernel.1 = (bf16[4,128,1024]{2,1,0:T(8,128)(2,1)}, f32[512,1024]{1,0:T(8,128)}, f32[8,128]{1,0:T(8,128)S(1)}) custom-call(s32[3]{0:T(128)S(1)} %pad_add_fusion.refs_0_, bf16[4,4,2,32,768]{4,3,2,1,0:T(8,128)(2,1)} %get-tuple-element.174.refs_1_, bf16[192,512]{1,0:T(8,128)(2,1)S(1)} %get-tuple-element.175.refs_2_.refs_6_, ...), custom_call_target="tpu_custom_call" | custom-call | flops 3300000000 | bytes 10800000 | tf_op jit(solution)/shard_map/qkv_back_kernel/pallas_call | solution.py:400
  212.3 3.5 %all-to-all-start.3 = ((bf16[4,128,1024]{2,1,0:T(8,128)(2,1)}), bf16[4,128,1024]{2,1,0:T(8,128)(2,1)S(1)}, u32[]{:S(2)}, u32[]{:S(2)}) async-start(bf16[4,128,1024]{2,1,0:T(8,128)(2,1)} %get-tuple-element.180), calls=%async_computation.3 | async-start | bytes 2097152 | tf_op jit(solution)/shard_map/all_to_all | solution.py:854
  215.9 7.5 %qkv_grad_kernel.1 = (bf16[4,4,32,896]{3,2,1,0:T(8,128)(2,1)}, bf16[2,4,32,896]{3,2,1,0:T(8,128)(2,1)S(1)}, bf16[2,4,32,896]{3,2,1,0:T(8,128)(2,1)S(1)}, f32[8,128]{1,0:T(8,128)S(1)}) custom-call(s32[3]{0:T(128)S(1)} %pad_add_fusion.refs_0_, s32[4]{0:T(128)S(1)} %bitcast.15, s32[1,128]{1,0:T(1,128)S(1)} %copy-done.5, ...), custom_call_target="tpu_custom_call" | custom-call | flops 6600000000 | bytes 21600000 | tf_op jit(solution)/shard_map/qkv_grad_kernel/pallas_call | solution.py:400
  225.9 3.2 %pair_kernel.1 = (bf16[4,32,896]{2,1,0:T(8,128)(2,1)}, bf16[4,32,896]{2,1,0:T(8,128)(2,1)S(1)}, bf16[4,32,896]{2,1,0:T(8,128)(2,1)S(1)}, bf16[4,32,896]{2,1,0:T(8,128)(2,1)S(1)}, f32[8,128]{1,0:T(8,128)S(1)}) custom-call(s32[3]{0:T(128)S(1)} %pad_add_fusion.refs_0_, bf16[4,4,32,896]{3,2,1,0:T(8,128)(2,1)} %get-tuple-element.186.refs_1_, ...), custom_call_target="tpu_custom_call" | custom-call | flops 2200000000 | bytes 7200000 | tf_op jit(solution)/shard_map/pair_kernel/pallas_call | solution.py:400
  233.7 1.5 ffn_last_kernel.1
  235.3 2.3 collective-permute-done.36.refs_2_
  237.6 4.8 %collective-permute-done.37.refs_3_ = bf16[4,32,896]{2,1,0:T(8,128)(2,1)S(1)} collective-permute-done((bf16[4,32,896]{2,1,0:T(8,128)(2,1)S(1)}, bf16[4,32,896]{2,1,0:T(8,128)(2,1)S(1)}, u32[]{:S(2)}, u32[]{:S(2)}) %collective-permute-start.37) | collective-permute-done | bytes 229408 | tf_op jit(solution)/shard_map/ppermute | solution.py:865
  242.5 2.3 quad_kernel.1
  244.8 2.1 collective-permute-start.39
  246.8 2.4 collective-permute-start.40
  249.3 3.9 %all-to-all-start.4 = ((bf16[4,32,1024]{2,1,0:T(8,128)(2,1)}), bf16[4,32,1024]{2,1,0:T(8,128)(2,1)S(1)}, u32[]{:S(2)}, u32[]{:S(2)}) async-start(bf16[4,32,1024]{2,1,0:T(8,128)(2,1)} %get-tuple-element.214), calls=%async_computation.5 | async-start | bytes 524288 | tf_op jit(solution)/shard_map/all_to_all | solution.py:854
  253.2 3.5 %first_back_kernel.1 = (f32[128,1024]{1,0:T(8,128)}, f32[8,128]{1,0:T(8,128)S(1)}) custom-call(s32[4]{0:T(128)S(1)} %bitcast.16, s32[1,128]{1,0:T(1,128)S(1)} %copy-done.5, f32[24,1024]{1,0:T(8,128)S(1)} %get-tuple-element.127.refs_2_.refs_0_.refs_3_, bf16[128,1024]{1,0:T(8,128)(2,1)} %bitcast.21, f32[128,1024]{1,0:T(8,128)} %get-tuple-element.173.refs_11_.refs_4_, ...), custom_call_target="tpu_custom_call" | custom-call | flops 2200000000 | bytes 7200000 | tf_op jit(solution)/shard_map/first_back_kernel/pallas_call | solution.py:400
  256.8 1.9 qkv_join_kernel.1
  258.7 1.4 up_join_kernel.1
  (81 shorter events, 22.5 us)
Async XLA Ops:
  7.2 43.2 %all-gather.6.cloned.1.call-start = ((), (), s32[]{:S(2)}) async-start(), calls=%async_computation.6 | async-start | bytes 1310720 | tf_op jit(solution)/shard_map/all_gather | solution.py:924
  9.9 19.6 %all-to-all-start = ((bf16[4,128,1024]{2,1,0:T(8,128)(2,1)}), bf16[4,128,1024]{2,1,0:T(8,128)(2,1)S(1)}, u32[]{:S(2)}, u32[]{:S(2)}) async-start(bf16[4,128,1024]{2,1,0:T(8,128)(2,1)} %broadcast_in_dim.14), calls=%async_computation | async-start | bytes 2097152 | tf_op jit(solution)/shard_map/all_to_all | solution.py:854
  15.1 82.8 %all-gather.8.cloned.1.call-start = ((), (), s32[]{:S(2)}) async-start(), calls=%async_computation.8 | async-start | bytes 1179648 | tf_op jit(solution)/shard_map/all_gather | solution.py:930
  15.2 16.8 %copy-start.2 = (bf16[128,1024]{1,0:T(8,128)(2,1)S(1)}, bf16[128,1024]{1,0:T(8,128)(2,1)}, u32[]{:S(2)}) copy-start(bf16[128,1024]{1,0:T(8,128)(2,1)} %refs_1_.7) | copy-start | bytes 786436
  15.2 16.8 %copy-start.3 = (bf16[32,1024]{1,0:T(8,128)(2,1)S(1)}, bf16[32,1024]{1,0:T(8,128)(2,1)}, u32[]{:S(2)}) copy-start(bf16[32,1024]{1,0:T(8,128)(2,1)} %refs_0_.4) | copy-start | bytes 196612
  17.3 4.5 %collective-permute-start = (bf16[32,896]{1,0:T(8,128)(2,1)S(1)}, bf16[32,896]{1,0:T(8,128)(2,1)S(1)}, u32[]{:S(2)}, u32[]{:S(2)}) collective-permute-start(bf16[32,896]{1,0:T(8,128)(2,1)S(1)} %get-tuple-element.119), channel_id=1, source_target_pairs={{0,8},{8,0},{16,24},{24,16},{1,9},{9,1},{17,25},{25,17},{2,10},{10... | collective-permute-start | bytes 172040 | tf_op jit(solution)/shard_map/ppermute | solution.py:871
  18.9 10.6 %collective-permute-start.1 = (bf16[32,896]{1,0:T(8,128)(2,1)S(1)}, bf16[32,896]{1,0:T(8,128)(2,1)S(1)}, u32[]{:S(2)}, u32[]{:S(2)}) collective-permute-start(bf16[32,896]{1,0:T(8,128)(2,1)S(1)} %get-tuple-element.120), channel_id=1, source_target_pairs={{0,16},{8,24},{16,0},{24,8},{1,17},{9,25},{17,1},{25,9},{2,18},{10... | collective-permute-start | bytes 172040 | tf_op jit(solution)/shard_map/ppermute | solution.py:871
  21.5 8.0 %collective-permute-start.2 = (bf16[32,896]{1,0:T(8,128)(2,1)S(1)}, bf16[32,896]{1,0:T(8,128)(2,1)S(1)}, u32[]{:S(2)}, u32[]{:S(2)}) collective-permute-start(bf16[32,896]{1,0:T(8,128)(2,1)S(1)} %get-tuple-element.121), channel_id=1, source_target_pairs={{0,24},{8,16},{16,8},{24,0},{1,25},{9,17},{17,9},{25,1},{2,26},{10... | collective-permute-start | bytes 172040 | tf_op jit(solution)/shard_map/ppermute | solution.py:871
  29.5 1.0 copy-start.6
  30.5 15.0 %copy-start.1 = (bf16[32,4096]{1,0:T(8,128)(2,1)S(1)}, bf16[32,4096]{1,0:T(8,128)(2,1)}, u32[]{:S(2)}) copy-start(bf16[32,4096]{1,0:T(8,128)(2,1)} %refs_0_.5) | copy-start | bytes 786436
  32.0 18.4 %copy-start.4 = (s32[1,4]{1,0:T(1,128)S(1)}, s32[1,4]{1,0:T(1,128)}, u32[]{:S(2)}) copy-start(s32[1,4]{1,0:T(1,128)} %param.20) | copy-start | bytes 52
  32.0 18.4 %copy-start.5 = (s32[1,128]{1,0:T(1,128)S(1)}, s32[1,128]{1,0:T(1,128)}, u32[]{:S(2)}) copy-start(s32[1,128]{1,0:T(1,128)} %refs_1_.9) | copy-start | bytes 1540
  33.2 9.4 %collective-permute-start.5 = (bf16[4,32,896]{2,1,0:T(8,128)(2,1)S(1)}, bf16[4,32,896]{2,1,0:T(8,128)(2,1)S(1)}, u32[]{:S(2)}, u32[]{:S(2)}) collective-permute-start(bf16[4,32,896]{2,1,0:T(8,128)(2,1)S(1)} %get-tuple-element.123.refs_4_), channel_id=1, source_target_pairs={{0,6},{2,4},{4,2},{6,0},{1,7},{3,5},{5,3},{7,1},{8,14},{10,12},{12... | collective-permute-start | bytes 688136 | tf_op jit(solution)/shard_map/ppermute | solution.py:866
  36.0 9.0 %collective-permute-start.4 = (bf16[4,32,896]{2,1,0:T(8,128)(2,1)S(1)}, bf16[4,32,896]{2,1,0:T(8,128)(2,1)S(1)}, u32[]{:S(2)}, u32[]{:S(2)}) collective-permute-start(bf16[4,32,896]{2,1,0:T(8,128)(2,1)S(1)} %get-tuple-element.123.refs_4_), channel_id=1, source_target_pairs={{0,4},{4,0},{1,5},{5,1},{2,6},{6,2},{3,7},{7,3},{8,12},{12,8},{9,1... | collective-permute-start | bytes 688136 | tf_op jit(solution)/shard_map/ppermute | solution.py:865
  36.5 8.5 %collective-permute-start.3 = (bf16[4,32,896]{2,1,0:T(8,128)(2,1)S(1)}, bf16[4,32,896]{2,1,0:T(8,128)(2,1)S(1)}, u32[]{:S(2)}, u32[]{:S(2)}) collective-permute-start(bf16[4,32,896]{2,1,0:T(8,128)(2,1)S(1)} %get-tuple-element.123.refs_4_), channel_id=1, source_target_pairs={{0,2},{2,0},{1,3},{3,1},{4,6},{6,4},{5,7},{7,5},{8,10},{10,8},{9,1... | collective-permute-start | bytes 688136 | tf_op jit(solution)/shard_map/ppermute | solution.py:864
  36.8 13.5 %collective-permute-start.6 = (bf16[4,32,896]{2,1,0:T(8,128)(2,1)S(1)}, bf16[4,32,896]{2,1,0:T(8,128)(2,1)S(1)}, u32[]{:S(2)}, u32[]{:S(2)}) collective-permute-start(bf16[4,32,896]{2,1,0:T(8,128)(2,1)S(1)} %get-tuple-element.123.refs_4_), channel_id=1, source_target_pairs={{0,1},{1,0},{2,3},{3,2},{4,5},{5,4},{6,7},{7,6},{8,9},{9,8},{10,11... | collective-permute-start | bytes 688136 | tf_op jit(solution)/shard_map/ppermute | solution.py:879
  42.6 7.7 %collective-permute-start.9 = (bf16[4,32,896]{2,1,0:T(8,128)(2,1)S(1)}, bf16[4,32,896]{2,1,0:T(8,128)(2,1)S(1)}, u32[]{:S(2)}, u32[]{:S(2)}) collective-permute-start(bf16[4,32,896]{2,1,0:T(8,128)(2,1)S(1)} %collective-permute-done.5.refs_7_), channel_id=1, source_target_pairs={{0,1},{1,0},{2,3},{3,2},{4,5},{5,4},{6,7},{7,6},{8,9},{9,8},{10,11... | collective-permute-start | bytes 688136 | tf_op jit(solution)/shard_map/ppermute | solution.py:879
  45.0 5.3 %collective-permute-start.8 = (bf16[4,32,896]{2,1,0:T(8,128)(2,1)S(1)}, bf16[4,32,896]{2,1,0:T(8,128)(2,1)S(1)}, u32[]{:S(2)}, u32[]{:S(2)}) collective-permute-start(bf16[4,32,896]{2,1,0:T(8,128)(2,1)S(1)} %collective-permute-done.4.refs_6_), channel_id=1, source_target_pairs={{0,1},{1,0},{2,3},{3,2},{4,5},{5,4},{6,7},{7,6},{8,9},{9,8},{10,11... | collective-permute-start | bytes 688136 | tf_op jit(solution)/shard_map/ppermute | solution.py:879
  45.0 5.4 %collective-permute-start.7 = (bf16[4,32,896]{2,1,0:T(8,128)(2,1)S(1)}, bf16[4,32,896]{2,1,0:T(8,128)(2,1)S(1)}, u32[]{:S(2)}, u32[]{:S(2)}) collective-permute-start(bf16[4,32,896]{2,1,0:T(8,128)(2,1)S(1)} %collective-permute-done.3.refs_5_), channel_id=1, source_target_pairs={{0,1},{1,0},{2,3},{3,2},{4,5},{5,4},{6,7},{7,6},{8,9},{9,8},{10,11... | collective-permute-start | bytes 688136 | tf_op jit(solution)/shard_map/ppermute | solution.py:879
  46.8 9.7 %all-to-all-start.1 = ((bf16[4,32,1024]{2,1,0:T(8,128)(2,1)}), bf16[4,32,1024]{2,1,0:T(8,128)(2,1)S(1)}, u32[]{:S(2)}, u32[]{:S(2)}) async-start(bf16[4,32,1024]{2,1,0:T(8,128)(2,1)} %get-tuple-element.132), calls=%async_computation.1 | async-start | bytes 524288 | tf_op jit(solution)/shard_map/all_to_all | solution.py:854
  50.2 78.9 %all-gather.10.cloned.1.call-start = ((), (), s32[]{:S(2)}) async-start(), calls=%async_computation.9 | async-start | bytes 4128768 | tf_op jit(solution)/shard_map/all_gather | solution.py:941
  57.9 174.8 %reduce-scatter.2.cloned.1.call-start = ((), (), s32[]{:S(2)}) async-start(), calls=%async_computation.7 | async-start | bytes 5308416 | tf_op jit(solution)/shard_map/reduce_scatter | solution.py:987
  57.9 7.8 %collective-permute-start.10 = (bf16[192,512]{1,0:T(8,128)(2,1)S(1)}, bf16[192,512]{1,0:T(8,128)(2,1)S(1)}, u32[]{:S(2)}, u32[]{:S(2)}) collective-permute-start(bf16[192,512]{1,0:T(8,128)(2,1)S(1)} %get-tuple-element.129), channel_id=1, source_target_pairs={{0,2},{2,0},{1,3},{3,1},{4,6},{6,4},{5,7},{7,5},{8,10},{10,8},{9,1... | collective-permute-start | bytes 589832 | tf_op jit(solution)/shard_map/ppermute | solution.py:864
  59.9 10.5 %collective-permute-start.11 = (bf16[192,512]{1,0:T(8,128)(2,1)S(1)}, bf16[192,512]{1,0:T(8,128)(2,1)S(1)}, u32[]{:S(2)}, u32[]{:S(2)}) collective-permute-start(bf16[192,512]{1,0:T(8,128)(2,1)S(1)} %get-tuple-element.130), channel_id=1, source_target_pairs={{0,4},{4,0},{1,5},{5,1},{2,6},{6,2},{3,7},{7,3},{8,12},{12,8},{9,1... | collective-permute-start | bytes 589832 | tf_op jit(solution)/shard_map/ppermute | solution.py:865
  61.4 9.0 %collective-permute-start.12 = (bf16[192,512]{1,0:T(8,128)(2,1)S(1)}, bf16[192,512]{1,0:T(8,128)(2,1)S(1)}, u32[]{:S(2)}, u32[]{:S(2)}) collective-permute-start(bf16[192,512]{1,0:T(8,128)(2,1)S(1)} %get-tuple-element.131), channel_id=1, source_target_pairs={{0,6},{2,4},{4,2},{6,0},{1,7},{3,5},{5,3},{7,1},{8,14},{10,12},{12... | collective-permute-start | bytes 589832 | tf_op jit(solution)/shard_map/ppermute | solution.py:866
  81.6 9.4 %collective-permute-start.13 = (bf16[64,512]{1,0:T(8,128)(2,1)S(1)}, bf16[64,512]{1,0:T(8,128)(2,1)S(1)}, u32[]{:S(2)}, u32[]{:S(2)}) collective-permute-start(bf16[64,512]{1,0:T(8,128)(2,1)S(1)} %get-tuple-element.136), channel_id=1, source_target_pairs={{0,8},{8,0},{16,24},{24,16},{1,9},{9,1},{17,25},{25,17},{2,10},{10... | collective-permute-start | bytes 196616 | tf_op jit(solution)/shard_map/ppermute | solution.py:871
  84.0 10.8 %collective-permute-start.14 = (bf16[64,512]{1,0:T(8,128)(2,1)S(1)}, bf16[64,512]{1,0:T(8,128)(2,1)S(1)}, u32[]{:S(2)}, u32[]{:S(2)}) collective-permute-start(bf16[64,512]{1,0:T(8,128)(2,1)S(1)} %get-tuple-element.137), channel_id=1, source_target_pairs={{0,16},{8,24},{16,0},{24,8},{1,17},{9,25},{17,1},{25,9},{2,18},{10... | collective-permute-start | bytes 196616 | tf_op jit(solution)/shard_map/ppermute | solution.py:871
  87.3 10.6 %collective-permute-start.15 = (bf16[64,512]{1,0:T(8,128)(2,1)S(1)}, bf16[64,512]{1,0:T(8,128)(2,1)S(1)}, u32[]{:S(2)}, u32[]{:S(2)}) collective-permute-start(bf16[64,512]{1,0:T(8,128)(2,1)S(1)} %get-tuple-element.138), channel_id=1, source_target_pairs={{0,24},{8,16},{16,8},{24,0},{1,25},{9,17},{17,9},{25,1},{2,26},{10... | collective-permute-start | bytes 196616 | tf_op jit(solution)/shard_map/ppermute | solution.py:871
  100.5 8.7 %collective-permute-start.16 = (bf16[128,1024]{1,0:T(8,128)(2,1)S(1)}, bf16[128,1024]{1,0:T(8,128)(2,1)S(1)}, u32[]{:S(2)}, u32[]{:S(2)}) collective-permute-start(bf16[128,1024]{1,0:T(8,128)(2,1)S(1)} %get-tuple-element.142), channel_id=1, source_target_pairs={{0,2},{2,0},{1,3},{3,1},{4,6},{6,4},{5,7},{7,5},{8,10},{10,8},{9,1... | collective-permute-start | bytes 786440 | tf_op jit(solution)/shard_map/ppermute | solution.py:864
  101.8 11.6 %collective-permute-start.17 = (bf16[128,1024]{1,0:T(8,128)(2,1)S(1)}, bf16[128,1024]{1,0:T(8,128)(2,1)S(1)}, u32[]{:S(2)}, u32[]{:S(2)}) collective-permute-start(bf16[128,1024]{1,0:T(8,128)(2,1)S(1)} %get-tuple-element.143), channel_id=1, source_target_pairs={{0,4},{4,0},{1,5},{5,1},{2,6},{6,2},{3,7},{7,3},{8,12},{12,8},{9,1... | collective-permute-start | bytes 786440 | tf_op jit(solution)/shard_map/ppermute | solution.py:865
  102.6 10.9 %collective-permute-start.18 = (bf16[128,1024]{1,0:T(8,128)(2,1)S(1)}, bf16[128,1024]{1,0:T(8,128)(2,1)S(1)}, u32[]{:S(2)}, u32[]{:S(2)}) collective-permute-start(bf16[128,1024]{1,0:T(8,128)(2,1)S(1)} %get-tuple-element.144), channel_id=1, source_target_pairs={{0,6},{2,4},{4,2},{6,0},{1,7},{3,5},{5,3},{7,1},{8,14},{10,12},{12... | collective-permute-start | bytes 786440 | tf_op jit(solution)/shard_map/ppermute | solution.py:866
  116.5 10.2 %collective-permute-start.21 = (bf16[128,1024]{1,0:T(8,128)(2,1)S(1)}, bf16[128,1024]{1,0:T(8,128)(2,1)S(1)}, u32[]{:S(2)}, u32[]{:S(2)}) collective-permute-start(bf16[128,1024]{1,0:T(8,128)(2,1)S(1)} %get-tuple-element.148.refs_2_.refs_3_), channel_id=1, source_target_pairs={{0,6},{2,4},{4,2},{6,0},{1,7},{3,5},{5,3},{7,1},{8,14},{10,12},{12... | collective-permute-start | bytes 786440 | tf_op jit(solution)/shard_map/ppermute | solution.py:866
  117.9 11.3 %collective-permute-start.20 = (bf16[128,1024]{1,0:T(8,128)(2,1)S(1)}, bf16[128,1024]{1,0:T(8,128)(2,1)S(1)}, u32[]{:S(2)}, u32[]{:S(2)}) collective-permute-start(bf16[128,1024]{1,0:T(8,128)(2,1)S(1)} %get-tuple-element.148.refs_2_.refs_3_), channel_id=1, source_target_pairs={{0,4},{4,0},{1,5},{5,1},{2,6},{6,2},{3,7},{7,3},{8,12},{12,8},{9,1... | collective-permute-start | bytes 786440 | tf_op jit(solution)/shard_map/ppermute | solution.py:865
  118.3 10.8 %collective-permute-start.19 = (bf16[128,1024]{1,0:T(8,128)(2,1)S(1)}, bf16[128,1024]{1,0:T(8,128)(2,1)S(1)}, u32[]{:S(2)}, u32[]{:S(2)}) collective-permute-start(bf16[128,1024]{1,0:T(8,128)(2,1)S(1)} %get-tuple-element.148.refs_2_.refs_3_), channel_id=1, source_target_pairs={{0,2},{2,0},{1,3},{3,1},{4,6},{6,4},{5,7},{7,5},{8,10},{10,8},{9,1... | collective-permute-start | bytes 786440 | tf_op jit(solution)/shard_map/ppermute | solution.py:864
  137.7 11.3 %collective-permute-start.22 = (bf16[128,1024]{1,0:T(8,128)(2,1)S(1)}, bf16[128,1024]{1,0:T(8,128)(2,1)S(1)}, u32[]{:S(2)}, u32[]{:S(2)}) collective-permute-start(bf16[128,1024]{1,0:T(8,128)(2,1)S(1)} %get-tuple-element.158), channel_id=1, source_target_pairs={{0,2},{2,0},{1,3},{3,1},{4,6},{6,4},{5,7},{7,5},{8,10},{10,8},{9,1... | collective-permute-start | bytes 786440 | tf_op jit(solution)/shard_map/ppermute | solution.py:864
  137.9 12.8 %collective-permute-start.23 = (bf16[128,1024]{1,0:T(8,128)(2,1)S(1)}, bf16[128,1024]{1,0:T(8,128)(2,1)S(1)}, u32[]{:S(2)}, u32[]{:S(2)}) collective-permute-start(bf16[128,1024]{1,0:T(8,128)(2,1)S(1)} %get-tuple-element.159), channel_id=1, source_target_pairs={{0,4},{4,0},{1,5},{5,1},{2,6},{6,2},{3,7},{7,3},{8,12},{12,8},{9,1... | collective-permute-start | bytes 786440 | tf_op jit(solution)/shard_map/ppermute | solution.py:865
  139.4 11.4 %collective-permute-start.24 = (bf16[128,1024]{1,0:T(8,128)(2,1)S(1)}, bf16[128,1024]{1,0:T(8,128)(2,1)S(1)}, u32[]{:S(2)}, u32[]{:S(2)}) collective-permute-start(bf16[128,1024]{1,0:T(8,128)(2,1)S(1)} %get-tuple-element.160), channel_id=1, source_target_pairs={{0,6},{2,4},{4,2},{6,0},{1,7},{3,5},{5,3},{7,1},{8,14},{10,12},{12... | collective-permute-start | bytes 786440 | tf_op jit(solution)/shard_map/ppermute | solution.py:866
  153.8 8.9 %collective-permute-start.27 = (bf16[128,1024]{1,0:T(8,128)(2,1)S(1)}, bf16[128,1024]{1,0:T(8,128)(2,1)S(1)}, u32[]{:S(2)}, u32[]{:S(2)}) collective-permute-start(bf16[128,1024]{1,0:T(8,128)(2,1)S(1)} %get-tuple-element.162.refs_3_), channel_id=1, source_target_pairs={{0,6},{2,4},{4,2},{6,0},{1,7},{3,5},{5,3},{7,1},{8,14},{10,12},{12... | collective-permute-start | bytes 786440 | tf_op jit(solution)/shard_map/ppermute | solution.py:866
  155.7 10.0 %collective-permute-start.26 = (bf16[128,1024]{1,0:T(8,128)(2,1)S(1)}, bf16[128,1024]{1,0:T(8,128)(2,1)S(1)}, u32[]{:S(2)}, u32[]{:S(2)}) collective-permute-start(bf16[128,1024]{1,0:T(8,128)(2,1)S(1)} %get-tuple-element.162.refs_3_), channel_id=1, source_target_pairs={{0,4},{4,0},{1,5},{5,1},{2,6},{6,2},{3,7},{7,3},{8,12},{12,8},{9,1... | collective-permute-start | bytes 786440 | tf_op jit(solution)/shard_map/ppermute | solution.py:865
  157.0 9.8 %collective-permute-start.25 = (bf16[128,1024]{1,0:T(8,128)(2,1)S(1)}, bf16[128,1024]{1,0:T(8,128)(2,1)S(1)}, u32[]{:S(2)}, u32[]{:S(2)}) collective-permute-start(bf16[128,1024]{1,0:T(8,128)(2,1)S(1)} %get-tuple-element.162.refs_3_), channel_id=1, source_target_pairs={{0,2},{2,0},{1,3},{3,1},{4,6},{6,4},{5,7},{7,5},{8,10},{10,8},{9,1... | collective-permute-start | bytes 786440 | tf_op jit(solution)/shard_map/ppermute | solution.py:864
  169.5 8.0 %collective-permute-start.28 = (bf16[64,512]{1,0:T(8,128)(2,1)S(1)}, bf16[64,512]{1,0:T(8,128)(2,1)S(1)}, u32[]{:S(2)}, u32[]{:S(2)}) collective-permute-start(bf16[64,512]{1,0:T(8,128)(2,1)S(1)} %get-tuple-element.166), channel_id=1, source_target_pairs={{0,8},{8,0},{16,24},{24,16},{1,9},{9,1},{17,25},{25,17},{2,10},{10... | collective-permute-start | bytes 196616 | tf_op jit(solution)/shard_map/ppermute | solution.py:871
  169.5 7.9 %collective-permute-start.29 = (bf16[64,512]{1,0:T(8,128)(2,1)S(1)}, bf16[64,512]{1,0:T(8,128)(2,1)S(1)}, u32[]{:S(2)}, u32[]{:S(2)}) collective-permute-start(bf16[64,512]{1,0:T(8,128)(2,1)S(1)} %get-tuple-element.167), channel_id=1, source_target_pairs={{0,16},{8,24},{16,0},{24,8},{1,17},{9,25},{17,1},{25,9},{2,18},{10... | collective-permute-start | bytes 196616 | tf_op jit(solution)/shard_map/ppermute | solution.py:871
  172.3 6.2 %collective-permute-start.30 = (bf16[64,512]{1,0:T(8,128)(2,1)S(1)}, bf16[64,512]{1,0:T(8,128)(2,1)S(1)}, u32[]{:S(2)}, u32[]{:S(2)}) collective-permute-start(bf16[64,512]{1,0:T(8,128)(2,1)S(1)} %get-tuple-element.168), channel_id=1, source_target_pairs={{0,24},{8,16},{16,8},{24,0},{1,25},{9,17},{17,9},{25,1},{2,26},{10... | collective-permute-start | bytes 196616 | tf_op jit(solution)/shard_map/ppermute | solution.py:871
  173.9 25.8 %all-to-all-start.2 = ((bf16[4,128,1024]{2,1,0:T(8,128)(2,1)}), bf16[4,128,1024]{2,1,0:T(8,128)(2,1)S(1)}, u32[]{:S(2)}, u32[]{:S(2)}) async-start(bf16[4,128,1024]{2,1,0:T(8,128)(2,1)} %get-tuple-element.154), calls=%async_computation.2 | async-start | bytes 2097152 | tf_op jit(solution)/shard_map/all_to_all | solution.py:854
  196.2 6.5 %collective-permute-start.31 = (bf16[192,512]{1,0:T(8,128)(2,1)S(1)}, bf16[192,512]{1,0:T(8,128)(2,1)S(1)}, u32[]{:S(2)}, u32[]{:S(2)}) collective-permute-start(bf16[192,512]{1,0:T(8,128)(2,1)S(1)} %get-tuple-element.176), channel_id=1, source_target_pairs={{0,2},{2,0},{1,3},{3,1},{4,6},{6,4},{5,7},{7,5},{8,10},{10,8},{9,1... | collective-permute-start | bytes 589832 | tf_op jit(solution)/shard_map/ppermute | solution.py:864
  197.7 8.6 %collective-permute-start.32 = (bf16[192,512]{1,0:T(8,128)(2,1)S(1)}, bf16[192,512]{1,0:T(8,128)(2,1)S(1)}, u32[]{:S(2)}, u32[]{:S(2)}) collective-permute-start(bf16[192,512]{1,0:T(8,128)(2,1)S(1)} %get-tuple-element.177), channel_id=1, source_target_pairs={{0,4},{4,0},{1,5},{5,1},{2,6},{6,2},{3,7},{7,3},{8,12},{12,8},{9,1... | collective-permute-start | bytes 589832 | tf_op jit(solution)/shard_map/ppermute | solution.py:865
  198.7 7.7 %collective-permute-start.33 = (bf16[192,512]{1,0:T(8,128)(2,1)S(1)}, bf16[192,512]{1,0:T(8,128)(2,1)S(1)}, u32[]{:S(2)}, u32[]{:S(2)}) collective-permute-start(bf16[192,512]{1,0:T(8,128)(2,1)S(1)} %get-tuple-element.178), channel_id=1, source_target_pairs={{0,6},{2,4},{4,2},{6,0},{1,7},{3,5},{5,3},{7,1},{8,14},{10,12},{12... | collective-permute-start | bytes 589832 | tf_op jit(solution)/shard_map/ppermute | solution.py:866
  212.3 37.0 %all-to-all-start.3 = ((bf16[4,128,1024]{2,1,0:T(8,128)(2,1)}), bf16[4,128,1024]{2,1,0:T(8,128)(2,1)S(1)}, u32[]{:S(2)}, u32[]{:S(2)}) async-start(bf16[4,128,1024]{2,1,0:T(8,128)(2,1)} %get-tuple-element.180), calls=%async_computation.3 | async-start | bytes 2097152 | tf_op jit(solution)/shard_map/all_to_all | solution.py:854
  223.3 1.9 collective-permute-start.34
  223.4 2.5 collective-permute-start.35
  229.1 8.5 %collective-permute-start.36 = (bf16[4,32,896]{2,1,0:T(8,128)(2,1)S(1)}, bf16[4,32,896]{2,1,0:T(8,128)(2,1)S(1)}, u32[]{:S(2)}, u32[]{:S(2)}) collective-permute-start(bf16[4,32,896]{2,1,0:T(8,128)(2,1)S(1)} %get-tuple-element.191), channel_id=1, source_target_pairs={{0,2},{2,0},{1,3},{3,1},{4,6},{6,4},{5,7},{7,5},{8,10},{10,8},{9,1... | collective-permute-start | bytes 688136 | tf_op jit(solution)/shard_map/ppermute | solution.py:864
  230.2 12.3 %collective-permute-start.37 = (bf16[4,32,896]{2,1,0:T(8,128)(2,1)S(1)}, bf16[4,32,896]{2,1,0:T(8,128)(2,1)S(1)}, u32[]{:S(2)}, u32[]{:S(2)}) collective-permute-start(bf16[4,32,896]{2,1,0:T(8,128)(2,1)S(1)} %get-tuple-element.192), channel_id=1, source_target_pairs={{0,4},{4,0},{1,5},{5,1},{2,6},{6,2},{3,7},{7,3},{8,12},{12,8},{9,1... | collective-permute-start | bytes 688136 | tf_op jit(solution)/shard_map/ppermute | solution.py:865
  231.4 11.0 %collective-permute-start.38 = (bf16[4,32,896]{2,1,0:T(8,128)(2,1)S(1)}, bf16[4,32,896]{2,1,0:T(8,128)(2,1)S(1)}, u32[]{:S(2)}, u32[]{:S(2)}) collective-permute-start(bf16[4,32,896]{2,1,0:T(8,128)(2,1)S(1)} %get-tuple-element.193), channel_id=1, source_target_pairs={{0,6},{2,4},{4,2},{6,0},{1,7},{3,5},{5,3},{7,1},{8,14},{10,12},{12... | collective-permute-start | bytes 688136 | tf_op jit(solution)/shard_map/ppermute | solution.py:866
  232.7 1.1 copy-start
  244.8 12.0 %collective-permute-start.39 = (bf16[32,896]{1,0:T(8,128)(2,1)S(1)}, bf16[32,896]{1,0:T(8,128)(2,1)S(1)}, u32[]{:S(2)}, u32[]{:S(2)}) collective-permute-start(bf16[32,896]{1,0:T(8,128)(2,1)S(1)} %get-tuple-element.200), channel_id=1, source_target_pairs={{0,8},{8,0},{16,24},{24,16},{1,9},{9,1},{17,25},{25,17},{2,10},{10... | collective-permute-start | bytes 172040 | tf_op jit(solution)/shard_map/ppermute | solution.py:871
  246.8 9.9 %collective-permute-start.40 = (bf16[32,896]{1,0:T(8,128)(2,1)S(1)}, bf16[32,896]{1,0:T(8,128)(2,1)S(1)}, u32[]{:S(2)}, u32[]{:S(2)}) collective-permute-start(bf16[32,896]{1,0:T(8,128)(2,1)S(1)} %get-tuple-element.201), channel_id=1, source_target_pairs={{0,16},{8,24},{16,0},{24,8},{1,17},{9,25},{17,1},{25,9},{2,18},{10... | collective-permute-start | bytes 172040 | tf_op jit(solution)/shard_map/ppermute | solution.py:871
  249.2 7.5 %collective-permute-start.41 = (bf16[32,896]{1,0:T(8,128)(2,1)S(1)}, bf16[32,896]{1,0:T(8,128)(2,1)S(1)}, u32[]{:S(2)}, u32[]{:S(2)}) collective-permute-start(bf16[32,896]{1,0:T(8,128)(2,1)S(1)} %get-tuple-element.202), channel_id=1, source_target_pairs={{0,24},{8,16},{16,8},{24,0},{1,25},{9,17},{17,9},{25,1},{2,26},{10... | collective-permute-start | bytes 172040 | tf_op jit(solution)/shard_map/ppermute | solution.py:871
  249.3 9.4 %all-to-all-start.4 = ((bf16[4,32,1024]{2,1,0:T(8,128)(2,1)}), bf16[4,32,1024]{2,1,0:T(8,128)(2,1)S(1)}, u32[]{:S(2)}, u32[]{:S(2)}) async-start(bf16[4,32,1024]{2,1,0:T(8,128)(2,1)} %get-tuple-element.214), calls=%async_computation.5 | async-start | bytes 524288 | tf_op jit(solution)/shard_map/all_to_all | solution.py:854
Sparse Core Ops, SparseCore 0:
  9.6 33.8 all-gather.5
  45.7 22.7 all-gather.7
  70.7 47.8 all-gather.9
  169.6 58.3 reduce-scatter.1

commit v4 on v3

--- a/solution.py
+++ b/solution.py
@@ -679,14 +679,15 @@
 
 
 def attend_back_kernel(count, mover, seg_row, b0, b1, b2, b3, c0, c1, c2, c3, lse,
-                       o0, o1, o2, o3, qa, ka, vt, vn, dot, dq, dk, dv):
+                       o0, o1, o2, o3, qa, ka, vt, vn, dot, dq, dk, dv, kt):
     fill_heads(seg_row, count, (b0, b1, b2, b3), qa, ka, vt)
     span = b0.shape[1]
     rows = seg_row.shape[1]
-    head, total = vt.shape
-    for k in range(PLANE):
+    head = vt.shape[0]
+    for k, block in enumerate((b0, b1, b2, b3)):
         cols = slice(k * span, (k + 1) * span)
         vn[cols, :] = vt[:, cols].T
+        kt[:, cols] = block[head : 2 * head, :]
         for s, block in enumerate((c0, c1, c2, c3)):
             dot[:, k * span + s * rows : k * span + (s + 1) * rows] = block[:, k * rows : (k + 1) * rows]
     dk[...] = jnp.zeros_like(dk)
@@ -694,19 +695,20 @@
     logs = lse
 
     def step(i, carry):
-        at = pl.ds(pl.multiple_of(i * 2 * rows, 2 * rows), 2 * rows)
-        scores = mul(ka[...], qa[:, at], 1, 0)
-        soft = jnp.exp(scores - logs[0:1, at])
-        d_out = dot[:, at]
-        d_soft = mul(vn[...], d_out, 1, 0)
-        delta = jnp.sum(soft * d_soft, 0, keepdims=True)
-        d_scores = (soft * (d_soft - delta)).astype(bf16)
-        dv[...] += mul(d_out, soft.astype(bf16), 1, 1)
-        dk[...] += mul(qa[0:head, at], d_scores, 1, 1)
-        dq[:, at] = (mul(ka[:, 0:head], d_scores, 0, 0) * score_scale).astype(bf16)
+        for k in (2 * i, 2 * i + 1):
+            at = pl.ds(pl.multiple_of(k * span, span), span)
+            scores = mul(ka[...], qa[:, at], 1, 0)
+            soft = jnp.exp(scores - logs[0:1, at])
+            d_out = dot[:, at]
+            d_soft = mul(vn[...], d_out, 1, 0)
+            delta = jnp.sum(soft * d_soft, 0, keepdims=True)
+            d_scores = (soft * (d_soft - delta)).astype(bf16)
+            dv[...] += mul(d_out, soft.astype(bf16), 1, 1)
+            dk[...] += mul(qa[0:head, at], d_scores, 1, 1)
+            dq[:, at] = (mul(kt[...], d_scores, 1, 0) * score_scale).astype(bf16)
         return carry
 
-    lax.fori_loop(0, total // (2 * rows), step, 0)
+    lax.fori_loop(0, PLANE // 2, step, 0)
     for k, out in enumerate((o0, o1, o2, o3)):
         cols = slice(k * span, (k + 1) * span)
         out[0:head, :] = dq[:, cols]
@@ -722,32 +724,30 @@
     return joined[...].reshape(3 * PLANE * head, -1)
 
 
-def qkv_back_kernel(mover, pos, w, g0, g1, g2, g3, out, back, joined):
-    grads = join_heads(pos[1], (g0, g1, g2, g3), joined)
-    rows, d = out.shape[1:]
-    found = mul(grads, w[...].reshape(d, -1), 0, 1)
-    back[...] = found
-    for s in range(DEPTH):
-        out[pos[0] ^ s] = found[s * rows : (s + 1) * rows, :].astype(bf16)
-
-
-def qkv_grad_kernel(mover, pos, lead, seg_row, vec, toks, n1, g0, g1, g2, g3, back, d_mid, d_mid_vec, d_up_b,
-                    mine, o0, o1, joined, d_vec, both):
+def qkv_back_kernel(mover, pos, lead, seg_row, vec, toks, n1, w, g0, g1, g2, g3, d_mid, d_mid_vec, d_up_b,
+                    r0, r1, r2, r3, mine, o0, o1, joined, d_vec, both):
     z, yx, core = pos[0], pos[1], pos[2]
-    rows, d = toks.shape[1:]
+    rows, d = r0.shape
     width = d // DEPTH
-    grads = join_heads(yx, (g0, g1, g2, g3), joined)
+    head = width // PLANE
     rw = mine.shape[2]
     cols = 3 * width
+    fr = mine.shape[3] - cols
+    for k, block in enumerate((g0, g1, g2, g3)):
+        for part in range(3):
+            joined[part * PLANE + (yx ^ k)] = block[part * head : (part + 1) * head, :]
+    grads = joined[...].reshape(cols, DEPTH * rows)
     grad = mul(n1[...], grads, 0, 1).astype(bf16)
+    back = mul(grads, w[...].reshape(d, cols), 0, 1)
     hot = lead_hot(lead, seg_row)
     shift = mul(hot, vec[0:LEADS, :].astype(bf16), 0, 0)
     gain = vec_row(vec, ROW_G1)
     d_gain = jnp.zeros((1, d), f32)
     d_bias = jnp.zeros((1, d), f32)
     d_emb = d_mid[...]
-    for s in range(DEPTH):
+    for s, out in enumerate((r0, r1, r2, r3)):
         piece = back[s * rows : (s + 1) * rows, :]
+        out[...] = piece.astype(out.dtype)
         normal, inv = row_stats(toks[z ^ s].astype(f32) + shift)
         d_gain = d_gain + jnp.sum(piece * normal, 0, keepdims=True)
         d_bias = d_bias + jnp.sum(piece, 0, keepdims=True)
@@ -764,31 +764,26 @@
     d_vec[ROW_VB : ROW_VB + 1, at] = sums[0:1, 2 * width :]
     for i, row in enumerate((ROW_G2, ROW_B2, ROW_DB, ROW_OB)):
         d_vec[row : row + 1, :] = d_mid_vec[i : i + 1, :]
-    small = d_vec[...].astype(bf16)
-    fr = mine.shape[3] - cols
+    small = d_vec[...]
+    mark = lax.broadcasted_iota(jnp.int32, (rw, fr), 0) == VEC_ROWS
     for zz in range(DEPTH):
         for k in range(PLANE):
             for c in range(2):
                 i = (zz * PLANE + k) * 2 + c
-                side = jnp.concatenate([small[:, i * rw : (i + 1) * rw], jnp.zeros((rw, fr - rw), bf16)], 1)
+                side = jnp.concatenate([small[:, i * rw : (i + 1) * rw], jnp.zeros((rw, fr - rw), f32)], 1)
                 start = (c * DEPTH + zz) * fr
-                last = jnp.where(yx == k, d_up_b[:, start : start + fr], 0.0).astype(bf16)
-                mark = lax.broadcasted_iota(jnp.int32, (rw, fr), 0) == VEC_ROWS
-                whole = jnp.concatenate(
-                    [grad[i * rw : (i + 1) * rw, :], jnp.where(mark, last.astype(f32), side.astype(f32)).astype(bf16)], 1
-                )
-                both[zz, k, c] = whole
+                last = jnp.where(yx == k, d_up_b[:, start : start + fr], 0.0)
+                side = jnp.where(mark, last, side).astype(bf16)
+                both[zz, k, c] = jnp.concatenate([grad[i * rw : (i + 1) * rw, :], side], 1)
     mover.start(both.at[0:2, :, 1 - core], o0)
     mover.start(both.at[2:4, :, 1 - core], o1)
     mover.start(both.at[:, :, core], mine)
 
 
-def first_back_kernel(mover, lead, seg_row, vec, tok, d_mid, blocks, out):
+def first_back_kernel(mover, lead, seg_row, vec, tok, d_mid, r0, r1, r2, r3, out):
     shift = mul(lead_hot(lead, seg_row), vec[0:LEADS, :].astype(bf16), 0, 0)
     normal, inv = row_stats(tok[...].astype(f32) + shift)
-    dy = blocks[0].astype(f32)
-    for s in range(1, DEPTH):
-        dy = dy + blocks[s].astype(f32)
+    dy = r0[...].astype(f32) + r1[...].astype(f32) + r2[...].astype(f32) + r3[...].astype(f32)
     out[...] = d_mid[...] + norm_back(dy * vec_row(vec, ROW_G1), normal, inv)
 
 
@@ -799,16 +794,16 @@
     out[...] = total.astype(bf16)
 
 
-def pair_kernel(mover, pos, mine, o0, o1, p0, p1, p2, p3, total):
-    yx = pos[1]
-    total[0:2] = (mine[0:2].astype(f32) + o0[...].astype(f32)).astype(bf16)
-    total[2:4] = (mine[2:4].astype(f32) + o1[...].astype(f32)).astype(bf16)
-    for k, out in enumerate((p0, p1, p2, p3)):
-        mover.start(total.at[:, yx ^ k], out)
-
-
-def quad_kernel(mover, pos, b0, b1, b2, b3, o0, o1, o2, o3, total):
-    found = b0[...].astype(f32) + b1[...].astype(f32) + b2[...].astype(f32) + b3[...].astype(f32)
+def pair_kernel(mover, mine, o0, o1, out):
+    for k in range(PLANE):
+        out[k, 0:2] = (mine[0:2, k].astype(f32) + o0[:, k].astype(f32)).astype(bf16)
+        out[k, 2:4] = (mine[2:4, k].astype(f32) + o1[:, k].astype(f32)).astype(bf16)
+
+
+def quad_kernel(mover, pos, blocks, o0, o1, o2, o3, total):
+    found = blocks[0].astype(f32)
+    for k in range(1, PLANE):
+        found = found + blocks[k].astype(f32)
     total[...] = found.astype(bf16)
     for u, out in enumerate((o0, o1, o2, o3)):
         out[...] = total[pos[0] ^ u]
@@ -842,9 +837,9 @@
 
 COSTS = {
     "q_prep_kernel": (1, 4), "q_stack_kernel": (1, 4), "up_prep_kernel": (1, 4), "shard_kernel": (1, 4), "first_shard_kernel": (1, 4), "qkv_kernel": (5, 20),
-    "attend_kernel": (11, 16), "out_kernel": (2, 12), "norm_kernel": (2, 8), "ffn_kernel": (8, 32), "ffn_grad_kernel": (8, 32),
-    "branch_kernel": (2, 12), "out_back_kernel": (3, 12), "attend_back_kernel": (19, 24),
-    "qkv_back_kernel": (3, 16), "qkv_grad_kernel": (6, 24), "first_back_kernel": (2, 8), "layer_out_kernel": (1, 8),
+    "attend_kernel": (9, 24), "out_kernel": (2, 12), "norm_kernel": (2, 8), "ffn_kernel": (8, 32), "ffn_grad_kernel": (8, 32),
+    "branch_kernel": (2, 12), "out_back_kernel": (3, 12), "attend_back_kernel": (15, 32),
+    "qkv_back_kernel": (10, 28), "first_back_kernel": (2, 8), "layer_out_kernel": (1, 8),
     "pair_kernel": (2, 8), "quad_kernel": (1, 8), "qkv_join_kernel": (1, 4), "up_join_kernel": (2, 8), "ffn_last_kernel": (1, 8),
 }
 PLANE_AXES = ("y", "x")
@@ -922,14 +917,13 @@
         )
     )
     toks = lax.all_gather(tok, "z", axis=0)
-    d_outs = trade(jnp.broadcast_to(d_rows[None], (PLANE, rows, d)), PLANE_AXES)
-    (q_stack,) = call(q_stack_kernel, [((DEPTH, rw, side), bf16)], [pos, *q_rows], after=[d_outs])
-    q_plane = across((q_stack,) * PLANE)
-    q_other = [core_swap(block) for block in q_plane]
     (first_shard,) = call(first_shard_kernel, [((2, rw, d), bf16, "far")], [out_weight, down_weight])
     first = lax.all_gather(first_shard, ("z", "g"), axis=0).reshape(DEPTH, 2, 2, rw, d)
     (up_cols,) = call(up_prep_kernel, [((PLANE, rw, ff), bf16)], [up_weight])
     up_cols = trade(up_cols, PLANE_AXES)
+    (q_stack,) = call(q_stack_kernel, [((DEPTH, rw, side), bf16)], [pos, *q_rows], after=[up_cols])
+    q_plane = across((q_stack,) * PLANE)
+    q_other = [core_swap(block) for block in q_plane]
     n1, w_qkv, vec, up_b, *blocks = call(
         qkv_kernel,
         [((span, d), bf16, "far"), ((DEPTH, PLANE, 2, rw, width), bf16, "raw"), ((VEC_ROWS, d), f32), ((1, ff), f32)]
@@ -941,6 +935,7 @@
     ff_all = lax.all_gather(ff_shard, ("z", "g"), axis=0).reshape(DEPTH, 2, 2 * PLANE - 1, rw, d)
     blocks = across(blocks)
 
+    d_outs = trade(jnp.broadcast_to(d_rows[None], (PLANE, rows, d)), PLANE_AXES)
     *att_parts, lse = call(
         functools.partial(attend_kernel, count),
         [((head, PLANE * rows), bf16)] * 4 + [((8, group), f32)],
@@ -952,6 +947,7 @@
         out_kernel,
         [((rows, d), f32)] + [((rows, d), bf16)] * 3 + [((DEPTH * head, span), bf16), ((DEPTH, 2, rw, d), bf16)],
         [pos, *att_parts, Raw(first)],
+        after=[d_outs],
     )
     parts = across(parts)
     middle, n2 = call(norm_kernel, [((rows, d), f32, "far"), ((rows, d), bf16)], [lead, seg_row, vec, Far(tok), *parts])
@@ -994,37 +990,29 @@
         [((3 * head, span), bf16)] * 4,
         [seg_row, *blocks, *d_att, lse],
         [((128, group), bf16), ((group, 128), bf16), ((head, group), bf16), ((group, head), bf16),
-         ((head, group), bf16), ((head, group), bf16), ((head, group), f32), ((head, group), f32)],
+         ((head, group), bf16), ((head, group), bf16), ((head, group), f32), ((head, group), f32), ((head, group), bf16)],
     )
     d_blocks = across(d_blocks)
     (layer_out,) = call(layer_out_kernel, [((rows, d), bf16)], [vec, Far(middle), outs])
-    returned, back = call(
+    r0, r1, r2, r3, mine, o0, o1 = call(
         qkv_back_kernel,
-        [((DEPTH, rows, d), bf16), ((span, d), f32, "far")],
-        [pos, Far(w_qkv), *d_blocks],
-        [((3 * PLANE, head, span), bf16)],
-    )
-    returned = trade(returned, ("z",))
-    mine, o0, o1 = call(
-        qkv_grad_kernel,
-        [((DEPTH, PLANE, rw, side), bf16, "raw")] + [((DEPTH // 2, PLANE, rw, side), bf16)] * 2,
-        [pos, lead, seg_row, vec, Far(toks), Far(n1), *d_blocks, Far(back), Far(d_mid), d_mid_vec, d_up_b],
+        [((rows, d), f32)] + [((rows, d), bf16)] * 3
+        + [((DEPTH, PLANE, rw, side), bf16)] + [((DEPTH // 2, PLANE, rw, side), bf16)] * 2,
+        [pos, lead, seg_row, vec, Far(toks), Far(n1), Far(w_qkv), *d_blocks, Far(d_mid), d_mid_vec, d_up_b],
         [((3 * PLANE, head, span), bf16), ((rw, d), f32), ((DEPTH, PLANE, 2, rw, side), bf16)],
     )
-    quads = call(
-        pair_kernel,
-        [((DEPTH, rw, side), bf16, "raw")] + [((DEPTH, rw, side), bf16)] * 3,
-        [pos, Far(mine), core_swap(o0), core_swap(o1)],
-        [((DEPTH, PLANE, rw, side), bf16)],
-    )
-    quads = across(quads)
+    returned = along((r0, r1, r2, r3))
+    (quads,) = call(
+        pair_kernel, [((PLANE, DEPTH, rw, side), bf16)], [mine, core_swap(o0), core_swap(o1)]
+    )
+    quads = trade(quads, PLANE_AXES)
+    cols = along(call(quad_kernel, [((rw, side), bf16)] * 4, [pos, quads], [((DEPTH, rw, side), bf16)]))
     ups, d_down, d_out_weight = call(
         ffn_last_kernel, [((PLANE, rw, ff), bf16), ((fr, d), f32), ((rw, d), f32)], [ff_grad]
     )
     ups = trade(ups, PLANE_AXES)
-    cols = along(call(quad_kernel, [((rw, side), bf16)] * 4, [pos, Far(quads[0]), *quads[1:]], [((DEPTH, rw, side), bf16)]))
     (d_tokens,) = call(
-        first_back_kernel, [((rows, d), f32)], [lead, seg_row, vec, Far(tok), Far(d_mid), returned]
+        first_back_kernel, [((rows, d), f32)], [lead, seg_row, vec, Far(tok), Far(d_mid), *returned]
     )
     d_qkv, table, d_g1, d_b1, d_qb, d_vb, d_ob, d_g2, d_b2, d_db, d_ub = call(
         qkv_join_kernel,

time: 268 us -> 257 us (0.959)
  Pallas kernels: 99.7 us -> 87.7 us
  waiting for transfers between devices: 78.8 us -> 74.3 us
  starting transfers between devices: 69.8 us -> 74.2 us
    pallas_call x23 -> x22, Pallas kernels: 99.7 us -> 87.7 us  [run(): pl.pallas_call(body, name=name, out_shape=[HBM(o[0], o[1]) if o[2] else j...]
    ppermute x8 -> x7, waiting for transfers between devices: 13.3 us -> 3 us  [across(): lax.ppermute(blocks[1], 'x', swap)]
    all_to_all x5, waiting for transfers between devices: 0.01 us -> 8.15 us  [trade(): return lax.all_to_all(blocks, axes, split_axis=0, concat_axis=0, tiled=True)]
    ppermute x8 -> x7, waiting for transfers between devices: 27 us -> 19.2 us  [across(): lax.ppermute(blocks[2], 'y', swap)]
    ppermute x12 -> x15, starting transfers between devices: 20.5 us -> 25.9 us  [to_depth(): return lax.ppermute(block, 'z', [(i, i ^ step) for i in range(DEPTH)])]
    ppermute x12 -> x15, waiting for transfers between devices: 17.9 us -> 21.1 us  [to_depth(): return lax.ppermute(block, 'z', [(i, i ^ step) for i in range(DEPTH)])]
    ppermute x8 -> x7, starting transfers between devices: 8.19 us -> 5.49 us  [across(): lax.ppermute(blocks[2], 'y', swap)]
    ppermute x8 -> x7, starting transfers between devices: 11.7 us -> 13.8 us  [across(): lax.ppermute(blocks[3], ('y', 'x'), [(i, i ^ 3) for i in range(PLANE)])]
  transfers between devices with their start and end apart: 51 -> 51, of which waited for: 23 -> 25; matrix products, arithmetic and copies ran while one was open for 1% -> 0% of each run, Pallas kernels for 32% -> 28%
where the time goes in v4:
time: 257 us; the launch traced here: 256 us
  Pallas kernels  87.7 us (34%)
  waiting for transfers between devices  74.3 us (29%)
  starting transfers between devices  74.2 us (29%)
  between operations  14.2 us (6%)
  local copies, waits for them, and re-layouts  5.63 us (2%)
    pallas_call x22, Pallas kernels, run(): pl.pallas_call(body, name=name, out_shape=[HBM(o[0], o[1]) if o[2] else j...  87.7 us
    ppermute x15, starting transfers between devices, to_depth(): return lax.ppermute(block, 'z', [(i, i ^ step) for i in range(DEPTH)])  25.9 us
    ppermute x15, waiting for transfers between devices, to_depth(): return lax.ppermute(block, 'z', [(i, i ^ step) for i in range(DEPTH)])  21.1 us
    all_to_all x5, starting transfers between devices, trade(): return lax.all_to_all(blocks, axes, split_axis=0, concat_axis=0, tiled=True)  20.1 us
    ppermute x7, waiting for transfers between devices, across(): lax.ppermute(blocks[2], 'y', swap)  19.2 us
    ppermute x7, waiting for transfers between devices, across(): lax.ppermute(blocks[3], ('y', 'x'), [(i, i ^ 3) for i in range(PLANE)])  18.8 us
    ppermute x7, starting transfers between devices, across(): lax.ppermute(blocks[3], ('y', 'x'), [(i, i ^ 3) for i in range(PLANE)])  13.8 us
    all_to_all x5, waiting for transfers between devices, trade(): return lax.all_to_all(blocks, axes, split_axis=0, concat_axis=0, tiled=True)  8.15 us
  transfers between devices with their start and end apart: 51, of which 25 were waited for; matrix products, arithmetic and copies ran while one was open for 0% of the time, Pallas kernels for 28%

profile of v4, /device:TPU:0, one launch (start us, length us, event | category | flops | bytes accessed | tf_op | source)
XLA Modules:
  0.0 256.1 jit_solution(12900477714604735179)
XLA Ops:
  8.1 2.1 q_prep_kernel.1
  13.2 1.3 up_prep_kernel.1
  14.6 5.2 %all-to-all-start = ((bf16[4,32,1024]{2,1,0:T(8,128)(2,1)}), bf16[4,32,1024]{2,1,0:T(8,128)(2,1)S(1)}, u32[]{:S(2)}, u32[]{:S(2)}) async-start(bf16[4,32,1024]{2,1,0:T(8,128)(2,1)} %get-tuple-element.122), calls=%async_computation | async-start | bytes 524288 | tf_op jit(solution)/shard_map/all_to_all | solution.py:849
  19.7 1.6 collective-permute-start
  21.3 2.6 %collective-permute-start.1 = (bf16[32,896]{1,0:T(8,128)(2,1)S(1)}, bf16[32,896]{1,0:T(8,128)(2,1)S(1)}, u32[]{:S(2)}, u32[]{:S(2)}) collective-permute-start(bf16[32,896]{1,0:T(8,128)(2,1)S(1)} %get-tuple-element.118), channel_id=1, source_target_pairs={{0,16},{8,24},{16,0},{24,8},{1,17},{9,25},{17,1},{25,9},{2,18},{10... | collective-permute-start | bytes 172040 | tf_op jit(solution)/shard_map/ppermute | solution.py:866
  24.1 2.9 %collective-permute-done.refs_2_ = bf16[32,896]{1,0:T(8,128)(2,1)S(1)} collective-permute-done((bf16[32,896]{1,0:T(8,128)(2,1)S(1)}, bf16[32,896]{1,0:T(8,128)(2,1)S(1)}, u32[]{:S(2)}, u32[]{:S(2)}) %collective-permute-start) | collective-permute-done | bytes 57376 | tf_op jit(solution)/shard_map/ppermute | solution.py:866
  27.0 5.6 %collective-permute-done.1.refs_3_ = bf16[32,896]{1,0:T(8,128)(2,1)S(1)} collective-permute-done((bf16[32,896]{1,0:T(8,128)(2,1)S(1)}, bf16[32,896]{1,0:T(8,128)(2,1)S(1)}, u32[]{:S(2)}, u32[]{:S(2)}) %collective-permute-start.1) | collective-permute-done | bytes 57376 | tf_op jit(solution)/shard_map/ppermute | solution.py:866
  33.3 1.4 q_stack_kernel.1
  34.8 2.9 %collective-permute-start.5 = (bf16[4,32,896]{2,1,0:T(8,128)(2,1)S(1)}, bf16[4,32,896]{2,1,0:T(8,128)(2,1)S(1)}, u32[]{:S(2)}, u32[]{:S(2)}) collective-permute-start(bf16[4,32,896]{2,1,0:T(8,128)(2,1)S(1)} %get-tuple-element.124.refs_4_), channel_id=1, source_target_pairs={{0,6},{2,4},{4,2},{6,0},{1,7},{3,5},{5,3},{7,1},{8,14},{10,12},{12... | collective-permute-start | bytes 688136 | tf_op jit(solution)/shard_map/ppermute | solution.py:861
  38.3 5.2 %collective-permute-done.5.refs_7_ = bf16[4,32,896]{2,1,0:T(8,128)(2,1)S(1)} collective-permute-done((bf16[4,32,896]{2,1,0:T(8,128)(2,1)S(1)}, bf16[4,32,896]{2,1,0:T(8,128)(2,1)S(1)}, u32[]{:S(2)}, u32[]{:S(2)}) %collective-permute-start.5) | collective-permute-done | bytes 229408 | tf_op jit(solution)/shard_map/ppermute | solution.py:861
  43.6 2.3 collective-permute-done.4.refs_6_
  47.7 6.1 %qkv_kernel.1 = (bf16[512,1024]{1,0:T(8,128)(2,1)}, bf16[4,4,2,32,768]{4,3,2,1,0:T(8,128)(2,1)}, f32[24,1024]{1,0:T(8,128)S(1)}, f32[1,1024]{1,0:T(1,128)S(1)}, ...) custom-call(s32[3]{0:T(128)S(1)} %pad_add_fusion.refs_0_, ...), custom_call_target="tpu_custom_call" | custom-call | flops 5500000256 | bytes 18000000 | tf_op jit(solution)/shard_map/qkv_kernel/pallas_call | solution.py:400
  53.9 1.4 shard_kernel.1
  55.3 1.6 collective-permute-start.10
  60.0 4.2 %all-to-all-start.1 = ((bf16[4,128,1024]{2,1,0:T(8,128)(2,1)}), bf16[4,128,1024]{2,1,0:T(8,128)(2,1)}, u32[]{:S(2)}, u32[]{:S(2)}) async-start(bf16[4,128,1024]{2,1,0:T(8,128)(2,1)} %broadcast_in_dim.14), calls=%async_computation.1 | async-start | bytes 2097152 | tf_op jit(solution)/shard_map/all_to_all | solution.py:849
  64.3 8.3 %collective-permute-done.11.refs_3_ = bf16[192,512]{1,0:T(8,128)(2,1)S(1)} collective-permute-done((bf16[192,512]{1,0:T(8,128)(2,1)S(1)}, bf16[192,512]{1,0:T(8,128)(2,1)S(1)}, u32[]{:S(2)}, u32[]{:S(2)}) %collective-permute-start.11) | collective-permute-done | bytes 196640 | tf_op jit(solution)/shard_map/ppermute | solution.py:860
  72.6 11.2 %attend_kernel.1 = (bf16[64,512]{1,0:T(8,128)(2,1)S(1)}, bf16[64,512]{1,0:T(8,128)(2,1)S(1)}, bf16[64,512]{1,0:T(8,128)(2,1)S(1)}, bf16[64,512]{1,0:T(8,128)(2,1...) custom-call(s32[1,128]{1,0:T(1,128)S(1)} %copy-done.8, bf16[192,512]{1,0:T(8,128)(2,1)S(1)} %get-tuple-element.127.refs_1_, ...), custom_call_target="tpu_custom_call" | custom-call | flops 9900000256 | bytes 32400000 | tf_op jit(solution)/shard_map/attend_kernel/pallas_call | solution.py:400
  83.7 4.8 %collective-permute-start.13 = (bf16[64,512]{1,0:T(8,128)(2,1)S(1)}, bf16[64,512]{1,0:T(8,128)(2,1)S(1)}, u32[]{:S(2)}, u32[]{:S(2)}) collective-permute-start(bf16[64,512]{1,0:T(8,128)(2,1)S(1)} %get-tuple-element.134), channel_id=1, source_target_pairs={{0,8},{8,0},{16,24},{24,16},{1,9},{9,1},{17,25},{25,17},{2,10},{10... | collective-permute-start | bytes 196616 | tf_op jit(solution)/shard_map/ppermute | solution.py:866
  88.6 1.9 collective-permute-start.14
  90.4 1.4 collective-permute-start.15
  91.8 2.1 collective-permute-done.13.refs_2_
  94.0 4.5 %collective-permute-done.14.refs_3_ = bf16[64,512]{1,0:T(8,128)(2,1)S(1)} collective-permute-done((bf16[64,512]{1,0:T(8,128)(2,1)S(1)}, bf16[64,512]{1,0:T(8,128)(2,1)S(1)}, u32[]{:S(2)}, u32[]{:S(2)}) %collective-permute-start.14) | collective-permute-done | bytes 65568 | tf_op jit(solution)/shard_map/ppermute | solution.py:866
  99.7 2.6 %out_kernel.1 = (f32[128,1024]{1,0:T(8,128)S(1)}, bf16[128,1024]{1,0:T(8,128)(2,1)S(1)}, bf16[128,1024]{1,0:T(8,128)(2,1)S(1)}, bf16[128,1024]{1,0:T(8,128)(2,1)...) custom-call(s32[3]{0:T(128)S(1)} %pad_add_fusion.refs_0_, ...), custom_call_target="tpu_custom_call" | custom-call | flops 2200000000 | bytes 7200000 | tf_op jit(solution)/shard_map/out_kernel/pallas_call | solution.py:400
  102.4 1.7 collective-permute-start.17
  104.1 1.8 collective-permute-start.18
  105.9 2.9 %collective-permute-done.16.refs_5_ = bf16[128,1024]{1,0:T(8,128)(2,1)S(1)} collective-permute-done((bf16[128,1024]{1,0:T(8,128)(2,1)S(1)}, bf16[128,1024]{1,0:T(8,128)(2,1)S(1)}, u32[]{:S(2)}, u32[]{:S(2)}) %collective-permute-start.16) | collective-permute-done | bytes 262176 | tf_op jit(solution)/shard_map/ppermute | solution.py:859
  108.9 3.7 %collective-permute-done.18.refs_7_ = bf16[128,1024]{1,0:T(8,128)(2,1)S(1)} collective-permute-done((bf16[128,1024]{1,0:T(8,128)(2,1)S(1)}, bf16[128,1024]{1,0:T(8,128)(2,1)S(1)}, u32[]{:S(2)}, u32[]{:S(2)}) %collective-permute-start.18) | collective-permute-done | bytes 262176 | tf_op jit(solution)/shard_map/ppermute | solution.py:861
  112.6 2.9 %norm_kernel.1 = (f32[128,1024]{1,0:T(8,128)}, bf16[128,1024]{1,0:T(8,128)(2,1)S(1)}, f32[8,128]{1,0:T(8,128)S(1)}) custom-call(s32[4]{0:T(128)S(1)} %bitcast.14, s32[1,128]{1,0:T(1,128)S(1)} %copy-done.8, f32[24,1024]{1,0:T(8,128)S(1)} %get-tuple-element.126.refs_2_.refs_0_.refs_3_, bf16[128,1024]{1,0:T(8,128)(2,1)} %bitcast.20, ...), custom_call_target="tpu_custom_call" | custom-call | flops 2200000000 | bytes 7200000 | tf_op jit(solution)/shard_map/norm_kernel/pallas_call | solution.py:400
  115.5 5.1 %collective-permute-start.21 = (bf16[128,1024]{1,0:T(8,128)(2,1)S(1)}, bf16[128,1024]{1,0:T(8,128)(2,1)S(1)}, u32[]{:S(2)}, u32[]{:S(2)}) collective-permute-start(bf16[128,1024]{1,0:T(8,128)(2,1)S(1)} %get-tuple-element.146.refs_2_.refs_3_), channel_id=1, source_target_pairs={{0,6},{2,4},{4,2},{6,0},{1,7},{3,5},{5,3},{7,1},{8,14},{10,12},{12... | collective-permute-start | bytes 786440 | tf_op jit(solution)/shard_map/ppermute | solution.py:861
  121.2 3.8 %collective-permute-done.21.refs_5_.refs_6_ = bf16[128,1024]{1,0:T(8,128)(2,1)S(1)} collective-permute-done((bf16[128,1024]{1,0:T(8,128)(2,1)S(1)}, bf16[128,1024]{1,0:T(8,128)(2,1)S(1)}, u32[]{:S(2)}, u32[]{:S(2)}) %collective-permute-start.21) | collective-permute-done | bytes 262176 | tf_op jit(solution)/shard_map/ppermute | solution.py:861
  125.0 2.7 %collective-permute-done.20.refs_4_.refs_5_ = bf16[128,1024]{1,0:T(8,128)(2,1)S(1)} collective-permute-done((bf16[128,1024]{1,0:T(8,128)(2,1)S(1)}, bf16[128,1024]{1,0:T(8,128)(2,1)S(1)}, u32[]{:S(2)}, u32[]{:S(2)}) %collective-permute-start.20) | collective-permute-done | bytes 262176 | tf_op jit(solution)/shard_map/ppermute | solution.py:860
  127.8 8.5 %ffn_kernel.1 = (bf16[512,1024]{1,0:T(8,128)(2,1)S(1)}, bf16[512,1024]{1,0:T(8,128)(2,1)S(1)}, f32[128,1024]{1,0:T(8,128)S(1)}, bf16[128,1024]{1,0:T(8,128)(2,1)...) custom-call(s32[3]{0:T(128)S(1)} %pad_add_fusion.refs_0_, ...), custom_call_target="tpu_custom_call" | custom-call | flops 8800000000 | bytes 28800000 | tf_op jit(solution)/shard_map/ffn_kernel/pallas_call | solution.py:400
  136.3 2.1 collective-permute-start.22
  139.9 7.7 %ffn_grad_kernel.1 = (bf16[4,2,9,32,1024]{4,3,2,1,0:T(8,128)(2,1)}, bf16[4,128,1024]{2,1,0:T(8,128)(2,1)}, f32[8,128]{1,0:T(8,128)S(1)}) custom-call(s32[3]{0:T(128)S(1)} %pad_add_fusion.refs_0_, bf16[512,1024]{1,0:T(8,128)(2,1)S(1)} %get-tuple-element.149.refs_1_, bf16[512,1024]{1,0:T(8,128)(2,1)S(1)} %get-tuple-element.150.refs_2_, ...), custom_call_target="tpu_custom_call" | custom-call | flops 8800000000 | bytes 28800000 | tf_op jit(solution)/shard_map/ffn_grad_kernel/pallas_call | solution.py:400
  147.7 3.9 %collective-permute-done.23.refs_5_ = bf16[128,1024]{1,0:T(8,128)(2,1)S(1)} collective-permute-done((bf16[128,1024]{1,0:T(8,128)(2,1)S(1)}, bf16[128,1024]{1,0:T(8,128)(2,1)S(1)}, u32[]{:S(2)}, u32[]{:S(2)}) %collective-permute-start.23) | collective-permute-done | bytes 262176 | tf_op jit(solution)/shard_map/ppermute | solution.py:860
  151.5 3.0 %branch_kernel.1 = (f32[128,1024]{1,0:T(8,128)}, bf16[128,1024]{1,0:T(8,128)(2,1)S(1)}, f32[8,1024]{1,0:T(8,128)S(1)}, f32[8,128]{1,0:T(8,128)S(1)}) custom-call(f32[24,1024]{1,0:T(8,128)S(1)} %get-tuple-element.126.refs_2_.refs_0_.refs_3_, f32[128,1024]{1,0:T(8,128)} %get-tuple-element.144.refs_1_, bf16[128,1024]{1,0:T(8,128)(2,1)} %bitcast.18, ...), custom_call_target="tpu_custom_call" | custom-call | flops 2200000000 | bytes 7200000 | tf_op jit(solution)/shard_map/branch_kernel/pallas_call | solution.py:400
  154.7 3.4 %collective-permute-start.25 = (bf16[128,1024]{1,0:T(8,128)(2,1)S(1)}, bf16[128,1024]{1,0:T(8,128)(2,1)S(1)}, u32[]{:S(2)}, u32[]{:S(2)}) collective-permute-start(bf16[128,1024]{1,0:T(8,128)(2,1)S(1)} %get-tuple-element.160.refs_3_), channel_id=1, source_target_pairs={{0,2},{2,0},{1,3},{3,1},{4,6},{6,4},{5,7},{7,5},{8,10},{10,8},{9,1... | collective-permute-start | bytes 786440 | tf_op jit(solution)/shard_map/ppermute | solution.py:859
  158.1 3.9 %collective-permute-done.27.refs_6_ = bf16[128,1024]{1,0:T(8,128)(2,1)S(1)} collective-permute-done((bf16[128,1024]{1,0:T(8,128)(2,1)S(1)}, bf16[128,1024]{1,0:T(8,128)(2,1)S(1)}, u32[]{:S(2)}, u32[]{:S(2)}) %collective-permute-start.27) | collective-permute-done | bytes 262176 | tf_op jit(solution)/shard_map/ppermute | solution.py:861
  162.0 1.9 collective-permute-done.26.refs_5_
  163.9 2.7 %out_back_kernel.1 = (bf16[64,512]{1,0:T(8,128)(2,1)S(1)}, bf16[64,512]{1,0:T(8,128)(2,1)S(1)}, bf16[64,512]{1,0:T(8,128)(2,1)S(1)}, bf16[64,512]{1,0:T(8,128)(2...) custom-call(s32[3]{0:T(128)S(1)} %pad_add_fusion.refs_0_, ...), custom_call_target="tpu_custom_call", output_to_operand_aliasing={{4}: (7, {})} | custom-call | flops 3300000000 | bytes 10800000 | tf_op jit(solution)/shard_map/out_back_kernel/pallas_call | solution.py:400
  167.3 2.2 collective-permute-start.29
  169.5 1.5 collective-permute-start.30
  171.0 3.5 %all-to-all-start.2 = ((bf16[4,128,1024]{2,1,0:T(8,128)(2,1)}), bf16[4,128,1024]{2,1,0:T(8,128)(2,1)S(1)}, u32[]{:S(2)}, u32[]{:S(2)}) async-start(bf16[4,128,1024]{2,1,0:T(8,128)(2,1)} %get-tuple-element.152), calls=%async_computation.2 | async-start | bytes 2097152 | tf_op jit(solution)/shard_map/all_to_all | solution.py:849
  174.6 1.8 collective-permute-done.30.refs_8_
  176.4 13.5 %attend_back_kernel.1 = (bf16[192,512]{1,0:T(8,128)(2,1)S(1)}, bf16[192,512]{1,0:T(8,128)(2,1)S(1)}, bf16[192,512]{1,0:T(8,128)(2,1)S(1)}, bf16[192,512]{1,0:T(8,128)(2,1)S(1)}, f32[8,128]{1,0:T(8,128)S(1)}) custom-call(s32[1,128]{1,0:T(1,128)S(1)} %copy-done.8, bf16[192,512]{1,0:T(8,128)(2,1)S(1)} %get-tuple-element.127.refs_1_, ...), custom_call_target="tpu_custom_call" | custom-call | flops 16499999744 | bytes 54000000 | tf_op jit(solution)/shard_map/attend_back_kernel/pallas_call | solution.py:400
  190.2 1.5 collective-permute-start.32
  191.7 1.8 collective-permute-start.33
  193.5 2.5 layer_out_kernel.1
  196.0 2.2 collective-permute-done.33.refs_10_
  199.2 8.1 %qkv_back_kernel.1 = (f32[128,1024]{1,0:T(8,128)S(1)}, bf16[128,1024]{1,0:T(8,128)(2,1)S(1)}, bf16[128,1024]{1,0:T(8,128)(2,1)S(1)}, bf16[128,1024]{1,0:T(8,128)...) custom-call(s32[3]{0:T(128)S(1)} %pad_add_fusion.refs_0_, ...), custom_call_target="tpu_custom_call" | custom-call | flops 11000000512 | bytes 36000000 | tf_op jit(solution)/shard_map/qkv_back_kernel/pallas_call | solution.py:400
  209.8 1.7 pair_kernel.1
  211.5 3.8 %all-to-all-start.3 = ((bf16[4,4,32,896]{3,2,1,0:T(8,128)(2,1)}), bf16[4,4,32,896]{3,2,1,0:T(8,128)(2,1)S(1)}, u32[]{:S(2)}, u32[]{:S(2)}) async-start(bf16[4,4,32,896]{3,2,1,0:T(8,128)(2,1)} %get-tuple-element.190), calls=%async_computation.4 | async-start | bytes 1835008 | tf_op jit(solution)/shard_map/all_to_all | solution.py:849
  215.4 2.8 %collective-permute-start.35 = (bf16[128,1024]{1,0:T(8,128)(2,1)S(1)}, bf16[128,1024]{1,0:T(8,128)(2,1)S(1)}, u32[]{:S(2)}, u32[]{:S(2)}) collective-permute-start(bf16[128,1024]{1,0:T(8,128)(2,1)S(1)} %get-tuple-element.183), channel_id=1, source_target_pairs={{0,16},{8,24},{16,0},{24,8},{1,17},{9,25},{17,1},{25,9},{2,18},{10... | collective-permute-start | bytes 786440 | tf_op jit(solution)/shard_map/ppermute | solution.py:866
  218.2 1.5 collective-permute-start.36
  219.8 8.1 %all-to-all-done.3.refs_1_ = bf16[4,4,32,896]{3,2,1,0:T(8,128)(2,1)S(1)} async-done(((bf16[4,4,32,896]{3,2,1,0:T(8,128)(2,1)}), bf16[4,4,32,896]{3,2,1,0:T(8,128)(2,1)S(1)}, u32[]{:S(2)}, u32[]{:S(2)}) %all-to-all-start.3) | async-done | bytes 917536 | tf_op jit(solution)/shard_map/all_to_all | solution.py:849
  227.9 1.3 quad_kernel.1
  229.3 2.8 %collective-permute-start.40 = (bf16[32,896]{1,0:T(8,128)(2,1)S(1)}, bf16[32,896]{1,0:T(8,128)(2,1)S(1)}, u32[]{:S(2)}, u32[]{:S(2)}) collective-permute-start(bf16[32,896]{1,0:T(8,128)(2,1)S(1)} %get-tuple-element.197), channel_id=1, source_target_pairs={{0,16},{8,24},{16,0},{24,8},{1,17},{9,25},{17,1},{25,9},{2,18},{10... | collective-permute-start | bytes 172040 | tf_op jit(solution)/shard_map/ppermute | solution.py:866
  233.1 1.5 ffn_last_kernel.1
  234.7 3.4 %all-to-all-start.4 = ((bf16[4,32,1024]{2,1,0:T(8,128)(2,1)}), bf16[4,32,1024]{2,1,0:T(8,128)(2,1)S(1)}, u32[]{:S(2)}, u32[]{:S(2)}) async-start(bf16[4,32,1024]{2,1,0:T(8,128)(2,1)} %get-tuple-element.210), calls=%async_computation.5 | async-start | bytes 524288 | tf_op jit(solution)/shard_map/all_to_all | solution.py:849
  238.1 1.7 collective-permute-start.41
  239.8 3.5 %first_back_kernel.1 = (f32[128,1024]{1,0:T(8,128)}, f32[8,128]{1,0:T(8,128)S(1)}) custom-call(s32[4]{0:T(128)S(1)} %bitcast.16, s32[1,128]{1,0:T(1,128)S(1)} %copy-done.8, f32[24,1024]{1,0:T(8,128)S(1)} %get-tuple-element.126.refs_2_.refs_0_.refs_3_, bf16[128,1024]{1,0:T(8,128)(2,1)} %bitcast.21, f32[128,1024]{1,0:T(8,128)} %get-tuple-element.171.refs_11_.refs_4_, ...), custom_call_target="tpu_custom_call" | custom-call | flops 2200000000 | bytes 7200000 | tf_op jit(solution)/shard_map/first_back_kernel/pallas_call | solution.py:400
  243.3 2.9 %collective-permute-done.40.refs_3_ = bf16[32,896]{1,0:T(8,128)(2,1)S(1)} collective-permute-done((bf16[32,896]{1,0:T(8,128)(2,1)S(1)}, bf16[32,896]{1,0:T(8,128)(2,1)S(1)}, u32[]{:S(2)}, u32[]{:S(2)}) %collective-permute-start.40) | collective-permute-done | bytes 57376 | tf_op jit(solution)/shard_map/ppermute | solution.py:866
  246.2 1.9 qkv_join_kernel.1
  248.2 1.4 up_join_kernel.1
  (90 shorter events, 19.9 us)
Async XLA Ops:
  7.2 6.0 %copy-start.3 = (bf16[32,4096]{1,0:T(8,128)(2,1)S(1)}, bf16[32,4096]{1,0:T(8,128)(2,1)}, u32[]{:S(2)}) copy-start(bf16[32,4096]{1,0:T(8,128)(2,1)} %refs_0_.5) | copy-start | bytes 786436
  7.2 40.5 %all-gather.6.cloned.1.call-start = ((), (), s32[]{:S(2)}) async-start(), calls=%async_computation.6 | async-start | bytes 1310720 | tf_op jit(solution)/shard_map/all_gather | solution.py:919
  7.9 83.9 %all-gather.8.cloned.1.call-start = ((), (), s32[]{:S(2)}) async-start(), calls=%async_computation.8 | async-start | bytes 1179648 | tf_op jit(solution)/shard_map/all_gather | solution.py:921
  10.1 1.0 copy-start.4
  11.1 0.8 copy-start.6
  13.2 34.6 %copy-start.7 = (s32[1,4]{1,0:T(1,128)S(1)}, s32[1,4]{1,0:T(1,128)}, u32[]{:S(2)}) copy-start(s32[1,4]{1,0:T(1,128)} %param.20) | copy-start | bytes 52
  13.2 34.5 %copy-start.8 = (s32[1,128]{1,0:T(1,128)S(1)}, s32[1,128]{1,0:T(1,128)}, u32[]{:S(2)}) copy-start(s32[1,128]{1,0:T(1,128)} %refs_1_.9) | copy-start | bytes 1540
  14.6 18.1 %all-to-all-start = ((bf16[4,32,1024]{2,1,0:T(8,128)(2,1)}), bf16[4,32,1024]{2,1,0:T(8,128)(2,1)S(1)}, u32[]{:S(2)}, u32[]{:S(2)}) async-start(bf16[4,32,1024]{2,1,0:T(8,128)(2,1)} %get-tuple-element.122), calls=%async_computation | async-start | bytes 524288 | tf_op jit(solution)/shard_map/all_to_all | solution.py:849
  19.7 108.0 %all-gather.10.cloned.1.call-start = ((), (), s32[]{:S(2)}) async-start(), calls=%async_computation.9 | async-start | bytes 4128768 | tf_op jit(solution)/shard_map/all_gather | solution.py:935
  19.7 7.3 %collective-permute-start = (bf16[32,896]{1,0:T(8,128)(2,1)S(1)}, bf16[32,896]{1,0:T(8,128)(2,1)S(1)}, u32[]{:S(2)}, u32[]{:S(2)}) collective-permute-start(bf16[32,896]{1,0:T(8,128)(2,1)S(1)} %get-tuple-element.117), channel_id=1, source_target_pairs={{0,8},{8,0},{16,24},{24,16},{1,9},{9,1},{17,25},{25,17},{2,10},{10... | collective-permute-start | bytes 172040 | tf_op jit(solution)/shard_map/ppermute | solution.py:866
  21.3 11.3 %collective-permute-start.1 = (bf16[32,896]{1,0:T(8,128)(2,1)S(1)}, bf16[32,896]{1,0:T(8,128)(2,1)S(1)}, u32[]{:S(2)}, u32[]{:S(2)}) collective-permute-start(bf16[32,896]{1,0:T(8,128)(2,1)S(1)} %get-tuple-element.118), channel_id=1, source_target_pairs={{0,16},{8,24},{16,0},{24,8},{1,17},{9,25},{17,1},{25,9},{2,18},{10... | collective-permute-start | bytes 172040 | tf_op jit(solution)/shard_map/ppermute | solution.py:866
  23.9 8.7 %collective-permute-start.2 = (bf16[32,896]{1,0:T(8,128)(2,1)S(1)}, bf16[32,896]{1,0:T(8,128)(2,1)S(1)}, u32[]{:S(2)}, u32[]{:S(2)}) collective-permute-start(bf16[32,896]{1,0:T(8,128)(2,1)S(1)} %get-tuple-element.119), channel_id=1, source_target_pairs={{0,24},{8,16},{16,8},{24,0},{1,25},{9,17},{17,9},{25,1},{2,26},{10... | collective-permute-start | bytes 172040 | tf_op jit(solution)/shard_map/ppermute | solution.py:866
  32.6 0.7 copy-start
  34.8 8.8 %collective-permute-start.5 = (bf16[4,32,896]{2,1,0:T(8,128)(2,1)S(1)}, bf16[4,32,896]{2,1,0:T(8,128)(2,1)S(1)}, u32[]{:S(2)}, u32[]{:S(2)}) collective-permute-start(bf16[4,32,896]{2,1,0:T(8,128)(2,1)S(1)} %get-tuple-element.124.refs_4_), channel_id=1, source_target_pairs={{0,6},{2,4},{4,2},{6,0},{1,7},{3,5},{5,3},{7,1},{8,14},{10,12},{12... | collective-permute-start | bytes 688136 | tf_op jit(solution)/shard_map/ppermute | solution.py:861
  37.7 8.2 %collective-permute-start.4 = (bf16[4,32,896]{2,1,0:T(8,128)(2,1)S(1)}, bf16[4,32,896]{2,1,0:T(8,128)(2,1)S(1)}, u32[]{:S(2)}, u32[]{:S(2)}) collective-permute-start(bf16[4,32,896]{2,1,0:T(8,128)(2,1)S(1)} %get-tuple-element.124.refs_4_), channel_id=1, source_target_pairs={{0,4},{4,0},{1,5},{5,1},{2,6},{6,2},{3,7},{7,3},{8,12},{12,8},{9,1... | collective-permute-start | bytes 688136 | tf_op jit(solution)/shard_map/ppermute | solution.py:860
  38.3 7.7 %collective-permute-start.3 = (bf16[4,32,896]{2,1,0:T(8,128)(2,1)S(1)}, bf16[4,32,896]{2,1,0:T(8,128)(2,1)S(1)}, u32[]{:S(2)}, u32[]{:S(2)}) collective-permute-start(bf16[4,32,896]{2,1,0:T(8,128)(2,1)S(1)} %get-tuple-element.124.refs_4_), channel_id=1, source_target_pairs={{0,2},{2,0},{1,3},{3,1},{4,6},{6,4},{5,7},{7,5},{8,10},{10,8},{9,1... | collective-permute-start | bytes 688136 | tf_op jit(solution)/shard_map/ppermute | solution.py:859
  38.3 8.1 %collective-permute-start.6 = (bf16[4,32,896]{2,1,0:T(8,128)(2,1)S(1)}, bf16[4,32,896]{2,1,0:T(8,128)(2,1)S(1)}, u32[]{:S(2)}, u32[]{:S(2)}) collective-permute-start(bf16[4,32,896]{2,1,0:T(8,128)(2,1)S(1)} %get-tuple-element.124.refs_4_), channel_id=1, source_target_pairs={{0,1},{1,0},{2,3},{3,2},{4,5},{5,4},{6,7},{7,6},{8,9},{9,8},{10,11... | collective-permute-start | bytes 688136 | tf_op jit(solution)/shard_map/ppermute | solution.py:874
  43.6 2.9 %collective-permute-start.9 = (bf16[4,32,896]{2,1,0:T(8,128)(2,1)S(1)}, bf16[4,32,896]{2,1,0:T(8,128)(2,1)S(1)}, u32[]{:S(2)}, u32[]{:S(2)}) collective-permute-start(bf16[4,32,896]{2,1,0:T(8,128)(2,1)S(1)} %collective-permute-done.5.refs_7_), channel_id=1, source_target_pairs={{0,1},{1,0},{2,3},{3,2},{4,5},{5,4},{6,7},{7,6},{8,9},{9,8},{10,11... | collective-permute-start | bytes 688136 | tf_op jit(solution)/shard_map/ppermute | solution.py:874
  45.9 1.5 collective-permute-start.8
  46.0 1.7 collective-permute-start.7
  47.7 6.2 %copy-start.1 = (bf16[4,32,1024]{2,1,0:T(8,128)(2,1)S(1)}, bf16[4,32,1024]{2,1,0:T(8,128)(2,1)}, u32[]{:S(2)}) copy-start(bf16[4,32,1024]{2,1,0:T(8,128)(2,1)} %copy-done) | copy-start | bytes 786436
  47.7 6.2 %copy-start.5 = (bf16[128,1024]{1,0:T(8,128)(2,1)S(1)}, bf16[128,1024]{1,0:T(8,128)(2,1)}, u32[]{:S(2)}) copy-start(bf16[128,1024]{1,0:T(8,128)(2,1)} %refs_1_.7) | copy-start | bytes 786436
  53.9 5.0 %copy-start.11 = (bf16[1,128,1024]{2,1,0:T(8,128)(2,1)S(1)}, bf16[1,128,1024]{2,1,0:T(8,128)(2,1)}, u32[]{:S(2)}) copy-start(bf16[1,128,1024]{2,1,0:T(8,128)(2,1)} %param.35) | copy-start | bytes 786436
  55.3 9.0 %collective-permute-start.10 = (bf16[192,512]{1,0:T(8,128)(2,1)S(1)}, bf16[192,512]{1,0:T(8,128)(2,1)S(1)}, u32[]{:S(2)}, u32[]{:S(2)}) collective-permute-start(bf16[192,512]{1,0:T(8,128)(2,1)S(1)} %get-tuple-element.128), channel_id=1, source_target_pairs={{0,2},{2,0},{1,3},{3,1},{4,6},{6,4},{5,7},{7,5},{8,10},{10,8},{9,1... | collective-permute-start | bytes 589832 | tf_op jit(solution)/shard_map/ppermute | solution.py:859
  56.9 15.7 %collective-permute-start.11 = (bf16[192,512]{1,0:T(8,128)(2,1)S(1)}, bf16[192,512]{1,0:T(8,128)(2,1)S(1)}, u32[]{:S(2)}, u32[]{:S(2)}) collective-permute-start(bf16[192,512]{1,0:T(8,128)(2,1)S(1)} %get-tuple-element.129), channel_id=1, source_target_pairs={{0,4},{4,0},{1,5},{5,1},{2,6},{6,2},{3,7},{7,3},{8,12},{12,8},{9,1... | collective-permute-start | bytes 589832 | tf_op jit(solution)/shard_map/ppermute | solution.py:860
  57.7 14.9 %collective-permute-start.12 = (bf16[192,512]{1,0:T(8,128)(2,1)S(1)}, bf16[192,512]{1,0:T(8,128)(2,1)S(1)}, u32[]{:S(2)}, u32[]{:S(2)}) collective-permute-start(bf16[192,512]{1,0:T(8,128)(2,1)S(1)} %get-tuple-element.130), channel_id=1, source_target_pairs={{0,6},{2,4},{4,2},{6,0},{1,7},{3,5},{5,3},{7,1},{8,14},{10,12},{12... | collective-permute-start | bytes 589832 | tf_op jit(solution)/shard_map/ppermute | solution.py:861
  60.0 31.9 %all-to-all-start.1 = ((bf16[4,128,1024]{2,1,0:T(8,128)(2,1)}), bf16[4,128,1024]{2,1,0:T(8,128)(2,1)}, u32[]{:S(2)}, u32[]{:S(2)}) async-start(bf16[4,128,1024]{2,1,0:T(8,128)(2,1)} %broadcast_in_dim.14), calls=%async_computation.1 | async-start | bytes 2097152 | tf_op jit(solution)/shard_map/all_to_all | solution.py:849
  64.2 167.8 %reduce-scatter.2.cloned.1.call-start = ((), (), s32[]{:S(2)}) async-start(), calls=%async_computation.7 | async-start | bytes 5308416 | tf_op jit(solution)/shard_map/reduce_scatter | solution.py:983
  83.7 10.2 %collective-permute-start.13 = (bf16[64,512]{1,0:T(8,128)(2,1)S(1)}, bf16[64,512]{1,0:T(8,128)(2,1)S(1)}, u32[]{:S(2)}, u32[]{:S(2)}) collective-permute-start(bf16[64,512]{1,0:T(8,128)(2,1)S(1)} %get-tuple-element.134), channel_id=1, source_target_pairs={{0,8},{8,0},{16,24},{24,16},{1,9},{9,1},{17,25},{25,17},{2,10},{10... | collective-permute-start | bytes 196616 | tf_op jit(solution)/shard_map/ppermute | solution.py:866
  88.6 9.9 %collective-permute-start.14 = (bf16[64,512]{1,0:T(8,128)(2,1)S(1)}, bf16[64,512]{1,0:T(8,128)(2,1)S(1)}, u32[]{:S(2)}, u32[]{:S(2)}) collective-permute-start(bf16[64,512]{1,0:T(8,128)(2,1)S(1)} %get-tuple-element.135), channel_id=1, source_target_pairs={{0,16},{8,24},{16,0},{24,8},{1,17},{9,25},{17,1},{25,9},{2,18},{10... | collective-permute-start | bytes 196616 | tf_op jit(solution)/shard_map/ppermute | solution.py:866
  90.4 9.2 %collective-permute-start.15 = (bf16[64,512]{1,0:T(8,128)(2,1)S(1)}, bf16[64,512]{1,0:T(8,128)(2,1)S(1)}, u32[]{:S(2)}, u32[]{:S(2)}) collective-permute-start(bf16[64,512]{1,0:T(8,128)(2,1)S(1)} %get-tuple-element.136), channel_id=1, source_target_pairs={{0,24},{8,16},{16,8},{24,0},{1,25},{9,17},{17,9},{25,1},{2,26},{10... | collective-permute-start | bytes 196616 | tf_op jit(solution)/shard_map/ppermute | solution.py:866
  102.3 6.4 %collective-permute-start.16 = (bf16[128,1024]{1,0:T(8,128)(2,1)S(1)}, bf16[128,1024]{1,0:T(8,128)(2,1)S(1)}, u32[]{:S(2)}, u32[]{:S(2)}) collective-permute-start(bf16[128,1024]{1,0:T(8,128)(2,1)S(1)} %get-tuple-element.140), channel_id=1, source_target_pairs={{0,2},{2,0},{1,3},{3,1},{4,6},{6,4},{5,7},{7,5},{8,10},{10,8},{9,1... | collective-permute-start | bytes 786440 | tf_op jit(solution)/shard_map/ppermute | solution.py:859
  102.4 6.5 %collective-permute-start.17 = (bf16[128,1024]{1,0:T(8,128)(2,1)S(1)}, bf16[128,1024]{1,0:T(8,128)(2,1)S(1)}, u32[]{:S(2)}, u32[]{:S(2)}) collective-permute-start(bf16[128,1024]{1,0:T(8,128)(2,1)S(1)} %get-tuple-element.141), channel_id=1, source_target_pairs={{0,4},{4,0},{1,5},{5,1},{2,6},{6,2},{3,7},{7,3},{8,12},{12,8},{9,1... | collective-permute-start | bytes 786440 | tf_op jit(solution)/shard_map/ppermute | solution.py:860
  104.1 8.5 %collective-permute-start.18 = (bf16[128,1024]{1,0:T(8,128)(2,1)S(1)}, bf16[128,1024]{1,0:T(8,128)(2,1)S(1)}, u32[]{:S(2)}, u32[]{:S(2)}) collective-permute-start(bf16[128,1024]{1,0:T(8,128)(2,1)S(1)} %get-tuple-element.142), channel_id=1, source_target_pairs={{0,6},{2,4},{4,2},{6,0},{1,7},{3,5},{5,3},{7,1},{8,14},{10,12},{12... | collective-permute-start | bytes 786440 | tf_op jit(solution)/shard_map/ppermute | solution.py:861
  115.5 9.5 %collective-permute-start.21 = (bf16[128,1024]{1,0:T(8,128)(2,1)S(1)}, bf16[128,1024]{1,0:T(8,128)(2,1)S(1)}, u32[]{:S(2)}, u32[]{:S(2)}) collective-permute-start(bf16[128,1024]{1,0:T(8,128)(2,1)S(1)} %get-tuple-element.146.refs_2_.refs_3_), channel_id=1, source_target_pairs={{0,6},{2,4},{4,2},{6,0},{1,7},{3,5},{5,3},{7,1},{8,14},{10,12},{12... | collective-permute-start | bytes 786440 | tf_op jit(solution)/shard_map/ppermute | solution.py:861
  120.6 7.2 %collective-permute-start.20 = (bf16[128,1024]{1,0:T(8,128)(2,1)S(1)}, bf16[128,1024]{1,0:T(8,128)(2,1)S(1)}, u32[]{:S(2)}, u32[]{:S(2)}) collective-permute-start(bf16[128,1024]{1,0:T(8,128)(2,1)S(1)} %get-tuple-element.146.refs_2_.refs_3_), channel_id=1, source_target_pairs={{0,4},{4,0},{1,5},{5,1},{2,6},{6,2},{3,7},{7,3},{8,12},{12,8},{9,1... | collective-permute-start | bytes 786440 | tf_op jit(solution)/shard_map/ppermute | solution.py:860
  120.9 6.9 %collective-permute-start.19 = (bf16[128,1024]{1,0:T(8,128)(2,1)S(1)}, bf16[128,1024]{1,0:T(8,128)(2,1)S(1)}, u32[]{:S(2)}, u32[]{:S(2)}) collective-permute-start(bf16[128,1024]{1,0:T(8,128)(2,1)S(1)} %get-tuple-element.146.refs_2_.refs_3_), channel_id=1, source_target_pairs={{0,2},{2,0},{1,3},{3,1},{4,6},{6,4},{5,7},{7,5},{8,10},{10,8},{9,1... | collective-permute-start | bytes 786440 | tf_op jit(solution)/shard_map/ppermute | solution.py:859
  136.3 11.4 %collective-permute-start.22 = (bf16[128,1024]{1,0:T(8,128)(2,1)S(1)}, bf16[128,1024]{1,0:T(8,128)(2,1)S(1)}, u32[]{:S(2)}, u32[]{:S(2)}) collective-permute-start(bf16[128,1024]{1,0:T(8,128)(2,1)S(1)} %get-tuple-element.156), channel_id=1, source_target_pairs={{0,2},{2,0},{1,3},{3,1},{4,6},{6,4},{5,7},{7,5},{8,10},{10,8},{9,1... | collective-permute-start | bytes 786440 | tf_op jit(solution)/shard_map/ppermute | solution.py:859
  138.4 13.1 %collective-permute-start.23 = (bf16[128,1024]{1,0:T(8,128)(2,1)S(1)}, bf16[128,1024]{1,0:T(8,128)(2,1)S(1)}, u32[]{:S(2)}, u32[]{:S(2)}) collective-permute-start(bf16[128,1024]{1,0:T(8,128)(2,1)S(1)} %get-tuple-element.157), channel_id=1, source_target_pairs={{0,4},{4,0},{1,5},{5,1},{2,6},{6,2},{3,7},{7,3},{8,12},{12,8},{9,1... | collective-permute-start | bytes 786440 | tf_op jit(solution)/shard_map/ppermute | solution.py:860
  139.0 12.5 %collective-permute-start.24 = (bf16[128,1024]{1,0:T(8,128)(2,1)S(1)}, bf16[128,1024]{1,0:T(8,128)(2,1)S(1)}, u32[]{:S(2)}, u32[]{:S(2)}) collective-permute-start(bf16[128,1024]{1,0:T(8,128)(2,1)S(1)} %get-tuple-element.158), channel_id=1, source_target_pairs={{0,6},{2,4},{4,2},{6,0},{1,7},{3,5},{5,3},{7,1},{8,14},{10,12},{12... | collective-permute-start | bytes 786440 | tf_op jit(solution)/shard_map/ppermute | solution.py:861
  154.5 7.4 %collective-permute-start.27 = (bf16[128,1024]{1,0:T(8,128)(2,1)S(1)}, bf16[128,1024]{1,0:T(8,128)(2,1)S(1)}, u32[]{:S(2)}, u32[]{:S(2)}) collective-permute-start(bf16[128,1024]{1,0:T(8,128)(2,1)S(1)} %get-tuple-element.160.refs_3_), channel_id=1, source_target_pairs={{0,6},{2,4},{4,2},{6,0},{1,7},{3,5},{5,3},{7,1},{8,14},{10,12},{12... | collective-permute-start | bytes 786440 | tf_op jit(solution)/shard_map/ppermute | solution.py:861
  154.6 9.2 %collective-permute-start.26 = (bf16[128,1024]{1,0:T(8,128)(2,1)S(1)}, bf16[128,1024]{1,0:T(8,128)(2,1)S(1)}, u32[]{:S(2)}, u32[]{:S(2)}) collective-permute-start(bf16[128,1024]{1,0:T(8,128)(2,1)S(1)} %get-tuple-element.160.refs_3_), channel_id=1, source_target_pairs={{0,4},{4,0},{1,5},{5,1},{2,6},{6,2},{3,7},{7,3},{8,12},{12,8},{9,1... | collective-permute-start | bytes 786440 | tf_op jit(solution)/shard_map/ppermute | solution.py:860
  154.7 9.2 %collective-permute-start.25 = (bf16[128,1024]{1,0:T(8,128)(2,1)S(1)}, bf16[128,1024]{1,0:T(8,128)(2,1)S(1)}, u32[]{:S(2)}, u32[]{:S(2)}) collective-permute-start(bf16[128,1024]{1,0:T(8,128)(2,1)S(1)} %get-tuple-element.160.refs_3_), channel_id=1, source_target_pairs={{0,2},{2,0},{1,3},{3,1},{4,6},{6,4},{5,7},{7,5},{8,10},{10,8},{9,1... | collective-permute-start | bytes 786440 | tf_op jit(solution)/shard_map/ppermute | solution.py:859
  166.6 8.0 %collective-permute-start.28 = (bf16[64,512]{1,0:T(8,128)(2,1)S(1)}, bf16[64,512]{1,0:T(8,128)(2,1)S(1)}, u32[]{:S(2)}, u32[]{:S(2)}) collective-permute-start(bf16[64,512]{1,0:T(8,128)(2,1)S(1)} %get-tuple-element.164), channel_id=1, source_target_pairs={{0,8},{8,0},{16,24},{24,16},{1,9},{9,1},{17,25},{25,17},{2,10},{10... | collective-permute-start | bytes 196616 | tf_op jit(solution)/shard_map/ppermute | solution.py:866
  167.3 7.3 %collective-permute-start.29 = (bf16[64,512]{1,0:T(8,128)(2,1)S(1)}, bf16[64,512]{1,0:T(8,128)(2,1)S(1)}, u32[]{:S(2)}, u32[]{:S(2)}) collective-permute-start(bf16[64,512]{1,0:T(8,128)(2,1)S(1)} %get-tuple-element.165), channel_id=1, source_target_pairs={{0,16},{8,24},{16,0},{24,8},{1,17},{9,25},{17,1},{25,9},{2,18},{10... | collective-permute-start | bytes 196616 | tf_op jit(solution)/shard_map/ppermute | solution.py:866
  169.5 6.9 %collective-permute-start.30 = (bf16[64,512]{1,0:T(8,128)(2,1)S(1)}, bf16[64,512]{1,0:T(8,128)(2,1)S(1)}, u32[]{:S(2)}, u32[]{:S(2)}) collective-permute-start(bf16[64,512]{1,0:T(8,128)(2,1)S(1)} %get-tuple-element.166), channel_id=1, source_target_pairs={{0,24},{8,16},{16,8},{24,0},{1,25},{9,17},{17,9},{25,1},{2,26},{10... | collective-permute-start | bytes 196616 | tf_op jit(solution)/shard_map/ppermute | solution.py:866
  171.0 22.5 %all-to-all-start.2 = ((bf16[4,128,1024]{2,1,0:T(8,128)(2,1)}), bf16[4,128,1024]{2,1,0:T(8,128)(2,1)S(1)}, u32[]{:S(2)}, u32[]{:S(2)}) async-start(bf16[4,128,1024]{2,1,0:T(8,128)(2,1)} %get-tuple-element.152), calls=%async_computation.2 | async-start | bytes 2097152 | tf_op jit(solution)/shard_map/all_to_all | solution.py:849
  189.9 8.3 %copy-start.9 = (bf16[192,512]{1,0:T(8,128)(2,1)}, bf16[192,512]{1,0:T(8,128)(2,1)S(1)}, u32[]{:S(2)}) copy-start(bf16[192,512]{1,0:T(8,128)(2,1)S(1)} %get-tuple-element.174.refs_7_) | copy-start | bytes 589828
  189.9 6.1 %collective-permute-start.31 = (bf16[192,512]{1,0:T(8,128)(2,1)S(1)}, bf16[192,512]{1,0:T(8,128)(2,1)S(1)}, u32[]{:S(2)}, u32[]{:S(2)}) collective-permute-start(bf16[192,512]{1,0:T(8,128)(2,1)S(1)} %get-tuple-element.175), channel_id=1, source_target_pairs={{0,2},{2,0},{1,3},{3,1},{4,6},{6,4},{5,7},{7,5},{8,10},{10,8},{9,1... | collective-permute-start | bytes 589832 | tf_op jit(solution)/shard_map/ppermute | solution.py:859
  190.2 5.8 %collective-permute-start.32 = (bf16[192,512]{1,0:T(8,128)(2,1)S(1)}, bf16[192,512]{1,0:T(8,128)(2,1)S(1)}, u32[]{:S(2)}, u32[]{:S(2)}) collective-permute-start(bf16[192,512]{1,0:T(8,128)(2,1)S(1)} %get-tuple-element.176), channel_id=1, source_target_pairs={{0,4},{4,0},{1,5},{5,1},{2,6},{6,2},{3,7},{7,3},{8,12},{12,8},{9,1... | collective-permute-start | bytes 589832 | tf_op jit(solution)/shard_map/ppermute | solution.py:860
  191.7 6.6 %collective-permute-start.33 = (bf16[192,512]{1,0:T(8,128)(2,1)S(1)}, bf16[192,512]{1,0:T(8,128)(2,1)S(1)}, u32[]{:S(2)}, u32[]{:S(2)}) collective-permute-start(bf16[192,512]{1,0:T(8,128)(2,1)S(1)} %get-tuple-element.177), channel_id=1, source_target_pairs={{0,6},{2,4},{4,2},{6,0},{1,7},{3,5},{5,3},{7,1},{8,14},{10,12},{12... | collective-permute-start | bytes 589832 | tf_op jit(solution)/shard_map/ppermute | solution.py:861
  198.2 0.9 copy-start.10
  207.2 1.9 collective-permute-start.37
  207.3 2.5 collective-permute-start.38
  211.5 16.4 %all-to-all-start.3 = ((bf16[4,4,32,896]{3,2,1,0:T(8,128)(2,1)}), bf16[4,4,32,896]{3,2,1,0:T(8,128)(2,1)S(1)}, u32[]{:S(2)}, u32[]{:S(2)}) async-start(bf16[4,4,32,896]{3,2,1,0:T(8,128)(2,1)} %get-tuple-element.190), calls=%async_computation.4 | async-start | bytes 1835008 | tf_op jit(solution)/shard_map/all_to_all | solution.py:849
  215.3 22.8 %collective-permute-start.34 = (bf16[128,1024]{1,0:T(8,128)(2,1)S(1)}, bf16[128,1024]{1,0:T(8,128)(2,1)S(1)}, u32[]{:S(2)}, u32[]{:S(2)}) collective-permute-start(bf16[128,1024]{1,0:T(8,128)(2,1)S(1)} %get-tuple-element.182), channel_id=1, source_target_pairs={{0,8},{8,0},{16,24},{24,16},{1,9},{9,1},{17,25},{25,17},{2,10},{10... | collective-permute-start | bytes 786440 | tf_op jit(solution)/shard_map/ppermute | solution.py:866
  215.4 24.4 %collective-permute-start.35 = (bf16[128,1024]{1,0:T(8,128)(2,1)S(1)}, bf16[128,1024]{1,0:T(8,128)(2,1)S(1)}, u32[]{:S(2)}, u32[]{:S(2)}) collective-permute-start(bf16[128,1024]{1,0:T(8,128)(2,1)S(1)} %get-tuple-element.183), channel_id=1, source_target_pairs={{0,16},{8,24},{16,0},{24,8},{1,17},{9,25},{17,1},{25,9},{2,18},{10... | collective-permute-start | bytes 786440 | tf_op jit(solution)/shard_map/ppermute | solution.py:866
  218.2 21.6 %collective-permute-start.36 = (bf16[128,1024]{1,0:T(8,128)(2,1)S(1)}, bf16[128,1024]{1,0:T(8,128)(2,1)S(1)}, u32[]{:S(2)}, u32[]{:S(2)}) collective-permute-start(bf16[128,1024]{1,0:T(8,128)(2,1)S(1)} %get-tuple-element.184), channel_id=1, source_target_pairs={{0,24},{8,16},{16,8},{24,0},{1,25},{9,17},{17,9},{25,1},{2,26},{10... | collective-permute-start | bytes 786440 | tf_op jit(solution)/shard_map/ppermute | solution.py:866
  229.2 14.1 %collective-permute-start.39 = (bf16[32,896]{1,0:T(8,128)(2,1)S(1)}, bf16[32,896]{1,0:T(8,128)(2,1)S(1)}, u32[]{:S(2)}, u32[]{:S(2)}) collective-permute-start(bf16[32,896]{1,0:T(8,128)(2,1)S(1)} %get-tuple-element.196), channel_id=1, source_target_pairs={{0,8},{8,0},{16,24},{24,16},{1,9},{9,1},{17,25},{25,17},{2,10},{10... | collective-permute-start | bytes 172040 | tf_op jit(solution)/shard_map/ppermute | solution.py:866
  229.3 16.9 %collective-permute-start.40 = (bf16[32,896]{1,0:T(8,128)(2,1)S(1)}, bf16[32,896]{1,0:T(8,128)(2,1)S(1)}, u32[]{:S(2)}, u32[]{:S(2)}) collective-permute-start(bf16[32,896]{1,0:T(8,128)(2,1)S(1)} %get-tuple-element.197), channel_id=1, source_target_pairs={{0,16},{8,24},{16,0},{24,8},{1,17},{9,25},{17,1},{25,9},{2,18},{10... | collective-permute-start | bytes 172040 | tf_op jit(solution)/shard_map/ppermute | solution.py:866
  232.1 1.1 copy-start.2
  234.7 13.5 %all-to-all-start.4 = ((bf16[4,32,1024]{2,1,0:T(8,128)(2,1)}), bf16[4,32,1024]{2,1,0:T(8,128)(2,1)S(1)}, u32[]{:S(2)}, u32[]{:S(2)}) async-start(bf16[4,32,1024]{2,1,0:T(8,128)(2,1)} %get-tuple-element.210), calls=%async_computation.5 | async-start | bytes 524288 | tf_op jit(solution)/shard_map/all_to_all | solution.py:849
  238.1 8.1 %collective-permute-start.41 = (bf16[32,896]{1,0:T(8,128)(2,1)S(1)}, bf16[32,896]{1,0:T(8,128)(2,1)S(1)}, u32[]{:S(2)}, u32[]{:S(2)}) collective-permute-start(bf16[32,896]{1,0:T(8,128)(2,1)S(1)} %get-tuple-element.198), channel_id=1, source_target_pairs={{0,24},{8,16},{16,8},{24,0},{1,25},{9,17},{17,9},{25,1},{2,26},{10... | collective-permute-start | bytes 172040 | tf_op jit(solution)/shard_map/ppermute | solution.py:866
Sparse Core Ops, SparseCore 0:
  9.6 36.0 all-gather.5
  47.9 20.9 all-gather.7
  71.2 47.7 all-gather.9
  166.7 54.9 reduce-scatter.1

commit v5 on v4

--- a/solution.py
+++ b/solution.py
@@ -442,7 +442,8 @@
     return vec[row : row + 1, :].astype(f32)
 
 
-def q_prep_kernel(mover, pos, qkv, table, g1, b1, qb, vb, ob, g2, b2, db, ub, *outs):
+def q_prep_kernel(mover, pos, qkv, table, g1, b1, qb, vb, ob, g2, b2, db, ub, up, out_rows, down, o0, o1, o2, o3, cols, first):
+    outs = (o0, o1, o2, o3)
     z = pos[0]
     rw = qkv.shape[0]
     d = qkv.shape[1] // 3
@@ -461,26 +462,20 @@
             start = pl.multiple_of(part * d + (z ^ u) * width, width)
             out[:, part * width : (part + 1) * width] = qkv[:, pl.ds(start, width)]
         out[:, 3 * width :] = small
-
-
-def q_stack_kernel(mover, pos, b0, b1, b2, b3, out):
-    for u, block in enumerate((b0, b1, b2, b3)):
-        mover.start(block, out.at[pos[0] ^ u])
-
-
-def up_prep_kernel(mover, up, out):
     fr = up.shape[1] // (DEPTH * PLANE * 2)
     for k in range(PLANE):
         for c in range(2):
             for zz in range(DEPTH):
                 src = ((zz * PLANE + k) * 2 + c) * fr
                 dst = (c * DEPTH + zz) * fr
-                out[k, :, dst : dst + fr] = up[:, src : src + fr]
-
-
-def first_shard_kernel(mover, out_rows, down, out):
-    out[0] = out_rows[...]
-    out[1] = down[0 : out.shape[1], :]
+                cols[k, :, dst : dst + fr] = up[:, src : src + fr]
+    first[0] = out_rows[...]
+    first[1] = down[0:rw, :]
+
+
+def q_stack_kernel(mover, pos, b0, b1, b2, b3, out):
+    for u, block in enumerate((b0, b1, b2, b3)):
+        mover.start(block, out.at[pos[0] ^ u])
 
 
 def shard_kernel(mover, ups, down, out):
@@ -794,16 +789,16 @@
     out[...] = total.astype(bf16)
 
 
-def pair_kernel(mover, mine, o0, o1, out):
-    for k in range(PLANE):
-        out[k, 0:2] = (mine[0:2, k].astype(f32) + o0[:, k].astype(f32)).astype(bf16)
-        out[k, 2:4] = (mine[2:4, k].astype(f32) + o1[:, k].astype(f32)).astype(bf16)
-
-
-def quad_kernel(mover, pos, blocks, o0, o1, o2, o3, total):
-    found = blocks[0].astype(f32)
-    for k in range(1, PLANE):
-        found = found + blocks[k].astype(f32)
+def pair_kernel(mover, pos, mine, o0, o1, p0, p1, p2, p3, total):
+    yx = pos[1]
+    total[0:2] = (mine[0:2].astype(f32) + o0[...].astype(f32)).astype(bf16)
+    total[2:4] = (mine[2:4].astype(f32) + o1[...].astype(f32)).astype(bf16)
+    for k, out in enumerate((p0, p1, p2, p3)):
+        mover.start(total.at[:, yx ^ k], out)
+
+
+def quad_kernel(mover, pos, b0, b1, b2, b3, o0, o1, o2, o3, total):
+    found = b0[...].astype(f32) + b1[...].astype(f32) + b2[...].astype(f32) + b3[...].astype(f32)
     total[...] = found.astype(bf16)
     for u, out in enumerate((o0, o1, o2, o3)):
         out[...] = total[pos[0] ^ u]
@@ -836,7 +831,7 @@
 
 
 COSTS = {
-    "q_prep_kernel": (1, 4), "q_stack_kernel": (1, 4), "up_prep_kernel": (1, 4), "shard_kernel": (1, 4), "first_shard_kernel": (1, 4), "qkv_kernel": (5, 20),
+    "q_prep_kernel": (3, 6), "q_stack_kernel": (1, 4), "up_prep_kernel": (1, 4), "shard_kernel": (1, 4), "first_shard_kernel": (1, 4), "qkv_kernel": (5, 20),
     "attend_kernel": (9, 24), "out_kernel": (2, 12), "norm_kernel": (2, 8), "ffn_kernel": (8, 32), "ffn_grad_kernel": (8, 32),
     "branch_kernel": (2, 12), "out_back_kernel": (3, 12), "attend_back_kernel": (15, 32),
     "qkv_back_kernel": (10, 28), "first_back_kernel": (2, 8), "layer_out_kernel": (1, 8),
@@ -908,18 +903,16 @@
     call = functools.partial(run, order)
     side = width + -(-max(rw, fr) // 128) * 128
 
-    q_rows = along(
-        call(
-            q_prep_kernel,
-            [((rw, side), bf16)] * 4,
-            [pos]
-            + far((qkv_weight, lead_table, ln1_gain, ln1_bias, q_bias, v_bias, out_bias, ln2_gain, ln2_bias, down_bias, up_bias)),
-        )
-    )
+    *q_rows, up_cols, first_shard = call(
+        q_prep_kernel,
+        [((rw, side), bf16)] * 4 + [((PLANE, rw, ff), bf16), ((2, rw, d), bf16, "far")],
+        [pos]
+        + far((qkv_weight, lead_table, ln1_gain, ln1_bias, q_bias, v_bias, out_bias, ln2_gain, ln2_bias, down_bias, up_bias))
+        + far((up_weight, out_weight, down_weight)),
+    )
+    q_rows = along(q_rows)
     toks = lax.all_gather(tok, "z", axis=0)
-    (first_shard,) = call(first_shard_kernel, [((2, rw, d), bf16, "far")], [out_weight, down_weight])
     first = lax.all_gather(first_shard, ("z", "g"), axis=0).reshape(DEPTH, 2, 2, rw, d)
-    (up_cols,) = call(up_prep_kernel, [((PLANE, rw, ff), bf16)], [up_weight])
     up_cols = trade(up_cols, PLANE_AXES)
     (q_stack,) = call(q_stack_kernel, [((DEPTH, rw, side), bf16)], [pos, *q_rows], after=[up_cols])
     q_plane = across((q_stack,) * PLANE)
@@ -1002,11 +995,15 @@
         [((3 * PLANE, head, span), bf16), ((rw, d), f32), ((DEPTH, PLANE, 2, rw, side), bf16)],
     )
     returned = along((r0, r1, r2, r3))
-    (quads,) = call(
-        pair_kernel, [((PLANE, DEPTH, rw, side), bf16)], [mine, core_swap(o0), core_swap(o1)]
-    )
-    quads = trade(quads, PLANE_AXES)
-    cols = along(call(quad_kernel, [((rw, side), bf16)] * 4, [pos, quads], [((DEPTH, rw, side), bf16)]))
+    quads = across(
+        call(
+            pair_kernel,
+            [((DEPTH, rw, side), bf16)] * 4,
+            [pos, mine, core_swap(o0), core_swap(o1)],
+            [((DEPTH, PLANE, rw, side), bf16)],
+        )
+    )
+    cols = along(call(quad_kernel, [((rw, side), bf16)] * 4, [pos, *quads], [((DEPTH, rw, side), bf16)]))
     ups, d_down, d_out_weight = call(
         ffn_last_kernel, [((PLANE, rw, ff), bf16), ((fr, d), f32), ((rw, d), f32)], [ff_grad]
     )

time: 257 us -> 251 us (0.977)
  local copies, waits for them, and re-layouts: 5.63 us -> 2.9 us
    ppermute x7 -> x8, waiting for transfers between devices: 19.2 us -> 29.2 us  [across(): lax.ppermute(blocks[2], 'y', swap)]
    all_to_all x5 -> x4, waiting for transfers between devices: 8.15 us -> 0.01 us  [trade(): return lax.all_to_all(blocks, axes, split_axis=0, concat_axis=0, tiled=True)]
    all_to_all x5 -> x4, starting transfers between devices: 20.1 us -> 16.4 us  [trade(): return lax.all_to_all(blocks, axes, split_axis=0, concat_axis=0, tiled=True)]
    ppermute x7 -> x8, starting transfers between devices: 5.49 us -> 8.67 us  [across(): lax.ppermute(blocks[2], 'y', swap)]
    ppermute x7 -> x8, waiting for transfers between devices: 18.8 us -> 16 us  [across(): lax.ppermute(blocks[3], ('y', 'x'), [(i, i ^ 3) for i in range(PLANE)])]
    unnamed x24 -> x14, local copies, waits for them, and re-layouts: 4.52 us -> 1.8 us
    ppermute x7 -> x8, starting transfers between devices: 7.85 us -> 10.5 us  [across(): lax.ppermute(blocks[1], 'x', swap)]
    ppermute x7 -> x8, starting transfers between devices: 13.8 us -> 12.1 us  [across(): lax.ppermute(blocks[3], ('y', 'x'), [(i, i ^ 3) for i in range(PLANE)])]
  transfers between devices with their start and end apart: 51 -> 53, of which waited for: 25 -> 25; matrix products, arithmetic and copies ran while one was open for 0% -> 0% of each run, Pallas kernels for 28% -> 28%
where the time goes in v5:
time: 251 us
  Pallas kernels  87 us (35%)
  waiting for transfers between devices  74 us (29%)
  starting transfers between devices  72.4 us (29%)
  between operations  14.2 us (6%)
  local copies, waits for them, and re-layouts  2.9 us (1%)
    pallas_call x20, Pallas kernels, run(): pl.pallas_call(body, name=name, out_shape=[HBM(o[0], o[1]) if o[2] else j...  87 us
    ppermute x8, waiting for transfers between devices, across(): lax.ppermute(blocks[2], 'y', swap)  29.2 us
    ppermute x15, starting transfers between devices, to_depth(): return lax.ppermute(block, 'z', [(i, i ^ step) for i in range(DEPTH)])  23.8 us
    ppermute x15, waiting for transfers between devices, to_depth(): return lax.ppermute(block, 'z', [(i, i ^ step) for i in range(DEPTH)])  20.5 us
    all_to_all x4, starting transfers between devices, trade(): return lax.all_to_all(blocks, axes, split_axis=0, concat_axis=0, tiled=True)  16.4 us
    ppermute x8, waiting for transfers between devices, across(): lax.ppermute(blocks[3], ('y', 'x'), [(i, i ^ 3) for i in range(PLANE)])  16 us
    ppermute x8, starting transfers between devices, across(): lax.ppermute(blocks[3], ('y', 'x'), [(i, i ^ 3) for i in range(PLANE)])  12.1 us
    ppermute x8, starting transfers between devices, across(): lax.ppermute(blocks[1], 'x', swap)  10.5 us
  transfers between devices with their start and end apart: 53, of which 25 were waited for; matrix products, arithmetic and copies ran while one was open for 0% of the time, Pallas kernels for 28%

profile of v5, /device:TPU:0, one launch (start us, length us, event | category | flops | bytes accessed | tf_op | source)
XLA Modules:
  0.0 250.5 jit_solution(18311123006827808366)
XLA Ops:
  8.0 3.8 %q_prep_kernel.1 = (bf16[32,896]{1,0:T(8,128)(2,1)S(1)}, bf16[32,896]{1,0:T(8,128)(2,1)S(1)}, bf16[32,896]{1,0:T(8,128)(2,1)S(1)}, bf16[32,896]{1,0:T(8,128)(2,1...) custom-call(s32[3]{0:T(128)S(1)} %pad_add_fusion.refs_0_, ...), custom_call_target="tpu_custom_call" | custom-call | flops 3300000000 | bytes 10800000 | tf_op jit(solution)/shard_map/q_prep_kernel/pallas_call | solution.py:400
  11.9 5.2 %all-to-all-start = ((bf16[4,32,1024]{2,1,0:T(8,128)(2,1)}), bf16[4,32,1024]{2,1,0:T(8,128)(2,1)S(1)}, u32[]{:S(2)}, u32[]{:S(2)}) async-start(bf16[4,32,1024]{2,1,0:T(8,128)(2,1)} %get-tuple-element.121), calls=%async_computation | async-start | bytes 524288 | tf_op jit(solution)/shard_map/all_to_all | solution.py:844
  17.0 1.6 collective-permute-start
  18.6 2.6 %collective-permute-start.1 = (bf16[32,896]{1,0:T(8,128)(2,1)S(1)}, bf16[32,896]{1,0:T(8,128)(2,1)S(1)}, u32[]{:S(2)}, u32[]{:S(2)}) collective-permute-start(bf16[32,896]{1,0:T(8,128)(2,1)S(1)} %get-tuple-element.119), channel_id=1, source_target_pairs={{0,16},{8,24},{16,0},{24,8},{1,17},{9,25},{17,1},{25,9},{2,18},{10... | collective-permute-start | bytes 172040 | tf_op jit(solution)/shard_map/ppermute | solution.py:861
  21.4 6.8 %collective-permute-done.1.refs_3_ = bf16[32,896]{1,0:T(8,128)(2,1)S(1)} collective-permute-done((bf16[32,896]{1,0:T(8,128)(2,1)S(1)}, bf16[32,896]{1,0:T(8,128)(2,1)S(1)}, u32[]{:S(2)}, u32[]{:S(2)}) %collective-permute-start.1) | collective-permute-done | bytes 57376 | tf_op jit(solution)/shard_map/ppermute | solution.py:861
  29.1 1.4 q_stack_kernel.1
  30.5 3.4 %collective-permute-start.5 = (bf16[4,32,896]{2,1,0:T(8,128)(2,1)S(1)}, bf16[4,32,896]{2,1,0:T(8,128)(2,1)S(1)}, u32[]{:S(2)}, u32[]{:S(2)}) collective-permute-start(bf16[4,32,896]{2,1,0:T(8,128)(2,1)S(1)} %get-tuple-element.123.refs_4_), channel_id=1, source_target_pairs={{0,6},{2,4},{4,2},{6,0},{1,7},{3,5},{5,3},{7,1},{8,14},{10,12},{12... | collective-permute-start | bytes 688136 | tf_op jit(solution)/shard_map/ppermute | solution.py:856
  34.6 4.8 %collective-permute-done.5.refs_7_ = bf16[4,32,896]{2,1,0:T(8,128)(2,1)S(1)} collective-permute-done((bf16[4,32,896]{2,1,0:T(8,128)(2,1)S(1)}, bf16[4,32,896]{2,1,0:T(8,128)(2,1)S(1)}, u32[]{:S(2)}, u32[]{:S(2)}) %collective-permute-start.5) | collective-permute-done | bytes 229408 | tf_op jit(solution)/shard_map/ppermute | solution.py:856
  39.4 2.3 collective-permute-done.4.refs_6_
  43.6 6.1 %qkv_kernel.1 = (bf16[512,1024]{1,0:T(8,128)(2,1)}, bf16[4,4,2,32,768]{4,3,2,1,0:T(8,128)(2,1)}, f32[24,1024]{1,0:T(8,128)S(1)}, f32[1,1024]{1,0:T(1,128)S(1)}, ...) custom-call(s32[3]{0:T(128)S(1)} %pad_add_fusion.refs_0_, ...), custom_call_target="tpu_custom_call" | custom-call | flops 5500000256 | bytes 18000000 | tf_op jit(solution)/shard_map/qkv_kernel/pallas_call | solution.py:400
  49.7 1.4 shard_kernel.1
  51.1 1.9 collective-permute-start.10
  53.0 1.5 collective-permute-start.11
  55.8 4.2 %all-to-all-start.1 = ((bf16[4,128,1024]{2,1,0:T(8,128)(2,1)}), bf16[4,128,1024]{2,1,0:T(8,128)(2,1)}, u32[]{:S(2)}, u32[]{:S(2)}) async-start(bf16[4,128,1024]{2,1,0:T(8,128)(2,1)} %broadcast_in_dim.14), calls=%async_computation.1 | async-start | bytes 2097152 | tf_op jit(solution)/shard_map/all_to_all | solution.py:844
  60.1 9.6 %collective-permute-done.11.refs_3_ = bf16[192,512]{1,0:T(8,128)(2,1)S(1)} collective-permute-done((bf16[192,512]{1,0:T(8,128)(2,1)S(1)}, bf16[192,512]{1,0:T(8,128)(2,1)S(1)}, u32[]{:S(2)}, u32[]{:S(2)}) %collective-permute-start.11) | collective-permute-done | bytes 196640 | tf_op jit(solution)/shard_map/ppermute | solution.py:855
  69.6 11.2 %attend_kernel.1 = (bf16[64,512]{1,0:T(8,128)(2,1)S(1)}, bf16[64,512]{1,0:T(8,128)(2,1)S(1)}, bf16[64,512]{1,0:T(8,128)(2,1)S(1)}, bf16[64,512]{1,0:T(8,128)(2,1...) custom-call(s32[1,128]{1,0:T(1,128)S(1)} %copy-done.5, bf16[192,512]{1,0:T(8,128)(2,1)S(1)} %get-tuple-element.126.refs_1_, ...), custom_call_target="tpu_custom_call" | custom-call | flops 9900000256 | bytes 32400000 | tf_op jit(solution)/shard_map/attend_kernel/pallas_call | solution.py:400
  80.8 2.0 collective-permute-start.13
  82.9 1.4 collective-permute-start.14
  84.3 1.4 collective-permute-start.15
  85.7 3.0 %collective-permute-done.13.refs_2_ = bf16[64,512]{1,0:T(8,128)(2,1)S(1)} collective-permute-done((bf16[64,512]{1,0:T(8,128)(2,1)S(1)}, bf16[64,512]{1,0:T(8,128)(2,1)S(1)}, u32[]{:S(2)}, u32[]{:S(2)}) %collective-permute-start.13) | collective-permute-done | bytes 65568 | tf_op jit(solution)/shard_map/ppermute | solution.py:861
  88.6 2.7 %collective-permute-done.14.refs_3_ = bf16[64,512]{1,0:T(8,128)(2,1)S(1)} collective-permute-done((bf16[64,512]{1,0:T(8,128)(2,1)S(1)}, bf16[64,512]{1,0:T(8,128)(2,1)S(1)}, u32[]{:S(2)}, u32[]{:S(2)}) %collective-permute-start.14) | collective-permute-done | bytes 65568 | tf_op jit(solution)/shard_map/ppermute | solution.py:861
  91.4 2.1 collective-permute-done.15.refs_4_
  93.5 2.6 %out_kernel.1 = (f32[128,1024]{1,0:T(8,128)S(1)}, bf16[128,1024]{1,0:T(8,128)(2,1)S(1)}, bf16[128,1024]{1,0:T(8,128)(2,1)S(1)}, bf16[128,1024]{1,0:T(8,128)(2,1)...) custom-call(s32[3]{0:T(128)S(1)} %pad_add_fusion.refs_0_, ...), custom_call_target="tpu_custom_call" | custom-call | flops 2200000000 | bytes 7200000 | tf_op jit(solution)/shard_map/out_kernel/pallas_call | solution.py:400
  96.2 2.9 %collective-permute-start.17 = (bf16[128,1024]{1,0:T(8,128)(2,1)S(1)}, bf16[128,1024]{1,0:T(8,128)(2,1)S(1)}, u32[]{:S(2)}, u32[]{:S(2)}) collective-permute-start(bf16[128,1024]{1,0:T(8,128)(2,1)S(1)} %get-tuple-element.140), channel_id=1, source_target_pairs={{0,4},{4,0},{1,5},{5,1},{2,6},{6,2},{3,7},{7,3},{8,12},{12,8},{9,1... | collective-permute-start | bytes 786440 | tf_op jit(solution)/shard_map/ppermute | solution.py:855
  99.2 1.4 collective-permute-start.18
  100.6 2.0 collective-permute-done.16.refs_5_
  102.6 7.2 %collective-permute-done.17.refs_6_ = bf16[128,1024]{1,0:T(8,128)(2,1)S(1)} collective-permute-done((bf16[128,1024]{1,0:T(8,128)(2,1)S(1)}, bf16[128,1024]{1,0:T(8,128)(2,1)S(1)}, u32[]{:S(2)}, u32[]{:S(2)}) %collective-permute-start.17) | collective-permute-done | bytes 262176 | tf_op jit(solution)/shard_map/ppermute | solution.py:855
  109.8 2.9 %norm_kernel.1 = (f32[128,1024]{1,0:T(8,128)}, bf16[128,1024]{1,0:T(8,128)(2,1)S(1)}, f32[8,128]{1,0:T(8,128)S(1)}) custom-call(s32[4]{0:T(128)S(1)} %bitcast.14, s32[1,128]{1,0:T(1,128)S(1)} %copy-done.5, f32[24,1024]{1,0:T(8,128)S(1)} %get-tuple-element.125.refs_2_.refs_0_.refs_3_, bf16[128,1024]{1,0:T(8,128)(2,1)} %bitcast.20, ...), custom_call_target="tpu_custom_call" | custom-call | flops 2200000000 | bytes 7200000 | tf_op jit(solution)/shard_map/norm_kernel/pallas_call | solution.py:400
  112.7 4.2 %collective-permute-start.21 = (bf16[128,1024]{1,0:T(8,128)(2,1)S(1)}, bf16[128,1024]{1,0:T(8,128)(2,1)S(1)}, u32[]{:S(2)}, u32[]{:S(2)}) collective-permute-start(bf16[128,1024]{1,0:T(8,128)(2,1)S(1)} %get-tuple-element.145.refs_2_.refs_3_), channel_id=1, source_target_pairs={{0,6},{2,4},{4,2},{6,0},{1,7},{3,5},{5,3},{7,1},{8,14},{10,12},{12... | collective-permute-start | bytes 786440 | tf_op jit(solution)/shard_map/ppermute | solution.py:856
  117.6 3.8 %collective-permute-done.21.refs_5_.refs_6_ = bf16[128,1024]{1,0:T(8,128)(2,1)S(1)} collective-permute-done((bf16[128,1024]{1,0:T(8,128)(2,1)S(1)}, bf16[128,1024]{1,0:T(8,128)(2,1)S(1)}, u32[]{:S(2)}, u32[]{:S(2)}) %collective-permute-start.21) | collective-permute-done | bytes 262176 | tf_op jit(solution)/shard_map/ppermute | solution.py:856
  121.4 2.7 %collective-permute-done.20.refs_4_.refs_5_ = bf16[128,1024]{1,0:T(8,128)(2,1)S(1)} collective-permute-done((bf16[128,1024]{1,0:T(8,128)(2,1)S(1)}, bf16[128,1024]{1,0:T(8,128)(2,1)S(1)}, u32[]{:S(2)}, u32[]{:S(2)}) %collective-permute-start.20) | collective-permute-done | bytes 262176 | tf_op jit(solution)/shard_map/ppermute | solution.py:855
  124.1 8.5 %ffn_kernel.1 = (bf16[512,1024]{1,0:T(8,128)(2,1)S(1)}, bf16[512,1024]{1,0:T(8,128)(2,1)S(1)}, f32[128,1024]{1,0:T(8,128)S(1)}, bf16[128,1024]{1,0:T(8,128)(2,1)...) custom-call(s32[3]{0:T(128)S(1)} %pad_add_fusion.refs_0_, ...), custom_call_target="tpu_custom_call" | custom-call | flops 8800000000 | bytes 28800000 | tf_op jit(solution)/shard_map/ffn_kernel/pallas_call | solution.py:400
  132.7 2.1 collective-permute-start.22
  136.3 7.7 %ffn_grad_kernel.1 = (bf16[4,2,9,32,1024]{4,3,2,1,0:T(8,128)(2,1)}, bf16[4,128,1024]{2,1,0:T(8,128)(2,1)}, f32[8,128]{1,0:T(8,128)S(1)}) custom-call(s32[3]{0:T(128)S(1)} %pad_add_fusion.refs_0_, bf16[512,1024]{1,0:T(8,128)(2,1)S(1)} %get-tuple-element.148.refs_1_, bf16[512,1024]{1,0:T(8,128)(2,1)S(1)} %get-tuple-element.149.refs_2_, ...), custom_call_target="tpu_custom_call" | custom-call | flops 8800000000 | bytes 28800000 | tf_op jit(solution)/shard_map/ffn_grad_kernel/pallas_call | solution.py:400
  144.1 2.8 %collective-permute-done.23.refs_5_ = bf16[128,1024]{1,0:T(8,128)(2,1)S(1)} collective-permute-done((bf16[128,1024]{1,0:T(8,128)(2,1)S(1)}, bf16[128,1024]{1,0:T(8,128)(2,1)S(1)}, u32[]{:S(2)}, u32[]{:S(2)}) %collective-permute-start.23) | collective-permute-done | bytes 262176 | tf_op jit(solution)/shard_map/ppermute | solution.py:855
  146.9 3.0 %branch_kernel.1 = (f32[128,1024]{1,0:T(8,128)}, bf16[128,1024]{1,0:T(8,128)(2,1)S(1)}, f32[8,1024]{1,0:T(8,128)S(1)}, f32[8,128]{1,0:T(8,128)S(1)}) custom-call(f32[24,1024]{1,0:T(8,128)S(1)} %get-tuple-element.125.refs_2_.refs_0_.refs_3_, f32[128,1024]{1,0:T(8,128)} %get-tuple-element.143.refs_1_, bf16[128,1024]{1,0:T(8,128)(2,1)} %bitcast.18, ...), custom_call_target="tpu_custom_call" | custom-call | flops 2200000000 | bytes 7200000 | tf_op jit(solution)/shard_map/branch_kernel/pallas_call | solution.py:400
  150.6 2.9 %collective-permute-start.25 = (bf16[128,1024]{1,0:T(8,128)(2,1)S(1)}, bf16[128,1024]{1,0:T(8,128)(2,1)S(1)}, u32[]{:S(2)}, u32[]{:S(2)}) collective-permute-start(bf16[128,1024]{1,0:T(8,128)(2,1)S(1)} %get-tuple-element.159.refs_3_), channel_id=1, source_target_pairs={{0,2},{2,0},{1,3},{3,1},{4,6},{6,4},{5,7},{7,5},{8,10},{10,8},{9,1... | collective-permute-start | bytes 786440 | tf_op jit(solution)/shard_map/ppermute | solution.py:854
  153.5 3.9 %collective-permute-done.27.refs_6_ = bf16[128,1024]{1,0:T(8,128)(2,1)S(1)} collective-permute-done((bf16[128,1024]{1,0:T(8,128)(2,1)S(1)}, bf16[128,1024]{1,0:T(8,128)(2,1)S(1)}, u32[]{:S(2)}, u32[]{:S(2)}) %collective-permute-start.27) | collective-permute-done | bytes 262176 | tf_op jit(solution)/shard_map/ppermute | solution.py:856
  157.4 1.9 collective-permute-done.26.refs_5_
  159.2 2.7 %out_back_kernel.1 = (bf16[64,512]{1,0:T(8,128)(2,1)S(1)}, bf16[64,512]{1,0:T(8,128)(2,1)S(1)}, bf16[64,512]{1,0:T(8,128)(2,1)S(1)}, bf16[64,512]{1,0:T(8,128)(2...) custom-call(s32[3]{0:T(128)S(1)} %pad_add_fusion.refs_0_, ...), custom_call_target="tpu_custom_call", output_to_operand_aliasing={{4}: (7, {})} | custom-call | flops 3300000000 | bytes 10800000 | tf_op jit(solution)/shard_map/out_back_kernel/pallas_call | solution.py:400
  162.3 4.1 %collective-permute-start.30 = (bf16[64,512]{1,0:T(8,128)(2,1)S(1)}, bf16[64,512]{1,0:T(8,128)(2,1)S(1)}, u32[]{:S(2)}, u32[]{:S(2)}) collective-permute-start(bf16[64,512]{1,0:T(8,128)(2,1)S(1)} %get-tuple-element.165), channel_id=1, source_target_pairs={{0,24},{8,16},{16,8},{24,0},{1,25},{9,17},{17,9},{25,1},{2,26},{10... | collective-permute-start | bytes 196616 | tf_op jit(solution)/shard_map/ppermute | solution.py:861
  166.4 3.5 %all-to-all-start.2 = ((bf16[4,128,1024]{2,1,0:T(8,128)(2,1)}), bf16[4,128,1024]{2,1,0:T(8,128)(2,1)S(1)}, u32[]{:S(2)}, u32[]{:S(2)}) async-start(bf16[4,128,1024]{2,1,0:T(8,128)(2,1)} %get-tuple-element.151), calls=%async_computation.2 | async-start | bytes 2097152 | tf_op jit(solution)/shard_map/all_to_all | solution.py:844
  170.0 13.5 %attend_back_kernel.1 = (bf16[192,512]{1,0:T(8,128)(2,1)S(1)}, bf16[192,512]{1,0:T(8,128)(2,1)S(1)}, bf16[192,512]{1,0:T(8,128)(2,1)S(1)}, bf16[192,512]{1,0:T(8,128)(2,1)S(1)}, f32[8,128]{1,0:T(8,128)S(1)}) custom-call(s32[1,128]{1,0:T(1,128)S(1)} %copy-done.5, bf16[192,512]{1,0:T(8,128)(2,1)S(1)} %get-tuple-element.126.refs_1_, ...), custom_call_target="tpu_custom_call" | custom-call | flops 16499999744 | bytes 54000000 | tf_op jit(solution)/shard_map/attend_back_kernel/pallas_call | solution.py:400
  183.5 2.0 collective-permute-start.31
  185.5 1.5 collective-permute-start.32
  187.1 2.5 layer_out_kernel.1
  189.6 2.7 %collective-permute-done.32.refs_9_ = bf16[192,512]{1,0:T(8,128)(2,1)S(1)} collective-permute-done((bf16[192,512]{1,0:T(8,128)(2,1)S(1)}, bf16[192,512]{1,0:T(8,128)(2,1)S(1)}, u32[]{:S(2)}, u32[]{:S(2)}) %collective-permute-start.32) | collective-permute-done | bytes 196640 | tf_op jit(solution)/shard_map/ppermute | solution.py:855
  192.3 1.2 collective-permute-done.33.refs_10_
  193.6 8.0 %qkv_back_kernel.1 = (f32[128,1024]{1,0:T(8,128)S(1)}, bf16[128,1024]{1,0:T(8,128)(2,1)S(1)}, bf16[128,1024]{1,0:T(8,128)(2,1)S(1)}, bf16[128,1024]{1,0:T(8,128)...) custom-call(s32[3]{0:T(128)S(1)} %pad_add_fusion.refs_0_, ...), custom_call_target="tpu_custom_call" | custom-call | flops 11000000512 | bytes 36000000 | tf_op jit(solution)/shard_map/qkv_back_kernel/pallas_call | solution.py:400
  202.2 1.3 collective-permute-done.37.refs_2_
  204.2 1.9 pair_kernel.1
  208.0 1.8 collective-permute-start.41
  209.7 3.1 %collective-permute-start.35 = (bf16[128,1024]{1,0:T(8,128)(2,1)S(1)}, bf16[128,1024]{1,0:T(8,128)(2,1)S(1)}, u32[]{:S(2)}, u32[]{:S(2)}) collective-permute-start(bf16[128,1024]{1,0:T(8,128)(2,1)S(1)} %get-tuple-element.182), channel_id=1, source_target_pairs={{0,16},{8,24},{16,0},{24,8},{1,17},{9,25},{17,1},{25,9},{2,18},{10... | collective-permute-start | bytes 786440 | tf_op jit(solution)/shard_map/ppermute | solution.py:861
  212.8 1.9 collective-permute-done.39.refs_2_
  214.7 2.5 %collective-permute-start.36 = (bf16[128,1024]{1,0:T(8,128)(2,1)S(1)}, bf16[128,1024]{1,0:T(8,128)(2,1)S(1)}, u32[]{:S(2)}, u32[]{:S(2)}) collective-permute-start(bf16[128,1024]{1,0:T(8,128)(2,1)S(1)} %get-tuple-element.183), channel_id=1, source_target_pairs={{0,24},{8,16},{16,8},{24,0},{1,25},{9,17},{17,9},{25,1},{2,26},{10... | collective-permute-start | bytes 786440 | tf_op jit(solution)/shard_map/ppermute | solution.py:861
  217.2 2.2 collective-permute-done.41.refs_4_
  219.5 1.3 quad_kernel.1
  220.9 3.4 %collective-permute-start.43 = (bf16[32,896]{1,0:T(8,128)(2,1)S(1)}, bf16[32,896]{1,0:T(8,128)(2,1)S(1)}, u32[]{:S(2)}, u32[]{:S(2)}) collective-permute-start(bf16[32,896]{1,0:T(8,128)(2,1)S(1)} %get-tuple-element.199), channel_id=1, source_target_pairs={{0,16},{8,24},{16,0},{24,8},{1,17},{9,25},{17,1},{25,9},{2,18},{10... | collective-permute-start | bytes 172040 | tf_op jit(solution)/shard_map/ppermute | solution.py:861
  225.4 1.5 ffn_last_kernel.1
  226.9 3.4 %all-to-all-start.3 = ((bf16[4,32,1024]{2,1,0:T(8,128)(2,1)}), bf16[4,32,1024]{2,1,0:T(8,128)(2,1)S(1)}, u32[]{:S(2)}, u32[]{:S(2)}) async-start(bf16[4,32,1024]{2,1,0:T(8,128)(2,1)} %get-tuple-element.212), calls=%async_computation.4 | async-start | bytes 524288 | tf_op jit(solution)/shard_map/all_to_all | solution.py:844
  231.4 3.5 %first_back_kernel.1 = (f32[128,1024]{1,0:T(8,128)}, f32[8,128]{1,0:T(8,128)S(1)}) custom-call(s32[4]{0:T(128)S(1)} %bitcast.16, s32[1,128]{1,0:T(1,128)S(1)} %copy-done.5, f32[24,1024]{1,0:T(8,128)S(1)} %get-tuple-element.125.refs_2_.refs_0_.refs_3_, bf16[128,1024]{1,0:T(8,128)(2,1)} %bitcast.21, f32[128,1024]{1,0:T(8,128)} %get-tuple-element.170.refs_11_.refs_4_, ...), custom_call_target="tpu_custom_call" | custom-call | flops 2200000000 | bytes 7200000 | tf_op jit(solution)/shard_map/first_back_kernel/pallas_call | solution.py:400
  234.9 5.7 %collective-permute-done.43.refs_3_ = bf16[32,896]{1,0:T(8,128)(2,1)S(1)} collective-permute-done((bf16[32,896]{1,0:T(8,128)(2,1)S(1)}, bf16[32,896]{1,0:T(8,128)(2,1)S(1)}, u32[]{:S(2)}, u32[]{:S(2)}) %collective-permute-start.43) | collective-permute-done | bytes 57376 | tf_op jit(solution)/shard_map/ppermute | solution.py:861
  240.6 1.9 qkv_join_kernel.1
  242.5 1.4 up_join_kernel.1
  (82 shorter events, 14.4 us)
Async XLA Ops:
  7.2 36.4 %all-gather.6.cloned.1.call-start = ((), (), s32[]{:S(2)}) async-start(), calls=%async_computation.5 | async-start | bytes 1310720 | tf_op jit(solution)/shard_map/all_gather | solution.py:914
  7.9 77.8 %all-gather.8.cloned.1.call-start = ((), (), s32[]{:S(2)}) async-start(), calls=%async_computation.7 | async-start | bytes 1179648 | tf_op jit(solution)/shard_map/all_gather | solution.py:915
  11.8 31.7 %copy-start.4 = (s32[1,4]{1,0:T(1,128)S(1)}, s32[1,4]{1,0:T(1,128)}, u32[]{:S(2)}) copy-start(s32[1,4]{1,0:T(1,128)} %param.20) | copy-start | bytes 52
  11.8 31.7 %copy-start.5 = (s32[1,128]{1,0:T(1,128)S(1)}, s32[1,128]{1,0:T(1,128)}, u32[]{:S(2)}) copy-start(s32[1,128]{1,0:T(1,128)} %refs_1_.7) | copy-start | bytes 1540
  11.9 16.5 %all-to-all-start = ((bf16[4,32,1024]{2,1,0:T(8,128)(2,1)}), bf16[4,32,1024]{2,1,0:T(8,128)(2,1)S(1)}, u32[]{:S(2)}, u32[]{:S(2)}) async-start(bf16[4,32,1024]{2,1,0:T(8,128)(2,1)} %get-tuple-element.121), calls=%async_computation | async-start | bytes 524288 | tf_op jit(solution)/shard_map/all_to_all | solution.py:844
  17.0 107.1 %all-gather.10.cloned.1.call-start = ((), (), s32[]{:S(2)}) async-start(), calls=%async_computation.8 | async-start | bytes 4128768 | tf_op jit(solution)/shard_map/all_gather | solution.py:928
  17.0 4.4 %collective-permute-start = (bf16[32,896]{1,0:T(8,128)(2,1)S(1)}, bf16[32,896]{1,0:T(8,128)(2,1)S(1)}, u32[]{:S(2)}, u32[]{:S(2)}) collective-permute-start(bf16[32,896]{1,0:T(8,128)(2,1)S(1)} %get-tuple-element.118), channel_id=1, source_target_pairs={{0,8},{8,0},{16,24},{24,16},{1,9},{9,1},{17,25},{25,17},{2,10},{10... | collective-permute-start | bytes 172040 | tf_op jit(solution)/shard_map/ppermute | solution.py:861
  18.6 9.7 %collective-permute-start.1 = (bf16[32,896]{1,0:T(8,128)(2,1)S(1)}, bf16[32,896]{1,0:T(8,128)(2,1)S(1)}, u32[]{:S(2)}, u32[]{:S(2)}) collective-permute-start(bf16[32,896]{1,0:T(8,128)(2,1)S(1)} %get-tuple-element.119), channel_id=1, source_target_pairs={{0,16},{8,24},{16,0},{24,8},{1,17},{9,25},{17,1},{25,9},{2,18},{10... | collective-permute-start | bytes 172040 | tf_op jit(solution)/shard_map/ppermute | solution.py:861
  21.2 7.2 %collective-permute-start.2 = (bf16[32,896]{1,0:T(8,128)(2,1)S(1)}, bf16[32,896]{1,0:T(8,128)(2,1)S(1)}, u32[]{:S(2)}, u32[]{:S(2)}) collective-permute-start(bf16[32,896]{1,0:T(8,128)(2,1)S(1)} %get-tuple-element.120), channel_id=1, source_target_pairs={{0,24},{8,16},{16,8},{24,0},{1,25},{9,17},{17,9},{25,1},{2,26},{10... | collective-permute-start | bytes 172040 | tf_op jit(solution)/shard_map/ppermute | solution.py:861
  28.4 0.7 copy-start
  30.5 8.9 %collective-permute-start.5 = (bf16[4,32,896]{2,1,0:T(8,128)(2,1)S(1)}, bf16[4,32,896]{2,1,0:T(8,128)(2,1)S(1)}, u32[]{:S(2)}, u32[]{:S(2)}) collective-permute-start(bf16[4,32,896]{2,1,0:T(8,128)(2,1)S(1)} %get-tuple-element.123.refs_4_), channel_id=1, source_target_pairs={{0,6},{2,4},{4,2},{6,0},{1,7},{3,5},{5,3},{7,1},{8,14},{10,12},{12... | collective-permute-start | bytes 688136 | tf_op jit(solution)/shard_map/ppermute | solution.py:856
  34.0 7.8 %collective-permute-start.4 = (bf16[4,32,896]{2,1,0:T(8,128)(2,1)S(1)}, bf16[4,32,896]{2,1,0:T(8,128)(2,1)S(1)}, u32[]{:S(2)}, u32[]{:S(2)}) collective-permute-start(bf16[4,32,896]{2,1,0:T(8,128)(2,1)S(1)} %get-tuple-element.123.refs_4_), channel_id=1, source_target_pairs={{0,4},{4,0},{1,5},{5,1},{2,6},{6,2},{3,7},{7,3},{8,12},{12,8},{9,1... | collective-permute-start | bytes 688136 | tf_op jit(solution)/shard_map/ppermute | solution.py:855
  34.5 7.5 %collective-permute-start.3 = (bf16[4,32,896]{2,1,0:T(8,128)(2,1)S(1)}, bf16[4,32,896]{2,1,0:T(8,128)(2,1)S(1)}, u32[]{:S(2)}, u32[]{:S(2)}) collective-permute-start(bf16[4,32,896]{2,1,0:T(8,128)(2,1)S(1)} %get-tuple-element.123.refs_4_), channel_id=1, source_target_pairs={{0,2},{2,0},{1,3},{3,1},{4,6},{6,4},{5,7},{7,5},{8,10},{10,8},{9,1... | collective-permute-start | bytes 688136 | tf_op jit(solution)/shard_map/ppermute | solution.py:854
  34.6 7.6 %collective-permute-start.6 = (bf16[4,32,896]{2,1,0:T(8,128)(2,1)S(1)}, bf16[4,32,896]{2,1,0:T(8,128)(2,1)S(1)}, u32[]{:S(2)}, u32[]{:S(2)}) collective-permute-start(bf16[4,32,896]{2,1,0:T(8,128)(2,1)S(1)} %get-tuple-element.123.refs_4_), channel_id=1, source_target_pairs={{0,1},{1,0},{2,3},{3,2},{4,5},{5,4},{6,7},{7,6},{8,9},{9,8},{10,11... | collective-permute-start | bytes 688136 | tf_op jit(solution)/shard_map/ppermute | solution.py:869
  39.4 2.8 %collective-permute-start.9 = (bf16[4,32,896]{2,1,0:T(8,128)(2,1)S(1)}, bf16[4,32,896]{2,1,0:T(8,128)(2,1)S(1)}, u32[]{:S(2)}, u32[]{:S(2)}) collective-permute-start(bf16[4,32,896]{2,1,0:T(8,128)(2,1)S(1)} %collective-permute-done.5.refs_7_), channel_id=1, source_target_pairs={{0,1},{1,0},{2,3},{3,2},{4,5},{5,4},{6,7},{7,6},{8,9},{9,8},{10,11... | collective-permute-start | bytes 688136 | tf_op jit(solution)/shard_map/ppermute | solution.py:869
  41.7 1.5 collective-permute-start.8
  42.0 1.6 collective-permute-start.7
  43.5 6.1 %copy-start.1 = (bf16[4,32,1024]{2,1,0:T(8,128)(2,1)S(1)}, bf16[4,32,1024]{2,1,0:T(8,128)(2,1)}, u32[]{:S(2)}) copy-start(bf16[4,32,1024]{2,1,0:T(8,128)(2,1)} %copy-done) | copy-start | bytes 786436
  43.6 6.2 %copy-start.3 = (bf16[128,1024]{1,0:T(8,128)(2,1)S(1)}, bf16[128,1024]{1,0:T(8,128)(2,1)}, u32[]{:S(2)}) copy-start(bf16[128,1024]{1,0:T(8,128)(2,1)} %refs_1_.5) | copy-start | bytes 786436
  49.7 5.0 %copy-start.6 = (bf16[1,128,1024]{2,1,0:T(8,128)(2,1)S(1)}, bf16[1,128,1024]{2,1,0:T(8,128)(2,1)}, u32[]{:S(2)}) copy-start(bf16[1,128,1024]{2,1,0:T(8,128)(2,1)} %param.35) | copy-start | bytes 786436
  51.1 9.0 %collective-permute-start.10 = (bf16[192,512]{1,0:T(8,128)(2,1)S(1)}, bf16[192,512]{1,0:T(8,128)(2,1)S(1)}, u32[]{:S(2)}, u32[]{:S(2)}) collective-permute-start(bf16[192,512]{1,0:T(8,128)(2,1)S(1)} %get-tuple-element.127), channel_id=1, source_target_pairs={{0,2},{2,0},{1,3},{3,1},{4,6},{6,4},{5,7},{7,5},{8,10},{10,8},{9,1... | collective-permute-start | bytes 589832 | tf_op jit(solution)/shard_map/ppermute | solution.py:854
  53.0 16.6 %collective-permute-start.11 = (bf16[192,512]{1,0:T(8,128)(2,1)S(1)}, bf16[192,512]{1,0:T(8,128)(2,1)S(1)}, u32[]{:S(2)}, u32[]{:S(2)}) collective-permute-start(bf16[192,512]{1,0:T(8,128)(2,1)S(1)} %get-tuple-element.128), channel_id=1, source_target_pairs={{0,4},{4,0},{1,5},{5,1},{2,6},{6,2},{3,7},{7,3},{8,12},{12,8},{9,1... | collective-permute-start | bytes 589832 | tf_op jit(solution)/shard_map/ppermute | solution.py:855
  54.5 15.2 %collective-permute-start.12 = (bf16[192,512]{1,0:T(8,128)(2,1)S(1)}, bf16[192,512]{1,0:T(8,128)(2,1)S(1)}, u32[]{:S(2)}, u32[]{:S(2)}) collective-permute-start(bf16[192,512]{1,0:T(8,128)(2,1)S(1)} %get-tuple-element.129), channel_id=1, source_target_pairs={{0,6},{2,4},{4,2},{6,0},{1,7},{3,5},{5,3},{7,1},{8,14},{10,12},{12... | collective-permute-start | bytes 589832 | tf_op jit(solution)/shard_map/ppermute | solution.py:856
  55.8 29.9 %all-to-all-start.1 = ((bf16[4,128,1024]{2,1,0:T(8,128)(2,1)}), bf16[4,128,1024]{2,1,0:T(8,128)(2,1)}, u32[]{:S(2)}, u32[]{:S(2)}) async-start(bf16[4,128,1024]{2,1,0:T(8,128)(2,1)} %broadcast_in_dim.14), calls=%async_computation.1 | async-start | bytes 2097152 | tf_op jit(solution)/shard_map/all_to_all | solution.py:844
  60.0 164.3 %reduce-scatter.2.cloned.1.call-start = ((), (), s32[]{:S(2)}) async-start(), calls=%async_computation.6 | async-start | bytes 5308416 | tf_op jit(solution)/shard_map/reduce_scatter | solution.py:976
  80.8 7.8 %collective-permute-start.13 = (bf16[64,512]{1,0:T(8,128)(2,1)S(1)}, bf16[64,512]{1,0:T(8,128)(2,1)S(1)}, u32[]{:S(2)}, u32[]{:S(2)}) collective-permute-start(bf16[64,512]{1,0:T(8,128)(2,1)S(1)} %get-tuple-element.133), channel_id=1, source_target_pairs={{0,8},{8,0},{16,24},{24,16},{1,9},{9,1},{17,25},{25,17},{2,10},{10... | collective-permute-start | bytes 196616 | tf_op jit(solution)/shard_map/ppermute | solution.py:861
  82.9 8.5 %collective-permute-start.14 = (bf16[64,512]{1,0:T(8,128)(2,1)S(1)}, bf16[64,512]{1,0:T(8,128)(2,1)S(1)}, u32[]{:S(2)}, u32[]{:S(2)}) collective-permute-start(bf16[64,512]{1,0:T(8,128)(2,1)S(1)} %get-tuple-element.134), channel_id=1, source_target_pairs={{0,16},{8,24},{16,0},{24,8},{1,17},{9,25},{17,1},{25,9},{2,18},{10... | collective-permute-start | bytes 196616 | tf_op jit(solution)/shard_map/ppermute | solution.py:861
  84.3 9.2 %collective-permute-start.15 = (bf16[64,512]{1,0:T(8,128)(2,1)S(1)}, bf16[64,512]{1,0:T(8,128)(2,1)S(1)}, u32[]{:S(2)}, u32[]{:S(2)}) collective-permute-start(bf16[64,512]{1,0:T(8,128)(2,1)S(1)} %get-tuple-element.135), channel_id=1, source_target_pairs={{0,24},{8,16},{16,8},{24,0},{1,25},{9,17},{17,9},{25,1},{2,26},{10... | collective-permute-start | bytes 196616 | tf_op jit(solution)/shard_map/ppermute | solution.py:861
  96.1 6.4 %collective-permute-start.16 = (bf16[128,1024]{1,0:T(8,128)(2,1)S(1)}, bf16[128,1024]{1,0:T(8,128)(2,1)S(1)}, u32[]{:S(2)}, u32[]{:S(2)}) collective-permute-start(bf16[128,1024]{1,0:T(8,128)(2,1)S(1)} %get-tuple-element.139), channel_id=1, source_target_pairs={{0,2},{2,0},{1,3},{3,1},{4,6},{6,4},{5,7},{7,5},{8,10},{10,8},{9,1... | collective-permute-start | bytes 786440 | tf_op jit(solution)/shard_map/ppermute | solution.py:854
  96.2 13.6 %collective-permute-start.17 = (bf16[128,1024]{1,0:T(8,128)(2,1)S(1)}, bf16[128,1024]{1,0:T(8,128)(2,1)S(1)}, u32[]{:S(2)}, u32[]{:S(2)}) collective-permute-start(bf16[128,1024]{1,0:T(8,128)(2,1)S(1)} %get-tuple-element.140), channel_id=1, source_target_pairs={{0,4},{4,0},{1,5},{5,1},{2,6},{6,2},{3,7},{7,3},{8,12},{12,8},{9,1... | collective-permute-start | bytes 786440 | tf_op jit(solution)/shard_map/ppermute | solution.py:855
  99.2 10.6 %collective-permute-start.18 = (bf16[128,1024]{1,0:T(8,128)(2,1)S(1)}, bf16[128,1024]{1,0:T(8,128)(2,1)S(1)}, u32[]{:S(2)}, u32[]{:S(2)}) collective-permute-start(bf16[128,1024]{1,0:T(8,128)(2,1)S(1)} %get-tuple-element.141), channel_id=1, source_target_pairs={{0,6},{2,4},{4,2},{6,0},{1,7},{3,5},{5,3},{7,1},{8,14},{10,12},{12... | collective-permute-start | bytes 786440 | tf_op jit(solution)/shard_map/ppermute | solution.py:856
  112.7 8.7 %collective-permute-start.21 = (bf16[128,1024]{1,0:T(8,128)(2,1)S(1)}, bf16[128,1024]{1,0:T(8,128)(2,1)S(1)}, u32[]{:S(2)}, u32[]{:S(2)}) collective-permute-start(bf16[128,1024]{1,0:T(8,128)(2,1)S(1)} %get-tuple-element.145.refs_2_.refs_3_), channel_id=1, source_target_pairs={{0,6},{2,4},{4,2},{6,0},{1,7},{3,5},{5,3},{7,1},{8,14},{10,12},{12... | collective-permute-start | bytes 786440 | tf_op jit(solution)/shard_map/ppermute | solution.py:856
  117.0 7.2 %collective-permute-start.20 = (bf16[128,1024]{1,0:T(8,128)(2,1)S(1)}, bf16[128,1024]{1,0:T(8,128)(2,1)S(1)}, u32[]{:S(2)}, u32[]{:S(2)}) collective-permute-start(bf16[128,1024]{1,0:T(8,128)(2,1)S(1)} %get-tuple-element.145.refs_2_.refs_3_), channel_id=1, source_target_pairs={{0,4},{4,0},{1,5},{5,1},{2,6},{6,2},{3,7},{7,3},{8,12},{12,8},{9,1... | collective-permute-start | bytes 786440 | tf_op jit(solution)/shard_map/ppermute | solution.py:855
  117.0 7.2 %collective-permute-start.19 = (bf16[128,1024]{1,0:T(8,128)(2,1)S(1)}, bf16[128,1024]{1,0:T(8,128)(2,1)S(1)}, u32[]{:S(2)}, u32[]{:S(2)}) collective-permute-start(bf16[128,1024]{1,0:T(8,128)(2,1)S(1)} %get-tuple-element.145.refs_2_.refs_3_), channel_id=1, source_target_pairs={{0,2},{2,0},{1,3},{3,1},{4,6},{6,4},{5,7},{7,5},{8,10},{10,8},{9,1... | collective-permute-start | bytes 786440 | tf_op jit(solution)/shard_map/ppermute | solution.py:854
  132.7 11.4 %collective-permute-start.22 = (bf16[128,1024]{1,0:T(8,128)(2,1)S(1)}, bf16[128,1024]{1,0:T(8,128)(2,1)S(1)}, u32[]{:S(2)}, u32[]{:S(2)}) collective-permute-start(bf16[128,1024]{1,0:T(8,128)(2,1)S(1)} %get-tuple-element.155), channel_id=1, source_target_pairs={{0,2},{2,0},{1,3},{3,1},{4,6},{6,4},{5,7},{7,5},{8,10},{10,8},{9,1... | collective-permute-start | bytes 786440 | tf_op jit(solution)/shard_map/ppermute | solution.py:854
  134.8 12.1 %collective-permute-start.23 = (bf16[128,1024]{1,0:T(8,128)(2,1)S(1)}, bf16[128,1024]{1,0:T(8,128)(2,1)S(1)}, u32[]{:S(2)}, u32[]{:S(2)}) collective-permute-start(bf16[128,1024]{1,0:T(8,128)(2,1)S(1)} %get-tuple-element.156), channel_id=1, source_target_pairs={{0,4},{4,0},{1,5},{5,1},{2,6},{6,2},{3,7},{7,3},{8,12},{12,8},{9,1... | collective-permute-start | bytes 786440 | tf_op jit(solution)/shard_map/ppermute | solution.py:855
  135.4 11.5 %collective-permute-start.24 = (bf16[128,1024]{1,0:T(8,128)(2,1)S(1)}, bf16[128,1024]{1,0:T(8,128)(2,1)S(1)}, u32[]{:S(2)}, u32[]{:S(2)}) collective-permute-start(bf16[128,1024]{1,0:T(8,128)(2,1)S(1)} %get-tuple-element.157), channel_id=1, source_target_pairs={{0,6},{2,4},{4,2},{6,0},{1,7},{3,5},{5,3},{7,1},{8,14},{10,12},{12... | collective-permute-start | bytes 786440 | tf_op jit(solution)/shard_map/ppermute | solution.py:856
  149.9 7.4 %collective-permute-start.27 = (bf16[128,1024]{1,0:T(8,128)(2,1)S(1)}, bf16[128,1024]{1,0:T(8,128)(2,1)S(1)}, u32[]{:S(2)}, u32[]{:S(2)}) collective-permute-start(bf16[128,1024]{1,0:T(8,128)(2,1)S(1)} %get-tuple-element.159.refs_3_), channel_id=1, source_target_pairs={{0,6},{2,4},{4,2},{6,0},{1,7},{3,5},{5,3},{7,1},{8,14},{10,12},{12... | collective-permute-start | bytes 786440 | tf_op jit(solution)/shard_map/ppermute | solution.py:856
  150.0 9.2 %collective-permute-start.26 = (bf16[128,1024]{1,0:T(8,128)(2,1)S(1)}, bf16[128,1024]{1,0:T(8,128)(2,1)S(1)}, u32[]{:S(2)}, u32[]{:S(2)}) collective-permute-start(bf16[128,1024]{1,0:T(8,128)(2,1)S(1)} %get-tuple-element.159.refs_3_), channel_id=1, source_target_pairs={{0,4},{4,0},{1,5},{5,1},{2,6},{6,2},{3,7},{7,3},{8,12},{12,8},{9,1... | collective-permute-start | bytes 786440 | tf_op jit(solution)/shard_map/ppermute | solution.py:855
  150.6 8.7 %collective-permute-start.25 = (bf16[128,1024]{1,0:T(8,128)(2,1)S(1)}, bf16[128,1024]{1,0:T(8,128)(2,1)S(1)}, u32[]{:S(2)}, u32[]{:S(2)}) collective-permute-start(bf16[128,1024]{1,0:T(8,128)(2,1)S(1)} %get-tuple-element.159.refs_3_), channel_id=1, source_target_pairs={{0,2},{2,0},{1,3},{3,1},{4,6},{6,4},{5,7},{7,5},{8,10},{10,8},{9,1... | collective-permute-start | bytes 786440 | tf_op jit(solution)/shard_map/ppermute | solution.py:854
  161.9 8.0 %collective-permute-start.28 = (bf16[64,512]{1,0:T(8,128)(2,1)S(1)}, bf16[64,512]{1,0:T(8,128)(2,1)S(1)}, u32[]{:S(2)}, u32[]{:S(2)}) collective-permute-start(bf16[64,512]{1,0:T(8,128)(2,1)S(1)} %get-tuple-element.163), channel_id=1, source_target_pairs={{0,8},{8,0},{16,24},{24,16},{1,9},{9,1},{17,25},{25,17},{2,10},{10... | collective-permute-start | bytes 196616 | tf_op jit(solution)/shard_map/ppermute | solution.py:861
  162.0 7.9 %collective-permute-start.29 = (bf16[64,512]{1,0:T(8,128)(2,1)S(1)}, bf16[64,512]{1,0:T(8,128)(2,1)S(1)}, u32[]{:S(2)}, u32[]{:S(2)}) collective-permute-start(bf16[64,512]{1,0:T(8,128)(2,1)S(1)} %get-tuple-element.164), channel_id=1, source_target_pairs={{0,16},{8,24},{16,0},{24,8},{1,17},{9,25},{17,1},{25,9},{2,18},{10... | collective-permute-start | bytes 196616 | tf_op jit(solution)/shard_map/ppermute | solution.py:861
  162.3 7.6 %collective-permute-start.30 = (bf16[64,512]{1,0:T(8,128)(2,1)S(1)}, bf16[64,512]{1,0:T(8,128)(2,1)S(1)}, u32[]{:S(2)}, u32[]{:S(2)}) collective-permute-start(bf16[64,512]{1,0:T(8,128)(2,1)S(1)} %get-tuple-element.165), channel_id=1, source_target_pairs={{0,24},{8,16},{16,8},{24,0},{1,25},{9,17},{17,9},{25,1},{2,26},{10... | collective-permute-start | bytes 196616 | tf_op jit(solution)/shard_map/ppermute | solution.py:861
  166.4 20.7 %all-to-all-start.2 = ((bf16[4,128,1024]{2,1,0:T(8,128)(2,1)}), bf16[4,128,1024]{2,1,0:T(8,128)(2,1)S(1)}, u32[]{:S(2)}, u32[]{:S(2)}) async-start(bf16[4,128,1024]{2,1,0:T(8,128)(2,1)} %get-tuple-element.151), calls=%async_computation.2 | async-start | bytes 2097152 | tf_op jit(solution)/shard_map/all_to_all | solution.py:844
  183.5 6.1 %collective-permute-start.31 = (bf16[192,512]{1,0:T(8,128)(2,1)S(1)}, bf16[192,512]{1,0:T(8,128)(2,1)S(1)}, u32[]{:S(2)}, u32[]{:S(2)}) collective-permute-start(bf16[192,512]{1,0:T(8,128)(2,1)S(1)} %get-tuple-element.174), channel_id=1, source_target_pairs={{0,2},{2,0},{1,3},{3,1},{4,6},{6,4},{5,7},{7,5},{8,10},{10,8},{9,1... | collective-permute-start | bytes 589832 | tf_op jit(solution)/shard_map/ppermute | solution.py:854
  185.5 6.8 %collective-permute-start.32 = (bf16[192,512]{1,0:T(8,128)(2,1)S(1)}, bf16[192,512]{1,0:T(8,128)(2,1)S(1)}, u32[]{:S(2)}, u32[]{:S(2)}) collective-permute-start(bf16[192,512]{1,0:T(8,128)(2,1)S(1)} %get-tuple-element.175), channel_id=1, source_target_pairs={{0,4},{4,0},{1,5},{5,1},{2,6},{6,2},{3,7},{7,3},{8,12},{12,8},{9,1... | collective-permute-start | bytes 589832 | tf_op jit(solution)/shard_map/ppermute | solution.py:855
  187.0 6.6 %collective-permute-start.33 = (bf16[192,512]{1,0:T(8,128)(2,1)S(1)}, bf16[192,512]{1,0:T(8,128)(2,1)S(1)}, u32[]{:S(2)}, u32[]{:S(2)}) collective-permute-start(bf16[192,512]{1,0:T(8,128)(2,1)S(1)} %get-tuple-element.176), channel_id=1, source_target_pairs={{0,6},{2,4},{4,2},{6,0},{1,7},{3,5},{5,3},{7,1},{8,14},{10,12},{12... | collective-permute-start | bytes 589832 | tf_op jit(solution)/shard_map/ppermute | solution.py:856
  201.6 1.9 collective-permute-start.37
  201.7 2.6 %collective-permute-start.38 = (bf16[2,4,32,896]{3,2,1,0:T(8,128)(2,1)S(1)}, bf16[2,4,32,896]{3,2,1,0:T(8,128)(2,1)S(1)}, u32[]{:S(2)}, u32[]{:S(2)}) collective-permute-start(bf16[2,4,32,896]{3,2,1,0:T(8,128)(2,1)S(1)} %get-tuple-element.187), channel_id=1, source_target_pairs={{0,1},{1,0},{2,3},{3,2},{4,5},{5,4},{6,7},{7,6},{8,9},{9,8},{10,11... | collective-permute-start | bytes 1376264 | tf_op jit(solution)/shard_map/ppermute | solution.py:869
  206.2 8.5 %collective-permute-start.39 = (bf16[4,32,896]{2,1,0:T(8,128)(2,1)S(1)}, bf16[4,32,896]{2,1,0:T(8,128)(2,1)S(1)}, u32[]{:S(2)}, u32[]{:S(2)}) collective-permute-start(bf16[4,32,896]{2,1,0:T(8,128)(2,1)S(1)} %get-tuple-element.190), channel_id=1, source_target_pairs={{0,2},{2,0},{1,3},{3,1},{4,6},{6,4},{5,7},{7,5},{8,10},{10,8},{9,1... | collective-permute-start | bytes 688136 | tf_op jit(solution)/shard_map/ppermute | solution.py:854
  206.9 10.3 %collective-permute-start.40 = (bf16[4,32,896]{2,1,0:T(8,128)(2,1)S(1)}, bf16[4,32,896]{2,1,0:T(8,128)(2,1)S(1)}, u32[]{:S(2)}, u32[]{:S(2)}) collective-permute-start(bf16[4,32,896]{2,1,0:T(8,128)(2,1)S(1)} %get-tuple-element.191), channel_id=1, source_target_pairs={{0,4},{4,0},{1,5},{5,1},{2,6},{6,2},{3,7},{7,3},{8,12},{12,8},{9,1... | collective-permute-start | bytes 688136 | tf_op jit(solution)/shard_map/ppermute | solution.py:855
  208.0 11.5 %collective-permute-start.41 = (bf16[4,32,896]{2,1,0:T(8,128)(2,1)S(1)}, bf16[4,32,896]{2,1,0:T(8,128)(2,1)S(1)}, u32[]{:S(2)}, u32[]{:S(2)}) collective-permute-start(bf16[4,32,896]{2,1,0:T(8,128)(2,1)S(1)} %get-tuple-element.192), channel_id=1, source_target_pairs={{0,6},{2,4},{4,2},{6,0},{1,7},{3,5},{5,3},{7,1},{8,14},{10,12},{12... | collective-permute-start | bytes 688136 | tf_op jit(solution)/shard_map/ppermute | solution.py:856
  209.7 20.6 %collective-permute-start.34 = (bf16[128,1024]{1,0:T(8,128)(2,1)S(1)}, bf16[128,1024]{1,0:T(8,128)(2,1)S(1)}, u32[]{:S(2)}, u32[]{:S(2)}) collective-permute-start(bf16[128,1024]{1,0:T(8,128)(2,1)S(1)} %get-tuple-element.181), channel_id=1, source_target_pairs={{0,8},{8,0},{16,24},{24,16},{1,9},{9,1},{17,25},{25,17},{2,10},{10... | collective-permute-start | bytes 786440 | tf_op jit(solution)/shard_map/ppermute | solution.py:861
  209.7 21.6 %collective-permute-start.35 = (bf16[128,1024]{1,0:T(8,128)(2,1)S(1)}, bf16[128,1024]{1,0:T(8,128)(2,1)S(1)}, u32[]{:S(2)}, u32[]{:S(2)}) collective-permute-start(bf16[128,1024]{1,0:T(8,128)(2,1)S(1)} %get-tuple-element.182), channel_id=1, source_target_pairs={{0,16},{8,24},{16,0},{24,8},{1,17},{9,25},{17,1},{25,9},{2,18},{10... | collective-permute-start | bytes 786440 | tf_op jit(solution)/shard_map/ppermute | solution.py:861
  214.7 16.7 %collective-permute-start.36 = (bf16[128,1024]{1,0:T(8,128)(2,1)S(1)}, bf16[128,1024]{1,0:T(8,128)(2,1)S(1)}, u32[]{:S(2)}, u32[]{:S(2)}) collective-permute-start(bf16[128,1024]{1,0:T(8,128)(2,1)S(1)} %get-tuple-element.183), channel_id=1, source_target_pairs={{0,24},{8,16},{16,8},{24,0},{1,25},{9,17},{17,9},{25,1},{2,26},{10... | collective-permute-start | bytes 786440 | tf_op jit(solution)/shard_map/ppermute | solution.py:861
  220.8 14.1 %collective-permute-start.42 = (bf16[32,896]{1,0:T(8,128)(2,1)S(1)}, bf16[32,896]{1,0:T(8,128)(2,1)S(1)}, u32[]{:S(2)}, u32[]{:S(2)}) collective-permute-start(bf16[32,896]{1,0:T(8,128)(2,1)S(1)} %get-tuple-element.198), channel_id=1, source_target_pairs={{0,8},{8,0},{16,24},{24,16},{1,9},{9,1},{17,25},{25,17},{2,10},{10... | collective-permute-start | bytes 172040 | tf_op jit(solution)/shard_map/ppermute | solution.py:861
  220.9 19.7 %collective-permute-start.43 = (bf16[32,896]{1,0:T(8,128)(2,1)S(1)}, bf16[32,896]{1,0:T(8,128)(2,1)S(1)}, u32[]{:S(2)}, u32[]{:S(2)}) collective-permute-start(bf16[32,896]{1,0:T(8,128)(2,1)S(1)} %get-tuple-element.199), channel_id=1, source_target_pairs={{0,16},{8,24},{16,0},{24,8},{1,17},{9,25},{17,1},{25,9},{2,18},{10... | collective-permute-start | bytes 172040 | tf_op jit(solution)/shard_map/ppermute | solution.py:861
  224.3 1.1 copy-start.2
  226.9 15.6 %all-to-all-start.3 = ((bf16[4,32,1024]{2,1,0:T(8,128)(2,1)}), bf16[4,32,1024]{2,1,0:T(8,128)(2,1)S(1)}, u32[]{:S(2)}, u32[]{:S(2)}) async-start(bf16[4,32,1024]{2,1,0:T(8,128)(2,1)} %get-tuple-element.212), calls=%async_computation.4 | async-start | bytes 524288 | tf_op jit(solution)/shard_map/all_to_all | solution.py:844
  230.3 10.3 %collective-permute-start.44 = (bf16[32,896]{1,0:T(8,128)(2,1)S(1)}, bf16[32,896]{1,0:T(8,128)(2,1)S(1)}, u32[]{:S(2)}, u32[]{:S(2)}) collective-permute-start(bf16[32,896]{1,0:T(8,128)(2,1)S(1)} %get-tuple-element.200), channel_id=1, source_target_pairs={{0,24},{8,16},{16,8},{24,0},{1,25},{9,17},{17,9},{25,1},{2,26},{10... | collective-permute-start | bytes 172040 | tf_op jit(solution)/shard_map/ppermute | solution.py:861
Sparse Core Ops, SparseCore 0:
  9.6 33.5 all-gather.5
  45.3 22.7 all-gather.7
  70.4 47.0 all-gather.9
  162.1 53.2 reduce-scatter.1

commit v6 on v5

--- a/solution.py
+++ b/solution.py
@@ -478,14 +478,9 @@
         mover.start(block, out.at[pos[0] ^ u])
 
 
-def shard_kernel(mover, ups, down, out):
-    out[0:PLANE] = ups[...]
-    out[PLANE:] = down[out.shape[1] :, :].reshape(PLANE - 1, -1, down.shape[1])
-
-
 def qkv_kernel(mover, pos, lead, seg_row, toks, *refs):
     z, yx, c = pos[0], pos[1], pos[2]
-    qa, qc, (n1, w_out, vec, up_b, o0, o1, o2, o3, w, proj) = refs[:4], refs[4:8], refs[8:]
+    qa, qc, (ups, down, shard, n1, w_out, vec, up_b, o0, o1, o2, o3, w, proj) = refs[:4], refs[4:8], refs[8:]
     rows, d = toks.shape[1:]
     width = d // DEPTH
     head = width // PLANE
@@ -493,6 +488,8 @@
     fr = w.shape[4] - 3 * width
     pending = [mover.start(qa[k], w.at[:, yx ^ k, c]) for k in range(PLANE)]
     pending += [mover.start(qc[k], w.at[:, yx ^ k, 1 - c]) for k in range(PLANE)]
+    shard[0:PLANE] = ups[...]
+    shard[PLANE:] = down[shard.shape[1] :, :].reshape(PLANE - 1, -1, down.shape[1])
     mover.wait(pending)
     mover.start(w.at[:, :, :, :, 0 : 3 * width], w_out)
     for zz in range(DEPTH):
@@ -831,7 +828,7 @@
 
 
 COSTS = {
-    "q_prep_kernel": (3, 6), "q_stack_kernel": (1, 4), "up_prep_kernel": (1, 4), "shard_kernel": (1, 4), "first_shard_kernel": (1, 4), "qkv_kernel": (5, 20),
+    "q_prep_kernel": (3, 6), "q_stack_kernel": (1, 4), "up_prep_kernel": (1, 4),  "first_shard_kernel": (1, 4), "qkv_kernel": (5, 20),
     "attend_kernel": (9, 24), "out_kernel": (2, 12), "norm_kernel": (2, 8), "ffn_kernel": (8, 32), "ffn_grad_kernel": (8, 32),
     "branch_kernel": (2, 12), "out_back_kernel": (3, 12), "attend_back_kernel": (15, 32),
     "qkv_back_kernel": (10, 28), "first_back_kernel": (2, 8), "layer_out_kernel": (1, 8),
@@ -917,14 +914,13 @@
     (q_stack,) = call(q_stack_kernel, [((DEPTH, rw, side), bf16)], [pos, *q_rows], after=[up_cols])
     q_plane = across((q_stack,) * PLANE)
     q_other = [core_swap(block) for block in q_plane]
-    n1, w_qkv, vec, up_b, *blocks = call(
+    ff_shard, n1, w_qkv, vec, up_b, *blocks = call(
         qkv_kernel,
-        [((span, d), bf16, "far"), ((DEPTH, PLANE, 2, rw, width), bf16, "raw"), ((VEC_ROWS, d), f32), ((1, ff), f32)]
+        [((2 * PLANE - 1, rw, d), bf16, "far"), ((span, d), bf16, "far"), ((DEPTH, PLANE, 2, rw, width), bf16, "raw"), ((VEC_ROWS, d), f32), ((1, ff), f32)]
         + [((3 * head, span), bf16)] * 4,
-        [pos, lead, seg_row, Far(toks), *q_plane, *q_other],
+        [pos, lead, seg_row, Far(toks), *q_plane, *q_other, up_cols, Far(down_weight)],
         [((DEPTH, PLANE, 2, rw, side), bf16), ((3 * PLANE, head, span), bf16)],
     )
-    (ff_shard,) = call(shard_kernel, [((2 * PLANE - 1, rw, d), bf16, "far")], [up_cols, down_weight])
     ff_all = lax.all_gather(ff_shard, ("z", "g"), axis=0).reshape(DEPTH, 2, 2 * PLANE - 1, rw, d)
     blocks = across(blocks)
 

time: 251 us -> 251 us (level)
    pallas_call x20 -> x19, Pallas kernels: 87 us -> 86 us  [run(): pl.pallas_call(body, name=name, out_shape=[HBM(o[0], o[1]) if o[2] else j...]
where the time goes in v6:
time: 251 us; the launch traced here: 250 us
  Pallas kernels  86 us (34%)
  waiting for transfers between devices  73.9 us (29%)
  starting transfers between devices  72.4 us (29%)
  between operations  14.1 us (6%)
  local copies, waits for them, and re-layouts  3.82 us (2%)
    pallas_call x19, Pallas kernels, run(): pl.pallas_call(body, name=name, out_shape=[HBM(o[0], o[1]) if o[2] else j...  86 us
    ppermute x8, waiting for transfers between devices, across(): lax.ppermute(blocks[2], 'y', swap)  29.1 us
    ppermute x15, starting transfers between devices, to_depth(): return lax.ppermute(block, 'z', [(i, i ^ step) for i in range(DEPTH)])  23.8 us
    ppermute x15, waiting for transfers between devices, to_depth(): return lax.ppermute(block, 'z', [(i, i ^ step) for i in range(DEPTH)])  20.5 us
    all_to_all x4, starting transfers between devices, trade(): return lax.all_to_all(blocks, axes, split_axis=0, concat_axis=0, tiled=True)  16.4 us
    ppermute x8, waiting for transfers between devices, across(): lax.ppermute(blocks[3], ('y', 'x'), [(i, i ^ 3) for i in range(PLANE)])  16 us
    ppermute x8, starting transfers between devices, across(): lax.ppermute(blocks[3], ('y', 'x'), [(i, i ^ 3) for i in range(PLANE)])  12.1 us
    ppermute x8, starting transfers between devices, across(): lax.ppermute(blocks[1], 'x', swap)  10.4 us
  transfers between devices with their start and end apart: 53, of which 25 were waited for; matrix products, arithmetic and copies ran while one was open for 0% of the time, Pallas kernels for 28%

profile of v6, /device:TPU:0, one launch (start us, length us, event | category | flops | bytes accessed | tf_op | source)
XLA Modules:
  0.0 250.3 jit_solution(11336839858813032274)
XLA Ops:
  8.0 3.8 %q_prep_kernel.1 = (bf16[32,896]{1,0:T(8,128)(2,1)S(1)}, bf16[32,896]{1,0:T(8,128)(2,1)S(1)}, bf16[32,896]{1,0:T(8,128)(2,1)S(1)}, bf16[32,896]{1,0:T(8,128)(2,1...) custom-call(s32[3]{0:T(128)S(1)} %pad_add_fusion.refs_0_, ...), custom_call_target="tpu_custom_call" | custom-call | flops 3300000000 | bytes 10800000 | tf_op jit(solution)/shard_map/q_prep_kernel/pallas_call | solution.py:400
  11.9 5.2 %all-to-all-start = ((bf16[4,32,1024]{2,1,0:T(8,128)(2,1)}), bf16[4,32,1024]{2,1,0:T(8,128)(2,1)S(1)}, u32[]{:S(2)}, u32[]{:S(2)}) async-start(bf16[4,32,1024]{2,1,0:T(8,128)(2,1)} %get-tuple-element.120), calls=%async_computation | async-start | bytes 524288 | tf_op jit(solution)/shard_map/all_to_all | solution.py:841
  17.0 1.6 collective-permute-start
  18.6 2.6 %collective-permute-start.1 = (bf16[32,896]{1,0:T(8,128)(2,1)S(1)}, bf16[32,896]{1,0:T(8,128)(2,1)S(1)}, u32[]{:S(2)}, u32[]{:S(2)}) collective-permute-start(bf16[32,896]{1,0:T(8,128)(2,1)S(1)} %get-tuple-element.118), channel_id=1, source_target_pairs={{0,16},{8,24},{16,0},{24,8},{1,17},{9,25},{17,1},{25,9},{2,18},{10... | collective-permute-start | bytes 172040 | tf_op jit(solution)/shard_map/ppermute | solution.py:858
  21.4 6.8 %collective-permute-done.1.refs_3_ = bf16[32,896]{1,0:T(8,128)(2,1)S(1)} collective-permute-done((bf16[32,896]{1,0:T(8,128)(2,1)S(1)}, bf16[32,896]{1,0:T(8,128)(2,1)S(1)}, u32[]{:S(2)}, u32[]{:S(2)}) %collective-permute-start.1) | collective-permute-done | bytes 57376 | tf_op jit(solution)/shard_map/ppermute | solution.py:858
  29.1 1.4 q_stack_kernel.1
  30.5 3.4 %collective-permute-start.5 = (bf16[4,32,896]{2,1,0:T(8,128)(2,1)S(1)}, bf16[4,32,896]{2,1,0:T(8,128)(2,1)S(1)}, u32[]{:S(2)}, u32[]{:S(2)}) collective-permute-start(bf16[4,32,896]{2,1,0:T(8,128)(2,1)S(1)} %get-tuple-element.122.refs_4_), channel_id=1, source_target_pairs={{0,6},{2,4},{4,2},{6,0},{1,7},{3,5},{5,3},{7,1},{8,14},{10,12},{12... | collective-permute-start | bytes 688136 | tf_op jit(solution)/shard_map/ppermute | solution.py:853
  34.6 4.8 %collective-permute-done.5.refs_7_ = bf16[4,32,896]{2,1,0:T(8,128)(2,1)S(1)} collective-permute-done((bf16[4,32,896]{2,1,0:T(8,128)(2,1)S(1)}, bf16[4,32,896]{2,1,0:T(8,128)(2,1)S(1)}, u32[]{:S(2)}, u32[]{:S(2)}) %collective-permute-start.5) | collective-permute-done | bytes 229408 | tf_op jit(solution)/shard_map/ppermute | solution.py:853
  39.4 2.3 collective-permute-done.4.refs_6_
  44.5 6.5 %qkv_kernel.1 = (bf16[7,32,1024]{2,1,0:T(8,128)(2,1)}, bf16[512,1024]{1,0:T(8,128)(2,1)}, bf16[4,4,2,32,768]{4,3,2,1,0:T(8,128)(2,1)}, f32[24,1024]{1,0:T(8,128)...) custom-call(s32[3]{0:T(128)S(1)} %pad_add_fusion.refs_0_, ...), custom_call_target="tpu_custom_call" | custom-call | flops 5500000256 | bytes 18000000 | tf_op jit(solution)/shard_map/qkv_kernel/pallas_call | solution.py:400
  51.1 1.9 collective-permute-start.10
  53.0 1.5 collective-permute-start.11
  54.6 1.1 broadcast_in_dim.14
  55.7 4.2 %all-to-all-start.1 = ((bf16[4,128,1024]{2,1,0:T(8,128)(2,1)}), bf16[4,128,1024]{2,1,0:T(8,128)(2,1)}, u32[]{:S(2)}, u32[]{:S(2)}) async-start(bf16[4,128,1024]{2,1,0:T(8,128)(2,1)} %broadcast_in_dim.14), calls=%async_computation.1 | async-start | bytes 2097152 | tf_op jit(solution)/shard_map/all_to_all | solution.py:841
  60.0 9.6 %collective-permute-done.11.refs_3_ = bf16[192,512]{1,0:T(8,128)(2,1)S(1)} collective-permute-done((bf16[192,512]{1,0:T(8,128)(2,1)S(1)}, bf16[192,512]{1,0:T(8,128)(2,1)S(1)}, u32[]{:S(2)}, u32[]{:S(2)}) %collective-permute-start.11) | collective-permute-done | bytes 196640 | tf_op jit(solution)/shard_map/ppermute | solution.py:852
  69.6 11.2 %attend_kernel.1 = (bf16[64,512]{1,0:T(8,128)(2,1)S(1)}, bf16[64,512]{1,0:T(8,128)(2,1)S(1)}, bf16[64,512]{1,0:T(8,128)(2,1)S(1)}, bf16[64,512]{1,0:T(8,128)(2,1...) custom-call(s32[1,128]{1,0:T(1,128)S(1)} %copy-done.4, bf16[192,512]{1,0:T(8,128)(2,1)S(1)} %get-tuple-element.125.refs_1_, ...), custom_call_target="tpu_custom_call" | custom-call | flops 9900000256 | bytes 32400000 | tf_op jit(solution)/shard_map/attend_kernel/pallas_call | solution.py:400
  80.8 2.0 collective-permute-start.13
  82.8 1.4 collective-permute-start.14
  84.3 1.4 collective-permute-start.15
  85.7 2.9 %collective-permute-done.13.refs_2_ = bf16[64,512]{1,0:T(8,128)(2,1)S(1)} collective-permute-done((bf16[64,512]{1,0:T(8,128)(2,1)S(1)}, bf16[64,512]{1,0:T(8,128)(2,1)S(1)}, u32[]{:S(2)}, u32[]{:S(2)}) %collective-permute-start.13) | collective-permute-done | bytes 65568 | tf_op jit(solution)/shard_map/ppermute | solution.py:858
  88.6 2.7 %collective-permute-done.14.refs_3_ = bf16[64,512]{1,0:T(8,128)(2,1)S(1)} collective-permute-done((bf16[64,512]{1,0:T(8,128)(2,1)S(1)}, bf16[64,512]{1,0:T(8,128)(2,1)S(1)}, u32[]{:S(2)}, u32[]{:S(2)}) %collective-permute-start.14) | collective-permute-done | bytes 65568 | tf_op jit(solution)/shard_map/ppermute | solution.py:858
  91.3 2.2 collective-permute-done.15.refs_4_
  93.5 2.6 %out_kernel.1 = (f32[128,1024]{1,0:T(8,128)S(1)}, bf16[128,1024]{1,0:T(8,128)(2,1)S(1)}, bf16[128,1024]{1,0:T(8,128)(2,1)S(1)}, bf16[128,1024]{1,0:T(8,128)(2,1)...) custom-call(s32[3]{0:T(128)S(1)} %pad_add_fusion.refs_0_, ...), custom_call_target="tpu_custom_call" | custom-call | flops 2200000000 | bytes 7200000 | tf_op jit(solution)/shard_map/out_kernel/pallas_call | solution.py:400
  96.2 2.9 %collective-permute-start.17 = (bf16[128,1024]{1,0:T(8,128)(2,1)S(1)}, bf16[128,1024]{1,0:T(8,128)(2,1)S(1)}, u32[]{:S(2)}, u32[]{:S(2)}) collective-permute-start(bf16[128,1024]{1,0:T(8,128)(2,1)S(1)} %get-tuple-element.138), channel_id=1, source_target_pairs={{0,4},{4,0},{1,5},{5,1},{2,6},{6,2},{3,7},{7,3},{8,12},{12,8},{9,1... | collective-permute-start | bytes 786440 | tf_op jit(solution)/shard_map/ppermute | solution.py:852
  99.1 1.4 collective-permute-start.18
  100.5 2.0 collective-permute-done.16.refs_5_
  102.6 7.2 %collective-permute-done.17.refs_6_ = bf16[128,1024]{1,0:T(8,128)(2,1)S(1)} collective-permute-done((bf16[128,1024]{1,0:T(8,128)(2,1)S(1)}, bf16[128,1024]{1,0:T(8,128)(2,1)S(1)}, u32[]{:S(2)}, u32[]{:S(2)}) %collective-permute-start.17) | collective-permute-done | bytes 262176 | tf_op jit(solution)/shard_map/ppermute | solution.py:852
  109.7 2.9 %norm_kernel.1 = (f32[128,1024]{1,0:T(8,128)}, bf16[128,1024]{1,0:T(8,128)(2,1)S(1)}, f32[8,128]{1,0:T(8,128)S(1)}) custom-call(s32[4]{0:T(128)S(1)} %bitcast.14, s32[1,128]{1,0:T(1,128)S(1)} %copy-done.4, f32[24,1024]{1,0:T(8,128)S(1)} %get-tuple-element.124.refs_2_.refs_0_.refs_3_, bf16[128,1024]{1,0:T(8,128)(2,1)} %bitcast.20, ...), custom_call_target="tpu_custom_call" | custom-call | flops 2200000000 | bytes 7200000 | tf_op jit(solution)/shard_map/norm_kernel/pallas_call | solution.py:400
  112.6 4.2 %collective-permute-start.21 = (bf16[128,1024]{1,0:T(8,128)(2,1)S(1)}, bf16[128,1024]{1,0:T(8,128)(2,1)S(1)}, u32[]{:S(2)}, u32[]{:S(2)}) collective-permute-start(bf16[128,1024]{1,0:T(8,128)(2,1)S(1)} %get-tuple-element.143.refs_2_.refs_3_), channel_id=1, source_target_pairs={{0,6},{2,4},{4,2},{6,0},{1,7},{3,5},{5,3},{7,1},{8,14},{10,12},{12... | collective-permute-start | bytes 786440 | tf_op jit(solution)/shard_map/ppermute | solution.py:853
  117.5 3.8 %collective-permute-done.21.refs_5_.refs_6_ = bf16[128,1024]{1,0:T(8,128)(2,1)S(1)} collective-permute-done((bf16[128,1024]{1,0:T(8,128)(2,1)S(1)}, bf16[128,1024]{1,0:T(8,128)(2,1)S(1)}, u32[]{:S(2)}, u32[]{:S(2)}) %collective-permute-start.21) | collective-permute-done | bytes 262176 | tf_op jit(solution)/shard_map/ppermute | solution.py:853
  121.3 2.7 %collective-permute-done.20.refs_4_.refs_5_ = bf16[128,1024]{1,0:T(8,128)(2,1)S(1)} collective-permute-done((bf16[128,1024]{1,0:T(8,128)(2,1)S(1)}, bf16[128,1024]{1,0:T(8,128)(2,1)S(1)}, u32[]{:S(2)}, u32[]{:S(2)}) %collective-permute-start.20) | collective-permute-done | bytes 262176 | tf_op jit(solution)/shard_map/ppermute | solution.py:852
  124.0 8.5 %ffn_kernel.1 = (bf16[512,1024]{1,0:T(8,128)(2,1)S(1)}, bf16[512,1024]{1,0:T(8,128)(2,1)S(1)}, f32[128,1024]{1,0:T(8,128)S(1)}, bf16[128,1024]{1,0:T(8,128)(2,1)...) custom-call(s32[3]{0:T(128)S(1)} %pad_add_fusion.refs_0_, ...), custom_call_target="tpu_custom_call" | custom-call | flops 8800000000 | bytes 28800000 | tf_op jit(solution)/shard_map/ffn_kernel/pallas_call | solution.py:400
  132.6 2.1 collective-permute-start.22
  136.2 7.7 %ffn_grad_kernel.1 = (bf16[4,2,9,32,1024]{4,3,2,1,0:T(8,128)(2,1)}, bf16[4,128,1024]{2,1,0:T(8,128)(2,1)}, f32[8,128]{1,0:T(8,128)S(1)}) custom-call(s32[3]{0:T(128)S(1)} %pad_add_fusion.refs_0_, bf16[512,1024]{1,0:T(8,128)(2,1)S(1)} %get-tuple-element.146.refs_1_, bf16[512,1024]{1,0:T(8,128)(2,1)S(1)} %get-tuple-element.147.refs_2_, ...), custom_call_target="tpu_custom_call" | custom-call | flops 8800000000 | bytes 28800000 | tf_op jit(solution)/shard_map/ffn_grad_kernel/pallas_call | solution.py:400
  144.0 2.7 %collective-permute-done.23.refs_5_ = bf16[128,1024]{1,0:T(8,128)(2,1)S(1)} collective-permute-done((bf16[128,1024]{1,0:T(8,128)(2,1)S(1)}, bf16[128,1024]{1,0:T(8,128)(2,1)S(1)}, u32[]{:S(2)}, u32[]{:S(2)}) %collective-permute-start.23) | collective-permute-done | bytes 262176 | tf_op jit(solution)/shard_map/ppermute | solution.py:852
  146.7 3.0 %branch_kernel.1 = (f32[128,1024]{1,0:T(8,128)}, bf16[128,1024]{1,0:T(8,128)(2,1)S(1)}, f32[8,1024]{1,0:T(8,128)S(1)}, f32[8,128]{1,0:T(8,128)S(1)}) custom-call(f32[24,1024]{1,0:T(8,128)S(1)} %get-tuple-element.124.refs_2_.refs_0_.refs_3_, f32[128,1024]{1,0:T(8,128)} %get-tuple-element.141.refs_1_, bf16[128,1024]{1,0:T(8,128)(2,1)} %bitcast.18, ...), custom_call_target="tpu_custom_call" | custom-call | flops 2200000000 | bytes 7200000 | tf_op jit(solution)/shard_map/branch_kernel/pallas_call | solution.py:400
  150.5 2.8 %collective-permute-start.25 = (bf16[128,1024]{1,0:T(8,128)(2,1)S(1)}, bf16[128,1024]{1,0:T(8,128)(2,1)S(1)}, u32[]{:S(2)}, u32[]{:S(2)}) collective-permute-start(bf16[128,1024]{1,0:T(8,128)(2,1)S(1)} %get-tuple-element.157.refs_3_), channel_id=1, source_target_pairs={{0,2},{2,0},{1,3},{3,1},{4,6},{6,4},{5,7},{7,5},{8,10},{10,8},{9,1... | collective-permute-start | bytes 786440 | tf_op jit(solution)/shard_map/ppermute | solution.py:851
  153.3 3.9 %collective-permute-done.27.refs_6_ = bf16[128,1024]{1,0:T(8,128)(2,1)S(1)} collective-permute-done((bf16[128,1024]{1,0:T(8,128)(2,1)S(1)}, bf16[128,1024]{1,0:T(8,128)(2,1)S(1)}, u32[]{:S(2)}, u32[]{:S(2)}) %collective-permute-start.27) | collective-permute-done | bytes 262176 | tf_op jit(solution)/shard_map/ppermute | solution.py:853
  157.2 1.9 collective-permute-done.26.refs_5_
  159.1 2.7 %out_back_kernel.1 = (bf16[64,512]{1,0:T(8,128)(2,1)S(1)}, bf16[64,512]{1,0:T(8,128)(2,1)S(1)}, bf16[64,512]{1,0:T(8,128)(2,1)S(1)}, bf16[64,512]{1,0:T(8,128)(2...) custom-call(s32[3]{0:T(128)S(1)} %pad_add_fusion.refs_0_, ...), custom_call_target="tpu_custom_call", output_to_operand_aliasing={{4}: (7, {})} | custom-call | flops 3300000000 | bytes 10800000 | tf_op jit(solution)/shard_map/out_back_kernel/pallas_call | solution.py:400
  162.3 3.9 %collective-permute-start.30 = (bf16[64,512]{1,0:T(8,128)(2,1)S(1)}, bf16[64,512]{1,0:T(8,128)(2,1)S(1)}, u32[]{:S(2)}, u32[]{:S(2)}) collective-permute-start(bf16[64,512]{1,0:T(8,128)(2,1)S(1)} %get-tuple-element.163), channel_id=1, source_target_pairs={{0,24},{8,16},{16,8},{24,0},{1,25},{9,17},{17,9},{25,1},{2,26},{10... | collective-permute-start | bytes 196616 | tf_op jit(solution)/shard_map/ppermute | solution.py:858
  166.2 3.5 %all-to-all-start.2 = ((bf16[4,128,1024]{2,1,0:T(8,128)(2,1)}), bf16[4,128,1024]{2,1,0:T(8,128)(2,1)S(1)}, u32[]{:S(2)}, u32[]{:S(2)}) async-start(bf16[4,128,1024]{2,1,0:T(8,128)(2,1)} %get-tuple-element.149), calls=%async_computation.2 | async-start | bytes 2097152 | tf_op jit(solution)/shard_map/all_to_all | solution.py:841
  169.8 13.5 %attend_back_kernel.1 = (bf16[192,512]{1,0:T(8,128)(2,1)S(1)}, bf16[192,512]{1,0:T(8,128)(2,1)S(1)}, bf16[192,512]{1,0:T(8,128)(2,1)S(1)}, bf16[192,512]{1,0:T(8,128)(2,1)S(1)}, f32[8,128]{1,0:T(8,128)S(1)}) custom-call(s32[1,128]{1,0:T(1,128)S(1)} %copy-done.4, bf16[192,512]{1,0:T(8,128)(2,1)S(1)} %get-tuple-element.125.refs_1_, ...), custom_call_target="tpu_custom_call" | custom-call | flops 16499999744 | bytes 54000000 | tf_op jit(solution)/shard_map/attend_back_kernel/pallas_call | solution.py:400
  183.3 2.0 collective-permute-start.31
  185.3 1.5 collective-permute-start.32
  186.9 2.5 layer_out_kernel.1
  189.4 2.7 %collective-permute-done.32.refs_9_ = bf16[192,512]{1,0:T(8,128)(2,1)S(1)} collective-permute-done((bf16[192,512]{1,0:T(8,128)(2,1)S(1)}, bf16[192,512]{1,0:T(8,128)(2,1)S(1)}, u32[]{:S(2)}, u32[]{:S(2)}) %collective-permute-start.32) | collective-permute-done | bytes 196640 | tf_op jit(solution)/shard_map/ppermute | solution.py:852
  192.1 1.2 collective-permute-done.33.refs_10_
  193.4 8.0 %qkv_back_kernel.1 = (f32[128,1024]{1,0:T(8,128)S(1)}, bf16[128,1024]{1,0:T(8,128)(2,1)S(1)}, bf16[128,1024]{1,0:T(8,128)(2,1)S(1)}, bf16[128,1024]{1,0:T(8,128)...) custom-call(s32[3]{0:T(128)S(1)} %pad_add_fusion.refs_0_, ...), custom_call_target="tpu_custom_call" | custom-call | flops 11000000512 | bytes 36000000 | tf_op jit(solution)/shard_map/qkv_back_kernel/pallas_call | solution.py:400
  202.0 1.3 collective-permute-done.37.refs_2_
  204.1 1.9 pair_kernel.1
  207.8 1.8 collective-permute-start.41
  209.6 3.1 %collective-permute-start.35 = (bf16[128,1024]{1,0:T(8,128)(2,1)S(1)}, bf16[128,1024]{1,0:T(8,128)(2,1)S(1)}, u32[]{:S(2)}, u32[]{:S(2)}) collective-permute-start(bf16[128,1024]{1,0:T(8,128)(2,1)S(1)} %get-tuple-element.180), channel_id=1, source_target_pairs={{0,16},{8,24},{16,0},{24,8},{1,17},{9,25},{17,1},{25,9},{2,18},{10... | collective-permute-start | bytes 786440 | tf_op jit(solution)/shard_map/ppermute | solution.py:858
  212.6 1.9 collective-permute-done.39.refs_2_
  214.5 2.5 %collective-permute-start.36 = (bf16[128,1024]{1,0:T(8,128)(2,1)S(1)}, bf16[128,1024]{1,0:T(8,128)(2,1)S(1)}, u32[]{:S(2)}, u32[]{:S(2)}) collective-permute-start(bf16[128,1024]{1,0:T(8,128)(2,1)S(1)} %get-tuple-element.181), channel_id=1, source_target_pairs={{0,24},{8,16},{16,8},{24,0},{1,25},{9,17},{17,9},{25,1},{2,26},{10... | collective-permute-start | bytes 786440 | tf_op jit(solution)/shard_map/ppermute | solution.py:858
  217.0 2.2 collective-permute-done.41.refs_4_
  219.3 1.3 quad_kernel.1
  220.7 3.4 %collective-permute-start.43 = (bf16[32,896]{1,0:T(8,128)(2,1)S(1)}, bf16[32,896]{1,0:T(8,128)(2,1)S(1)}, u32[]{:S(2)}, u32[]{:S(2)}) collective-permute-start(bf16[32,896]{1,0:T(8,128)(2,1)S(1)} %get-tuple-element.197), channel_id=1, source_target_pairs={{0,16},{8,24},{16,0},{24,8},{1,17},{9,25},{17,1},{25,9},{2,18},{10... | collective-permute-start | bytes 172040 | tf_op jit(solution)/shard_map/ppermute | solution.py:858
  225.2 1.5 ffn_last_kernel.1
  226.7 3.4 %all-to-all-start.3 = ((bf16[4,32,1024]{2,1,0:T(8,128)(2,1)}), bf16[4,32,1024]{2,1,0:T(8,128)(2,1)S(1)}, u32[]{:S(2)}, u32[]{:S(2)}) async-start(bf16[4,32,1024]{2,1,0:T(8,128)(2,1)} %get-tuple-element.210), calls=%async_computation.4 | async-start | bytes 524288 | tf_op jit(solution)/shard_map/all_to_all | solution.py:841
  231.2 3.5 %first_back_kernel.1 = (f32[128,1024]{1,0:T(8,128)}, f32[8,128]{1,0:T(8,128)S(1)}) custom-call(s32[4]{0:T(128)S(1)} %bitcast.16, s32[1,128]{1,0:T(1,128)S(1)} %copy-done.4, f32[24,1024]{1,0:T(8,128)S(1)} %get-tuple-element.124.refs_2_.refs_0_.refs_3_, bf16[128,1024]{1,0:T(8,128)(2,1)} %bitcast.21, f32[128,1024]{1,0:T(8,128)} %get-tuple-element.168.refs_11_.refs_4_, ...), custom_call_target="tpu_custom_call" | custom-call | flops 2200000000 | bytes 7200000 | tf_op jit(solution)/shard_map/first_back_kernel/pallas_call | solution.py:400
  234.7 5.7 %collective-permute-done.43.refs_3_ = bf16[32,896]{1,0:T(8,128)(2,1)S(1)} collective-permute-done((bf16[32,896]{1,0:T(8,128)(2,1)S(1)}, bf16[32,896]{1,0:T(8,128)(2,1)S(1)}, u32[]{:S(2)}, u32[]{:S(2)}) %collective-permute-start.43) | collective-permute-done | bytes 57376 | tf_op jit(solution)/shard_map/ppermute | solution.py:858
  240.4 1.9 qkv_join_kernel.1
  242.4 1.4 up_join_kernel.1
  (79 shorter events, 14.5 us)
Async XLA Ops:
  7.2 36.4 %all-gather.6.cloned.1.call-start = ((), (), s32[]{:S(2)}) async-start(), calls=%async_computation.5 | async-start | bytes 1310720 | tf_op jit(solution)/shard_map/all_gather | solution.py:911
  7.9 77.7 %all-gather.8.cloned.1.call-start = ((), (), s32[]{:S(2)}) async-start(), calls=%async_computation.7 | async-start | bytes 1179648 | tf_op jit(solution)/shard_map/all_gather | solution.py:912
  11.8 31.7 %copy-start.3 = (s32[1,4]{1,0:T(1,128)S(1)}, s32[1,4]{1,0:T(1,128)}, u32[]{:S(2)}) copy-start(s32[1,4]{1,0:T(1,128)} %param.20) | copy-start | bytes 52
  11.8 31.7 %copy-start.4 = (s32[1,128]{1,0:T(1,128)S(1)}, s32[1,128]{1,0:T(1,128)}, u32[]{:S(2)}) copy-start(s32[1,128]{1,0:T(1,128)} %refs_1_.5) | copy-start | bytes 1540
  11.9 16.5 %all-to-all-start = ((bf16[4,32,1024]{2,1,0:T(8,128)(2,1)}), bf16[4,32,1024]{2,1,0:T(8,128)(2,1)S(1)}, u32[]{:S(2)}, u32[]{:S(2)}) async-start(bf16[4,32,1024]{2,1,0:T(8,128)(2,1)} %get-tuple-element.120), calls=%async_computation | async-start | bytes 524288 | tf_op jit(solution)/shard_map/all_to_all | solution.py:841
  17.0 107.0 %all-gather.10.cloned.1.call-start = ((), (), s32[]{:S(2)}) async-start(), calls=%async_computation.8 | async-start | bytes 4128768 | tf_op jit(solution)/shard_map/all_gather | solution.py:924
  17.0 4.4 %collective-permute-start = (bf16[32,896]{1,0:T(8,128)(2,1)S(1)}, bf16[32,896]{1,0:T(8,128)(2,1)S(1)}, u32[]{:S(2)}, u32[]{:S(2)}) collective-permute-start(bf16[32,896]{1,0:T(8,128)(2,1)S(1)} %get-tuple-element.117), channel_id=1, source_target_pairs={{0,8},{8,0},{16,24},{24,16},{1,9},{9,1},{17,25},{25,17},{2,10},{10... | collective-permute-start | bytes 172040 | tf_op jit(solution)/shard_map/ppermute | solution.py:858
  18.6 9.7 %collective-permute-start.1 = (bf16[32,896]{1,0:T(8,128)(2,1)S(1)}, bf16[32,896]{1,0:T(8,128)(2,1)S(1)}, u32[]{:S(2)}, u32[]{:S(2)}) collective-permute-start(bf16[32,896]{1,0:T(8,128)(2,1)S(1)} %get-tuple-element.118), channel_id=1, source_target_pairs={{0,16},{8,24},{16,0},{24,8},{1,17},{9,25},{17,1},{25,9},{2,18},{10... | collective-permute-start | bytes 172040 | tf_op jit(solution)/shard_map/ppermute | solution.py:858
  21.2 7.2 %collective-permute-start.2 = (bf16[32,896]{1,0:T(8,128)(2,1)S(1)}, bf16[32,896]{1,0:T(8,128)(2,1)S(1)}, u32[]{:S(2)}, u32[]{:S(2)}) collective-permute-start(bf16[32,896]{1,0:T(8,128)(2,1)S(1)} %get-tuple-element.119), channel_id=1, source_target_pairs={{0,24},{8,16},{16,8},{24,0},{1,25},{9,17},{17,9},{25,1},{2,26},{10... | collective-permute-start | bytes 172040 | tf_op jit(solution)/shard_map/ppermute | solution.py:858
  28.4 0.7 copy-start
  30.5 8.9 %collective-permute-start.5 = (bf16[4,32,896]{2,1,0:T(8,128)(2,1)S(1)}, bf16[4,32,896]{2,1,0:T(8,128)(2,1)S(1)}, u32[]{:S(2)}, u32[]{:S(2)}) collective-permute-start(bf16[4,32,896]{2,1,0:T(8,128)(2,1)S(1)} %get-tuple-element.122.refs_4_), channel_id=1, source_target_pairs={{0,6},{2,4},{4,2},{6,0},{1,7},{3,5},{5,3},{7,1},{8,14},{10,12},{12... | collective-permute-start | bytes 688136 | tf_op jit(solution)/shard_map/ppermute | solution.py:853
  34.0 7.8 %collective-permute-start.4 = (bf16[4,32,896]{2,1,0:T(8,128)(2,1)S(1)}, bf16[4,32,896]{2,1,0:T(8,128)(2,1)S(1)}, u32[]{:S(2)}, u32[]{:S(2)}) collective-permute-start(bf16[4,32,896]{2,1,0:T(8,128)(2,1)S(1)} %get-tuple-element.122.refs_4_), channel_id=1, source_target_pairs={{0,4},{4,0},{1,5},{5,1},{2,6},{6,2},{3,7},{7,3},{8,12},{12,8},{9,1... | collective-permute-start | bytes 688136 | tf_op jit(solution)/shard_map/ppermute | solution.py:852
  34.5 7.5 %collective-permute-start.3 = (bf16[4,32,896]{2,1,0:T(8,128)(2,1)S(1)}, bf16[4,32,896]{2,1,0:T(8,128)(2,1)S(1)}, u32[]{:S(2)}, u32[]{:S(2)}) collective-permute-start(bf16[4,32,896]{2,1,0:T(8,128)(2,1)S(1)} %get-tuple-element.122.refs_4_), channel_id=1, source_target_pairs={{0,2},{2,0},{1,3},{3,1},{4,6},{6,4},{5,7},{7,5},{8,10},{10,8},{9,1... | collective-permute-start | bytes 688136 | tf_op jit(solution)/shard_map/ppermute | solution.py:851
  34.6 7.6 %collective-permute-start.6 = (bf16[4,32,896]{2,1,0:T(8,128)(2,1)S(1)}, bf16[4,32,896]{2,1,0:T(8,128)(2,1)S(1)}, u32[]{:S(2)}, u32[]{:S(2)}) collective-permute-start(bf16[4,32,896]{2,1,0:T(8,128)(2,1)S(1)} %get-tuple-element.122.refs_4_), channel_id=1, source_target_pairs={{0,1},{1,0},{2,3},{3,2},{4,5},{5,4},{6,7},{7,6},{8,9},{9,8},{10,11... | collective-permute-start | bytes 688136 | tf_op jit(solution)/shard_map/ppermute | solution.py:866
  39.4 2.8 %collective-permute-start.9 = (bf16[4,32,896]{2,1,0:T(8,128)(2,1)S(1)}, bf16[4,32,896]{2,1,0:T(8,128)(2,1)S(1)}, u32[]{:S(2)}, u32[]{:S(2)}) collective-permute-start(bf16[4,32,896]{2,1,0:T(8,128)(2,1)S(1)} %collective-permute-done.5.refs_7_), channel_id=1, source_target_pairs={{0,1},{1,0},{2,3},{3,2},{4,5},{5,4},{6,7},{7,6},{8,9},{9,8},{10,11... | collective-permute-start | bytes 688136 | tf_op jit(solution)/shard_map/ppermute | solution.py:866
  41.7 1.5 collective-permute-start.8
  42.0 1.6 collective-permute-start.7
  43.5 1.0 copy-start.1
  44.5 10.1 %copy-start.5 = (bf16[1,128,1024]{2,1,0:T(8,128)(2,1)S(1)}, bf16[1,128,1024]{2,1,0:T(8,128)(2,1)}, u32[]{:S(2)}) copy-start(bf16[1,128,1024]{2,1,0:T(8,128)(2,1)} %param.35) | copy-start | bytes 786436
  51.1 9.0 %collective-permute-start.10 = (bf16[192,512]{1,0:T(8,128)(2,1)S(1)}, bf16[192,512]{1,0:T(8,128)(2,1)S(1)}, u32[]{:S(2)}, u32[]{:S(2)}) collective-permute-start(bf16[192,512]{1,0:T(8,128)(2,1)S(1)} %get-tuple-element.126), channel_id=1, source_target_pairs={{0,2},{2,0},{1,3},{3,1},{4,6},{6,4},{5,7},{7,5},{8,10},{10,8},{9,1... | collective-permute-start | bytes 589832 | tf_op jit(solution)/shard_map/ppermute | solution.py:851
  53.0 16.6 %collective-permute-start.11 = (bf16[192,512]{1,0:T(8,128)(2,1)S(1)}, bf16[192,512]{1,0:T(8,128)(2,1)S(1)}, u32[]{:S(2)}, u32[]{:S(2)}) collective-permute-start(bf16[192,512]{1,0:T(8,128)(2,1)S(1)} %get-tuple-element.127), channel_id=1, source_target_pairs={{0,4},{4,0},{1,5},{5,1},{2,6},{6,2},{3,7},{7,3},{8,12},{12,8},{9,1... | collective-permute-start | bytes 589832 | tf_op jit(solution)/shard_map/ppermute | solution.py:852
  54.5 15.2 %collective-permute-start.12 = (bf16[192,512]{1,0:T(8,128)(2,1)S(1)}, bf16[192,512]{1,0:T(8,128)(2,1)S(1)}, u32[]{:S(2)}, u32[]{:S(2)}) collective-permute-start(bf16[192,512]{1,0:T(8,128)(2,1)S(1)} %get-tuple-element.128), channel_id=1, source_target_pairs={{0,6},{2,4},{4,2},{6,0},{1,7},{3,5},{5,3},{7,1},{8,14},{10,12},{12... | collective-permute-start | bytes 589832 | tf_op jit(solution)/shard_map/ppermute | solution.py:853
  55.7 29.9 %all-to-all-start.1 = ((bf16[4,128,1024]{2,1,0:T(8,128)(2,1)}), bf16[4,128,1024]{2,1,0:T(8,128)(2,1)}, u32[]{:S(2)}, u32[]{:S(2)}) async-start(bf16[4,128,1024]{2,1,0:T(8,128)(2,1)} %broadcast_in_dim.14), calls=%async_computation.1 | async-start | bytes 2097152 | tf_op jit(solution)/shard_map/all_to_all | solution.py:841
  60.0 164.1 %reduce-scatter.2.cloned.1.call-start = ((), (), s32[]{:S(2)}) async-start(), calls=%async_computation.6 | async-start | bytes 5308416 | tf_op jit(solution)/shard_map/reduce_scatter | solution.py:972
  80.8 7.8 %collective-permute-start.13 = (bf16[64,512]{1,0:T(8,128)(2,1)S(1)}, bf16[64,512]{1,0:T(8,128)(2,1)S(1)}, u32[]{:S(2)}, u32[]{:S(2)}) collective-permute-start(bf16[64,512]{1,0:T(8,128)(2,1)S(1)} %get-tuple-element.131), channel_id=1, source_target_pairs={{0,8},{8,0},{16,24},{24,16},{1,9},{9,1},{17,25},{25,17},{2,10},{10... | collective-permute-start | bytes 196616 | tf_op jit(solution)/shard_map/ppermute | solution.py:858
  82.8 8.5 %collective-permute-start.14 = (bf16[64,512]{1,0:T(8,128)(2,1)S(1)}, bf16[64,512]{1,0:T(8,128)(2,1)S(1)}, u32[]{:S(2)}, u32[]{:S(2)}) collective-permute-start(bf16[64,512]{1,0:T(8,128)(2,1)S(1)} %get-tuple-element.132), channel_id=1, source_target_pairs={{0,16},{8,24},{16,0},{24,8},{1,17},{9,25},{17,1},{25,9},{2,18},{10... | collective-permute-start | bytes 196616 | tf_op jit(solution)/shard_map/ppermute | solution.py:858
  84.3 9.2 %collective-permute-start.15 = (bf16[64,512]{1,0:T(8,128)(2,1)S(1)}, bf16[64,512]{1,0:T(8,128)(2,1)S(1)}, u32[]{:S(2)}, u32[]{:S(2)}) collective-permute-start(bf16[64,512]{1,0:T(8,128)(2,1)S(1)} %get-tuple-element.133), channel_id=1, source_target_pairs={{0,24},{8,16},{16,8},{24,0},{1,25},{9,17},{17,9},{25,1},{2,26},{10... | collective-permute-start | bytes 196616 | tf_op jit(solution)/shard_map/ppermute | solution.py:858
  96.1 6.4 %collective-permute-start.16 = (bf16[128,1024]{1,0:T(8,128)(2,1)S(1)}, bf16[128,1024]{1,0:T(8,128)(2,1)S(1)}, u32[]{:S(2)}, u32[]{:S(2)}) collective-permute-start(bf16[128,1024]{1,0:T(8,128)(2,1)S(1)} %get-tuple-element.137), channel_id=1, source_target_pairs={{0,2},{2,0},{1,3},{3,1},{4,6},{6,4},{5,7},{7,5},{8,10},{10,8},{9,1... | collective-permute-start | bytes 786440 | tf_op jit(solution)/shard_map/ppermute | solution.py:851
  96.2 13.5 %collective-permute-start.17 = (bf16[128,1024]{1,0:T(8,128)(2,1)S(1)}, bf16[128,1024]{1,0:T(8,128)(2,1)S(1)}, u32[]{:S(2)}, u32[]{:S(2)}) collective-permute-start(bf16[128,1024]{1,0:T(8,128)(2,1)S(1)} %get-tuple-element.138), channel_id=1, source_target_pairs={{0,4},{4,0},{1,5},{5,1},{2,6},{6,2},{3,7},{7,3},{8,12},{12,8},{9,1... | collective-permute-start | bytes 786440 | tf_op jit(solution)/shard_map/ppermute | solution.py:852
  99.1 10.6 %collective-permute-start.18 = (bf16[128,1024]{1,0:T(8,128)(2,1)S(1)}, bf16[128,1024]{1,0:T(8,128)(2,1)S(1)}, u32[]{:S(2)}, u32[]{:S(2)}) collective-permute-start(bf16[128,1024]{1,0:T(8,128)(2,1)S(1)} %get-tuple-element.139), channel_id=1, source_target_pairs={{0,6},{2,4},{4,2},{6,0},{1,7},{3,5},{5,3},{7,1},{8,14},{10,12},{12... | collective-permute-start | bytes 786440 | tf_op jit(solution)/shard_map/ppermute | solution.py:853
  112.6 8.7 %collective-permute-start.21 = (bf16[128,1024]{1,0:T(8,128)(2,1)S(1)}, bf16[128,1024]{1,0:T(8,128)(2,1)S(1)}, u32[]{:S(2)}, u32[]{:S(2)}) collective-permute-start(bf16[128,1024]{1,0:T(8,128)(2,1)S(1)} %get-tuple-element.143.refs_2_.refs_3_), channel_id=1, source_target_pairs={{0,6},{2,4},{4,2},{6,0},{1,7},{3,5},{5,3},{7,1},{8,14},{10,12},{12... | collective-permute-start | bytes 786440 | tf_op jit(solution)/shard_map/ppermute | solution.py:853
  116.9 7.2 %collective-permute-start.20 = (bf16[128,1024]{1,0:T(8,128)(2,1)S(1)}, bf16[128,1024]{1,0:T(8,128)(2,1)S(1)}, u32[]{:S(2)}, u32[]{:S(2)}) collective-permute-start(bf16[128,1024]{1,0:T(8,128)(2,1)S(1)} %get-tuple-element.143.refs_2_.refs_3_), channel_id=1, source_target_pairs={{0,4},{4,0},{1,5},{5,1},{2,6},{6,2},{3,7},{7,3},{8,12},{12,8},{9,1... | collective-permute-start | bytes 786440 | tf_op jit(solution)/shard_map/ppermute | solution.py:852
  116.9 7.2 %collective-permute-start.19 = (bf16[128,1024]{1,0:T(8,128)(2,1)S(1)}, bf16[128,1024]{1,0:T(8,128)(2,1)S(1)}, u32[]{:S(2)}, u32[]{:S(2)}) collective-permute-start(bf16[128,1024]{1,0:T(8,128)(2,1)S(1)} %get-tuple-element.143.refs_2_.refs_3_), channel_id=1, source_target_pairs={{0,2},{2,0},{1,3},{3,1},{4,6},{6,4},{5,7},{7,5},{8,10},{10,8},{9,1... | collective-permute-start | bytes 786440 | tf_op jit(solution)/shard_map/ppermute | solution.py:851
  132.6 11.4 %collective-permute-start.22 = (bf16[128,1024]{1,0:T(8,128)(2,1)S(1)}, bf16[128,1024]{1,0:T(8,128)(2,1)S(1)}, u32[]{:S(2)}, u32[]{:S(2)}) collective-permute-start(bf16[128,1024]{1,0:T(8,128)(2,1)S(1)} %get-tuple-element.153), channel_id=1, source_target_pairs={{0,2},{2,0},{1,3},{3,1},{4,6},{6,4},{5,7},{7,5},{8,10},{10,8},{9,1... | collective-permute-start | bytes 786440 | tf_op jit(solution)/shard_map/ppermute | solution.py:851
  134.7 12.0 %collective-permute-start.23 = (bf16[128,1024]{1,0:T(8,128)(2,1)S(1)}, bf16[128,1024]{1,0:T(8,128)(2,1)S(1)}, u32[]{:S(2)}, u32[]{:S(2)}) collective-permute-start(bf16[128,1024]{1,0:T(8,128)(2,1)S(1)} %get-tuple-element.154), channel_id=1, source_target_pairs={{0,4},{4,0},{1,5},{5,1},{2,6},{6,2},{3,7},{7,3},{8,12},{12,8},{9,1... | collective-permute-start | bytes 786440 | tf_op jit(solution)/shard_map/ppermute | solution.py:852
  135.3 11.4 %collective-permute-start.24 = (bf16[128,1024]{1,0:T(8,128)(2,1)S(1)}, bf16[128,1024]{1,0:T(8,128)(2,1)S(1)}, u32[]{:S(2)}, u32[]{:S(2)}) collective-permute-start(bf16[128,1024]{1,0:T(8,128)(2,1)S(1)} %get-tuple-element.155), channel_id=1, source_target_pairs={{0,6},{2,4},{4,2},{6,0},{1,7},{3,5},{5,3},{7,1},{8,14},{10,12},{12... | collective-permute-start | bytes 786440 | tf_op jit(solution)/shard_map/ppermute | solution.py:853
  149.7 7.4 %collective-permute-start.27 = (bf16[128,1024]{1,0:T(8,128)(2,1)S(1)}, bf16[128,1024]{1,0:T(8,128)(2,1)S(1)}, u32[]{:S(2)}, u32[]{:S(2)}) collective-permute-start(bf16[128,1024]{1,0:T(8,128)(2,1)S(1)} %get-tuple-element.157.refs_3_), channel_id=1, source_target_pairs={{0,6},{2,4},{4,2},{6,0},{1,7},{3,5},{5,3},{7,1},{8,14},{10,12},{12... | collective-permute-start | bytes 786440 | tf_op jit(solution)/shard_map/ppermute | solution.py:853
  149.8 9.2 %collective-permute-start.26 = (bf16[128,1024]{1,0:T(8,128)(2,1)S(1)}, bf16[128,1024]{1,0:T(8,128)(2,1)S(1)}, u32[]{:S(2)}, u32[]{:S(2)}) collective-permute-start(bf16[128,1024]{1,0:T(8,128)(2,1)S(1)} %get-tuple-element.157.refs_3_), channel_id=1, source_target_pairs={{0,4},{4,0},{1,5},{5,1},{2,6},{6,2},{3,7},{7,3},{8,12},{12,8},{9,1... | collective-permute-start | bytes 786440 | tf_op jit(solution)/shard_map/ppermute | solution.py:852
  150.5 8.6 %collective-permute-start.25 = (bf16[128,1024]{1,0:T(8,128)(2,1)S(1)}, bf16[128,1024]{1,0:T(8,128)(2,1)S(1)}, u32[]{:S(2)}, u32[]{:S(2)}) collective-permute-start(bf16[128,1024]{1,0:T(8,128)(2,1)S(1)} %get-tuple-element.157.refs_3_), channel_id=1, source_target_pairs={{0,2},{2,0},{1,3},{3,1},{4,6},{6,4},{5,7},{7,5},{8,10},{10,8},{9,1... | collective-permute-start | bytes 786440 | tf_op jit(solution)/shard_map/ppermute | solution.py:851
  161.8 8.0 %collective-permute-start.28 = (bf16[64,512]{1,0:T(8,128)(2,1)S(1)}, bf16[64,512]{1,0:T(8,128)(2,1)S(1)}, u32[]{:S(2)}, u32[]{:S(2)}) collective-permute-start(bf16[64,512]{1,0:T(8,128)(2,1)S(1)} %get-tuple-element.161), channel_id=1, source_target_pairs={{0,8},{8,0},{16,24},{24,16},{1,9},{9,1},{17,25},{25,17},{2,10},{10... | collective-permute-start | bytes 196616 | tf_op jit(solution)/shard_map/ppermute | solution.py:858
  161.8 7.9 %collective-permute-start.29 = (bf16[64,512]{1,0:T(8,128)(2,1)S(1)}, bf16[64,512]{1,0:T(8,128)(2,1)S(1)}, u32[]{:S(2)}, u32[]{:S(2)}) collective-permute-start(bf16[64,512]{1,0:T(8,128)(2,1)S(1)} %get-tuple-element.162), channel_id=1, source_target_pairs={{0,16},{8,24},{16,0},{24,8},{1,17},{9,25},{17,1},{25,9},{2,18},{10... | collective-permute-start | bytes 196616 | tf_op jit(solution)/shard_map/ppermute | solution.py:858
  162.3 7.4 %collective-permute-start.30 = (bf16[64,512]{1,0:T(8,128)(2,1)S(1)}, bf16[64,512]{1,0:T(8,128)(2,1)S(1)}, u32[]{:S(2)}, u32[]{:S(2)}) collective-permute-start(bf16[64,512]{1,0:T(8,128)(2,1)S(1)} %get-tuple-element.163), channel_id=1, source_target_pairs={{0,24},{8,16},{16,8},{24,0},{1,25},{9,17},{17,9},{25,1},{2,26},{10... | collective-permute-start | bytes 196616 | tf_op jit(solution)/shard_map/ppermute | solution.py:858
  166.2 20.7 %all-to-all-start.2 = ((bf16[4,128,1024]{2,1,0:T(8,128)(2,1)}), bf16[4,128,1024]{2,1,0:T(8,128)(2,1)S(1)}, u32[]{:S(2)}, u32[]{:S(2)}) async-start(bf16[4,128,1024]{2,1,0:T(8,128)(2,1)} %get-tuple-element.149), calls=%async_computation.2 | async-start | bytes 2097152 | tf_op jit(solution)/shard_map/all_to_all | solution.py:841
  183.3 6.1 %collective-permute-start.31 = (bf16[192,512]{1,0:T(8,128)(2,1)S(1)}, bf16[192,512]{1,0:T(8,128)(2,1)S(1)}, u32[]{:S(2)}, u32[]{:S(2)}) collective-permute-start(bf16[192,512]{1,0:T(8,128)(2,1)S(1)} %get-tuple-element.172), channel_id=1, source_target_pairs={{0,2},{2,0},{1,3},{3,1},{4,6},{6,4},{5,7},{7,5},{8,10},{10,8},{9,1... | collective-permute-start | bytes 589832 | tf_op jit(solution)/shard_map/ppermute | solution.py:851
  185.3 6.8 %collective-permute-start.32 = (bf16[192,512]{1,0:T(8,128)(2,1)S(1)}, bf16[192,512]{1,0:T(8,128)(2,1)S(1)}, u32[]{:S(2)}, u32[]{:S(2)}) collective-permute-start(bf16[192,512]{1,0:T(8,128)(2,1)S(1)} %get-tuple-element.173), channel_id=1, source_target_pairs={{0,4},{4,0},{1,5},{5,1},{2,6},{6,2},{3,7},{7,3},{8,12},{12,8},{9,1... | collective-permute-start | bytes 589832 | tf_op jit(solution)/shard_map/ppermute | solution.py:852
  186.8 6.6 %collective-permute-start.33 = (bf16[192,512]{1,0:T(8,128)(2,1)S(1)}, bf16[192,512]{1,0:T(8,128)(2,1)S(1)}, u32[]{:S(2)}, u32[]{:S(2)}) collective-permute-start(bf16[192,512]{1,0:T(8,128)(2,1)S(1)} %get-tuple-element.174), channel_id=1, source_target_pairs={{0,6},{2,4},{4,2},{6,0},{1,7},{3,5},{5,3},{7,1},{8,14},{10,12},{12... | collective-permute-start | bytes 589832 | tf_op jit(solution)/shard_map/ppermute | solution.py:853
  201.4 1.9 collective-permute-start.37
  201.5 2.6 %collective-permute-start.38 = (bf16[2,4,32,896]{3,2,1,0:T(8,128)(2,1)S(1)}, bf16[2,4,32,896]{3,2,1,0:T(8,128)(2,1)S(1)}, u32[]{:S(2)}, u32[]{:S(2)}) collective-permute-start(bf16[2,4,32,896]{3,2,1,0:T(8,128)(2,1)S(1)} %get-tuple-element.185), channel_id=1, source_target_pairs={{0,1},{1,0},{2,3},{3,2},{4,5},{5,4},{6,7},{7,6},{8,9},{9,8},{10,11... | collective-permute-start | bytes 1376264 | tf_op jit(solution)/shard_map/ppermute | solution.py:866
  206.0 8.5 %collective-permute-start.39 = (bf16[4,32,896]{2,1,0:T(8,128)(2,1)S(1)}, bf16[4,32,896]{2,1,0:T(8,128)(2,1)S(1)}, u32[]{:S(2)}, u32[]{:S(2)}) collective-permute-start(bf16[4,32,896]{2,1,0:T(8,128)(2,1)S(1)} %get-tuple-element.188), channel_id=1, source_target_pairs={{0,2},{2,0},{1,3},{3,1},{4,6},{6,4},{5,7},{7,5},{8,10},{10,8},{9,1... | collective-permute-start | bytes 688136 | tf_op jit(solution)/shard_map/ppermute | solution.py:851
  206.7 10.3 %collective-permute-start.40 = (bf16[4,32,896]{2,1,0:T(8,128)(2,1)S(1)}, bf16[4,32,896]{2,1,0:T(8,128)(2,1)S(1)}, u32[]{:S(2)}, u32[]{:S(2)}) collective-permute-start(bf16[4,32,896]{2,1,0:T(8,128)(2,1)S(1)} %get-tuple-element.189), channel_id=1, source_target_pairs={{0,4},{4,0},{1,5},{5,1},{2,6},{6,2},{3,7},{7,3},{8,12},{12,8},{9,1... | collective-permute-start | bytes 688136 | tf_op jit(solution)/shard_map/ppermute | solution.py:852
  207.8 11.5 %collective-permute-start.41 = (bf16[4,32,896]{2,1,0:T(8,128)(2,1)S(1)}, bf16[4,32,896]{2,1,0:T(8,128)(2,1)S(1)}, u32[]{:S(2)}, u32[]{:S(2)}) collective-permute-start(bf16[4,32,896]{2,1,0:T(8,128)(2,1)S(1)} %get-tuple-element.190), channel_id=1, source_target_pairs={{0,6},{2,4},{4,2},{6,0},{1,7},{3,5},{5,3},{7,1},{8,14},{10,12},{12... | collective-permute-start | bytes 688136 | tf_op jit(solution)/shard_map/ppermute | solution.py:853
  209.6 20.6 %collective-permute-start.34 = (bf16[128,1024]{1,0:T(8,128)(2,1)S(1)}, bf16[128,1024]{1,0:T(8,128)(2,1)S(1)}, u32[]{:S(2)}, u32[]{:S(2)}) collective-permute-start(bf16[128,1024]{1,0:T(8,128)(2,1)S(1)} %get-tuple-element.179), channel_id=1, source_target_pairs={{0,8},{8,0},{16,24},{24,16},{1,9},{9,1},{17,25},{25,17},{2,10},{10... | collective-permute-start | bytes 786440 | tf_op jit(solution)/shard_map/ppermute | solution.py:858
  209.6 21.6 %collective-permute-start.35 = (bf16[128,1024]{1,0:T(8,128)(2,1)S(1)}, bf16[128,1024]{1,0:T(8,128)(2,1)S(1)}, u32[]{:S(2)}, u32[]{:S(2)}) collective-permute-start(bf16[128,1024]{1,0:T(8,128)(2,1)S(1)} %get-tuple-element.180), channel_id=1, source_target_pairs={{0,16},{8,24},{16,0},{24,8},{1,17},{9,25},{17,1},{25,9},{2,18},{10... | collective-permute-start | bytes 786440 | tf_op jit(solution)/shard_map/ppermute | solution.py:858
  214.5 16.7 %collective-permute-start.36 = (bf16[128,1024]{1,0:T(8,128)(2,1)S(1)}, bf16[128,1024]{1,0:T(8,128)(2,1)S(1)}, u32[]{:S(2)}, u32[]{:S(2)}) collective-permute-start(bf16[128,1024]{1,0:T(8,128)(2,1)S(1)} %get-tuple-element.181), channel_id=1, source_target_pairs={{0,24},{8,16},{16,8},{24,0},{1,25},{9,17},{17,9},{25,1},{2,26},{10... | collective-permute-start | bytes 786440 | tf_op jit(solution)/shard_map/ppermute | solution.py:858
  220.6 14.1 %collective-permute-start.42 = (bf16[32,896]{1,0:T(8,128)(2,1)S(1)}, bf16[32,896]{1,0:T(8,128)(2,1)S(1)}, u32[]{:S(2)}, u32[]{:S(2)}) collective-permute-start(bf16[32,896]{1,0:T(8,128)(2,1)S(1)} %get-tuple-element.196), channel_id=1, source_target_pairs={{0,8},{8,0},{16,24},{24,16},{1,9},{9,1},{17,25},{25,17},{2,10},{10... | collective-permute-start | bytes 172040 | tf_op jit(solution)/shard_map/ppermute | solution.py:858
  220.7 19.7 %collective-permute-start.43 = (bf16[32,896]{1,0:T(8,128)(2,1)S(1)}, bf16[32,896]{1,0:T(8,128)(2,1)S(1)}, u32[]{:S(2)}, u32[]{:S(2)}) collective-permute-start(bf16[32,896]{1,0:T(8,128)(2,1)S(1)} %get-tuple-element.197), channel_id=1, source_target_pairs={{0,16},{8,24},{16,0},{24,8},{1,17},{9,25},{17,1},{25,9},{2,18},{10... | collective-permute-start | bytes 172040 | tf_op jit(solution)/shard_map/ppermute | solution.py:858
  224.1 1.1 copy-start.2
  226.7 15.6 %all-to-all-start.3 = ((bf16[4,32,1024]{2,1,0:T(8,128)(2,1)}), bf16[4,32,1024]{2,1,0:T(8,128)(2,1)S(1)}, u32[]{:S(2)}, u32[]{:S(2)}) async-start(bf16[4,32,1024]{2,1,0:T(8,128)(2,1)} %get-tuple-element.210), calls=%async_computation.4 | async-start | bytes 524288 | tf_op jit(solution)/shard_map/all_to_all | solution.py:841
  230.2 10.3 %collective-permute-start.44 = (bf16[32,896]{1,0:T(8,128)(2,1)S(1)}, bf16[32,896]{1,0:T(8,128)(2,1)S(1)}, u32[]{:S(2)}, u32[]{:S(2)}) collective-permute-start(bf16[32,896]{1,0:T(8,128)(2,1)S(1)} %get-tuple-element.198), channel_id=1, source_target_pairs={{0,24},{8,16},{16,8},{24,0},{1,25},{9,17},{17,9},{25,1},{2,26},{10... | collective-permute-start | bytes 172040 | tf_op jit(solution)/shard_map/ppermute | solution.py:858
Sparse Core Ops, SparseCore 0:
  9.6 33.5 all-gather.5
  45.3 22.7 all-gather.7
  70.4 46.9 all-gather.9
  161.9 53.2 reduce-scatter.1
